TPU v7x, 32 devices: a whole 2x2x4 slice. The times are simulated.
32 devices in a mesh: scen: 2 (over y), lon: 4 (over z), lat: 2 (over x), gau: 2 (over core).
Axes of the slice: x: 2, y: 2, z: 4, core: 2. Of those that a mesh axis runs over, the one named last changes fastest.
Arguments:
- depth: float32 [512, 2048], P(('lat', 'gau'), 'lon'), may hold values from 3 to 6
- surface: float32 [1024, 2048], P(('scen', 'lat', 'gau'), 'lon'), parts along dimension 0, may hold values from -3 to 3
- friction: float32 [512, 2048], P(('lat', 'gau'), 'lon'), may hold values from 0.002 to 0.06
- wet: int32 [512, 2048], P(('lat', 'gau'), 'lon'), may hold values 0 or 1
- coastal_tiles: int32 [8], replicated, may hold values from 0 to 15, as said below
- gauge_route: int32 [512, 1], P(('scen', 'lon', 'lat', 'gau')), parts along dimension 0, may hold values from 0 to 7; in each aligned block of 16 rows (0 to 15, 16 to 31, ...) at most 2 rows name the same one
- gauge_cell: int32 [512], P(('scen', 'lon', 'lat', 'gau')), parts along dimension 0, may hold values from 0 to 65535
- gauge_times: int32 [512, 2, 4], P(('scen', 'lon', 'lat', 'gau')), parts along dimension 0, may hold values from 0 to 7
- gauge_resid: float32 [512, 2, 4], P(('scen', 'lon', 'lat', 'gau')), parts along dimension 0, may hold values from -6 to 6
Outputs:
- smoothed_grad: float32 [1024, 2048], P(('scen', 'lat', 'gau'), 'lon'), parts along dimension 0
There are 2 independent parts, one for each index of `scen`. A program takes and returns all parts, laid end to end along the dimension named above; an argument that names none is the same for every part. Nothing has to cross between parts.
Inputs may be any that keep to these rules, and one draw needn't show every extreme that they name: `coastal_tiles`: 8 distinct tile numbers. `gauge_route`: among the 16 gauges of one owner (aligned blocks of rows) no entry is named more than 2 times; in every draw some owner names one entry exactly 2 times.
All inputs are finite; a program needn't handle non-finite values. No bound on the sum of `wet` on one device may be relied on, other than what follows from the above.
Results may differ from a plain program's by a relative error of at most 0.00022.
Values sent between devices are 32-bit elements; how exact they have to be, the bound alone decides.
No kernel may reach another device: no remote copies, remote signals or barrier semaphores. Data moves between devices by JAX's collectives and lax.ppermute only.
A program may use at most 64 MiB of HBM per device.

v0:
```python
import jax
import jax.numpy as jnp
from jax import lax
from jax.sharding import PartitionSpec as P

STEPS_BLOCK = 8
CAP = 2


courant = 0.45
depth_floor = 0.1


def with_halo(cells, sides, width):
    for axis, dim in sides:
        count = lax.axis_size(axis)
        ends = count - 1
        head = lax.slice_in_dim(cells, 0, width, axis=dim)
        tail = lax.slice_in_dim(cells, cells.shape[dim] - width, cells.shape[dim], axis=dim)
        cells = jnp.concatenate(
            [
                lax.ppermute(tail, axis, [(i, (i + 1) % count) for i in range(ends)]),
                cells,
                lax.ppermute(head, axis, [((i + 1) % count, i) for i in range(ends)]),
            ],
            axis=dim,
        )
    return cells


def sectioned_step(state, total_depth, strength):
    surface_adj, flux_x, flux_y = state
    extended = with_halo(surface_adj, (("lon", 1), (("lat", "gau"), 0)), 1)
    east_west = (extended[1:-1, 2:] - extended[1:-1, :-2]) * 0.5
    north_south = (extended[2:, 1:-1] - extended[:-2, 1:-1]) * 0.5
    new_x = strength * (flux_x + courant * east_west)
    new_y = strength * (flux_y + courant * north_south)
    carried = jnp.stack([total_depth * new_x, total_depth * new_y])
    beside_all = with_halo(carried, (("lon", 2), (("lat", "gau"), 1)), 1)
    spread_term = (beside_all[0, 1:-1, 2:] - beside_all[0, 1:-1, :-2]) * 0.5 + (
        beside_all[1, 2:, 1:-1] - beside_all[1, :-2, 1:-1]
    ) * 0.5
    return (surface_adj + courant * spread_term, new_x, new_y)


def build_forcing(rows, places, height, width):
    levels = rows.shape[-1]
    flat_rows = rows.reshape(-1, levels)
    cells = places.reshape(-1).astype(jnp.int32)
    row_onehot = ((cells // width)[:, None] == jnp.arange(height, dtype=jnp.int32)[None, :]).astype(
        jnp.float32
    )
    col_onehot = ((cells % width)[:, None] == jnp.arange(width, dtype=jnp.int32)[None, :]).astype(
        jnp.float32
    )
    weighted = (flat_rows[:, :, None] * row_onehot[:, None, :]).reshape(
        flat_rows.shape[0], levels * height
    )
    forcing = lax.dot_general(
        weighted,
        col_onehot,
        (((0,), (0,)), ((), ())),
        precision=lax.Precision.HIGHEST,
        preferred_element_type=jnp.float32,
    )
    return forcing.reshape(levels, height, width)


def run_block(state, forcing, stepper):
    count = forcing.shape[0]

    def advance(index, carry):
        level = count - 1 - index
        push = lax.dynamic_index_in_dim(forcing, level, 0, keepdims=False)
        return stepper((carry[0] + push, carry[1], carry[2]))

    return lax.fori_loop(0, count, advance, state)


def local(
    depth, surface, friction, wet, coastal_tiles, gauge_route, gauge_cell, gauge_times, gauge_resid
):
    height, width = depth.shape
    wet_float = wet.astype(jnp.float32)
    total_depth = jnp.maximum(depth + surface, depth_floor)
    strength = (1.0 - friction) * wet_float
    tiles = lax.axis_size(("lon", "lat", "gau"))
    owned = gauge_route.shape[0]
    blocks = gauge_resid.shape[1]
    levels_count = STEPS_BLOCK
    route = gauge_route[:, 0]
    coast_count = coastal_tiles.shape[0]
    matches = route[:, None] == jnp.arange(coast_count, dtype=jnp.int32)[None, :]
    target = jnp.sum(jnp.where(matches, coastal_tiles[None, :], 0), axis=1)
    order = jnp.arange(owned, dtype=jnp.int32)
    earlier = (route[:, None] == route[None, :]) & (order[:, None] > order[None, :])
    slot = jnp.sum(earlier.astype(jnp.int32), axis=1)
    column = target * CAP + slot
    select = (column[:, None] == jnp.arange(tiles * CAP, dtype=jnp.int32)[None, :]).astype(
        jnp.float32
    )
    levels = jnp.arange(levels_count, dtype=jnp.int32)
    series = jnp.sum(
        gauge_resid[..., None] * (gauge_times[..., None] == levels).astype(jnp.float32), axis=2
    )
    send_series = lax.dot_general(
        select,
        series.reshape(owned, blocks * levels_count),
        (((0,), (0,)), ((), ())),
        precision=lax.Precision.HIGHEST,
        preferred_element_type=jnp.float32,
    ).reshape(tiles, CAP, blocks, levels_count)
    send_place = lax.dot_general(
        select,
        gauge_cell.astype(jnp.float32)[:, None],
        (((0,), (0,)), ((), ())),
        precision=lax.Precision.HIGHEST,
        preferred_element_type=jnp.float32,
    ).reshape(tiles, CAP)

    def stepper(state):
        return sectioned_step(state, total_depth, strength)

    zeros = jnp.zeros((height, width), jnp.float32)
    state = (zeros, zeros, zeros)
    for block in reversed(range(blocks)):
        rows, places = (
            lax.all_to_all(
                send_series[:, :, block, :],
                ("lon", "lat", "gau"),
                split_axis=0,
                concat_axis=0,
                tiled=True,
            ),
            lax.all_to_all(
                send_place, ("lon", "lat", "gau"), split_axis=0, concat_axis=0, tiled=True
            ),
        )
        forcing = build_forcing(rows, places, height, width)
        state = run_block(state, forcing, stepper)
    grad = state[0] * wet_float
    length = 2.0 * width
    my_start = lax.axis_index("lon") * width
    outputs = my_start + jnp.arange(width, dtype=jnp.int32)
    piece = lax.all_gather(grad, "lon", axis=1, tiled=True)
    inputs = jnp.arange(piece.shape[1], dtype=jnp.int32)
    kernel = jnp.exp(-jnp.abs(inputs[:, None] - outputs[None, :]).astype(jnp.float32) / length)
    return jnp.dot(
        piece, kernel, precision=lax.Precision.HIGHEST, preferred_element_type=jnp.float32
    )


def solution(mesh):
    in_specs = (
        P(("lat", "gau"), "lon"),
        P(("scen", "lat", "gau"), "lon"),
        P(("lat", "gau"), "lon"),
        P(("lat", "gau"), "lon"),
        P(),
        P(("scen", "lon", "lat", "gau"), None),
        P(("scen", "lon", "lat", "gau")),
        P(("scen", "lon", "lat", "gau"), None, None),
        P(("scen", "lon", "lat", "gau"), None, None),
    )
    out_specs = P(("scen", "lat", "gau"), "lon")
    return jax.shard_map(local, mesh=mesh, in_specs=in_specs, out_specs=out_specs, check_vma=False)
```

profile of v0, /device:TPU:0, one launch (start us, length us, event | category | flops | bytes accessed | tf_op | source)
XLA Modules:
  0.0 641.5 jit_solution(3714691453826822251)
XLA Ops:
  9.8 7.4 %all-to-all-start.1 = ((f32[16,1,2]{2,1,0:T(1,128)}), f32[16,1,2]{2,1,0:T(1,128)S(1)}, u32[]{:S(2)}, u32[]{:S(2)}) async-start(f32[16,1,2]{2,1,0:T(1,128)} %copy.33), calls=%async_computation.1 | async-start | bytes 16384 | tf_op jit(solution)/shard_map/all_to_all | solution.py:135
  23.6 3.5 all-to-all-start
  27.2 6.3 all-to-all-done
  33.5 3.5 all-to-all-start.2
  37.1 6.3 all-to-all-done.2
  48.4 273.3 %while.42 = (s32[]{:T(128)}, f32[128,512]{1,0:T(8,128)S(1)}, f32[128,512]{1,0:T(8,128)S(1)}, f32[128,512]{1,0:T(8,128)S(1)}, f32[8,128,512]{2,1,0:T(8,128)}, /*i...) while((s32[]{:T(128)}, f32[128,512]{1,0:T(8,128)S(1)}, ...), condition=%wide.region_4.5_spmd.clone, body=%wide.region_3.4_spmd.clone.sunk | while | flops 2564647 | bytes 5602058 | solution.py:77
  53.7 4.3 collective-permute-done.9
  64.9 4.6 collective-permute-start.13
  80.3 4.3 collective-permute-start.8
  86.6 4.3 collective-permute-done.9
  99.6 4.6 collective-permute-start.13
  107.0 3.1 collective-permute-start.14
  115.0 4.3 collective-permute-start.8
  121.2 4.3 collective-permute-done.9
  134.2 4.6 collective-permute-start.13
  141.6 3.1 collective-permute-start.14
  149.6 4.3 collective-permute-start.8
  155.8 4.3 collective-permute-done.9
  168.8 4.6 collective-permute-start.13
  176.2 3.1 collective-permute-start.14
  184.2 4.3 collective-permute-start.8
  190.5 4.3 collective-permute-done.9
  203.5 4.6 collective-permute-start.13
  218.9 4.3 collective-permute-start.8
  225.1 4.3 collective-permute-done.9
  238.1 4.6 collective-permute-start.13
  245.5 3.1 collective-permute-start.14
  253.5 4.3 collective-permute-start.8
  259.7 4.3 collective-permute-done.9
  272.7 4.6 collective-permute-start.13
  280.1 3.1 collective-permute-start.14
  288.1 4.3 collective-permute-start.8
  294.4 4.3 collective-permute-done.9
  307.4 4.6 collective-permute-start.13
  321.7 277.4 %while.41 = (s32[]{:T(128)}, f32[128,512]{1,0:T(8,128)S(1)}, f32[128,512]{1,0:T(8,128)S(1)}, f32[128,512]{1,0:T(8,128)S(1)}, f32[8,128,512]{2,1,0:T(8,128)}, /*i...) while((s32[]{:T(128)}, f32[128,512]{1,0:T(8,128)S(1)}, ...), condition=%wide.region_6.7_spmd, body=%wide.region_5.6_spmd.sunk | while | flops 2368038 | bytes 5602047 | solution.py:77
  322.8 4.3 collective-permute-start
  329.0 4.3 collective-permute-done.1
  342.1 4.6 collective-permute-start.5
  349.5 3.1 collective-permute-start.6
  357.5 4.3 collective-permute-start
  363.7 4.3 collective-permute-done.1
  376.7 4.6 collective-permute-start.5
  392.1 4.3 collective-permute-start
  398.4 4.3 collective-permute-done.1
  411.4 4.6 collective-permute-start.5
  418.8 3.1 collective-permute-start.6
  426.8 4.3 collective-permute-start
  433.0 4.3 collective-permute-done.1
  446.1 4.6 collective-permute-start.5
  461.5 4.3 collective-permute-start
  467.7 4.3 collective-permute-done.1
  480.7 4.6 collective-permute-start.5
  488.1 3.1 collective-permute-start.6
  496.1 4.3 collective-permute-start
  502.4 4.3 collective-permute-done.1
  515.4 4.6 collective-permute-start.5
  530.8 4.3 collective-permute-start
  537.0 4.3 collective-permute-done.1
  550.1 4.6 collective-permute-start.5
  565.5 4.3 collective-permute-start
  571.7 4.3 collective-permute-done.1
  584.7 4.6 collective-permute-start.5
  599.8 29.4 %all-gather.2.cloned.1.call-done = f32[128,2048]{1,0:T(8,128)} async-done(((f32[128,512]{1,0:T(8,128)}), f32[128,2048]{1,0:T(8,128)}) %all-gather.2.cloned.1.call-update) | async-done | bytes 1048592 | tf_op jit(solution)/shard_map/all_gather | solution.py:145
  629.2 5.5 fusion.28
  (342 shorter events, 332.5 us)
Async XLA Ops:
  9.8 13.8 %all-to-all-start.1 = ((f32[16,1,2]{2,1,0:T(1,128)}), f32[16,1,2]{2,1,0:T(1,128)S(1)}, u32[]{:S(2)}, u32[]{:S(2)}) async-start(f32[16,1,2]{2,1,0:T(1,128)} %copy.33), calls=%async_computation.1 | async-start | bytes 16384 | tf_op jit(solution)/shard_map/all_to_all | solution.py:135
  23.6 9.9 %all-to-all-start = ((f32[16,2,8]{2,1,0:T(2,128)}), f32[16,2,8]{2,1,0:T(2,128)S(1)}, u32[]{:S(2)}, u32[]{:S(2)}) async-start(f32[16,2,8]{2,1,0:T(2,128)} %copy.32), calls=%async_computation | async-start | bytes 32768 | tf_op jit(solution)/shard_map/all_to_all | solution.py:128
  33.5 10.0 %all-to-all-start.2 = ((f32[16,2,8]{2,1,0:T(2,128)}), f32[16,2,8]{2,1,0:T(2,128)S(1)}, u32[]{:S(2)}, u32[]{:S(2)}) async-start(f32[16,2,8]{2,1,0:T(2,128)} %copy.35), calls=%async_computation.2 | async-start | bytes 32768 | tf_op jit(solution)/shard_map/all_to_all | solution.py:128
  37.0 592.2 %all-gather.2.cloned.1.call-start = ((), (), s32[]{:S(2)}) async-start(), calls=%async_computation.3 | async-start | bytes 1310720 | tf_op jit(solution)/shard_map/all_gather | solution.py:145
  51.8 6.2 collective-permute-start.9
  63.6 6.9 %collective-permute-start.12 = (f32[2,128,1]{2,1,0:T(8,128)S(1)}, f32[2,128,1]{2,1,0:T(8,128)S(1)}, u32[]{:S(2)}, u32[]{:S(2)}) collective-permute-start(f32[2,128,1]{2,1,0:T(8,128)S(1)} %get-tuple-element.627), channel_id=1, source_target_pairs={{4,0},{8,4},{12,8},{5,1},{9,5},{13,9},{6,2},{10,6},{14,10},{7,3},{... | collective-permute-start | bytes 3080 | tf_op jit(solution)/shard_map/while/body/eval_jaxpr/ppermute | solution.py:24
  64.9 7.3 %collective-permute-start.13 = (f32[2,128,1]{2,1,0:T(8,128)S(1)}, f32[2,128,1]{2,1,0:T(8,128)S(1)}, u32[]{:S(2)}, u32[]{:S(2)}) collective-permute-start(f32[2,128,1]{2,1,0:T(8,128)S(1)} %get-tuple-element.628), channel_id=1, source_target_pairs={{0,4},{4,8},{8,12},{1,5},{5,9},{9,13},{2,6},{6,10},{10,14},{3,7},{... | collective-permute-start | bytes 3080 | tf_op jit(solution)/shard_map/while/body/eval_jaxpr/ppermute | solution.py:22
  80.3 6.2 collective-permute-start.8
  84.7 6.2 collective-permute-start.9
  98.3 6.9 %collective-permute-start.12 = (f32[2,128,1]{2,1,0:T(8,128)S(1)}, f32[2,128,1]{2,1,0:T(8,128)S(1)}, u32[]{:S(2)}, u32[]{:S(2)}) collective-permute-start(f32[2,128,1]{2,1,0:T(8,128)S(1)} %get-tuple-element.627), channel_id=1, source_target_pairs={{4,0},{8,4},{12,8},{5,1},{9,5},{13,9},{6,2},{10,6},{14,10},{7,3},{... | collective-permute-start | bytes 3080 | tf_op jit(solution)/shard_map/while/body/eval_jaxpr/ppermute | solution.py:24
  99.6 7.3 %collective-permute-start.13 = (f32[2,128,1]{2,1,0:T(8,128)S(1)}, f32[2,128,1]{2,1,0:T(8,128)S(1)}, u32[]{:S(2)}, u32[]{:S(2)}) collective-permute-start(f32[2,128,1]{2,1,0:T(8,128)S(1)} %get-tuple-element.628), channel_id=1, source_target_pairs={{0,4},{4,8},{8,12},{1,5},{5,9},{9,13},{2,6},{6,10},{10,14},{3,7},{... | collective-permute-start | bytes 3080 | tf_op jit(solution)/shard_map/while/body/eval_jaxpr/ppermute | solution.py:22
  115.0 6.2 collective-permute-start.8
  132.9 6.9 %collective-permute-start.12 = (f32[2,128,1]{2,1,0:T(8,128)S(1)}, f32[2,128,1]{2,1,0:T(8,128)S(1)}, u32[]{:S(2)}, u32[]{:S(2)}) collective-permute-start(f32[2,128,1]{2,1,0:T(8,128)S(1)} %get-tuple-element.627), channel_id=1, source_target_pairs={{4,0},{8,4},{12,8},{5,1},{9,5},{13,9},{6,2},{10,6},{14,10},{7,3},{... | collective-permute-start | bytes 3080 | tf_op jit(solution)/shard_map/while/body/eval_jaxpr/ppermute | solution.py:24
  134.2 7.3 %collective-permute-start.13 = (f32[2,128,1]{2,1,0:T(8,128)S(1)}, f32[2,128,1]{2,1,0:T(8,128)S(1)}, u32[]{:S(2)}, u32[]{:S(2)}) collective-permute-start(f32[2,128,1]{2,1,0:T(8,128)S(1)} %get-tuple-element.628), channel_id=1, source_target_pairs={{0,4},{4,8},{8,12},{1,5},{5,9},{9,13},{2,6},{6,10},{10,14},{3,7},{... | collective-permute-start | bytes 3080 | tf_op jit(solution)/shard_map/while/body/eval_jaxpr/ppermute | solution.py:22
  149.6 6.2 collective-permute-start.8
  154.0 6.2 collective-permute-start.9
  167.5 6.9 %collective-permute-start.12 = (f32[2,128,1]{2,1,0:T(8,128)S(1)}, f32[2,128,1]{2,1,0:T(8,128)S(1)}, u32[]{:S(2)}, u32[]{:S(2)}) collective-permute-start(f32[2,128,1]{2,1,0:T(8,128)S(1)} %get-tuple-element.627), channel_id=1, source_target_pairs={{4,0},{8,4},{12,8},{5,1},{9,5},{13,9},{6,2},{10,6},{14,10},{7,3},{... | collective-permute-start | bytes 3080 | tf_op jit(solution)/shard_map/while/body/eval_jaxpr/ppermute | solution.py:24
  168.8 7.3 %collective-permute-start.13 = (f32[2,128,1]{2,1,0:T(8,128)S(1)}, f32[2,128,1]{2,1,0:T(8,128)S(1)}, u32[]{:S(2)}, u32[]{:S(2)}) collective-permute-start(f32[2,128,1]{2,1,0:T(8,128)S(1)} %get-tuple-element.628), channel_id=1, source_target_pairs={{0,4},{4,8},{8,12},{1,5},{5,9},{9,13},{2,6},{6,10},{10,14},{3,7},{... | collective-permute-start | bytes 3080 | tf_op jit(solution)/shard_map/while/body/eval_jaxpr/ppermute | solution.py:22
  184.2 6.2 collective-permute-start.8
  188.6 6.2 collective-permute-start.9
  202.2 6.9 %collective-permute-start.12 = (f32[2,128,1]{2,1,0:T(8,128)S(1)}, f32[2,128,1]{2,1,0:T(8,128)S(1)}, u32[]{:S(2)}, u32[]{:S(2)}) collective-permute-start(f32[2,128,1]{2,1,0:T(8,128)S(1)} %get-tuple-element.627), channel_id=1, source_target_pairs={{4,0},{8,4},{12,8},{5,1},{9,5},{13,9},{6,2},{10,6},{14,10},{7,3},{... | collective-permute-start | bytes 3080 | tf_op jit(solution)/shard_map/while/body/eval_jaxpr/ppermute | solution.py:24
  203.5 7.3 %collective-permute-start.13 = (f32[2,128,1]{2,1,0:T(8,128)S(1)}, f32[2,128,1]{2,1,0:T(8,128)S(1)}, u32[]{:S(2)}, u32[]{:S(2)}) collective-permute-start(f32[2,128,1]{2,1,0:T(8,128)S(1)} %get-tuple-element.628), channel_id=1, source_target_pairs={{0,4},{4,8},{8,12},{1,5},{5,9},{9,13},{2,6},{6,10},{10,14},{3,7},{... | collective-permute-start | bytes 3080 | tf_op jit(solution)/shard_map/while/body/eval_jaxpr/ppermute | solution.py:22
  218.9 6.2 collective-permute-start.8
  236.8 6.9 %collective-permute-start.12 = (f32[2,128,1]{2,1,0:T(8,128)S(1)}, f32[2,128,1]{2,1,0:T(8,128)S(1)}, u32[]{:S(2)}, u32[]{:S(2)}) collective-permute-start(f32[2,128,1]{2,1,0:T(8,128)S(1)} %get-tuple-element.627), channel_id=1, source_target_pairs={{4,0},{8,4},{12,8},{5,1},{9,5},{13,9},{6,2},{10,6},{14,10},{7,3},{... | collective-permute-start | bytes 3080 | tf_op jit(solution)/shard_map/while/body/eval_jaxpr/ppermute | solution.py:24
  238.1 7.3 %collective-permute-start.13 = (f32[2,128,1]{2,1,0:T(8,128)S(1)}, f32[2,128,1]{2,1,0:T(8,128)S(1)}, u32[]{:S(2)}, u32[]{:S(2)}) collective-permute-start(f32[2,128,1]{2,1,0:T(8,128)S(1)} %get-tuple-element.628), channel_id=1, source_target_pairs={{0,4},{4,8},{8,12},{1,5},{5,9},{9,13},{2,6},{6,10},{10,14},{3,7},{... | collective-permute-start | bytes 3080 | tf_op jit(solution)/shard_map/while/body/eval_jaxpr/ppermute | solution.py:22
  253.5 6.2 collective-permute-start.8
  257.8 6.2 collective-permute-start.9
  271.4 6.9 %collective-permute-start.12 = (f32[2,128,1]{2,1,0:T(8,128)S(1)}, f32[2,128,1]{2,1,0:T(8,128)S(1)}, u32[]{:S(2)}, u32[]{:S(2)}) collective-permute-start(f32[2,128,1]{2,1,0:T(8,128)S(1)} %get-tuple-element.627), channel_id=1, source_target_pairs={{4,0},{8,4},{12,8},{5,1},{9,5},{13,9},{6,2},{10,6},{14,10},{7,3},{... | collective-permute-start | bytes 3080 | tf_op jit(solution)/shard_map/while/body/eval_jaxpr/ppermute | solution.py:24
  272.7 7.3 %collective-permute-start.13 = (f32[2,128,1]{2,1,0:T(8,128)S(1)}, f32[2,128,1]{2,1,0:T(8,128)S(1)}, u32[]{:S(2)}, u32[]{:S(2)}) collective-permute-start(f32[2,128,1]{2,1,0:T(8,128)S(1)} %get-tuple-element.628), channel_id=1, source_target_pairs={{0,4},{4,8},{8,12},{1,5},{5,9},{9,13},{2,6},{6,10},{10,14},{3,7},{... | collective-permute-start | bytes 3080 | tf_op jit(solution)/shard_map/while/body/eval_jaxpr/ppermute | solution.py:22
  288.1 6.2 collective-permute-start.8
  292.5 6.2 collective-permute-start.9
  306.1 6.9 %collective-permute-start.12 = (f32[2,128,1]{2,1,0:T(8,128)S(1)}, f32[2,128,1]{2,1,0:T(8,128)S(1)}, u32[]{:S(2)}, u32[]{:S(2)}) collective-permute-start(f32[2,128,1]{2,1,0:T(8,128)S(1)} %get-tuple-element.627), channel_id=1, source_target_pairs={{4,0},{8,4},{12,8},{5,1},{9,5},{13,9},{6,2},{10,6},{14,10},{7,3},{... | collective-permute-start | bytes 3080 | tf_op jit(solution)/shard_map/while/body/eval_jaxpr/ppermute | solution.py:24
  307.4 7.3 %collective-permute-start.13 = (f32[2,128,1]{2,1,0:T(8,128)S(1)}, f32[2,128,1]{2,1,0:T(8,128)S(1)}, u32[]{:S(2)}, u32[]{:S(2)}) collective-permute-start(f32[2,128,1]{2,1,0:T(8,128)S(1)} %get-tuple-element.628), channel_id=1, source_target_pairs={{0,4},{4,8},{8,12},{1,5},{5,9},{9,13},{2,6},{6,10},{10,14},{3,7},{... | collective-permute-start | bytes 3080 | tf_op jit(solution)/shard_map/while/body/eval_jaxpr/ppermute | solution.py:22
  322.8 6.2 collective-permute-start
  327.2 6.2 collective-permute-start.1
  340.8 6.9 %collective-permute-start.4 = (f32[2,128,1]{2,1,0:T(8,128)S(1)}, f32[2,128,1]{2,1,0:T(8,128)S(1)}, u32[]{:S(2)}, u32[]{:S(2)}) collective-permute-start(f32[2,128,1]{2,1,0:T(8,128)S(1)} %get-tuple-element.608), channel_id=1, source_target_pairs={{4,0},{8,4},{12,8},{5,1},{9,5},{13,9},{6,2},{10,6},{14,10},{7,3},{... | collective-permute-start | bytes 3080 | tf_op jit(solution)/shard_map/while/body/eval_jaxpr/ppermute | solution.py:24
  342.1 7.3 %collective-permute-start.5 = (f32[2,128,1]{2,1,0:T(8,128)S(1)}, f32[2,128,1]{2,1,0:T(8,128)S(1)}, u32[]{:S(2)}, u32[]{:S(2)}) collective-permute-start(f32[2,128,1]{2,1,0:T(8,128)S(1)} %get-tuple-element.609), channel_id=1, source_target_pairs={{0,4},{4,8},{8,12},{1,5},{5,9},{9,13},{2,6},{6,10},{10,14},{3,7},{... | collective-permute-start | bytes 3080 | tf_op jit(solution)/shard_map/while/body/eval_jaxpr/ppermute | solution.py:22
  357.5 6.2 collective-permute-start
  361.8 6.2 collective-permute-start.1
  375.4 6.9 %collective-permute-start.4 = (f32[2,128,1]{2,1,0:T(8,128)S(1)}, f32[2,128,1]{2,1,0:T(8,128)S(1)}, u32[]{:S(2)}, u32[]{:S(2)}) collective-permute-start(f32[2,128,1]{2,1,0:T(8,128)S(1)} %get-tuple-element.608), channel_id=1, source_target_pairs={{4,0},{8,4},{12,8},{5,1},{9,5},{13,9},{6,2},{10,6},{14,10},{7,3},{... | collective-permute-start | bytes 3080 | tf_op jit(solution)/shard_map/while/body/eval_jaxpr/ppermute | solution.py:24
  376.7 7.3 %collective-permute-start.5 = (f32[2,128,1]{2,1,0:T(8,128)S(1)}, f32[2,128,1]{2,1,0:T(8,128)S(1)}, u32[]{:S(2)}, u32[]{:S(2)}) collective-permute-start(f32[2,128,1]{2,1,0:T(8,128)S(1)} %get-tuple-element.609), channel_id=1, source_target_pairs={{0,4},{4,8},{8,12},{1,5},{5,9},{9,13},{2,6},{6,10},{10,14},{3,7},{... | collective-permute-start | bytes 3080 | tf_op jit(solution)/shard_map/while/body/eval_jaxpr/ppermute | solution.py:22
  392.1 6.2 collective-permute-start
  396.5 6.2 collective-permute-start.1
  410.1 6.9 %collective-permute-start.4 = (f32[2,128,1]{2,1,0:T(8,128)S(1)}, f32[2,128,1]{2,1,0:T(8,128)S(1)}, u32[]{:S(2)}, u32[]{:S(2)}) collective-permute-start(f32[2,128,1]{2,1,0:T(8,128)S(1)} %get-tuple-element.608), channel_id=1, source_target_pairs={{4,0},{8,4},{12,8},{5,1},{9,5},{13,9},{6,2},{10,6},{14,10},{7,3},{... | collective-permute-start | bytes 3080 | tf_op jit(solution)/shard_map/while/body/eval_jaxpr/ppermute | solution.py:24
  411.4 7.3 %collective-permute-start.5 = (f32[2,128,1]{2,1,0:T(8,128)S(1)}, f32[2,128,1]{2,1,0:T(8,128)S(1)}, u32[]{:S(2)}, u32[]{:S(2)}) collective-permute-start(f32[2,128,1]{2,1,0:T(8,128)S(1)} %get-tuple-element.609), channel_id=1, source_target_pairs={{0,4},{4,8},{8,12},{1,5},{5,9},{9,13},{2,6},{6,10},{10,14},{3,7},{... | collective-permute-start | bytes 3080 | tf_op jit(solution)/shard_map/while/body/eval_jaxpr/ppermute | solution.py:22
  426.8 6.2 collective-permute-start
  431.2 6.2 collective-permute-start.1
  444.8 6.9 %collective-permute-start.4 = (f32[2,128,1]{2,1,0:T(8,128)S(1)}, f32[2,128,1]{2,1,0:T(8,128)S(1)}, u32[]{:S(2)}, u32[]{:S(2)}) collective-permute-start(f32[2,128,1]{2,1,0:T(8,128)S(1)} %get-tuple-element.608), channel_id=1, source_target_pairs={{4,0},{8,4},{12,8},{5,1},{9,5},{13,9},{6,2},{10,6},{14,10},{7,3},{... | collective-permute-start | bytes 3080 | tf_op jit(solution)/shard_map/while/body/eval_jaxpr/ppermute | solution.py:24
  446.1 7.3 %collective-permute-start.5 = (f32[2,128,1]{2,1,0:T(8,128)S(1)}, f32[2,128,1]{2,1,0:T(8,128)S(1)}, u32[]{:S(2)}, u32[]{:S(2)}) collective-permute-start(f32[2,128,1]{2,1,0:T(8,128)S(1)} %get-tuple-element.609), channel_id=1, source_target_pairs={{0,4},{4,8},{8,12},{1,5},{5,9},{9,13},{2,6},{6,10},{10,14},{3,7},{... | collective-permute-start | bytes 3080 | tf_op jit(solution)/shard_map/while/body/eval_jaxpr/ppermute | solution.py:22
  461.5 6.2 collective-permute-start
  465.8 6.2 collective-permute-start.1
  479.4 6.9 %collective-permute-start.4 = (f32[2,128,1]{2,1,0:T(8,128)S(1)}, f32[2,128,1]{2,1,0:T(8,128)S(1)}, u32[]{:S(2)}, u32[]{:S(2)}) collective-permute-start(f32[2,128,1]{2,1,0:T(8,128)S(1)} %get-tuple-element.608), channel_id=1, source_target_pairs={{4,0},{8,4},{12,8},{5,1},{9,5},{13,9},{6,2},{10,6},{14,10},{7,3},{... | collective-permute-start | bytes 3080 | tf_op jit(solution)/shard_map/while/body/eval_jaxpr/ppermute | solution.py:24
  480.7 7.3 %collective-permute-start.5 = (f32[2,128,1]{2,1,0:T(8,128)S(1)}, f32[2,128,1]{2,1,0:T(8,128)S(1)}, u32[]{:S(2)}, u32[]{:S(2)}) collective-permute-start(f32[2,128,1]{2,1,0:T(8,128)S(1)} %get-tuple-element.609), channel_id=1, source_target_pairs={{0,4},{4,8},{8,12},{1,5},{5,9},{9,13},{2,6},{6,10},{10,14},{3,7},{... | collective-permute-start | bytes 3080 | tf_op jit(solution)/shard_map/while/body/eval_jaxpr/ppermute | solution.py:22
  496.1 6.2 collective-permute-start
  500.5 6.2 collective-permute-start.1
  514.1 6.9 %collective-permute-start.4 = (f32[2,128,1]{2,1,0:T(8,128)S(1)}, f32[2,128,1]{2,1,0:T(8,128)S(1)}, u32[]{:S(2)}, u32[]{:S(2)}) collective-permute-start(f32[2,128,1]{2,1,0:T(8,128)S(1)} %get-tuple-element.608), channel_id=1, source_target_pairs={{4,0},{8,4},{12,8},{5,1},{9,5},{13,9},{6,2},{10,6},{14,10},{7,3},{... | collective-permute-start | bytes 3080 | tf_op jit(solution)/shard_map/while/body/eval_jaxpr/ppermute | solution.py:24
  515.4 7.3 %collective-permute-start.5 = (f32[2,128,1]{2,1,0:T(8,128)S(1)}, f32[2,128,1]{2,1,0:T(8,128)S(1)}, u32[]{:S(2)}, u32[]{:S(2)}) collective-permute-start(f32[2,128,1]{2,1,0:T(8,128)S(1)} %get-tuple-element.609), channel_id=1, source_target_pairs={{0,4},{4,8},{8,12},{1,5},{5,9},{9,13},{2,6},{6,10},{10,14},{3,7},{... | collective-permute-start | bytes 3080 | tf_op jit(solution)/shard_map/while/body/eval_jaxpr/ppermute | solution.py:22
  530.8 6.2 collective-permute-start
  535.2 6.2 collective-permute-start.1
  548.8 6.9 %collective-permute-start.4 = (f32[2,128,1]{2,1,0:T(8,128)S(1)}, f32[2,128,1]{2,1,0:T(8,128)S(1)}, u32[]{:S(2)}, u32[]{:S(2)}) collective-permute-start(f32[2,128,1]{2,1,0:T(8,128)S(1)} %get-tuple-element.608), channel_id=1, source_target_pairs={{4,0},{8,4},{12,8},{5,1},{9,5},{13,9},{6,2},{10,6},{14,10},{7,3},{... | collective-permute-start | bytes 3080 | tf_op jit(solution)/shard_map/while/body/eval_jaxpr/ppermute | solution.py:24
  550.1 7.3 %collective-permute-start.5 = (f32[2,128,1]{2,1,0:T(8,128)S(1)}, f32[2,128,1]{2,1,0:T(8,128)S(1)}, u32[]{:S(2)}, u32[]{:S(2)}) collective-permute-start(f32[2,128,1]{2,1,0:T(8,128)S(1)} %get-tuple-element.609), channel_id=1, source_target_pairs={{0,4},{4,8},{8,12},{1,5},{5,9},{9,13},{2,6},{6,10},{10,14},{3,7},{... | collective-permute-start | bytes 3080 | tf_op jit(solution)/shard_map/while/body/eval_jaxpr/ppermute | solution.py:22
  565.5 6.2 collective-permute-start
  583.4 6.9 %collective-permute-start.4 = (f32[2,128,1]{2,1,0:T(8,128)S(1)}, f32[2,128,1]{2,1,0:T(8,128)S(1)}, u32[]{:S(2)}, u32[]{:S(2)}) collective-permute-start(f32[2,128,1]{2,1,0:T(8,128)S(1)} %get-tuple-element.608), channel_id=1, source_target_pairs={{4,0},{8,4},{12,8},{5,1},{9,5},{13,9},{6,2},{10,6},{14,10},{7,3},{... | collective-permute-start | bytes 3080 | tf_op jit(solution)/shard_map/while/body/eval_jaxpr/ppermute | solution.py:24
  584.7 7.3 %collective-permute-start.5 = (f32[2,128,1]{2,1,0:T(8,128)S(1)}, f32[2,128,1]{2,1,0:T(8,128)S(1)}, u32[]{:S(2)}, u32[]{:S(2)}) collective-permute-start(f32[2,128,1]{2,1,0:T(8,128)S(1)} %get-tuple-element.609), channel_id=1, source_target_pairs={{0,4},{4,8},{8,12},{1,5},{5,9},{9,13},{2,6},{6,10},{10,14},{3,7},{... | collective-permute-start | bytes 3080 | tf_op jit(solution)/shard_map/while/body/eval_jaxpr/ppermute | solution.py:22
  (69 other events, 556.2 us)
Sparse Core Ops, SparseCore 0:
  599.9 29.2 all-gather.1
where the time goes:
time: 648 us; the launch traced here: 642 us
  starting transfers between devices  332 us (51%)
  waiting for transfers between devices  245 us (38%)
  other arithmetic  34.9 us (5%)
  between operations  13.5 us (2%)
  matrix products  11.3 us (2%)
    ppermute x64, starting transfers between devices, with_halo(): lax.ppermute(tail, axis, [(i, (i + 1) % count) for i in range(ends)])  235 us
    ppermute x64, waiting for transfers between devices, with_halo(): lax.ppermute(head, axis, [((i + 1) % count, i) for i in range(ends)])  162 us
    ppermute x64, starting transfers between devices, with_halo(): lax.ppermute(head, axis, [((i + 1) % count, i) for i in range(ends)])  82.7 us
    ppermute x64, waiting for transfers between devices, with_halo(): lax.ppermute(tail, axis, [(i, (i + 1) % count) for i in range(ends)])  37.4 us
    all_gather x1, waiting for transfers between devices, local(): piece = lax.all_gather(grad, 'lon', axis=1, tiled=True)  29.4 us
    add x16, other arithmetic, advance(): return stepper((carry[0] + push, carry[1], carry[2]))  15.9 us
  transfers between devices with their start and end apart: 132, of which 100 were waited for; matrix products, arithmetic and copies ran while one was open for 1% of the time, Pallas kernels for 0%

commit v1 on v0

v1 whole, which is shorter than its diff:
```python
import functools
import math

import jax
import jax.numpy as jnp
from jax import lax
from jax.experimental import pallas as pl
from jax.experimental.pallas import tpu as pltpu
from jax.sharding import PartitionSpec as P

STEPS_BLOCK = 8
LANES = 128
PAD = 8
SEG = 32

courant = 0.45
depth_floor = 0.1

GRID_AXES = ("lon", "lat", "gau")
ROW_AXES = ("lat", "gau")
VMEM_LIMIT = 48 * 1024 * 1024


def roll_lanes(x, shift):
    shift = shift % LANES
    return x if shift == 0 else pltpu.roll(x, shift, 1)


def lane_iota(rows):
    return lax.broadcasted_iota(jnp.int32, (rows, LANES), 1)


def pack_lanes(pieces):
    rows = pieces[0][0].shape[0]
    segment = lane_iota(rows) // SEG
    packed = jnp.zeros((rows, LANES), jnp.float32)
    for place, (array, first) in enumerate(pieces):
        packed = jnp.where(segment == place, roll_lanes(array, place * SEG - first), packed)
    return packed


def gauge_place(owned):
    if owned <= LANES - 2 * SEG:
        return 0, 2 * SEG, SEG
    assert owned <= LANES
    return SEG, 0, SEG + 24


def prepare(
    halo, depth_ref, surface_ref, friction_ref, wet_ref, coast_ref, route_ref, cell_ref, times_ref, resid_ref,
    keep_ref, gain_ref, parcel_ref, south_ref, north_ref, east_ref, west_ref, block_ref,
):
    height, width = depth_ref.shape
    scale = (courant * 0.5) ** 2
    depth = jnp.maximum(depth_ref[...] + surface_ref[...], depth_floor)
    keep = (1.0 - friction_ref[...]) * wet_ref[...].astype(jnp.float32)
    gain = (scale * depth) * keep
    keep_ref[...] = keep
    gain_ref[...] = gain
    south_ref[0] = keep[height - halo :]
    south_ref[1] = gain[height - halo :]
    north_ref[0] = keep[:halo]
    north_ref[1] = gain[:halo]
    half = height // 2
    first, last = slice(0, LANES), slice(width - LANES, width)
    end = LANES - halo
    east_ref[...] = pack_lanes(
        [(keep[:half, last], end), (gain[:half, last], end), (keep[half:, last], end), (gain[half:, last], end)]
    )
    west_ref[...] = pack_lanes(
        [(keep[:half, first], 0), (gain[:half, first], 0), (keep[half:, first], 0), (gain[half:, first], 0)]
    )

    row_tiles = lax.axis_size("lat") * lax.axis_size("gau")
    owned = route_ref.shape[1]
    blocks, samples = times_ref.shape[:2]
    route = route_ref[...]
    target = jnp.zeros_like(route)
    for entry in range(coast_ref.shape[0]):
        target = jnp.where(route == entry, coast_ref[entry], target)
    cell = cell_ref[...]
    row_bits, width_bits = int(math.log2(row_tiles)), int(math.log2(width))
    assert row_tiles == 1 << row_bits and width == 1 << width_bits
    grid_row = (target & (row_tiles - 1)) * height + (cell >> width_bits)
    grid_col = (target >> row_bits) * width + (cell & (width - 1))
    block_ref[...] = jnp.zeros_like(block_ref)
    levels = lax.broadcasted_iota(jnp.int32, (STEPS_BLOCK, owned), 0)
    for block in range(blocks):
        times, resid = times_ref[block], resid_ref[block]
        series = jnp.zeros((STEPS_BLOCK, owned), jnp.float32)
        for sample in range(samples):
            series = series + jnp.where(times[sample : sample + 1] == levels, resid[sample : sample + 1], 0.0)
        block_ref[block * STEPS_BLOCK : (block + 1) * STEPS_BLOCK, :owned] = series
    at = blocks * STEPS_BLOCK
    block_ref[at : at + 1, :owned] = grid_row.astype(jnp.float32)
    block_ref[at + 1 : at + 2, :owned] = grid_col.astype(jnp.float32)
    top, lane, _ = gauge_place(owned)
    gauges = roll_lanes(block_ref[...], lane)
    tiles = parcel_ref.shape[0]

    def put(tile, carry):
        parcel_ref[tile, top : top + 24, :] = gauges
        return carry

    lax.fori_loop(0, tiles, put, 0, unroll=tiles <= 16)

    my_lon = lax.axis_index("lon")
    my_row = lax.axis_index("lat") * lax.axis_size("gau") + lax.axis_index("gau")
    lons = lax.axis_size("lon")
    full = jnp.zeros((SEG, LANES), jnp.float32)
    if top == 0:
        full = jnp.concatenate([gauges, jnp.zeros((SEG - 24, LANES), jnp.float32)], axis=0)
    segment = lane_iota(SEG) // SEG
    for d_row in (-1, 1):
        rows = slice(0, halo) if d_row < 0 else slice(height - halo, height)
        for d_lon in (-1, 1):
            cols, start = (first, 0) if d_lon < 0 else (last, end)
            corner = jnp.where(segment == 0, roll_lanes(keep[rows, cols], -start), full)
            corner = jnp.where(segment == 1, roll_lanes(gain[rows, cols], SEG - start), corner)
            to_row, to_lon = my_row + d_row, my_lon + d_lon
            there = (to_row >= 0) & (to_row < row_tiles) & (to_lon >= 0) & (to_lon < lons)

            @pl.when(there)
            def _():
                parcel_ref[to_lon * row_tiles + to_row, 0:SEG, :] = corner


def shift_from(planes, shift, lanes):
    count = len(planes)
    rolled = [roll_lanes(plane, -shift) for plane in planes]
    if shift > 0:
        return [jnp.where(lanes >= LANES - shift, rolled[(c + 1) % count], rolled[c]) for c in range(count)]
    return [jnp.where(lanes < -shift, rolled[(c - 1) % count], rolled[c]) for c in range(count)]


def sweep(
    steps, owned, keep_ref, gain_ref, top_ref, bottom_ref, left_ref, right_ref, parcel_ref,
    grad_ref, sums_ref,
    a, fx, fy, keep_x, gain_x, keep_y, gain_y, keep_all, gain_all, force, series_ref, rows_hot, cols_hot,
):
    height, width = keep_ref.shape
    halo = 2 * steps
    inner = width // LANES
    planes = inner + 1
    rows_all = a.shape[1]
    base = PAD + halo
    row_tiles = lax.axis_size("lat") * lax.axis_size("gau")
    lons = lax.axis_size("lon")
    my_lon = lax.axis_index("lon")
    my_row = lax.axis_index("lat") * lax.axis_size("gau") + lax.axis_index("gau")
    end = LANES - halo

    for ref in (a, fx, fy):
        ref[...] = jnp.zeros_like(ref)

    half = height // 2
    segment = lane_iota(half) // SEG
    for kind, (source, whole) in enumerate(((keep_ref, keep_all), (gain_ref, gain_all))):
        for c in range(planes):
            whole[c, 0:PAD, :] = jnp.zeros((PAD, LANES), jnp.float32)
            whole[c, rows_all - PAD :, :] = jnp.zeros((PAD, LANES), jnp.float32)
        for c in range(inner):
            cols = slice(c * LANES, (c + 1) * LANES)
            whole[c, base : base + height, :] = source[:, cols]
            whole[c, PAD:base, :] = top_ref[kind, :, cols]
            whole[c, base + height : base + height + halo, :] = bottom_ref[kind, :, cols]
        for part in range(2):
            piece = 2 * part + kind
            from_left = roll_lanes(left_ref[...], end - piece * SEG)
            from_right = roll_lanes(right_ref[...], -piece * SEG)
            both = jnp.where(segment == 0, from_right, jnp.where(segment == LANES // SEG - 1, from_left, 0.0))
            whole[inner, base + part * half : base + (part + 1) * half, :] = both
        corner_segment = lane_iota(SEG) // SEG
        for d_row, at in ((-1, PAD), (1, base + height)):
            found = jnp.zeros((SEG, LANES), jnp.float32)
            for d_lon in (-1, 1):
                row, lon = my_row + d_row, my_lon + d_lon
                there = (row >= 0) & (row < row_tiles) & (lon >= 0) & (lon < lons)
                source_tile = jnp.where(there, lon * row_tiles + row, 0)
                block = parcel_ref[source_tile, 0:SEG, :]
                goal = 0 if d_lon > 0 else end
                block = roll_lanes(block, goal - kind * SEG)
                there_scale = jnp.where(there, 1, 0)
                found = jnp.where((corner_segment == goal // SEG) & (there_scale == 1), block, found)
            whole[inner, at : at + halo, :] = found

    lanes8 = lane_iota(8)
    for whole, by_x, by_y in ((keep_all, keep_x, keep_y), (gain_all, gain_x, gain_y)):
        for r in range(PAD, rows_all - PAD, 8):
            shifted = shift_from([whole[c, r : r + 8, :] for c in range(planes)], 1, lanes8)
            for c in range(planes):
                by_x[c, r : r + 8, :] = shifted[c]
                by_y[c, r : r + 8, :] = whole[c, r + 1 : r + 9, :]

    top, lane, _ = gauge_place(owned)
    group = rows_hot.shape[1] // owned
    wide = group * owned
    sources = parcel_ref.shape[0]
    groups = sources // group
    per_plane = LANES // owned
    row_shift = (base - my_row * height).astype(jnp.float32)
    col_shift = (-my_lon * width).astype(jnp.float32)

    def gather_gauges(index):
        for part in range(wide // LANES):
            total = jnp.zeros((24, LANES), jnp.float32)
            lanes24 = lane_iota(24)
            for i in range(per_plane):
                source = index * group + part * per_plane + i
                block = roll_lanes(parcel_ref[source, top : top + 24, :], i * owned - lane)
                total = jnp.where((lanes24 >= i * owned) & (lanes24 < (i + 1) * owned), block, total)
            cols = slice(part * LANES, (part + 1) * LANES)
            series_ref[:, cols] = total[:steps]
            row = total[steps : steps + 1] + row_shift
            col = total[steps + 1 : steps + 2] + col_shift
            col = jnp.where((col >= -halo) & (col < 0), col + float(planes * LANES), jnp.where(col < width + halo, col, -1.0))
            at = lax.broadcasted_iota(jnp.int32, (rows_all, LANES), 0).astype(jnp.float32)
            rows_hot[:, cols] = (at == row).astype(jnp.float32)
            by_gauge = jnp.transpose(jnp.broadcast_to(col, (LANES, LANES)))
            for c in range(planes):
                place = (lane_iota(LANES) + c * LANES).astype(jnp.float32)
                cols_hot[part * LANES : (part + 1) * LANES, c * LANES : (c + 1) * LANES] = (
                    (by_gauge == place).astype(jnp.float32).astype(jnp.bfloat16)
                )

    def forcing(level, lo, hi):
        def product():
            value = series_ref[pl.ds(level, 1), :]
            high = value.astype(jnp.bfloat16).astype(jnp.float32)
            low = value - high
            hot = rows_hot[lo:hi, :]
            return jnp.dot(
                (hot * high).astype(jnp.bfloat16), cols_hot[...], preferred_element_type=jnp.float32
            ) + jnp.dot((hot * low).astype(jnp.bfloat16), cols_hot[...], preferred_element_type=jnp.float32)

        def store(total, add):
            for c in range(planes):
                piece = total[:, c * LANES : (c + 1) * LANES]
                force[c, lo:hi, :] = force[c, lo:hi, :] + piece if add else piece

        if groups == 1:
            store(product(), False)
        else:
            force[...] = jnp.zeros_like(force)

            def more(index, carry):
                gather_gauges(index)
                store(product(), True)
                return carry

            lax.fori_loop(0, groups, more, 0)

    if groups == 1:
        gather_gauges(0)

    col_valid = jnp.where(lanes8 < LANES // 2, jnp.where(my_lon < lons - 1, 1.0, 0.0), jnp.where(my_lon > 0, 1.0, 0.0))
    col_mask = jnp.where((lanes8 < halo) | (lanes8 >= end), col_valid, 0.0)
    above = jnp.where(my_row > 0, 1.0, 0.0)
    below = jnp.where(my_row < row_tiles - 1, 1.0, 0.0)

    def advance(lo, hi, forced):
        for r in range(lo, hi, 8):
            here = [a[c, r : r + 8, :] for c in range(planes)]
            ahead = shift_from(here, 2, lanes8)
            new_x = [
                keep_x[c, r : r + 8, :] * fx[c, r : r + 8, :] + gain_x[c, r : r + 8, :] * (ahead[c] - here[c])
                for c in range(planes)
            ]
            behind = shift_from(new_x, -2, lanes8)
            for c in range(planes):
                new_y = keep_y[c, r : r + 8, :] * fy[c, r : r + 8, :] + gain_y[c, r : r + 8, :] * (
                    a[c, r + 2 : r + 10, :] - here[c]
                )
                fx[c, r : r + 8, :] = new_x[c]
                fy[c, r : r + 8, :] = new_y
                value = here[c] + (new_x[c] - behind[c]) + (new_y - fy[c, r - 2 : r + 6, :])
                if c == inner:
                    value = value * col_mask
                if r == base - 8:
                    value = value * above
                if r == base + height:
                    value = value * below
                if forced:
                    value = value + force[c, r : r + 8, :]
                a[c, r : r + 8, :] = value

    lo, hi = PAD, rows_all - PAD
    forcing(steps - 1, lo, hi)
    for c in range(planes):
        a[c, lo:hi, :] = force[c, lo:hi, :]
    done = 0
    while done < steps - 1:
        spare = (2 * done) // 8 * 8
        bounds = (PAD + spare, rows_all - PAD - spare)
        until = min(done + 4, steps - 1)

        def body(step, carry, bounds=bounds):
            forcing(steps - 2 - step, *bounds)
            advance(*bounds, True)
            return carry

        lax.fori_loop(done, until, body, 0)
        done = until
    spare = (2 * done) // 8 * 8
    advance(PAD + spare, rows_all - PAD - spare, False)

    for c in range(inner):
        cols = slice(c * LANES, (c + 1) * LANES)
        grad_ref[:, cols] = a[c, base : base + height, :]


def weigh(grad_in, wet_ref, grad_ref, sums_ref):
    height, width = grad_in.shape
    length = 2.0 * width
    grad = grad_in[...] * wet_ref[...].astype(jnp.float32)
    grad_ref[...] = grad
    kind = lax.broadcasted_iota(jnp.int32, (8, width), 0)
    column = lax.broadcasted_iota(jnp.int32, (8, width), 1)
    steps_off = jnp.where(kind == 0, column, width - 1 - column).astype(jnp.float32)
    weights = jnp.where(kind < 2, jnp.exp(-steps_off / length), 0.0)
    sums = lax.dot_general(
        weights, grad, (((1,), (1,)), ((), ())), precision=lax.Precision.HIGHEST, preferred_element_type=jnp.float32
    )
    for i in range(sums_ref.shape[0]):
        sums_ref[i] = sums


def smooth(grad_ref, out_ref):
    width = grad_ref.shape[1]
    length = 2.0 * width
    row = lax.broadcasted_iota(jnp.int32, (width, width), 0)
    column = lax.broadcasted_iota(jnp.int32, (width, width), 1)
    kernel = jnp.exp(-jnp.abs(row - column).astype(jnp.float32) / length)
    out_ref[...] = jnp.dot(
        grad_ref[...], kernel, precision=lax.Precision.HIGHEST, preferred_element_type=jnp.float32
    )


def finish(own_ref, sums_ref, out_ref):
    width = own_ref.shape[1]
    length = 2.0 * width
    count = sums_ref.shape[0]
    me = lax.axis_index("lon")
    row = lax.broadcasted_iota(jnp.int32, (count, width), 0)
    column = lax.broadcasted_iota(jnp.int32, (count, width), 1)
    strip, kind = row >> 3, row & 7
    left = (kind == 0) & (strip > me)
    right = (kind == 1) & (strip < me)
    away = jnp.where(left, (strip - me) * width - column, (me - strip - 1) * width + column + 1)
    weights = jnp.where(left | right, jnp.exp(-jnp.maximum(away, 0).astype(jnp.float32) / length), 0.0)
    out_ref[...] = own_ref[...] + lax.dot_general(
        sums_ref[...], weights, (((0,), (0,)), ((), ())), precision=lax.Precision.HIGHEST,
        preferred_element_type=jnp.float32,
    )


def f32(*shape):
    return jax.ShapeDtypeStruct(shape, jnp.float32)


def vmem(count):
    return [pl.BlockSpec(memory_space=pltpu.VMEM)] * count


def local(depth, surface, friction, wet, coastal_tiles, gauge_route, gauge_cell, gauge_times, gauge_resid):
    height, width = depth.shape
    owned = gauge_route.shape[0]
    blocks = gauge_resid.shape[1]
    steps = blocks * STEPS_BLOCK
    halo = 2 * steps
    assert halo == SEG and height == LANES
    tiles = lax.axis_size(GRID_AXES)
    lons = lax.axis_size("lon")
    row_tiles = lax.axis_size(ROW_AXES)
    _, _, parcel_rows = gauge_place(owned)
    params = pltpu.CompilerParams(vmem_limit_bytes=VMEM_LIMIT)

    keep, gain, parcel, south, north, east, west = pl.pallas_call(
        functools.partial(prepare, halo),
        out_shape=(
            f32(height, width), f32(height, width), f32(tiles, parcel_rows, LANES),
            f32(2, halo, width), f32(2, halo, width), f32(height // 2, LANES), f32(height // 2, LANES),
        ),
        in_specs=vmem(4) + [pl.BlockSpec(memory_space=pltpu.SMEM)] + vmem(4),
        out_specs=tuple(vmem(7)),
        scratch_shapes=[pltpu.VMEM((24, LANES), jnp.float32)],
        compiler_params=params,
        name="prepare",
    )(
        depth, surface, friction, wet, coastal_tiles, gauge_route.reshape(1, owned), gauge_cell.reshape(1, owned),
        jnp.transpose(gauge_times, (1, 2, 0)), jnp.transpose(gauge_resid, (1, 2, 0)),
    )

    parcel = lax.all_to_all(parcel, GRID_AXES, split_axis=0, concat_axis=0, tiled=True)
    down = [(i, i + 1) for i in range(row_tiles - 1)]
    up = [(i + 1, i) for i in range(row_tiles - 1)]
    top = lax.ppermute(south, ROW_AXES, down)
    bottom = lax.ppermute(north, ROW_AXES, up)
    left = lax.ppermute(east, "lon", [(i, i + 1) for i in range(lons - 1)])
    right = lax.ppermute(west, "lon", [(i + 1, i) for i in range(lons - 1)])

    planes = width // LANES + 1
    rows_all = height + 2 * halo + 2 * PAD
    wide = max(2 * LANES, owned)
    plane = pltpu.VMEM((planes, rows_all, LANES), jnp.float32)
    grad = pl.pallas_call(
        functools.partial(sweep_call, steps, owned),
        out_shape=f32(height, width),
        in_specs=vmem(7),
        out_specs=vmem(1)[0],
        scratch_shapes=[plane] * 10 + [
            pltpu.VMEM((steps, wide), jnp.float32),
            pltpu.VMEM((rows_all, wide), jnp.float32),
            pltpu.VMEM((wide, planes * LANES), jnp.bfloat16),
        ],
        compiler_params=params,
        name="sweep",
    )(keep, gain, top, bottom, left, right, parcel)

    grad, sums = pl.pallas_call(
        weigh,
        out_shape=(f32(height, width), f32(lons, 8, height)),
        in_specs=vmem(2),
        out_specs=tuple(vmem(2)),
        compiler_params=params,
        name="weigh",
    )(grad, wet)
    sums = lax.all_to_all(sums, "lon", split_axis=0, concat_axis=0, tiled=True)
    own = pl.pallas_call(
        smooth, out_shape=f32(height, width), in_specs=vmem(1), out_specs=vmem(1)[0], compiler_params=params,
        cost_estimate=pl.CostEstimate(flops=6 * 2 * height * width * width, bytes_accessed=2 * 4 * height * width, transcendentals=width * width),
        name="smooth",
    )(grad)
    return pl.pallas_call(
        finish, out_shape=f32(height, width), in_specs=vmem(2), out_specs=vmem(1)[0], compiler_params=params, name="finish",
    )(own, sums.reshape(lons * 8, height))


def sweep_call(steps, owned, *refs):
    ins, grad_ref, scratch = refs[:7], refs[7], refs[8:]
    sweep(steps, owned, *ins, grad_ref, None, *scratch)


def solution(mesh):
    in_specs = (
        P(("lat", "gau"), "lon"),
        P(("scen", "lat", "gau"), "lon"),
        P(("lat", "gau"), "lon"),
        P(("lat", "gau"), "lon"),
        P(),
        P(("scen", "lon", "lat", "gau"), None),
        P(("scen", "lon", "lat", "gau")),
        P(("scen", "lon", "lat", "gau"), None, None),
        P(("scen", "lon", "lat", "gau"), None, None),
    )
    out_specs = P(("scen", "lat", "gau"), "lon")
    return jax.shard_map(local, mesh=mesh, in_specs=in_specs, out_specs=out_specs, check_vma=False)
```

time: 648 us -> 53.9 us (0.08)
  the two profiles are of different devices: /device:TPU:0 before, /device:TPU:2 now
where the time goes in v1:
time: 53.9 us; the launch traced here: 53.3 us
  starting transfers between devices  20.2 us (37%)
  Pallas kernels  18.6 us (35%)
  waiting for transfers between devices  9.22 us (17%)
  local copies, waits for them, and re-layouts  5.18 us (10%)
    pallas_call x1, Pallas kernels, local(): pl.pallas_call(functools.partial(sweep_call, steps, owned), out_shape=f32...  14.1 us
    all_to_all x1, starting transfers between devices, local(): lax.all_to_all(parcel, GRID_AXES, split_axis=0, concat_axis=0, tiled=True)  6.35 us
    unnamed x20, local copies, waits for them, and re-layouts  5.18 us
    all_to_all x1, waiting for transfers between devices, local(): sums = lax.all_to_all(sums, 'lon', split_axis=0, concat_axis=0, tiled=True)  4.71 us
    ppermute x1, waiting for transfers between devices, local(): right = lax.ppermute(west, 'lon', [(i + 1, i) for i in range(lons - 1)])  4.23 us
    all_to_all x1, starting transfers between devices, local(): sums = lax.all_to_all(sums, 'lon', split_axis=0, concat_axis=0, tiled=True)  3.63 us
    ppermute x1, starting transfers between devices, local(): bottom = lax.ppermute(north, ROW_AXES, up)  3.51 us
    ppermute x1, starting transfers between devices, local(): left = lax.ppermute(east, 'lon', [(i, i + 1) for i in range(lons - 1)])  3.37 us
  transfers between devices with their start and end apart: 6, of which 3 were waited for; matrix products, arithmetic and copies ran while one was open for 0% of the time, Pallas kernels for 2%

profile of v1, /device:TPU:2, one launch (start us, length us, event | category | flops | bytes accessed | tf_op | source)
XLA Modules:
  0.0 53.3 jit_solution(7507672740368527579)
XLA Ops:
  0.0 0.0 copy-start.5
  0.0 0.0 copy-start.7
  0.0 0.0 copy-start.8
  0.0 0.0 copy-start.9
  0.0 0.7 %copy-done.5 = s32[16,2,4]{0,2,1:T(4,128)S(1)} copy-done((s32[16,2,4]{0,2,1:T(4,128)S(1)}, s32[16,2,4]{0,2,1:T(4,128)}, u32[]{:S(2)}) %copy-start.5) | copy-done | bytes 536
  0.7 0.0 copy-done.7
  0.7 0.0 copy-done.8
  0.7 0.0 copy-done.9
  0.7 0.0 copy-start
  0.7 0.9 %copy-done = s32[128,512]{1,0:T(8,128)S(1)} copy-done((s32[128,512]{1,0:T(8,128)S(1)}, s32[128,512]{1,0:T(8,128)}, u32[]{:S(2)}) %copy-start) | copy-done | bytes 262168
  1.7 0.0 copy-start.2
  1.7 0.9 %copy-done.2 = f32[128,512]{1,0:T(8,128)S(1)} copy-done((f32[128,512]{1,0:T(8,128)S(1)}, f32[128,512]{1,0:T(8,128)}, u32[]{:S(2)}) %copy-start.2) | copy-done | bytes 262168
  2.6 0.0 copy-start.3
  2.6 0.9 %copy-done.3 = f32[128,512]{1,0:T(8,128)S(1)} copy-done((f32[128,512]{1,0:T(8,128)S(1)}, f32[128,512]{1,0:T(8,128)}, u32[]{:S(2)}) %copy-start.3) | copy-done | bytes 262168
  3.6 0.0 copy-start.4
  3.6 0.9 %copy-done.4 = f32[128,512]{1,0:T(8,128)S(1)} copy-done((f32[128,512]{1,0:T(8,128)S(1)}, f32[128,512]{1,0:T(8,128)}, u32[]{:S(2)}) %copy-start.4) | copy-done | bytes 262168
  4.5 0.0 copy-start.6
  4.5 0.7 %copy-done.6 = f32[16,2,4]{0,2,1:T(4,128)S(1)} copy-done((f32[16,2,4]{0,2,1:T(4,128)S(1)}, f32[16,2,4]{0,2,1:T(4,128)}, u32[]{:S(2)}) %copy-start.6) | copy-done | bytes 536
  5.2 1.6 %prepare.1 = (f32[128,512]{1,0:T(8,128)S(1)}, f32[128,512]{1,0:T(8,128)S(1)}, f32[16,32,128]{2,1,0:T(8,128)}, f32[2,32,512]{2,1,0:T(8,128)S(1)}, f32[2,32,512]{2...) custom-call(f32[128,512]{1,0:T(8,128)S(1)} %copy-done.2, f32[128,512]{1,0:T(8,128)S(1)} %copy-done.3, ...), custom_call_target="tpu_custom_call" | custom-call | tf_op jit(solution)/shard_map/prepare/pallas_call | solution.py:378
  6.8 6.4 %all-to-all-start = ((f32[16,32,128]{2,1,0:T(8,128)}), f32[16,32,128]{2,1,0:T(8,128)S(1)}, u32[]{:S(2)}, u32[]{:S(2)}) async-start(f32[16,32,128]{2,1,0:T(8,128)} %get-tuple-element.20), calls=%async_computation | async-start | bytes 524288 | tf_op jit(solution)/shard_map/all_to_all | solution.py:394
  13.1 2.0 %collective-permute-start = (f32[2,32,512]{2,1,0:T(8,128)S(1)}, f32[2,32,512]{2,1,0:T(8,128)S(1)}, u32[]{:S(2)}, u32[]{:S(2)}) collective-permute-start(f32[2,32,512]{2,1,0:T(8,128)S(1)} %get-tuple-element.16), channel_id=1, source_target_pairs={{0,1},{1,2},{2,3},{4,5},{5,6},{6,7},{8,9},{9,10},{10,11},{12,13},{... | collective-permute-start | bytes 393224 | tf_op jit(solution)/shard_map/ppermute | solution.py:397
  15.2 3.5 %collective-permute-start.1 = (f32[2,32,512]{2,1,0:T(8,128)S(1)}, f32[2,32,512]{2,1,0:T(8,128)S(1)}, u32[]{:S(2)}, u32[]{:S(2)}) collective-permute-start(f32[2,32,512]{2,1,0:T(8,128)S(1)} %get-tuple-element.17), channel_id=1, source_target_pairs={{1,0},{2,1},{3,2},{5,4},{6,5},{7,6},{9,8},{10,9},{11,10},{13,12},{... | collective-permute-start | bytes 393224 | tf_op jit(solution)/shard_map/ppermute | solution.py:398
  18.7 3.4 %collective-permute-start.2 = (f32[64,128]{1,0:T(8,128)S(1)}, f32[64,128]{1,0:T(8,128)S(1)}, u32[]{:S(2)}, u32[]{:S(2)}) collective-permute-start(f32[64,128]{1,0:T(8,128)S(1)} %get-tuple-element.18), channel_id=1, source_target_pairs={{0,4},{4,8},{8,12},{1,5},{5,9},{9,13},{2,6},{6,10},{10,14},{3,7},{... | collective-permute-start | bytes 98312 | tf_op jit(solution)/shard_map/ppermute | solution.py:399
  22.1 1.3 %collective-permute-start.3 = (f32[64,128]{1,0:T(8,128)S(1)}, f32[64,128]{1,0:T(8,128)S(1)}, u32[]{:S(2)}, u32[]{:S(2)}) collective-permute-start(f32[64,128]{1,0:T(8,128)S(1)} %get-tuple-element.19), channel_id=1, source_target_pairs={{4,0},{8,4},{12,8},{5,1},{9,5},{13,9},{6,2},{10,6},{14,10},{7,3},{... | collective-permute-start | bytes 98312 | tf_op jit(solution)/shard_map/ppermute | solution.py:400
  23.4 0.3 collective-permute-done.2.refs_4_
  23.6 4.2 %collective-permute-done.3.refs_5_ = f32[64,128]{1,0:T(8,128)S(1)} collective-permute-done((f32[64,128]{1,0:T(8,128)S(1)}, f32[64,128]{1,0:T(8,128)S(1)}, u32[]{:S(2)}, u32[]{:S(2)}) %collective-permute-start.3) | collective-permute-done | bytes 32800 | tf_op jit(solution)/shard_map/ppermute | solution.py:400
  27.9 0.0 collective-permute-done.refs_2_
  27.9 0.0 collective-permute-done.1.refs_3_
  27.9 0.0 all-to-all-done.refs_6_
  27.9 0.0 copy-start.1
  27.9 14.1 %sweep.1.grad_in = f32[128,512]{1,0:T(8,128)S(1)} custom-call(f32[128,512]{1,0:T(8,128)S(1)} %get-tuple-element.14.refs_0_, f32[128,512]{1,0:T(8,128)S(1)} %get-tuple-element.15.refs_1_, f32[2,32,512]{2,1,0:T(8,128)S(1)} %collective-permute-done.refs_2_, f32[2,32,512]{2,1,0:T(8,128)S(1)} %collective-permute-done.1.refs_3_, ...), custom_call_target="tpu_custom_call" | custom-call | tf_op jit(solution)/shard_map/sweep/pallas_call | solution.py:406
  42.0 0.0 copy-done.1
  42.0 1.0 %weigh.1 = (f32[128,512]{1,0:T(8,128)S(1)}, f32[4,8,128]{2,1,0:T(8,128)}) custom-call(f32[128,512]{1,0:T(8,128)S(1)} %sweep.1.grad_in, s32[128,512]{1,0:T(8,128)S(1)} %copy-done.1), custom_call_target="tpu_custom_call" | custom-call | tf_op jit(solution)/shard_map/weigh/pallas_call | solution.py:420
  43.0 3.6 %all-to-all-start.1 = ((f32[4,8,128]{2,1,0:T(8,128)}), f32[4,8,128]{2,1,0:T(8,128)S(1)}, u32[]{:S(2)}, u32[]{:S(2)}) async-start(f32[4,8,128]{2,1,0:T(8,128)} %get-tuple-element.22), calls=%async_computation.1 | async-start | bytes 32768 | tf_op jit(solution)/shard_map/all_to_all | solution.py:428
  46.6 0.9 %smooth.1.own_ref = f32[128,512]{1,0:T(8,128)S(1)} custom-call(f32[128,512]{1,0:T(8,128)S(1)} %get-tuple-element.21.grad_ref), custom_call_target="tpu_custom_call" | custom-call | flops 402653184 | bytes 524288 | tf_op jit(solution)/shard_map/smooth/pallas_call | solution.py:429
  47.5 4.7 %all-to-all-done.1 = f32[4,8,128]{2,1,0:T(8,128)S(1)} async-done(((f32[4,8,128]{2,1,0:T(8,128)}), f32[4,8,128]{2,1,0:T(8,128)S(1)}, u32[]{:S(2)}, u32[]{:S(2)}) %all-to-all-start.1) | async-done | bytes 16416 | tf_op jit(solution)/shard_map/all_to_all | solution.py:428
  52.2 1.1 %finish.1 = f32[128,512]{1,0:T(8,128)} custom-call(f32[128,512]{1,0:T(8,128)S(1)} %smooth.1.own_ref, f32[32,128]{1,0:T(8,128)S(1)} %bitcast.5), custom_call_target="tpu_custom_call" | custom-call | tf_op jit(solution)/shard_map/finish/pallas_call | solution.py:434
Async XLA Ops:
  0.0 0.7 %copy-start.5 = (s32[16,2,4]{0,2,1:T(4,128)S(1)}, s32[16,2,4]{0,2,1:T(4,128)}, u32[]{:S(2)}) copy-start(s32[16,2,4]{0,2,1:T(4,128)} %param.16) | copy-start | bytes 1540
  0.0 0.7 %copy-start.7 = (s32[8]{0:T(128)S(1)}, s32[8]{0:T(128)}, u32[]{:S(2)}) copy-start(s32[8]{0:T(128)} %coast_ref.1) | copy-start | bytes 100
  0.0 0.7 %copy-start.8 = (s32[16,1]{0,1:T(1,128)S(1)}, s32[16,1]{0,1:T(1,128)}, u32[]{:S(2)}) copy-start(s32[16,1]{0,1:T(1,128)} %param.14) | copy-start | bytes 196
  0.0 0.7 %copy-start.9 = (s32[16]{0:T(128)S(1)}, s32[16]{0:T(128)}, u32[]{:S(2)}) copy-start(s32[16]{0:T(128)} %param.15) | copy-start | bytes 196
  0.7 0.9 %copy-start = (s32[128,512]{1,0:T(8,128)S(1)}, s32[128,512]{1,0:T(8,128)}, u32[]{:S(2)}) copy-start(s32[128,512]{1,0:T(8,128)} %wet_ref.3) | copy-start | bytes 786436
  1.7 0.9 %copy-start.2 = (f32[128,512]{1,0:T(8,128)S(1)}, f32[128,512]{1,0:T(8,128)}, u32[]{:S(2)}) copy-start(f32[128,512]{1,0:T(8,128)} %depth_ref.1) | copy-start | bytes 786436
  2.6 0.9 %copy-start.3 = (f32[128,512]{1,0:T(8,128)S(1)}, f32[128,512]{1,0:T(8,128)}, u32[]{:S(2)}) copy-start(f32[128,512]{1,0:T(8,128)} %surface_ref.1) | copy-start | bytes 786436
  3.6 0.9 %copy-start.4 = (f32[128,512]{1,0:T(8,128)S(1)}, f32[128,512]{1,0:T(8,128)}, u32[]{:S(2)}) copy-start(f32[128,512]{1,0:T(8,128)} %friction_ref.1) | copy-start | bytes 786436
  4.5 0.7 %copy-start.6 = (f32[16,2,4]{0,2,1:T(4,128)S(1)}, f32[16,2,4]{0,2,1:T(4,128)}, u32[]{:S(2)}) copy-start(f32[16,2,4]{0,2,1:T(4,128)} %param.17) | copy-start | bytes 1540
  6.8 21.1 %all-to-all-start = ((f32[16,32,128]{2,1,0:T(8,128)}), f32[16,32,128]{2,1,0:T(8,128)S(1)}, u32[]{:S(2)}, u32[]{:S(2)}) async-start(f32[16,32,128]{2,1,0:T(8,128)} %get-tuple-element.20), calls=%async_computation | async-start | bytes 524288 | tf_op jit(solution)/shard_map/all_to_all | solution.py:394
  13.1 14.8 %collective-permute-start = (f32[2,32,512]{2,1,0:T(8,128)S(1)}, f32[2,32,512]{2,1,0:T(8,128)S(1)}, u32[]{:S(2)}, u32[]{:S(2)}) collective-permute-start(f32[2,32,512]{2,1,0:T(8,128)S(1)} %get-tuple-element.16), channel_id=1, source_target_pairs={{0,1},{1,2},{2,3},{4,5},{5,6},{6,7},{8,9},{9,10},{10,11},{12,13},{... | collective-permute-start | bytes 393224 | tf_op jit(solution)/shard_map/ppermute | solution.py:397
  15.2 12.7 %collective-permute-start.1 = (f32[2,32,512]{2,1,0:T(8,128)S(1)}, f32[2,32,512]{2,1,0:T(8,128)S(1)}, u32[]{:S(2)}, u32[]{:S(2)}) collective-permute-start(f32[2,32,512]{2,1,0:T(8,128)S(1)} %get-tuple-element.17), channel_id=1, source_target_pairs={{1,0},{2,1},{3,2},{5,4},{6,5},{7,6},{9,8},{10,9},{11,10},{13,12},{... | collective-permute-start | bytes 393224 | tf_op jit(solution)/shard_map/ppermute | solution.py:398
  18.7 5.0 %collective-permute-start.2 = (f32[64,128]{1,0:T(8,128)S(1)}, f32[64,128]{1,0:T(8,128)S(1)}, u32[]{:S(2)}, u32[]{:S(2)}) collective-permute-start(f32[64,128]{1,0:T(8,128)S(1)} %get-tuple-element.18), channel_id=1, source_target_pairs={{0,4},{4,8},{8,12},{1,5},{5,9},{9,13},{2,6},{6,10},{10,14},{3,7},{... | collective-permute-start | bytes 98312 | tf_op jit(solution)/shard_map/ppermute | solution.py:399
  22.1 5.8 %collective-permute-start.3 = (f32[64,128]{1,0:T(8,128)S(1)}, f32[64,128]{1,0:T(8,128)S(1)}, u32[]{:S(2)}, u32[]{:S(2)}) collective-permute-start(f32[64,128]{1,0:T(8,128)S(1)} %get-tuple-element.19), channel_id=1, source_target_pairs={{4,0},{8,4},{12,8},{5,1},{9,5},{13,9},{6,2},{10,6},{14,10},{7,3},{... | collective-permute-start | bytes 98312 | tf_op jit(solution)/shard_map/ppermute | solution.py:400
  27.9 14.1 %copy-start.1 = (s32[128,512]{1,0:T(8,128)S(1)}, s32[128,512]{1,0:T(8,128)}, u32[]{:S(2)}) copy-start(s32[128,512]{1,0:T(8,128)} %wet_ref.3) | copy-start | bytes 786436
  43.0 9.2 %all-to-all-start.1 = ((f32[4,8,128]{2,1,0:T(8,128)}), f32[4,8,128]{2,1,0:T(8,128)S(1)}, u32[]{:S(2)}, u32[]{:S(2)}) async-start(f32[4,8,128]{2,1,0:T(8,128)} %get-tuple-element.22), calls=%async_computation.1 | async-start | bytes 32768 | tf_op jit(solution)/shard_map/all_to_all | solution.py:428

commit v2 on v1

v2 whole, which is shorter than its diff:
```python
import functools
import math

import jax
import jax.numpy as jnp
from jax import lax
from jax.experimental import pallas as pl
from jax.experimental.pallas import tpu as pltpu
from jax.sharding import PartitionSpec as P

STEPS_BLOCK = 8
LANES = 128
PAD = 16
SEG = 32

courant = 0.45
depth_floor = 0.1

GRID_AXES = ("lon", "lat", "gau")
ROW_AXES = ("lat", "gau")
VMEM_LIMIT = 48 * 1024 * 1024


def roll_lanes(x, shift):
    shift = shift % LANES
    return x if shift == 0 else pltpu.roll(x, shift, 1)


def lane_iota(rows):
    return lax.broadcasted_iota(jnp.int32, (rows, LANES), 1)


def pack_lanes(pieces):
    rows = pieces[0][0].shape[0]
    segment = lane_iota(rows) // SEG
    packed = jnp.zeros((rows, LANES), jnp.float32)
    for place, (array, first) in enumerate(pieces):
        packed = jnp.where(segment == place, roll_lanes(array, place * SEG - first), packed)
    return packed


def gauge_rows(owned):
    if 3 * owned <= LANES:
        return STEPS_BLOCK, owned
    assert owned <= LANES
    return 3 * STEPS_BLOCK, 0


def my_place():
    row = lax.axis_index("lat") * lax.axis_size("gau") + lax.axis_index("gau")
    return row, lax.axis_index("lon"), lax.axis_size("lat") * lax.axis_size("gau"), lax.axis_size("lon")


def prepare(
    halo, keep_ref, gain_ref, coast_ref, route_ref, cell_ref, times_ref, resid_ref,
    parcel_ref, rows_ref, strips_ref, block_ref,
):
    height, width = keep_ref.shape
    my_row, my_lon, row_tiles, lons = my_place()
    keep, gain = keep_ref[...], gain_ref[...]
    half = height // 2
    first, last = slice(0, LANES), slice(width - LANES, width)
    end = LANES - halo

    owned = route_ref.shape[1]
    blocks, samples = times_ref.shape[:2]
    assert blocks == 2
    route, coast = route_ref[...], coast_ref[...]
    target = jnp.zeros_like(route)
    for entry in range(coast.shape[1]):
        target = jnp.where(route == entry, jnp.broadcast_to(coast[:, entry : entry + 1], route.shape), target)
    cell = cell_ref[...]
    row_bits, width_bits = int(math.log2(row_tiles)), int(math.log2(width))
    assert row_tiles == 1 << row_bits and width == 1 << width_bits
    grid_row = (target & (row_tiles - 1)) * height + (cell >> width_bits)
    grid_col = (target >> row_bits) * width + (cell & (width - 1))
    block_ref[...] = jnp.zeros_like(block_ref)
    levels = lax.broadcasted_iota(jnp.int32, (STEPS_BLOCK, owned), 0)
    for block in range(blocks):
        times, resid = times_ref[block], resid_ref[block]
        series = jnp.zeros((STEPS_BLOCK, owned), jnp.float32)
        for sample in range(samples):
            series = series + jnp.where(times[sample : sample + 1] == levels, resid[sample : sample + 1], 0.0)
        block_ref[block * STEPS_BLOCK : (block + 1) * STEPS_BLOCK, :owned] = series
    at = blocks * STEPS_BLOCK
    block_ref[at : at + 1, :owned] = grid_row.astype(jnp.float32)
    block_ref[at + 1 : at + 2, :owned] = grid_col.astype(jnp.float32)
    size, apart = gauge_rows(owned)
    gauges = block_ref[...]
    if size == STEPS_BLOCK:
        gauges = sum(
            roll_lanes(gauges[i * STEPS_BLOCK : (i + 1) * STEPS_BLOCK], i * apart) for i in range(3)
        )
    tiles = parcel_ref.shape[0]

    def put(tile, carry):
        parcel_ref[tile, 0:size, :] = gauges
        return carry

    lax.fori_loop(0, tiles, put, 0, unroll=tiles <= 16)

    for d_row in (-1, 1):
        top = 0 if d_row < 0 else height - halo
        for d_lon in (-1, 1):
            cols, start = (first, 0) if d_lon < 0 else (last, end)
            to_row, to_lon = my_row + d_row, my_lon + d_lon
            there = (to_row >= 0) & (to_row < row_tiles) & (to_lon >= 0) & (to_lon < lons)

            @pl.when(there)
            def _():
                for kind, source in enumerate((keep, gain)):
                    corner = pack_lanes([(source[top + 8 * i : top + 8 * i + 8, cols], start) for i in range(4)])
                    parcel_ref[to_lon * row_tiles + to_row, size + 8 * kind : size + 8 * kind + 8, :] = corner

        there = (my_row + d_row >= 0) & (my_row + d_row < row_tiles)

        @pl.when(there)
        def _():
            rows_ref[my_row + d_row, 0] = keep[top : top + halo]
            rows_ref[my_row + d_row, 1] = gain[top : top + halo]

    for d_lon in (-1, 1):
        cols, start = (first, 0) if d_lon < 0 else (last, end)
        there = (my_lon + d_lon >= 0) & (my_lon + d_lon < lons)

        @pl.when(there)
        def _():
            strips_ref[my_lon + d_lon] = pack_lanes(
                [(keep[:half, cols], start), (gain[:half, cols], start), (keep[half:, cols], start), (gain[half:, cols], start)]
            )


def shift_from(planes, shift, lanes):
    count = len(planes)
    rolled = [roll_lanes(plane, -shift) for plane in planes]
    if shift > 0:
        return [jnp.where(lanes >= LANES - shift, rolled[(c + 1) % count], rolled[c]) for c in range(count)]
    return [jnp.where(lanes < -shift, rolled[(c - 1) % count], rolled[c]) for c in range(count)]


def sweep(
    steps, owned, keep_ref, gain_ref, rows_ref, strips_ref, parcel_ref,
    grad_ref, sums_ref,
    a, fx, fy, keep_x, gain_x, keep_all, gain_all, force0, force1, series_ref, rows_hot, cols_hot,
):
    height, width = keep_ref.shape
    halo = 2 * steps
    inner = width // LANES
    planes = inner + 1
    rows_all = a.shape[1]
    base = PAD + halo
    my_row, my_lon, row_tiles, lons = my_place()
    end = LANES - halo
    size, apart = gauge_rows(owned)

    for ref in (a, fx, fy):
        ref[...] = jnp.zeros_like(ref)

    def known(condition, value):
        return jnp.where(jnp.where(condition, 1, 0) == 1, value, 0.0)

    half = height // 2
    has_top, has_bottom = my_row > 0, my_row < row_tiles - 1
    has_left, has_right = my_lon > 0, my_lon < lons - 1
    above, below = jnp.maximum(my_row - 1, 0), jnp.minimum(my_row + 1, row_tiles - 1)
    left, right = jnp.maximum(my_lon - 1, 0), jnp.minimum(my_lon + 1, lons - 1)
    for kind, (source, whole) in enumerate(((keep_ref, keep_all), (gain_ref, gain_all))):
        for c in range(planes):
            whole[c, 0:PAD, :] = jnp.zeros((PAD, LANES), jnp.float32)
            whole[c, rows_all - PAD :, :] = jnp.zeros((PAD, LANES), jnp.float32)
        for c in range(inner):
            cols = slice(c * LANES, (c + 1) * LANES)
            whole[c, base : base + height, :] = source[:, cols]
            whole[c, PAD:base, :] = known(has_top, rows_ref[above, kind, :, cols])
            whole[c, base + height : base + height + halo, :] = known(has_bottom, rows_ref[below, kind, :, cols])
        segment = lane_iota(half) // SEG
        from_left, from_right = strips_ref[left], strips_ref[right]
        for part in range(2):
            piece = 2 * part + kind
            by_left = known(has_left, roll_lanes(from_left, end - piece * SEG))
            by_right = known(has_right, roll_lanes(from_right, -piece * SEG))
            both = jnp.where(segment == 0, by_right, jnp.where(segment == LANES // SEG - 1, by_left, 0.0))
            whole[inner, base + part * half : base + (part + 1) * half, :] = both
        segment = lane_iota(8) // SEG
        for has_row, row, at in ((has_top, above, PAD), (has_bottom, below, base + height)):
            by_left = known(has_row & has_left, parcel_ref[left * row_tiles + row, size + 8 * kind : size + 8 * kind + 8, :])
            by_right = known(has_row & has_right, parcel_ref[right * row_tiles + row, size + 8 * kind : size + 8 * kind + 8, :])
            for i in range(4):
                both = jnp.where(
                    segment == 0, roll_lanes(by_right, -i * SEG),
                    jnp.where(segment == LANES // SEG - 1, roll_lanes(by_left, end - i * SEG), 0.0),
                )
                whole[inner, at + 8 * i : at + 8 * i + 8, :] = both

    lanes8 = lane_iota(8)
    for whole, by_x in ((keep_all, keep_x), (gain_all, gain_x)):
        for r in range(PAD, rows_all - PAD, 8):
            shifted = shift_from([whole[c, r : r + 8, :] for c in range(planes)], 1, lanes8)
            for c in range(planes):
                by_x[c, r : r + 8, :] = shifted[c]

    group = rows_hot.shape[1] // owned
    wide = group * owned
    groups = parcel_ref.shape[0] // group
    per_plane = LANES // owned
    row_shift = (base - my_row * height).astype(jnp.float32)
    col_shift = (-my_lon * width).astype(jnp.float32)

    def gather_gauges(index):
        lanes = lane_iota(STEPS_BLOCK)
        for part in range(wide // LANES):
            cols = slice(part * LANES, (part + 1) * LANES)
            fields = []
            for field in range(3):
                total = jnp.zeros((STEPS_BLOCK, LANES), jnp.float32)
                rows = slice(0, 8) if apart else slice(8 * field, 8 * field + 8)
                for i in range(per_plane):
                    source = index * group + part * per_plane + i
                    block = roll_lanes(parcel_ref[source, rows, :], i * owned - field * apart)
                    total = jnp.where((lanes >= i * owned) & (lanes < (i + 1) * owned), block, total)
                fields.append(total)
            series_ref[0:8, cols] = fields[0]
            series_ref[8:16, cols] = fields[1]
            row = fields[2][0:1] + row_shift
            col = fields[2][1:2] + col_shift
            col = jnp.where((col >= -halo) & (col < 0), col + float(planes * LANES), jnp.where(col < width + halo, col, -1.0))
            at = lax.broadcasted_iota(jnp.int32, (rows_all, LANES), 0).astype(jnp.float32)
            rows_hot[:, cols] = (at == row).astype(jnp.float32).astype(jnp.bfloat16)
            by_gauge = jnp.transpose(jnp.broadcast_to(col, (LANES, LANES)))
            for c in range(planes):
                place = (lane_iota(LANES) + c * LANES).astype(jnp.float32)
                cols_hot[part * LANES : (part + 1) * LANES, c * LANES : (c + 1) * LANES] = (
                    (by_gauge == place).astype(jnp.float32).astype(jnp.bfloat16)
                )

    def pieces_of(level, lo, hi, goal, add=False):
        lo, hi = lo // 16 * 16, -(-hi // 16) * 16
        value = series_ref[pl.ds(level, 1), :]
        high = value.astype(jnp.bfloat16)
        low = (value - high.astype(jnp.float32)).astype(jnp.bfloat16)
        hot = rows_hot[lo:hi, :]
        both = jnp.concatenate([hot * high, hot * low], axis=0)

        def piece(first, count):
            total = jnp.dot(
                both, cols_hot[:, first * LANES : (first + count) * LANES], preferred_element_type=jnp.float32
            )
            total = total[: hi - lo] + total[hi - lo :]
            for c in range(count):
                part = total[:, c * LANES : (c + 1) * LANES]
                goal[first + c, lo:hi, :] = goal[first + c, lo:hi, :] + part if add else part

        return [functools.partial(piece, first, min(2, planes - first)) for first in range(0, planes, 2)]

    def pieces_for(level, lo, hi, goal):
        if groups == 1:
            return pieces_of(level, lo, hi, goal)

        def whole():
            goal[...] = jnp.zeros_like(goal)

            def more(index, carry):
                gather_gauges(index)
                for piece in pieces_of(level, lo, hi, goal, True):
                    piece()
                return carry

            lax.fori_loop(0, groups, more, 0)

        return [whole]

    if groups == 1:
        gather_gauges(0)

    col_valid = jnp.where(lanes8 < LANES // 2, jnp.where(has_right, 1.0, 0.0), jnp.where(has_left, 1.0, 0.0))
    col_mask = jnp.where((lanes8 < halo) | (lanes8 >= end), col_valid, 0.0)
    row_above, row_below = jnp.where(has_top, 1.0, 0.0), jnp.where(has_bottom, 1.0, 0.0)

    def advance(step, force, pieces):
        spare = 2 * step // 8 * 8
        lo, hi = PAD + spare, rows_all - PAD - spare
        every = (hi - lo) // 8 // max(1, len(pieces))
        pieces = list(pieces)
        for r in range(lo, hi, 8):
            if pieces and (r - lo) // 8 % every == 0:
                pieces.pop(0)()
            here = [a[c, r : r + 8, :] for c in range(planes)]
            ahead = shift_from(here, 2, lanes8)
            new_x = [
                keep_x[c, r : r + 8, :] * fx[c, r : r + 8, :] + gain_x[c, r : r + 8, :] * (ahead[c] - here[c])
                for c in range(planes)
            ]
            behind = shift_from(new_x, -2, lanes8)
            for c in range(planes):
                new_y = keep_all[c, r + 1 : r + 9, :] * fy[c, r : r + 8, :] + gain_all[c, r + 1 : r + 9, :] * (
                    a[c, r + 2 : r + 10, :] - here[c]
                )
                fx[c, r : r + 8, :] = new_x[c]
                fy[c, r : r + 8, :] = new_y
                value = here[c] + (new_x[c] - behind[c]) + (new_y - fy[c, r - 2 : r + 6, :])
                if c == inner:
                    value = value * col_mask
                if r == base - 8:
                    value = value * row_above
                if r == base + height:
                    value = value * row_below
                if force is not None:
                    value = value + force[c, r : r + 8, :]
                a[c, r : r + 8, :] = value
        assert not pieces

    last = steps - 1
    for order, goal in ((0, a), (1, force1)):
        for piece in pieces_for(last - order, PAD, rows_all - PAD, goal):
            piece()

    def pair(step, like):
        for odd in range(2):
            spare = 2 * like // 8 * 8
            uses, makes = (force1, force0) if odd == 0 else (force0, force1)
            pieces = pieces_for(last - 2 - step - odd, PAD + spare, rows_all - PAD - spare, makes)
            advance(like, uses, pieces)

    for start in range(0, steps, 4):
        if start + 4 < steps:

            def body(index, carry, start=start):
                pair(start + 2 * index, start)
                return carry

            lax.fori_loop(0, 2, body, 0)
        else:
            pair(start, start)
            advance(start, force1, [])
            advance(start, None, [])

    grad = jnp.concatenate([a[c, base : base + height, :] for c in range(inner)], axis=1)
    grad = jnp.where(keep_ref[...] > 0.0, grad, 0.0)
    grad_ref[...] = grad
    length = 2.0 * width
    kind = lax.broadcasted_iota(jnp.int32, (8, width), 0)
    column = lax.broadcasted_iota(jnp.int32, (8, width), 1)
    steps_off = jnp.where(kind == 0, column, width - 1 - column).astype(jnp.float32)
    weights = jnp.where(kind < 2, jnp.exp(-steps_off / length), 0.0)
    sums = lax.dot_general(
        weights, grad, (((1,), (1,)), ((), ())), precision=lax.Precision.HIGHEST, preferred_element_type=jnp.float32
    )
    for i in range(sums_ref.shape[0]):
        sums_ref[i] = sums


def smooth(grad_ref, out_ref):
    width = grad_ref.shape[1]
    length = 2.0 * width
    row = lax.broadcasted_iota(jnp.int32, (width, width), 0)
    column = lax.broadcasted_iota(jnp.int32, (width, width), 1)
    kernel = jnp.exp(-jnp.abs(row - column).astype(jnp.float32) / length)
    out_ref[...] = jnp.dot(
        grad_ref[...], kernel, precision=lax.Precision.HIGHEST, preferred_element_type=jnp.float32
    )


def finish(own_ref, sums_ref, out_ref):
    width = own_ref.shape[1]
    length = 2.0 * width
    count = sums_ref.shape[0]
    me = lax.axis_index("lon")
    row = lax.broadcasted_iota(jnp.int32, (count, width), 0)
    column = lax.broadcasted_iota(jnp.int32, (count, width), 1)
    strip, kind = row >> 3, row & 7
    left = (kind == 0) & (strip > me)
    right = (kind == 1) & (strip < me)
    away = jnp.where(left, (strip - me) * width - column, (me - strip - 1) * width + column + 1)
    weights = jnp.where(left | right, jnp.exp(-jnp.maximum(away, 0).astype(jnp.float32) / length), 0.0)
    out_ref[...] = own_ref[...] + lax.dot_general(
        sums_ref[...], weights, (((0,), (0,)), ((), ())), precision=lax.Precision.HIGHEST,
        preferred_element_type=jnp.float32,
    )


def f32(*shape):
    return jax.ShapeDtypeStruct(shape, jnp.float32)


def vmem(count):
    return [pl.BlockSpec(memory_space=pltpu.VMEM)] * count


def local(depth, surface, friction, wet, coastal_tiles, gauge_route, gauge_cell, gauge_times, gauge_resid):
    height, width = depth.shape
    owned = gauge_route.shape[0]
    blocks = gauge_resid.shape[1]
    steps = blocks * STEPS_BLOCK
    halo = 2 * steps
    assert halo == SEG and height == LANES
    tiles = lax.axis_size(GRID_AXES)
    lons = lax.axis_size("lon")
    row_tiles = lax.axis_size(ROW_AXES)
    parcel_rows = gauge_rows(owned)[0] + 16
    params = pltpu.CompilerParams(vmem_limit_bytes=VMEM_LIMIT)

    keep = (1.0 - friction) * wet.astype(jnp.float32)
    gain = ((courant * 0.5) ** 2 * jnp.maximum(depth + surface, depth_floor)) * keep
    parcel, rows, strips = pl.pallas_call(
        functools.partial(prepare, halo),
        out_shape=(
            f32(tiles, parcel_rows, LANES), f32(row_tiles, 2, halo, width), f32(lons, height // 2, LANES),
        ),
        in_specs=vmem(7),
        out_specs=tuple(vmem(3)),
        scratch_shapes=[pltpu.VMEM((24, LANES), jnp.float32)],
        compiler_params=params,
        name="prepare",
    )(
        keep, gain, coastal_tiles.reshape(1, -1), gauge_route.reshape(1, owned), gauge_cell.reshape(1, owned),
        jnp.transpose(gauge_times, (1, 2, 0)), jnp.transpose(gauge_resid, (1, 2, 0)),
    )

    def exchange(array, axes):
        return lax.all_to_all(array, axes, split_axis=0, concat_axis=0, tiled=True)

    rows = exchange(rows, ROW_AXES)
    strips = exchange(strips, "lon")
    parcel = exchange(parcel, GRID_AXES)

    planes = width // LANES + 1
    rows_all = height + 2 * halo + 2 * PAD
    wide = max(2 * LANES, owned)
    plane = pltpu.VMEM((planes, rows_all, LANES), jnp.float32)
    grad, sums = pl.pallas_call(
        functools.partial(sweep, steps, owned),
        out_shape=(f32(height, width), f32(lons, 8, height)),
        in_specs=vmem(5),
        out_specs=tuple(vmem(2)),
        scratch_shapes=[plane] * 9 + [
            pltpu.VMEM((steps, wide), jnp.float32),
            pltpu.VMEM((rows_all, wide), jnp.bfloat16),
            pltpu.VMEM((wide, planes * LANES), jnp.bfloat16),
        ],
        compiler_params=params,
        name="sweep",
    )(keep, gain, rows, strips, parcel)

    sums = exchange(sums, "lon")
    own = pl.pallas_call(
        smooth, out_shape=f32(height, width), in_specs=vmem(1), out_specs=vmem(1)[0], compiler_params=params,
        cost_estimate=pl.CostEstimate(
            flops=6 * 2 * height * width * width, bytes_accessed=2 * 4 * height * width, transcendentals=width * width
        ),
        name="smooth",
    )(grad)
    return pl.pallas_call(
        finish, out_shape=f32(height, width), in_specs=vmem(2), out_specs=vmem(1)[0], compiler_params=params, name="finish",
    )(own, sums.reshape(lons * 8, height))


def solution(mesh):
    in_specs = (
        P(("lat", "gau"), "lon"),
        P(("scen", "lat", "gau"), "lon"),
        P(("lat", "gau"), "lon"),
        P(("lat", "gau"), "lon"),
        P(),
        P(("scen", "lon", "lat", "gau"), None),
        P(("scen", "lon", "lat", "gau")),
        P(("scen", "lon", "lat", "gau"), None, None),
        P(("scen", "lon", "lat", "gau"), None, None),
    )
    out_specs = P(("scen", "lat", "gau"), "lon")
    return jax.shard_map(local, mesh=mesh, in_specs=in_specs, out_specs=out_specs, check_vma=False)
```

time: 53.9 us -> 67.6 us (1.25)
  the two profiles are of different devices: /device:TPU:2 before, /device:TPU:0 now
where the time goes in v2:
time: 67.6 us; the launch traced here: 67.3 us
  blocking collectives  35.9 us (53%)
  Pallas kernels  21.4 us (32%)
  waiting for transfers between devices  4.67 us (7%)
  starting transfers between devices  3.25 us (5%)
  other arithmetic  1.3 us (2%)
    all_to_all x3, blocking collectives, exchange(): return lax.all_to_all(array, axes, split_axis=0, concat_axis=0, tiled=True)  35.9 us
    pallas_call x1, Pallas kernels, local(): pl.pallas_call(functools.partial(sweep, steps, owned), out_shape=(f32(hei...  19 us
    all_to_all x1, waiting for transfers between devices, exchange(): return lax.all_to_all(array, axes, split_axis=0, concat_axis=0, tiled=True)  4.67 us
    all_to_all x1, starting transfers between devices, exchange(): return lax.all_to_all(array, axes, split_axis=0, concat_axis=0, tiled=True)  3.25 us
  transfers between devices with their start and end apart: 1, of which 1 were waited for; matrix products, arithmetic and copies ran while one was open for 0% of the time, Pallas kernels for 1%

profile of v2, /device:TPU:0, one launch (start us, length us, event | category | flops | bytes accessed | tf_op | source)
XLA Modules:
  0.0 67.3 jit_solution(18164299789860916435)
XLA Ops:
  0.0 0.0 copy-start.4
  0.0 1.3 %multiply_multiply_fusion = (f32[128,512]{1,0:T(8,128)S(1)}, f32[128,512]{1,0:T(8,128)S(1)}) fusion(f32[128,512]{1,0:T(8,128)} %param.9, f32[128,512]{1,0:T(8,128)} %param.10, s32[128,512]{1,0:T(8,128)} %param.12, f32[128,512]{1,0:T(8,128)} %param.11), kind=kLoop, calls=%fused_computation | loop fusion | flops 458752 | bytes 1572864 | tf_op jit(solution)/shard_map/mul | solution.py:403
  1.3 0.0 copy-start.1
  1.3 0.0 copy-start
  1.3 0.0 copy-start.2
  1.3 0.0 copy-start.3
  1.4 0.0 copy-done.4
  1.4 0.6 copy-done.1
  2.0 0.0 copy-done
  2.0 0.0 copy-done.2
  2.0 0.0 copy-done.3
  2.0 0.3 prepare.1
  2.4 12.2 %all_to_all.20.strips_ref = f32[4,64,128]{2,1,0:T(8,128)S(1)} all-to-all(f32[4,64,128]{2,1,0:T(8,128)S(1)} %get-tuple-element.11), channel_id=1, replica_groups=mesh['scen'=2,'lon'=4,'lat'=2,'gau'=2] {'lon'}, dimensions={0} | all-to-all | bytes 262144 | tf_op jit(solution)/shard_map/all_to_all | solution.py:420
  14.6 12.5 %all_to_all.21.parcel_ref = f32[16,24,128]{2,1,0:T(8,128)S(1)} all-to-all(f32[16,24,128]{2,1,0:T(8,128)S(1)} %get-tuple-element.12), channel_id=1, replica_groups=mesh['scen'=2,'lon'=4,'lat'=2,'gau'=2] {'lon','lat','gau'}, dimensions={0} | all-to-all | bytes 393216 | tf_op jit(solution)/shard_map/all_to_all | solution.py:420
  27.1 11.2 %all_to_all.22.rows_ref = f32[4,2,32,512]{3,2,1,0:T(8,128)S(1)} all-to-all(f32[4,2,32,512]{3,2,1,0:T(8,128)S(1)} %get-tuple-element.10), channel_id=1, replica_groups=mesh['scen'=2,'lon'=4,'lat'=2,'gau'=2] {'lat','gau'}, dimensions={0} | all-to-all | bytes 1048576 | tf_op jit(solution)/shard_map/all_to_all | solution.py:420
  38.3 19.0 %sweep.1 = (f32[128,512]{1,0:T(8,128)S(1)}, f32[4,8,128]{2,1,0:T(8,128)}) custom-call(f32[128,512]{1,0:T(8,128)S(1)} %get-tuple-element.16.keep_ref, f32[128,512]{1,0:T(8,128)S(1)} %get-tuple-element.15.gain_ref, f32[4,2,32,512]{3,2,1,0:T(8,128)S(1)} %all_to_all.22.rows_ref, f32[4,64,128]{2,1,0:T(8,128)S(1)} %all_to_all.20.strips_ref, ...), custom_call_target="tpu_custom_call" | custom-call | tf_op jit(solution)/shard_map/sweep/pallas_call | solution.py:430
  57.3 3.3 %all-to-all-start.3 = ((f32[4,8,128]{2,1,0:T(8,128)}), f32[4,8,128]{2,1,0:T(8,128)S(1)}, u32[]{:S(2)}, u32[]{:S(2)}) async-start(f32[4,8,128]{2,1,0:T(8,128)} %get-tuple-element.14), calls=%async_computation.3 | async-start | bytes 32768 | tf_op jit(solution)/shard_map/all_to_all | solution.py:420
  60.6 0.9 %smooth.1.own_ref = f32[128,512]{1,0:T(8,128)S(1)} custom-call(f32[128,512]{1,0:T(8,128)S(1)} %get-tuple-element.13.grad_ref), custom_call_target="tpu_custom_call" | custom-call | flops 402653184 | bytes 524288 | tf_op jit(solution)/shard_map/smooth/pallas_call | solution.py:445
  61.5 4.7 %all-to-all-done.3 = f32[4,8,128]{2,1,0:T(8,128)S(1)} async-done(((f32[4,8,128]{2,1,0:T(8,128)}), f32[4,8,128]{2,1,0:T(8,128)S(1)}, u32[]{:S(2)}, u32[]{:S(2)}) %all-to-all-start.3) | async-done | bytes 16416 | tf_op jit(solution)/shard_map/all_to_all | solution.py:420
  66.1 1.1 %finish.1 = f32[128,512]{1,0:T(8,128)} custom-call(f32[128,512]{1,0:T(8,128)S(1)} %smooth.1.own_ref, f32[32,128]{1,0:T(8,128)S(1)} %bitcast.6), custom_call_target="tpu_custom_call" | custom-call | tf_op jit(solution)/shard_map/finish/pallas_call | solution.py:452
Async XLA Ops:
  0.0 1.4 %copy-start.4 = (s32[16]{0:T(128)S(1)}, s32[16]{0:T(128)}, u32[]{:S(2)}) copy-start(s32[16]{0:T(128)} %param.15) | copy-start | bytes 196
  1.3 0.7 %copy-start.1 = (f32[16,2,4]{0,2,1:T(4,128)S(1)}, f32[16,2,4]{0,2,1:T(4,128)}, u32[]{:S(2)}) copy-start(f32[16,2,4]{0,2,1:T(4,128)} %param.17) | copy-start | bytes 1540
  1.3 0.7 %copy-start = (s32[16,2,4]{0,2,1:T(4,128)S(1)}, s32[16,2,4]{0,2,1:T(4,128)}, u32[]{:S(2)}) copy-start(s32[16,2,4]{0,2,1:T(4,128)} %param.16) | copy-start | bytes 1540
  1.3 0.7 %copy-start.2 = (s32[8]{0:T(128)S(1)}, s32[8]{0:T(128)}, u32[]{:S(2)}) copy-start(s32[8]{0:T(128)} %param.13) | copy-start | bytes 100
  1.3 0.7 %copy-start.3 = (s32[16,1]{0,1:T(1,128)S(1)}, s32[16,1]{0,1:T(1,128)}, u32[]{:S(2)}) copy-start(s32[16,1]{0,1:T(1,128)} %param.14) | copy-start | bytes 196
  57.3 8.8 %all-to-all-start.3 = ((f32[4,8,128]{2,1,0:T(8,128)}), f32[4,8,128]{2,1,0:T(8,128)S(1)}, u32[]{:S(2)}, u32[]{:S(2)}) async-start(f32[4,8,128]{2,1,0:T(8,128)} %get-tuple-element.14), calls=%async_computation.3 | async-start | bytes 32768 | tf_op jit(solution)/shard_map/all_to_all | solution.py:420

commit v3 on v2

v3 whole, which is shorter than its diff:
```python
import functools
import math

import jax
import jax.numpy as jnp
from jax import lax
from jax.experimental import pallas as pl
from jax.experimental.pallas import tpu as pltpu
from jax.sharding import PartitionSpec as P

STEPS_BLOCK = 8
LANES = 128
SEG = 32

courant = 0.45
depth_floor = 0.1

GRID_AXES = ("lon", "lat", "gau")
ROW_AXES = ("lat", "gau")
VMEM_LIMIT = 16 * 1024 * 1024


def roll_lanes(x, shift):
    shift = shift % LANES
    return x if shift == 0 else pltpu.roll(x, shift, 1)


def lane_iota(rows):
    return lax.broadcasted_iota(jnp.int32, (rows, LANES), 1)


def pack_lanes(pieces):
    rows = pieces[0][0].shape[0]
    segment = lane_iota(rows) // SEG
    packed = jnp.zeros((rows, LANES), jnp.float32)
    for place, (array, first) in enumerate(pieces):
        packed = jnp.where(segment == place, roll_lanes(array, place * SEG - first), packed)
    return packed


def gauge_rows(owned):
    if 3 * owned <= LANES:
        return STEPS_BLOCK, owned
    assert owned <= LANES
    return 3 * STEPS_BLOCK, 0


def my_place():
    row = lax.axis_index("lat") * lax.axis_size("gau") + lax.axis_index("gau")
    return row, lax.axis_index("lon"), lax.axis_size("lat") * lax.axis_size("gau"), lax.axis_size("lon")


def prepare(
    halo, keep_ref, gain_ref, coast_ref, route_ref, cell_ref, times_ref, resid_ref,
    parcel_ref, south_ref, north_ref, east_ref, west_ref, block_ref,
):
    height, width = keep_ref.shape
    my_row, my_lon, row_tiles, lons = my_place()
    keep, gain = keep_ref[...], gain_ref[...]
    half = height // 2
    first, last = slice(0, LANES), slice(width - LANES, width)
    end = LANES - halo

    owned = route_ref.shape[1]
    blocks, samples = times_ref.shape[:2]
    assert blocks == 2
    route, coast = route_ref[...], coast_ref[...]
    target = jnp.zeros_like(route)
    for entry in range(coast.shape[1]):
        target = jnp.where(route == entry, jnp.broadcast_to(coast[:, entry : entry + 1], route.shape), target)
    cell = cell_ref[...]
    row_bits, width_bits = int(math.log2(row_tiles)), int(math.log2(width))
    assert row_tiles == 1 << row_bits and width == 1 << width_bits
    grid_row = (target & (row_tiles - 1)) * height + (cell >> width_bits)
    grid_col = (target >> row_bits) * width + (cell & (width - 1))
    block_ref[...] = jnp.zeros_like(block_ref)
    levels = lax.broadcasted_iota(jnp.int32, (STEPS_BLOCK, owned), 0)
    for block in range(blocks):
        times, resid = times_ref[block], resid_ref[block]
        series = jnp.zeros((STEPS_BLOCK, owned), jnp.float32)
        for sample in range(samples):
            series = series + jnp.where(times[sample : sample + 1] == levels, resid[sample : sample + 1], 0.0)
        block_ref[block * STEPS_BLOCK : (block + 1) * STEPS_BLOCK, :owned] = series
    at = blocks * STEPS_BLOCK
    block_ref[at : at + 1, :owned] = grid_row.astype(jnp.float32)
    block_ref[at + 1 : at + 2, :owned] = grid_col.astype(jnp.float32)
    size, apart = gauge_rows(owned)
    gauges = block_ref[...]
    if size == STEPS_BLOCK:
        gauges = sum(
            roll_lanes(gauges[i * STEPS_BLOCK : (i + 1) * STEPS_BLOCK], i * apart) for i in range(3)
        )
    tiles = parcel_ref.shape[0]

    def put(tile, carry):
        parcel_ref[tile, 0:size, :] = gauges
        return carry

    lax.fori_loop(0, tiles, put, 0, unroll=tiles <= 16)

    for d_row in (-1, 1):
        top = 0 if d_row < 0 else height - halo
        for d_lon in (-1, 1):
            cols, start = (first, 0) if d_lon < 0 else (last, end)
            to_row, to_lon = my_row + d_row, my_lon + d_lon
            there = (to_row >= 0) & (to_row < row_tiles) & (to_lon >= 0) & (to_lon < lons)

            @pl.when(there)
            def _():
                for kind, source in enumerate((keep, gain)):
                    corner = pack_lanes([(source[top + 8 * i : top + 8 * i + 8, cols], start) for i in range(4)])
                    parcel_ref[to_lon * row_tiles + to_row, size + 8 * kind : size + 8 * kind + 8, :] = corner

    south_ref[0], south_ref[1] = keep[height - halo :], gain[height - halo :]
    north_ref[0], north_ref[1] = keep[:halo], gain[:halo]
    for goal, cols, start in ((east_ref, last, end), (west_ref, first, 0)):
        goal[...] = pack_lanes(
            [(keep[:half, cols], start), (gain[:half, cols], start), (keep[half:, cols], start), (gain[half:, cols], start)]
        )


def shift_from(planes, shift, lanes):
    count = len(planes)
    rolled = [roll_lanes(plane, -shift) for plane in planes]
    if shift > 0:
        return [jnp.where(lanes >= LANES - shift, rolled[(c + 1) % count], rolled[c]) for c in range(count)]
    return [jnp.where(lanes < -shift, rolled[(c - 1) % count], rolled[c]) for c in range(count)]


def force(steps, halo, height, width, parcel_ref, force_ref, series_ref, rows_hot, cols_hot):
    planes, rows_all = force_ref.shape[1:3]
    my_row, my_lon, row_tiles, lons = my_place()
    wide = rows_hot.shape[1]
    tiles, parcel_rows = parcel_ref.shape[:2]
    size = parcel_rows - 16
    apart = wide // tiles if size == STEPS_BLOCK else 0
    owned = apart if apart else LANES
    group = wide // owned
    groups = tiles // group
    per_plane = LANES // owned
    blocks = rows_all // 8
    row_shift = (halo - my_row * height).astype(jnp.float32)
    col_shift = (-my_lon * width).astype(jnp.float32)
    place = lax.broadcasted_iota(jnp.int32, (rows_all, LANES), 0)
    at = ((place & 7) * blocks + (place >> 3)).astype(jnp.float32)

    def gather_gauges(index):
        lanes = lane_iota(STEPS_BLOCK)
        for part in range(wide // LANES):
            cols = slice(part * LANES, (part + 1) * LANES)
            fields = []
            for field in range(3):
                total = jnp.zeros((STEPS_BLOCK, LANES), jnp.float32)
                rows = slice(0, 8) if apart else slice(8 * field, 8 * field + 8)
                for i in range(per_plane):
                    source = index * group + part * per_plane + i
                    block = roll_lanes(parcel_ref[source, rows, :], i * owned - field * apart)
                    total = jnp.where((lanes >= i * owned) & (lanes < (i + 1) * owned), block, total)
                fields.append(total)
            series_ref[0:8, cols] = fields[0]
            series_ref[8:16, cols] = fields[1]
            row = fields[2][0:1] + row_shift
            col = fields[2][1:2] + col_shift
            col = jnp.where((col >= -halo) & (col < 0), col + float(planes * LANES), jnp.where(col < width + halo, col, -1.0))
            rows_hot[:, cols] = (at == row).astype(jnp.float32).astype(jnp.bfloat16)
            by_gauge = jnp.transpose(jnp.broadcast_to(col, (LANES, LANES)))
            for c in range(planes):
                spot = (lane_iota(LANES) + c * LANES).astype(jnp.float32)
                hot = (by_gauge == spot).astype(jnp.float32).astype(jnp.bfloat16)
                cols_hot[part * LANES : (part + 1) * LANES, c * LANES : (c + 1) * LANES] = hot
                cols_hot[wide + part * LANES : wide + (part + 1) * LANES, c * LANES : (c + 1) * LANES] = hot

    def level_of(level, add):
        value = series_ref[pl.ds(level, 1), :]
        high = value.astype(jnp.bfloat16)
        low = (value - high.astype(jnp.float32)).astype(jnp.bfloat16)
        hot = rows_hot[...]
        both = jnp.concatenate([hot * high, hot * low], axis=1)
        for first in range(0, planes, 2):
            count = min(2, planes - first)
            total = jnp.dot(
                both, cols_hot[:, first * LANES : (first + count) * LANES], preferred_element_type=jnp.float32
            )
            for c in range(count):
                part = total[:, c * LANES : (c + 1) * LANES]
                force_ref[level, first + c] = force_ref[level, first + c] + part if add else part

    def levels(add):
        def one(level, carry):
            level_of(level, add)
            return carry

        lax.fori_loop(0, steps, one, 0)

    gather_gauges(0)
    levels(False)
    if groups > 1:

        def more(index, carry):
            gather_gauges(index)
            levels(True)
            return carry

        lax.fori_loop(1, groups, more, 0)


def sweep(
    steps, keep_ref, gain_ref, top_ref, bottom_ref, left_ref, right_ref, parcel_ref, force_ref,
    grad_ref, sums_ref,
    a, fx, fy, keep_x, gain_x, keep_y, gain_y, plain,
):
    height, width = keep_ref.shape
    halo = 2 * steps
    inner = width // LANES
    planes = inner + 1
    rows_all = a.shape[1]
    blocks = rows_all // 8
    my_row, my_lon, row_tiles, lons = my_place()
    end = LANES - halo
    size = parcel_ref.shape[1] - 16
    has_top, has_bottom = my_row > 0, my_row < row_tiles - 1
    has_left, has_right = my_lon > 0, my_lon < lons - 1
    above, below = jnp.maximum(my_row - 1, 0), jnp.minimum(my_row + 1, row_tiles - 1)
    left, right = jnp.maximum(my_lon - 1, 0), jnp.minimum(my_lon + 1, lons - 1)
    lanes8 = lane_iota(8)

    def known(condition, value):
        return jnp.where(jnp.where(condition, 1, 0) == 1, value, 0.0)

    def up(value):
        return pltpu.roll(value, 7, 0)

    def down(value):
        return pltpu.roll(value, 1, 0)

    half = height // 2
    for kind, (source, by_x, by_y) in enumerate(((keep_ref, keep_x, keep_y), (gain_ref, gain_x, gain_y))):
        for c in range(inner):
            cols = slice(c * LANES, (c + 1) * LANES)
            plain[c, halo : halo + height, :] = source[:, cols]
            plain[c, 0:halo, :] = top_ref[kind, :, cols]
            plain[c, halo + height :, :] = bottom_ref[kind, :, cols]
        segment = lane_iota(half) // SEG
        for part in range(2):
            piece = 2 * part + kind
            by_left = roll_lanes(left_ref[...], end - piece * SEG)
            by_right = roll_lanes(right_ref[...], -piece * SEG)
            both = jnp.where(segment == 0, by_right, jnp.where(segment == LANES // SEG - 1, by_left, 0.0))
            plain[inner, halo + part * half : halo + (part + 1) * half, :] = both
        segment = lane_iota(8) // SEG
        for has_row, row, at in ((has_top, above, 0), (has_bottom, below, halo + height)):
            by_left = known(has_row & has_left, parcel_ref[left * row_tiles + row, size + 8 * kind : size + 8 * kind + 8, :])
            by_right = known(has_row & has_right, parcel_ref[right * row_tiles + row, size + 8 * kind : size + 8 * kind + 8, :])
            for i in range(4):
                both = jnp.where(
                    segment == 0, roll_lanes(by_right, -i * SEG),
                    jnp.where(segment == LANES // SEG - 1, roll_lanes(by_left, end - i * SEG), 0.0),
                )
                plain[inner, at + 8 * i : at + 8 * i + 8, :] = both
        for q in range(blocks):
            values = [plain[c, pl.ds(q, 8, stride=blocks), :] for c in range(planes)]
            shifted = shift_from(values, 1, lanes8)
            to = (q - 1) % blocks * 8
            for c in range(planes):
                by_x[c, 8 * q : 8 * q + 8, :] = shifted[c]
                by_y[c, to : to + 8, :] = up(values[c]) if q == 0 else values[c]

    for ref in (a, fx, fy):
        ref[...] = jnp.zeros_like(ref)

    col_valid = jnp.where(lanes8 < LANES // 2, jnp.where(has_right, 1.0, 0.0), jnp.where(has_left, 1.0, 0.0))
    col_mask = jnp.where((lanes8 < halo) | (lanes8 >= end), col_valid, 0.0)
    sublane = lax.broadcasted_iota(jnp.int32, (8, LANES), 0)
    row_mask = {}
    for row, there in ((halo - 1, has_top), (halo + height, has_bottom)):
        row_mask[row % blocks] = jnp.where(sublane == row // blocks, jnp.where(there, 1.0, 0.0), 1.0)
    every = range(planes)

    def step(index, carry):
        level = steps - 1 - index
        current, new_y = {}, {}

        def here(q):
            if q not in current:
                current[q] = [a[c, 8 * q : 8 * q + 8, :] + force_ref[level, c, 8 * q : 8 * q + 8, :] for c in every]
            return current[q]

        def move_y(q):
            near = here(q)
            ahead = here(q + 2) if q + 2 < blocks else [up(value) for value in here(q + 2 - blocks)]
            rows = slice(8 * q, 8 * q + 8)
            new_y[q] = [keep_y[c, rows, :] * fy[c, rows, :] + gain_y[c, rows, :] * (ahead[c] - near[c]) for c in every]
            for c in every:
                fy[c, rows, :] = new_y[q][c]

        def move(q):
            near = here(q)
            rows = slice(8 * q, 8 * q + 8)
            ahead = shift_from(near, 2, lanes8)
            new_x = [keep_x[c, rows, :] * fx[c, rows, :] + gain_x[c, rows, :] * (ahead[c] - near[c]) for c in every]
            behind = shift_from(new_x, -2, lanes8)
            before = new_y[q - 2] if q >= 2 else [down(value) for value in new_y[q - 2 + blocks]]
            for c in every:
                fx[c, rows, :] = new_x[c]
                value = near[c] + (new_x[c] - behind[c]) + (new_y[q][c] - before[c])
                if c == inner:
                    value = value * col_mask
                if q in row_mask:
                    value = value * row_mask[q]
                a[c, rows, :] = value

        move_y(0)
        move_y(1)
        for q in range(2, blocks):
            move_y(q)
            move(q)
        move(0)
        move(1)
        return carry

    lax.fori_loop(0, steps, step, 0)

    for r in range(0, height, 8):
        s, q = divmod(halo + r, blocks)
        for c in range(inner):
            cols = slice(c * LANES, (c + 1) * LANES)
            value = a[c, pl.ds(8 * q + s, 8, stride=8), :]
            grad_ref[r : r + 8, cols] = jnp.where(keep_ref[r : r + 8, cols] > 0.0, value, 0.0)
    length = 2.0 * width
    kind = lax.broadcasted_iota(jnp.int32, (8, width), 0)
    column = lax.broadcasted_iota(jnp.int32, (8, width), 1)
    steps_off = jnp.where(kind == 0, column, width - 1 - column).astype(jnp.float32)
    weights = jnp.where(kind < 2, jnp.exp(-steps_off / length), 0.0)
    sums = lax.dot_general(
        weights, grad_ref[...], (((1,), (1,)), ((), ())), precision=lax.Precision.HIGHEST,
        preferred_element_type=jnp.float32,
    )
    for i in range(sums_ref.shape[0]):
        sums_ref[i] = sums


def smooth(grad_ref, out_ref):
    width = grad_ref.shape[1]
    length = 2.0 * width
    row = lax.broadcasted_iota(jnp.int32, (width, width), 0)
    column = lax.broadcasted_iota(jnp.int32, (width, width), 1)
    kernel = jnp.exp(-jnp.abs(row - column).astype(jnp.float32) / length)
    out_ref[...] = jnp.dot(
        grad_ref[...], kernel, precision=lax.Precision.HIGHEST, preferred_element_type=jnp.float32
    )


def finish(own_ref, sums_ref, out_ref):
    width = own_ref.shape[1]
    length = 2.0 * width
    count = sums_ref.shape[0]
    me = lax.axis_index("lon")
    row = lax.broadcasted_iota(jnp.int32, (count, width), 0)
    column = lax.broadcasted_iota(jnp.int32, (count, width), 1)
    strip, kind = row >> 3, row & 7
    left = (kind == 0) & (strip > me)
    right = (kind == 1) & (strip < me)
    away = jnp.where(left, (strip - me) * width - column, (me - strip - 1) * width + column + 1)
    weights = jnp.where(left | right, jnp.exp(-jnp.maximum(away, 0).astype(jnp.float32) / length), 0.0)
    out_ref[...] = own_ref[...] + lax.dot_general(
        sums_ref[...], weights, (((0,), (0,)), ((), ())), precision=lax.Precision.HIGHEST,
        preferred_element_type=jnp.float32,
    )


def f32(*shape):
    return jax.ShapeDtypeStruct(shape, jnp.float32)


def vmem(count):
    return [pl.BlockSpec(memory_space=pltpu.VMEM)] * count


def local(depth, surface, friction, wet, coastal_tiles, gauge_route, gauge_cell, gauge_times, gauge_resid):
    height, width = depth.shape
    owned = gauge_route.shape[0]
    blocks = gauge_resid.shape[1]
    steps = blocks * STEPS_BLOCK
    halo = 2 * steps
    assert halo == SEG and height == LANES
    tiles = lax.axis_size(GRID_AXES)
    lons = lax.axis_size("lon")
    row_tiles = lax.axis_size(ROW_AXES)
    parcel_rows = gauge_rows(owned)[0] + 16
    params = pltpu.CompilerParams(vmem_limit_bytes=VMEM_LIMIT)

    keep = (1.0 - friction) * wet.astype(jnp.float32)
    gain = ((courant * 0.5) ** 2 * jnp.maximum(depth + surface, depth_floor)) * keep
    parcel, south, north, east, west = pl.pallas_call(
        functools.partial(prepare, halo),
        out_shape=(
            f32(tiles, parcel_rows, LANES), f32(2, halo, width), f32(2, halo, width),
            f32(height // 2, LANES), f32(height // 2, LANES),
        ),
        in_specs=vmem(7),
        out_specs=tuple(vmem(5)),
        scratch_shapes=[pltpu.VMEM((24, LANES), jnp.float32)],
        compiler_params=params,
        name="prepare",
    )(
        keep, gain, coastal_tiles.reshape(1, -1), gauge_route.reshape(1, owned), gauge_cell.reshape(1, owned),
        jnp.transpose(gauge_times, (1, 2, 0)), jnp.transpose(gauge_resid, (1, 2, 0)),
    )

    def exchange(array, axes):
        return lax.all_to_all(array, axes, split_axis=0, concat_axis=0, tiled=True)

    parcel = exchange(parcel, GRID_AXES)
    down = [(i, i + 1) for i in range(row_tiles - 1)]
    up = [(i + 1, i) for i in range(row_tiles - 1)]
    top = lax.ppermute(south, ROW_AXES, down)
    bottom = lax.ppermute(north, ROW_AXES, up)
    left = lax.ppermute(east, "lon", [(i, i + 1) for i in range(lons - 1)])
    right = lax.ppermute(west, "lon", [(i + 1, i) for i in range(lons - 1)])

    planes = width // LANES + 1
    rows_all = height + 2 * halo
    wide = max(2 * LANES, owned)
    pushes = pl.pallas_call(
        functools.partial(force, steps, halo, height, width),
        out_shape=f32(steps, planes, rows_all, LANES),
        in_specs=vmem(1),
        out_specs=vmem(1)[0],
        scratch_shapes=[
            pltpu.VMEM((steps, wide), jnp.float32),
            pltpu.VMEM((rows_all, wide), jnp.bfloat16),
            pltpu.VMEM((2 * wide, planes * LANES), jnp.bfloat16),
        ],
        compiler_params=params,
        cost_estimate=pl.CostEstimate(
            flops=4 * steps * rows_all * wide * planes * LANES, bytes_accessed=4 * steps * planes * rows_all * LANES,
            transcendentals=0,
        ),
        name="force",
    )(parcel)

    plane = pltpu.VMEM((planes, rows_all, LANES), jnp.float32)
    grad, sums = pl.pallas_call(
        functools.partial(sweep, steps),
        out_shape=(f32(height, width), f32(lons, 8, height)),
        in_specs=vmem(8),
        out_specs=tuple(vmem(2)),
        scratch_shapes=[plane] * 8,
        compiler_params=params,
        name="sweep",
    )(keep, gain, top, bottom, left, right, parcel, pushes)

    sums = exchange(sums, "lon")
    own = pl.pallas_call(
        smooth, out_shape=f32(height, width), in_specs=vmem(1), out_specs=vmem(1)[0], compiler_params=params,
        cost_estimate=pl.CostEstimate(
            flops=6 * 2 * height * width * width, bytes_accessed=2 * 4 * height * width, transcendentals=width * width
        ),
        name="smooth",
    )(grad)
    return pl.pallas_call(
        finish, out_shape=f32(height, width), in_specs=vmem(2), out_specs=vmem(1)[0], compiler_params=params, name="finish",
    )(own, sums.reshape(lons * 8, height))


def solution(mesh):
    in_specs = (
        P(("lat", "gau"), "lon"),
        P(("scen", "lat", "gau"), "lon"),
        P(("lat", "gau"), "lon"),
        P(("lat", "gau"), "lon"),
        P(),
        P(("scen", "lon", "lat", "gau"), None),
        P(("scen", "lon", "lat", "gau")),
        P(("scen", "lon", "lat", "gau"), None, None),
        P(("scen", "lon", "lat", "gau"), None, None),
    )
    out_specs = P(("scen", "lat", "gau"), "lon")
    return jax.shard_map(local, mesh=mesh, in_specs=in_specs, out_specs=out_specs, check_vma=False)
```

time: 67.6 us -> 59.5 us (0.88)
  the two profiles are of different devices: /device:TPU:0 before, /device:TPU:2 now
where the time goes in v3:
time: 59.5 us; the launch traced here: 59.1 us
  Pallas kernels  27.4 us (46%)
  starting transfers between devices  22.2 us (37%)
  waiting for transfers between devices  4.72 us (8%)
  local copies, waits for them, and re-layouts  3.33 us (6%)
  other arithmetic  1.29 us (2%)
    pallas_call x1, Pallas kernels, local(): pl.pallas_call(functools.partial(sweep, steps), out_shape=(f32(height, wi...  18.9 us
    all_to_all x2, starting transfers between devices, exchange(): return lax.all_to_all(array, axes, split_axis=0, concat_axis=0, tiled=True)  12 us
    pallas_call x1, Pallas kernels, local(): pl.pallas_call(functools.partial(force, steps, halo, height, width), out_...  5.51 us
    all_to_all x2, waiting for transfers between devices, exchange(): return lax.all_to_all(array, axes, split_axis=0, concat_axis=0, tiled=True)  4.71 us
    ppermute x1, starting transfers between devices, local(): bottom = lax.ppermute(north, ROW_AXES, up)  3.64 us
    ppermute x1, starting transfers between devices, local(): left = lax.ppermute(east, 'lon', [(i, i + 1) for i in range(lons - 1)])  3.36 us
    unnamed x10, local copies, waits for them, and re-layouts  3.33 us
    ppermute x1, starting transfers between devices, local(): top = lax.ppermute(south, ROW_AXES, down)  1.92 us
  transfers between devices with their start and end apart: 6, of which 1 were waited for; matrix products, arithmetic and copies ran while one was open for 0% of the time, Pallas kernels for 11%

profile of v3, /device:TPU:2, one launch (start us, length us, event | category | flops | bytes accessed | tf_op | source)
XLA Modules:
  0.0 59.1 jit_solution(17785238223889909244)
XLA Ops:
  0.0 1.3 %multiply_multiply_fusion = (f32[128,512]{1,0:T(8,128)S(1)}, f32[128,512]{1,0:T(8,128)S(1)}) fusion(f32[128,512]{1,0:T(8,128)} %param.9, f32[128,512]{1,0:T(8,128)} %param.10, s32[128,512]{1,0:T(8,128)} %param.12, f32[128,512]{1,0:T(8,128)} %param.11), kind=kLoop, calls=%fused_computation | loop fusion | flops 458752 | bytes 1572864 | tf_op jit(solution)/shard_map/mul | solution.py:393
  1.3 0.0 copy-start
  1.3 0.7 %copy-done = s32[16,2,4]{0,2,1:T(4,128)S(1)} copy-done((s32[16,2,4]{0,2,1:T(4,128)S(1)}, s32[16,2,4]{0,2,1:T(4,128)}, u32[]{:S(2)}) %copy-start) | copy-done | bytes 536
  2.0 0.0 copy-start.1
  2.0 0.7 %copy-done.1 = f32[16,2,4]{0,2,1:T(4,128)S(1)} copy-done((f32[16,2,4]{0,2,1:T(4,128)S(1)}, f32[16,2,4]{0,2,1:T(4,128)}, u32[]{:S(2)}) %copy-start.1) | copy-done | bytes 536
  2.7 0.0 copy-start.2
  2.7 0.7 %copy-done.2 = s32[8]{0:T(128)S(1)} copy-done((s32[8]{0:T(128)S(1)}, s32[8]{0:T(128)}, u32[]{:S(2)}) %copy-start.2) | copy-done | bytes 56
  3.3 0.0 copy-start.3
  3.3 0.7 %copy-done.3 = s32[16,1]{0,1:T(1,128)S(1)} copy-done((s32[16,1]{0,1:T(1,128)S(1)}, s32[16,1]{0,1:T(1,128)}, u32[]{:S(2)}) %copy-start.3) | copy-done | bytes 88
  4.0 0.0 copy-start.4
  4.0 0.7 %copy-done.4 = s32[16]{0:T(128)S(1)} copy-done((s32[16]{0:T(128)S(1)}, s32[16]{0:T(128)}, u32[]{:S(2)}) %copy-start.4) | copy-done | bytes 88
  4.6 1.0 %prepare.1 = (f32[16,24,128]{2,1,0:T(8,128)}, f32[2,32,512]{2,1,0:T(8,128)S(1)}, f32[2,32,512]{2,1,0:T(8,128)S(1)}, f32[64,128]{1,0:T(8,128)S(1)}, f32[64,128]{1,0:T(8,128)S(1)}) custom-call(f32[128,512]{1,0:T(8,128)S(1)} %get-tuple-element.20.keep_ref, f32[128,512]{1,0:T(8,128)S(1)} %get-tuple-element.19.gain_ref, s32[1,8]{1,0:T(1,128)S(1)} %bitcast.9, ...), custom_call_target="tpu_custom_call" | custom-call | tf_op jit(solution)/shard_map/prepare/pallas_call | solution.py:394
  5.6 6.3 %all-to-all-start = ((f32[16,24,128]{2,1,0:T(8,128)}), f32[16,24,128]{2,1,0:T(8,128)S(1)}, u32[]{:S(2)}, u32[]{:S(2)}) async-start(f32[16,24,128]{2,1,0:T(8,128)} %get-tuple-element.16), calls=%async_computation | async-start | bytes 393216 | tf_op jit(solution)/shard_map/all_to_all | solution.py:411
  11.9 3.4 %collective-permute-start.2 = (f32[64,128]{1,0:T(8,128)S(1)}, f32[64,128]{1,0:T(8,128)S(1)}, u32[]{:S(2)}, u32[]{:S(2)}) collective-permute-start(f32[64,128]{1,0:T(8,128)S(1)} %get-tuple-element.14), channel_id=1, source_target_pairs={{0,4},{4,8},{8,12},{1,5},{5,9},{9,13},{2,6},{6,10},{10,14},{3,7},{... | collective-permute-start | bytes 98312 | tf_op jit(solution)/shard_map/ppermute | solution.py:418
  15.3 1.3 %collective-permute-start.3 = (f32[64,128]{1,0:T(8,128)S(1)}, f32[64,128]{1,0:T(8,128)S(1)}, u32[]{:S(2)}, u32[]{:S(2)}) collective-permute-start(f32[64,128]{1,0:T(8,128)S(1)} %get-tuple-element.15), channel_id=1, source_target_pairs={{4,0},{8,4},{12,8},{5,1},{9,5},{13,9},{6,2},{10,6},{14,10},{7,3},{... | collective-permute-start | bytes 98312 | tf_op jit(solution)/shard_map/ppermute | solution.py:419
  16.6 1.9 %collective-permute-start = (f32[2,32,512]{2,1,0:T(8,128)S(1)}, f32[2,32,512]{2,1,0:T(8,128)S(1)}, u32[]{:S(2)}, u32[]{:S(2)}) collective-permute-start(f32[2,32,512]{2,1,0:T(8,128)S(1)} %get-tuple-element.12), channel_id=1, source_target_pairs={{0,1},{1,2},{2,3},{4,5},{5,6},{6,7},{8,9},{9,10},{10,11},{12,13},{... | collective-permute-start | bytes 393224 | tf_op jit(solution)/shard_map/ppermute | solution.py:416
  18.5 3.6 %collective-permute-start.1 = (f32[2,32,512]{2,1,0:T(8,128)S(1)}, f32[2,32,512]{2,1,0:T(8,128)S(1)}, u32[]{:S(2)}, u32[]{:S(2)}) collective-permute-start(f32[2,32,512]{2,1,0:T(8,128)S(1)} %get-tuple-element.13), channel_id=1, source_target_pairs={{1,0},{2,1},{3,2},{5,4},{6,5},{7,6},{9,8},{10,9},{11,10},{13,12},{... | collective-permute-start | bytes 393224 | tf_op jit(solution)/shard_map/ppermute | solution.py:417
  22.2 0.0 all-to-all-done.parcel_ref
  22.2 5.5 %force.1.force_ref = f32[16,5,192,128]{3,2,1,0:T(8,128)S(1)} custom-call(f32[16,24,128]{2,1,0:T(8,128)S(1)} %all-to-all-done.parcel_ref), custom_call_target="tpu_custom_call" | custom-call | flops 2013265920 | bytes 7864320 | tf_op jit(solution)/shard_map/force/pallas_call | solution.py:424
  27.7 0.0 collective-permute-done.2.left_ref
  27.7 0.0 collective-permute-done.3.right_ref
  27.7 0.0 collective-permute-done.top_ref
  27.7 0.0 collective-permute-done.1.bottom_ref
  27.8 18.9 %sweep.1 = (f32[128,512]{1,0:T(8,128)S(1)}, f32[4,8,128]{2,1,0:T(8,128)}) custom-call(f32[128,512]{1,0:T(8,128)S(1)} %get-tuple-element.20.keep_ref, f32[128,512]{1,0:T(8,128)S(1)} %get-tuple-element.19.gain_ref, f32[2,32,512]{2,1,0:T(8,128)S(1)} %collective-permute-done.top_ref, f32[2,32,512]{2,1,0:T(8,128)S(1)} %collective-permute-done.1.bottom_ref, ...), custom_call_target="tpu_custom_call" | custom-call | tf_op jit(solution)/shard_map/sweep/pallas_call | solution.py:443
  46.6 5.7 %all-to-all-start.1 = ((f32[4,8,128]{2,1,0:T(8,128)}), f32[4,8,128]{2,1,0:T(8,128)S(1)}, u32[]{:S(2)}, u32[]{:S(2)}) async-start(f32[4,8,128]{2,1,0:T(8,128)} %get-tuple-element.18), calls=%async_computation.1 | async-start | bytes 32768 | tf_op jit(solution)/shard_map/all_to_all | solution.py:411
  52.3 0.9 %smooth.1.own_ref = f32[128,512]{1,0:T(8,128)S(1)} custom-call(f32[128,512]{1,0:T(8,128)S(1)} %get-tuple-element.17.grad_ref), custom_call_target="tpu_custom_call" | custom-call | flops 402653184 | bytes 524288 | tf_op jit(solution)/shard_map/smooth/pallas_call | solution.py:454
  53.3 4.7 %all-to-all-done.1 = f32[4,8,128]{2,1,0:T(8,128)S(1)} async-done(((f32[4,8,128]{2,1,0:T(8,128)}), f32[4,8,128]{2,1,0:T(8,128)S(1)}, u32[]{:S(2)}, u32[]{:S(2)}) %all-to-all-start.1) | async-done | bytes 16416 | tf_op jit(solution)/shard_map/all_to_all | solution.py:411
  58.0 1.1 %finish.1 = f32[128,512]{1,0:T(8,128)} custom-call(f32[128,512]{1,0:T(8,128)S(1)} %smooth.1.own_ref, f32[32,128]{1,0:T(8,128)S(1)} %bitcast.6), custom_call_target="tpu_custom_call" | custom-call | tf_op jit(solution)/shard_map/finish/pallas_call | solution.py:461
Async XLA Ops:
  1.3 0.7 %copy-start = (s32[16,2,4]{0,2,1:T(4,128)S(1)}, s32[16,2,4]{0,2,1:T(4,128)}, u32[]{:S(2)}) copy-start(s32[16,2,4]{0,2,1:T(4,128)} %param.16) | copy-start | bytes 1540
  2.0 0.7 %copy-start.1 = (f32[16,2,4]{0,2,1:T(4,128)S(1)}, f32[16,2,4]{0,2,1:T(4,128)}, u32[]{:S(2)}) copy-start(f32[16,2,4]{0,2,1:T(4,128)} %param.17) | copy-start | bytes 1540
  2.7 0.7 %copy-start.2 = (s32[8]{0:T(128)S(1)}, s32[8]{0:T(128)}, u32[]{:S(2)}) copy-start(s32[8]{0:T(128)} %param.13) | copy-start | bytes 100
  3.3 0.7 %copy-start.3 = (s32[16,1]{0,1:T(1,128)S(1)}, s32[16,1]{0,1:T(1,128)}, u32[]{:S(2)}) copy-start(s32[16,1]{0,1:T(1,128)} %param.14) | copy-start | bytes 196
  4.0 0.7 %copy-start.4 = (s32[16]{0:T(128)S(1)}, s32[16]{0:T(128)}, u32[]{:S(2)}) copy-start(s32[16]{0:T(128)} %param.15) | copy-start | bytes 196
  5.6 16.5 %all-to-all-start = ((f32[16,24,128]{2,1,0:T(8,128)}), f32[16,24,128]{2,1,0:T(8,128)S(1)}, u32[]{:S(2)}, u32[]{:S(2)}) async-start(f32[16,24,128]{2,1,0:T(8,128)} %get-tuple-element.16), calls=%async_computation | async-start | bytes 393216 | tf_op jit(solution)/shard_map/all_to_all | solution.py:411
  11.9 15.8 %collective-permute-start.2 = (f32[64,128]{1,0:T(8,128)S(1)}, f32[64,128]{1,0:T(8,128)S(1)}, u32[]{:S(2)}, u32[]{:S(2)}) collective-permute-start(f32[64,128]{1,0:T(8,128)S(1)} %get-tuple-element.14), channel_id=1, source_target_pairs={{0,4},{4,8},{8,12},{1,5},{5,9},{9,13},{2,6},{6,10},{10,14},{3,7},{... | collective-permute-start | bytes 98312 | tf_op jit(solution)/shard_map/ppermute | solution.py:418
  15.3 12.4 %collective-permute-start.3 = (f32[64,128]{1,0:T(8,128)S(1)}, f32[64,128]{1,0:T(8,128)S(1)}, u32[]{:S(2)}, u32[]{:S(2)}) collective-permute-start(f32[64,128]{1,0:T(8,128)S(1)} %get-tuple-element.15), channel_id=1, source_target_pairs={{4,0},{8,4},{12,8},{5,1},{9,5},{13,9},{6,2},{10,6},{14,10},{7,3},{... | collective-permute-start | bytes 98312 | tf_op jit(solution)/shard_map/ppermute | solution.py:419
  16.6 11.1 %collective-permute-start = (f32[2,32,512]{2,1,0:T(8,128)S(1)}, f32[2,32,512]{2,1,0:T(8,128)S(1)}, u32[]{:S(2)}, u32[]{:S(2)}) collective-permute-start(f32[2,32,512]{2,1,0:T(8,128)S(1)} %get-tuple-element.12), channel_id=1, source_target_pairs={{0,1},{1,2},{2,3},{4,5},{5,6},{6,7},{8,9},{9,10},{10,11},{12,13},{... | collective-permute-start | bytes 393224 | tf_op jit(solution)/shard_map/ppermute | solution.py:416
  18.5 9.2 %collective-permute-start.1 = (f32[2,32,512]{2,1,0:T(8,128)S(1)}, f32[2,32,512]{2,1,0:T(8,128)S(1)}, u32[]{:S(2)}, u32[]{:S(2)}) collective-permute-start(f32[2,32,512]{2,1,0:T(8,128)S(1)} %get-tuple-element.13), channel_id=1, source_target_pairs={{1,0},{2,1},{3,2},{5,4},{6,5},{7,6},{9,8},{10,9},{11,10},{13,12},{... | collective-permute-start | bytes 393224 | tf_op jit(solution)/shard_map/ppermute | solution.py:417
  46.6 11.3 %all-to-all-start.1 = ((f32[4,8,128]{2,1,0:T(8,128)}), f32[4,8,128]{2,1,0:T(8,128)S(1)}, u32[]{:S(2)}, u32[]{:S(2)}) async-start(f32[4,8,128]{2,1,0:T(8,128)} %get-tuple-element.18), calls=%async_computation.1 | async-start | bytes 32768 | tf_op jit(solution)/shard_map/all_to_all | solution.py:411

commit v4 on v3

--- a/solution.py
+++ b/solution.py
@@ -11,6 +11,8 @@
 STEPS_BLOCK = 8
 LANES = 128
 SEG = 32
+LEVELS = 4
+CHUNK = 4
 
 courant = 0.45
 depth_floor = 0.1
@@ -51,7 +53,7 @@
 
 
 def prepare(
-    halo, keep_ref, gain_ref, coast_ref, route_ref, cell_ref, times_ref, resid_ref,
+    halo, blocks, samples, coast_count, keep_ref, gain_ref, gauge_ref,
     parcel_ref, south_ref, north_ref, east_ref, west_ref, block_ref,
 ):
     height, width = keep_ref.shape
@@ -61,25 +63,24 @@
     first, last = slice(0, LANES), slice(width - LANES, width)
     end = LANES - halo
 
-    owned = route_ref.shape[1]
-    blocks, samples = times_ref.shape[:2]
+    owned = gauge_ref.shape[1]
     assert blocks == 2
-    route, coast = route_ref[...], coast_ref[...]
+    count = blocks * samples
+    route, cell, coast = (gauge_ref[2 * count + i : 2 * count + i + 1, :].astype(jnp.int32) for i in range(3))
     target = jnp.zeros_like(route)
-    for entry in range(coast.shape[1]):
+    for entry in range(coast_count):
         target = jnp.where(route == entry, jnp.broadcast_to(coast[:, entry : entry + 1], route.shape), target)
-    cell = cell_ref[...]
     row_bits, width_bits = int(math.log2(row_tiles)), int(math.log2(width))
     assert row_tiles == 1 << row_bits and width == 1 << width_bits
     grid_row = (target & (row_tiles - 1)) * height + (cell >> width_bits)
     grid_col = (target >> row_bits) * width + (cell & (width - 1))
     block_ref[...] = jnp.zeros_like(block_ref)
-    levels = lax.broadcasted_iota(jnp.int32, (STEPS_BLOCK, owned), 0)
+    levels = lax.broadcasted_iota(jnp.int32, (STEPS_BLOCK, owned), 0).astype(jnp.float32)
     for block in range(blocks):
-        times, resid = times_ref[block], resid_ref[block]
         series = jnp.zeros((STEPS_BLOCK, owned), jnp.float32)
-        for sample in range(samples):
-            series = series + jnp.where(times[sample : sample + 1] == levels, resid[sample : sample + 1], 0.0)
+        for sample in range(block * samples, (block + 1) * samples):
+            times, resid = gauge_ref[sample : sample + 1, :], gauge_ref[count + sample : count + sample + 1, :]
+            series = series + jnp.where(times == levels, resid, 0.0)
         block_ref[block * STEPS_BLOCK : (block + 1) * STEPS_BLOCK, :owned] = series
     at = blocks * STEPS_BLOCK
     block_ref[at : at + 1, :owned] = grid_row.astype(jnp.float32)
@@ -170,28 +171,34 @@
                 cols_hot[part * LANES : (part + 1) * LANES, c * LANES : (c + 1) * LANES] = hot
                 cols_hot[wide + part * LANES : wide + (part + 1) * LANES, c * LANES : (c + 1) * LANES] = hot
 
-    def level_of(level, add):
-        value = series_ref[pl.ds(level, 1), :]
-        high = value.astype(jnp.bfloat16)
-        low = (value - high.astype(jnp.float32)).astype(jnp.bfloat16)
+    def levels_of(start, add):
         hot = rows_hot[...]
-        both = jnp.concatenate([hot * high, hot * low], axis=1)
+        both = []
+        for level in range(LEVELS):
+            value = series_ref[pl.ds(start + level, 1), :]
+            high = value.astype(jnp.bfloat16)
+            low = (value - high.astype(jnp.float32)).astype(jnp.bfloat16)
+            both.append(jnp.concatenate([hot * high, hot * low], axis=1))
+        both = jnp.concatenate(both, axis=0)
         for first in range(0, planes, 2):
             count = min(2, planes - first)
             total = jnp.dot(
                 both, cols_hot[:, first * LANES : (first + count) * LANES], preferred_element_type=jnp.float32
             )
-            for c in range(count):
-                part = total[:, c * LANES : (c + 1) * LANES]
-                force_ref[level, first + c] = force_ref[level, first + c] + part if add else part
+            for level in range(LEVELS):
+                for c in range(count):
+                    part = total[level * rows_all : (level + 1) * rows_all, c * LANES : (c + 1) * LANES]
+                    goal = (start + level, first + c)
+                    force_ref[goal] = force_ref[goal] + part if add else part
 
     def levels(add):
-        def one(level, carry):
-            level_of(level, add)
+        def one(index, carry):
+            levels_of(index * LEVELS, add)
             return carry
 
-        lax.fori_loop(0, steps, one, 0)
-
+        lax.fori_loop(0, steps // LEVELS, one, 0)
+
+    force_ref[steps] = jnp.zeros_like(force_ref[steps])
     gather_gauges(0)
     levels(False)
     if groups > 1:
@@ -213,7 +220,7 @@
     halo = 2 * steps
     inner = width // LANES
     planes = inner + 1
-    rows_all = a.shape[1]
+    rows_all = plain.shape[1]
     blocks = rows_all // 8
     my_row, my_lon, row_tiles, lons = my_place()
     end = LANES - halo
@@ -265,57 +272,69 @@
                 by_x[c, 8 * q : 8 * q + 8, :] = shifted[c]
                 by_y[c, to : to + 8, :] = up(values[c]) if q == 0 else values[c]
 
-    for ref in (a, fx, fy):
-        ref[...] = jnp.zeros_like(ref)
+    fx[...] = jnp.zeros_like(fx)
+    fy[...] = jnp.zeros_like(fy)
+    a[:, 0:rows_all, :] = force_ref[steps - 1]
 
     col_valid = jnp.where(lanes8 < LANES // 2, jnp.where(has_right, 1.0, 0.0), jnp.where(has_left, 1.0, 0.0))
     col_mask = jnp.where((lanes8 < halo) | (lanes8 >= end), col_valid, 0.0)
     sublane = lax.broadcasted_iota(jnp.int32, (8, LANES), 0)
-    row_mask = {}
-    for row, there in ((halo - 1, has_top), (halo + height, has_bottom)):
-        row_mask[row % blocks] = jnp.where(sublane == row // blocks, jnp.where(there, 1.0, 0.0), 1.0)
+    top_mask = jnp.where(sublane == (halo - 1) // blocks, jnp.where(has_top, 1.0, 0.0), 1.0)
+    bottom_mask = jnp.where(sublane == (halo + height) // blocks, jnp.where(has_bottom, 1.0, 0.0), 1.0)
     every = range(planes)
 
     def step(index, carry):
-        level = steps - 1 - index
-        current, new_y = {}, {}
-
-        def here(q):
-            if q not in current:
-                current[q] = [a[c, 8 * q : 8 * q + 8, :] + force_ref[level, c, 8 * q : 8 * q + 8, :] for c in every]
-            return current[q]
-
-        def move_y(q):
-            near = here(q)
-            ahead = here(q + 2) if q + 2 < blocks else [up(value) for value in here(q + 2 - blocks)]
-            rows = slice(8 * q, 8 * q + 8)
-            new_y[q] = [keep_y[c, rows, :] * fy[c, rows, :] + gain_y[c, rows, :] * (ahead[c] - near[c]) for c in every]
+        after = jnp.where(index == steps - 1, steps, steps - 2 - index)
+        for q in range(2):
             for c in every:
-                fy[c, rows, :] = new_y[q][c]
-
-        def move(q):
-            near = here(q)
-            rows = slice(8 * q, 8 * q + 8)
-            ahead = shift_from(near, 2, lanes8)
-            new_x = [keep_x[c, rows, :] * fx[c, rows, :] + gain_x[c, rows, :] * (ahead[c] - near[c]) for c in every]
-            behind = shift_from(new_x, -2, lanes8)
-            before = new_y[q - 2] if q >= 2 else [down(value) for value in new_y[q - 2 + blocks]]
+                a[c, rows_all + 8 * q : rows_all + 8 * q + 8, :] = up(a[c, 8 * q : 8 * q + 8, :])
+
+        def chunk(number, inner_carry):
+            start = pl.multiple_of(number * (8 * CHUNK), 8 * CHUNK)
+
+            def at(q):
+                return pl.ds(start + 8 * q, 8)
+
+            near = [[a[c, at(q), :] for c in every] for q in range(CHUNK + 2)]
+            new_y = [[fy[c, at(q), :] for c in every] for q in range(2)]
+            total, new_x = [], []
+            for q in range(CHUNK):
+                new_y.append(
+                    [
+                        keep_y[c, at(q), :] * fy[c, at(q + 2), :] + gain_y[c, at(q), :] * (near[q + 2][c] - near[q][c])
+                        for c in every
+                    ]
+                )
+                ahead = shift_from(near[q], 2, lanes8)
+                new_x.append(
+                    [keep_x[c, at(q), :] * fx[c, at(q), :] + gain_x[c, at(q), :] * (ahead[c] - near[q][c]) for c in every]
+                )
+                total.append([near[q][c] + (new_y[q + 2][c] - new_y[q][c]) for c in every])
+            behind = [shift_from(new_x[q], -2, lanes8) for q in range(CHUNK)]
+            for q in range(CHUNK):
+                for c in every:
+                    value = total[q][c] + (new_x[q][c] - behind[q][c])
+                    if c == inner:
+                        value = value * col_mask
+                    total[q][c] = value + force_ref[after, c, at(q), :]
+            for q in range(CHUNK):
+                for c in every:
+                    fx[c, at(q), :] = new_x[q][c]
+                    fy[c, at(q + 2), :] = new_y[q + 2][c]
+                    a[c, at(q), :] = total[q][c]
+            return inner_carry
+
+        fy[:, 0:16, :] = jnp.zeros((planes, 16, LANES), jnp.float32)
+        lax.fori_loop(0, blocks // CHUNK, chunk, 0)
+        for q in range(2):
             for c in every:
-                fx[c, rows, :] = new_x[c]
-                value = near[c] + (new_x[c] - behind[c]) + (new_y[q][c] - before[c])
-                if c == inner:
-                    value = value * col_mask
-                if q in row_mask:
-                    value = value * row_mask[q]
-                a[c, rows, :] = value
-
-        move_y(0)
-        move_y(1)
-        for q in range(2, blocks):
-            move_y(q)
-            move(q)
-        move(0)
-        move(1)
+                rows = slice(8 * q, 8 * q + 8)
+                past = down(fy[c, rows_all + 8 * q : rows_all + 8 * q + 8, :])
+                a[c, rows, :] = a[c, rows, :] - (past * col_mask if c == inner else past)
+        for row, mask in ((halo - 1, top_mask), (halo + height, bottom_mask)):
+            rows = slice(row % blocks * 8, row % blocks * 8 + 8)
+            for c in every:
+                a[c, rows, :] = a[c, rows, :] * mask
         return carry
 
     lax.fori_loop(0, steps, step, 0)
@@ -391,21 +410,32 @@
 
     keep = (1.0 - friction) * wet.astype(jnp.float32)
     gain = ((courant * 0.5) ** 2 * jnp.maximum(depth + surface, depth_floor)) * keep
+    samples, coast_count = gauge_resid.shape[2], coastal_tiles.shape[0]
+    assert coast_count <= owned
+
+    def by_gauge(array):
+        return jnp.transpose(array, (1, 2, 0)).reshape(blocks * samples, owned)
+
+    gauges = jnp.concatenate(
+        [
+            by_gauge(gauge_times).astype(jnp.float32), by_gauge(gauge_resid),
+            gauge_route.reshape(1, owned).astype(jnp.float32), gauge_cell.reshape(1, owned).astype(jnp.float32),
+            jnp.pad(coastal_tiles, (0, owned - coast_count)).reshape(1, owned).astype(jnp.float32),
+        ],
+        axis=0,
+    )
     parcel, south, north, east, west = pl.pallas_call(
-        functools.partial(prepare, halo),
+        functools.partial(prepare, halo, blocks, samples, coast_count),
         out_shape=(
             f32(tiles, parcel_rows, LANES), f32(2, halo, width), f32(2, halo, width),
             f32(height // 2, LANES), f32(height // 2, LANES),
         ),
-        in_specs=vmem(7),
+        in_specs=vmem(3),
         out_specs=tuple(vmem(5)),
         scratch_shapes=[pltpu.VMEM((24, LANES), jnp.float32)],
         compiler_params=params,
         name="prepare",
-    )(
-        keep, gain, coastal_tiles.reshape(1, -1), gauge_route.reshape(1, owned), gauge_cell.reshape(1, owned),
-        jnp.transpose(gauge_times, (1, 2, 0)), jnp.transpose(gauge_resid, (1, 2, 0)),
-    )
+    )(keep, gain, gauges)
 
     def exchange(array, axes):
         return lax.all_to_all(array, axes, split_axis=0, concat_axis=0, tiled=True)
@@ -423,7 +453,7 @@
     wide = max(2 * LANES, owned)
     pushes = pl.pallas_call(
         functools.partial(force, steps, halo, height, width),
-        out_shape=f32(steps, planes, rows_all, LANES),
+        out_shape=f32(steps + 1, planes, rows_all, LANES),
         in_specs=vmem(1),
         out_specs=vmem(1)[0],
         scratch_shapes=[
@@ -440,12 +470,13 @@
     )(parcel)
 
     plane = pltpu.VMEM((planes, rows_all, LANES), jnp.float32)
+    longer = pltpu.VMEM((planes, rows_all + 16, LANES), jnp.float32)
     grad, sums = pl.pallas_call(
         functools.partial(sweep, steps),
         out_shape=(f32(height, width), f32(lons, 8, height)),
         in_specs=vmem(8),
         out_specs=tuple(vmem(2)),
-        scratch_shapes=[plane] * 8,
+        scratch_shapes=[longer, plane, longer] + [plane] * 5,
         compiler_params=params,
         name="sweep",
     )(keep, gain, top, bottom, left, right, parcel, pushes)

time: 59.5 us -> 57.2 us (0.961)
  the two profiles are of different devices: /device:TPU:2 before, /device:TPU:1 now
where the time goes in v4:
time: 57.2 us; the launch traced here: 56.7 us
  Pallas kernels  25.3 us (44%)
  starting transfers between devices  22.8 us (40%)
  waiting for transfers between devices  4.48 us (8%)
  other arithmetic  3.31 us (6%)
  local copies, waits for them, and re-layouts  0.71 us (1%)
    pallas_call x1, Pallas kernels, local(): pl.pallas_call(functools.partial(sweep, steps), out_shape=(f32(height, wi...  18.9 us
    all_to_all x2, starting transfers between devices, exchange(): return lax.all_to_all(array, axes, split_axis=0, concat_axis=0, tiled=True)  12.7 us
    ppermute x1, starting transfers between devices, local(): top = lax.ppermute(south, ROW_AXES, down)  3.62 us
    all_to_all x2, waiting for transfers between devices, exchange(): return lax.all_to_all(array, axes, split_axis=0, concat_axis=0, tiled=True)  3.56 us
    pallas_call x1, Pallas kernels, local(): pl.pallas_call(functools.partial(force, steps, halo, height, width), out_...  3.4 us
    ppermute x1, starting transfers between devices, local(): left = lax.ppermute(east, 'lon', [(i, i + 1) for i in range(lons - 1)])  3.28 us
    ppermute x1, starting transfers between devices, local(): bottom = lax.ppermute(north, ROW_AXES, up)  1.92 us
    ppermute x1, starting transfers between devices, local(): right = lax.ppermute(west, 'lon', [(i + 1, i) for i in range(lons - 1)])  1.29 us
  transfers between devices with their start and end apart: 6, of which 2 were waited for; matrix products, arithmetic and copies ran while one was open for 0% of the time, Pallas kernels for 8%

profile of v4, /device:TPU:1, one launch (start us, length us, event | category | flops | bytes accessed | tf_op | source)
XLA Modules:
  0.0 56.7 jit_solution(5053224495514413810)
XLA Ops:
  0.0 0.7 %convert_bitcast_fusion.2 = f32[1,16]{1,0:T(1,128)S(1)} fusion(s32[16,1]{0,1:T(1,128)} %param.14), kind=kLoop, calls=%fused_computation.4 | loop fusion | flops 16 | bytes 128 | tf_op jit(solution)/shard_map/convert_element_type | solution.py:422
  0.7 0.7 %convert_element_type.39 = f32[16,2,4]{0,2,1:T(4,128)S(1)} convert(s32[16,2,4]{0,2,1:T(4,128)} %param.16) | non-fusion elementwise | flops 128 | bytes 1024 | tf_op jit(solution)/shard_map/convert_element_type | solution.py:421
  1.3 0.7 %convert_bitcast_fusion = (f32[1,16]{1,0:T(1,128)S(1)}, f32[1,16]{1,0:T(1,128)S(1)}) fusion(s32[8]{0:T(128)} %param.13, s32[16]{0:T(128)} %param.15), kind=kLoop, calls=%fused_computation.2 | loop fusion | flops 32 | bytes 224 | tf_op jit(solution)/shard_map/convert_element_type | solution.py:423
  2.0 1.3 %multiply_multiply_fusion = (f32[128,512]{1,0:T(8,128)S(1)}, f32[128,512]{1,0:T(8,128)S(1)}) fusion(f32[128,512]{1,0:T(8,128)} %param.9, f32[128,512]{1,0:T(8,128)} %param.10, s32[128,512]{1,0:T(8,128)} %param.12, f32[128,512]{1,0:T(8,128)} %param.11), kind=kLoop, calls=%fused_computation | loop fusion | flops 458752 | bytes 1572864 | tf_op jit(solution)/shard_map/mul | solution.py:412
  3.3 0.7 %concatenate.3.gauge_ref = f32[19,16]{1,0:T(8,128)S(1)} concatenate(f32[8,16]{1,0:T(8,128)S(1)} %bitcast.14, f32[8,16]{1,0:T(8,128)} %bitcast.15, f32[1,16]{1,0:T(1,128)S(1)} %convert_bitcast_fusion.2, f32[1,16]{1,0:T(1,128)S(1)} %get-tuple-element.22, f32[1,16]{1,0:T(1,128)S(1)} %get-tuple-element.21), dimensions={0} | concatenate | bytes 2432 | tf_op jit(solution)/shard_map/concatenate | solution.py:419
  4.0 1.0 %prepare.1 = (f32[16,24,128]{2,1,0:T(8,128)}, f32[2,32,512]{2,1,0:T(8,128)S(1)}, f32[2,32,512]{2,1,0:T(8,128)S(1)}, f32[64,128]{1,0:T(8,128)S(1)}, f32[64,128]{1,0:T(8,128)S(1)}) custom-call(f32[128,512]{1,0:T(8,128)S(1)} %get-tuple-element.20.keep_ref, f32[128,512]{1,0:T(8,128)S(1)} %get-tuple-element.19.gain_ref, f32[19,16]{1,0:T(8,128)S(1)} %concatenate.3.gauge_ref), custom_call_target="tpu_custom_call" | custom-call | tf_op jit(solution)/shard_map/prepare/pallas_call | solution.py:427
  5.0 7.3 %all-to-all-start = ((f32[16,24,128]{2,1,0:T(8,128)}), f32[16,24,128]{2,1,0:T(8,128)S(1)}, u32[]{:S(2)}, u32[]{:S(2)}) async-start(f32[16,24,128]{2,1,0:T(8,128)} %get-tuple-element.16), calls=%async_computation | async-start | bytes 393216 | tf_op jit(solution)/shard_map/all_to_all | solution.py:441
  12.3 3.3 %collective-permute-start.2 = (f32[64,128]{1,0:T(8,128)S(1)}, f32[64,128]{1,0:T(8,128)S(1)}, u32[]{:S(2)}, u32[]{:S(2)}) collective-permute-start(f32[64,128]{1,0:T(8,128)S(1)} %get-tuple-element.14), channel_id=1, source_target_pairs={{0,4},{4,8},{8,12},{1,5},{5,9},{9,13},{2,6},{6,10},{10,14},{3,7},{... | collective-permute-start | bytes 98312 | tf_op jit(solution)/shard_map/ppermute | solution.py:448
  15.6 1.3 %collective-permute-start.3 = (f32[64,128]{1,0:T(8,128)S(1)}, f32[64,128]{1,0:T(8,128)S(1)}, u32[]{:S(2)}, u32[]{:S(2)}) collective-permute-start(f32[64,128]{1,0:T(8,128)S(1)} %get-tuple-element.15), channel_id=1, source_target_pairs={{4,0},{8,4},{12,8},{5,1},{9,5},{13,9},{6,2},{10,6},{14,10},{7,3},{... | collective-permute-start | bytes 98312 | tf_op jit(solution)/shard_map/ppermute | solution.py:449
  16.9 3.6 %collective-permute-start = (f32[2,32,512]{2,1,0:T(8,128)S(1)}, f32[2,32,512]{2,1,0:T(8,128)S(1)}, u32[]{:S(2)}, u32[]{:S(2)}) collective-permute-start(f32[2,32,512]{2,1,0:T(8,128)S(1)} %get-tuple-element.12), channel_id=1, source_target_pairs={{0,1},{1,2},{2,3},{4,5},{5,6},{6,7},{8,9},{9,10},{10,11},{12,13},{... | collective-permute-start | bytes 393224 | tf_op jit(solution)/shard_map/ppermute | solution.py:446
  20.5 1.9 %collective-permute-start.1 = (f32[2,32,512]{2,1,0:T(8,128)S(1)}, f32[2,32,512]{2,1,0:T(8,128)S(1)}, u32[]{:S(2)}, u32[]{:S(2)}) collective-permute-start(f32[2,32,512]{2,1,0:T(8,128)S(1)} %get-tuple-element.13), channel_id=1, source_target_pairs={{1,0},{2,1},{3,2},{5,4},{6,5},{7,6},{9,8},{10,9},{11,10},{13,12},{... | collective-permute-start | bytes 393224 | tf_op jit(solution)/shard_map/ppermute | solution.py:447
  22.4 0.0 all-to-all-done.parcel_ref
  22.5 3.4 %force.1.force_ref = f32[17,5,192,128]{3,2,1,0:T(8,128)S(1)} custom-call(f32[16,24,128]{2,1,0:T(8,128)S(1)} %all-to-all-done.parcel_ref), custom_call_target="tpu_custom_call" | custom-call | flops 2013265920 | bytes 7864320 | tf_op jit(solution)/shard_map/force/pallas_call | solution.py:454
  25.9 0.0 collective-permute-done.2.left_ref
  25.9 0.0 collective-permute-done.3.right_ref
  25.9 0.0 collective-permute-done.top_ref
  25.9 0.9 %collective-permute-done.1.bottom_ref = f32[2,32,512]{2,1,0:T(8,128)S(1)} collective-permute-done((f32[2,32,512]{2,1,0:T(8,128)S(1)}, f32[2,32,512]{2,1,0:T(8,128)S(1)}, u32[]{:S(2)}, u32[]{:S(2)}) %collective-permute-start.1) | collective-permute-done | bytes 131104 | tf_op jit(solution)/shard_map/ppermute | solution.py:447
  26.8 18.9 %sweep.1 = (f32[128,512]{1,0:T(8,128)S(1)}, f32[4,8,128]{2,1,0:T(8,128)}) custom-call(f32[128,512]{1,0:T(8,128)S(1)} %get-tuple-element.20.keep_ref, f32[128,512]{1,0:T(8,128)S(1)} %get-tuple-element.19.gain_ref, f32[2,32,512]{2,1,0:T(8,128)S(1)} %collective-permute-done.top_ref, f32[2,32,512]{2,1,0:T(8,128)S(1)} %collective-permute-done.1.bottom_ref, ...), custom_call_target="tpu_custom_call" | custom-call | tf_op jit(solution)/shard_map/sweep/pallas_call | solution.py:474
  45.7 5.4 %all-to-all-start.1 = ((f32[4,8,128]{2,1,0:T(8,128)}), f32[4,8,128]{2,1,0:T(8,128)S(1)}, u32[]{:S(2)}, u32[]{:S(2)}) async-start(f32[4,8,128]{2,1,0:T(8,128)} %get-tuple-element.18), calls=%async_computation.1 | async-start | bytes 32768 | tf_op jit(solution)/shard_map/all_to_all | solution.py:441
  51.1 0.9 %smooth.1.own_ref = f32[128,512]{1,0:T(8,128)S(1)} custom-call(f32[128,512]{1,0:T(8,128)S(1)} %get-tuple-element.17.grad_ref), custom_call_target="tpu_custom_call" | custom-call | flops 402653184 | bytes 524288 | tf_op jit(solution)/shard_map/smooth/pallas_call | solution.py:485
  52.0 3.6 %all-to-all-done.1 = f32[4,8,128]{2,1,0:T(8,128)S(1)} async-done(((f32[4,8,128]{2,1,0:T(8,128)}), f32[4,8,128]{2,1,0:T(8,128)S(1)}, u32[]{:S(2)}, u32[]{:S(2)}) %all-to-all-start.1) | async-done | bytes 16416 | tf_op jit(solution)/shard_map/all_to_all | solution.py:441
  55.6 1.1 %finish.1 = f32[128,512]{1,0:T(8,128)} custom-call(f32[128,512]{1,0:T(8,128)S(1)} %smooth.1.own_ref, f32[32,128]{1,0:T(8,128)S(1)} %bitcast.13), custom_call_target="tpu_custom_call" | custom-call | tf_op jit(solution)/shard_map/finish/pallas_call | solution.py:492
Async XLA Ops:
  5.0 17.4 %all-to-all-start = ((f32[16,24,128]{2,1,0:T(8,128)}), f32[16,24,128]{2,1,0:T(8,128)S(1)}, u32[]{:S(2)}, u32[]{:S(2)}) async-start(f32[16,24,128]{2,1,0:T(8,128)} %get-tuple-element.16), calls=%async_computation | async-start | bytes 393216 | tf_op jit(solution)/shard_map/all_to_all | solution.py:441
  12.3 13.6 %collective-permute-start.2 = (f32[64,128]{1,0:T(8,128)S(1)}, f32[64,128]{1,0:T(8,128)S(1)}, u32[]{:S(2)}, u32[]{:S(2)}) collective-permute-start(f32[64,128]{1,0:T(8,128)S(1)} %get-tuple-element.14), channel_id=1, source_target_pairs={{0,4},{4,8},{8,12},{1,5},{5,9},{9,13},{2,6},{6,10},{10,14},{3,7},{... | collective-permute-start | bytes 98312 | tf_op jit(solution)/shard_map/ppermute | solution.py:448
  15.6 10.3 %collective-permute-start.3 = (f32[64,128]{1,0:T(8,128)S(1)}, f32[64,128]{1,0:T(8,128)S(1)}, u32[]{:S(2)}, u32[]{:S(2)}) collective-permute-start(f32[64,128]{1,0:T(8,128)S(1)} %get-tuple-element.15), channel_id=1, source_target_pairs={{4,0},{8,4},{12,8},{5,1},{9,5},{13,9},{6,2},{10,6},{14,10},{7,3},{... | collective-permute-start | bytes 98312 | tf_op jit(solution)/shard_map/ppermute | solution.py:449
  16.9 9.0 %collective-permute-start = (f32[2,32,512]{2,1,0:T(8,128)S(1)}, f32[2,32,512]{2,1,0:T(8,128)S(1)}, u32[]{:S(2)}, u32[]{:S(2)}) collective-permute-start(f32[2,32,512]{2,1,0:T(8,128)S(1)} %get-tuple-element.12), channel_id=1, source_target_pairs={{0,1},{1,2},{2,3},{4,5},{5,6},{6,7},{8,9},{9,10},{10,11},{12,13},{... | collective-permute-start | bytes 393224 | tf_op jit(solution)/shard_map/ppermute | solution.py:446
  20.5 6.3 %collective-permute-start.1 = (f32[2,32,512]{2,1,0:T(8,128)S(1)}, f32[2,32,512]{2,1,0:T(8,128)S(1)}, u32[]{:S(2)}, u32[]{:S(2)}) collective-permute-start(f32[2,32,512]{2,1,0:T(8,128)S(1)} %get-tuple-element.13), channel_id=1, source_target_pairs={{1,0},{2,1},{3,2},{5,4},{6,5},{7,6},{9,8},{10,9},{11,10},{13,12},{... | collective-permute-start | bytes 393224 | tf_op jit(solution)/shard_map/ppermute | solution.py:447
  45.7 9.9 %all-to-all-start.1 = ((f32[4,8,128]{2,1,0:T(8,128)}), f32[4,8,128]{2,1,0:T(8,128)S(1)}, u32[]{:S(2)}, u32[]{:S(2)}) async-start(f32[4,8,128]{2,1,0:T(8,128)} %get-tuple-element.18), calls=%async_computation.1 | async-start | bytes 32768 | tf_op jit(solution)/shard_map/all_to_all | solution.py:441

commit v5 on v4

--- a/solution.py
+++ b/solution.py
@@ -53,7 +53,7 @@
 
 
 def prepare(
-    halo, blocks, samples, coast_count, keep_ref, gain_ref, gauge_ref,
+    halo, blocks, samples, coast_count, keep_ref, gain_ref, gauge_ref, resid_ref,
     parcel_ref, south_ref, north_ref, east_ref, west_ref, block_ref,
 ):
     height, width = keep_ref.shape
@@ -63,10 +63,9 @@
     first, last = slice(0, LANES), slice(width - LANES, width)
     end = LANES - halo
 
-    owned = gauge_ref.shape[1]
+    owned = gauge_ref.shape[2]
     assert blocks == 2
-    count = blocks * samples
-    route, cell, coast = (gauge_ref[2 * count + i : 2 * count + i + 1, :].astype(jnp.int32) for i in range(3))
+    route, cell, coast = (gauge_ref[blocks, i : i + 1, :] for i in range(3))
     target = jnp.zeros_like(route)
     for entry in range(coast_count):
         target = jnp.where(route == entry, jnp.broadcast_to(coast[:, entry : entry + 1], route.shape), target)
@@ -75,11 +74,12 @@
     grid_row = (target & (row_tiles - 1)) * height + (cell >> width_bits)
     grid_col = (target >> row_bits) * width + (cell & (width - 1))
     block_ref[...] = jnp.zeros_like(block_ref)
-    levels = lax.broadcasted_iota(jnp.int32, (STEPS_BLOCK, owned), 0).astype(jnp.float32)
+    levels = lax.broadcasted_iota(jnp.int32, (STEPS_BLOCK, owned), 0)
     for block in range(blocks):
         series = jnp.zeros((STEPS_BLOCK, owned), jnp.float32)
-        for sample in range(block * samples, (block + 1) * samples):
-            times, resid = gauge_ref[sample : sample + 1, :], gauge_ref[count + sample : count + sample + 1, :]
+        for sample in range(samples):
+            times = gauge_ref[block, sample : sample + 1, :]
+            resid = resid_ref[block, sample : sample + 1, :]
             series = series + jnp.where(times == levels, resid, 0.0)
         block_ref[block * STEPS_BLOCK : (block + 1) * STEPS_BLOCK, :owned] = series
     at = blocks * STEPS_BLOCK
@@ -129,7 +129,7 @@
 
 
 def force(steps, halo, height, width, parcel_ref, force_ref, series_ref, rows_hot, cols_hot):
-    planes, rows_all = force_ref.shape[1:3]
+    planes, rows_all = force_ref.shape[1], height + 2 * halo
     my_row, my_lon, row_tiles, lons = my_place()
     wide = rows_hot.shape[1]
     tiles, parcel_rows = parcel_ref.shape[:2]
@@ -188,7 +188,7 @@
             for level in range(LEVELS):
                 for c in range(count):
                     part = total[level * rows_all : (level + 1) * rows_all, c * LANES : (c + 1) * LANES]
-                    goal = (start + level, first + c)
+                    goal = (start + level, first + c, slice(0, rows_all))
                     force_ref[goal] = force_ref[goal] + part if add else part
 
     def levels(add):
@@ -220,7 +220,7 @@
     halo = 2 * steps
     inner = width // LANES
     planes = inner + 1
-    rows_all = plain.shape[1]
+    rows_all = height + 2 * halo
     blocks = rows_all // 8
     my_row, my_lon, row_tiles, lons = my_place()
     end = LANES - halo
@@ -246,7 +246,7 @@
             cols = slice(c * LANES, (c + 1) * LANES)
             plain[c, halo : halo + height, :] = source[:, cols]
             plain[c, 0:halo, :] = top_ref[kind, :, cols]
-            plain[c, halo + height :, :] = bottom_ref[kind, :, cols]
+            plain[c, halo + height : rows_all, :] = bottom_ref[kind, :, cols]
         segment = lane_iota(half) // SEG
         for part in range(2):
             piece = 2 * part + kind
@@ -274,7 +274,7 @@
 
     fx[...] = jnp.zeros_like(fx)
     fy[...] = jnp.zeros_like(fy)
-    a[:, 0:rows_all, :] = force_ref[steps - 1]
+    a[:, 0:rows_all, :] = force_ref[steps - 1, :, 0:rows_all, :]
 
     col_valid = jnp.where(lanes8 < LANES // 2, jnp.where(has_right, 1.0, 0.0), jnp.where(has_left, 1.0, 0.0))
     col_mask = jnp.where((lanes8 < halo) | (lanes8 >= end), col_valid, 0.0)
@@ -391,6 +391,10 @@
     return jax.ShapeDtypeStruct(shape, jnp.float32)
 
 
+def spaced(rows):
+    return 8 * (rows // 8 | 1)
+
+
 def vmem(count):
     return [pl.BlockSpec(memory_space=pltpu.VMEM)] * count
 
@@ -413,29 +417,31 @@
     samples, coast_count = gauge_resid.shape[2], coastal_tiles.shape[0]
     assert coast_count <= owned
 
-    def by_gauge(array):
-        return jnp.transpose(array, (1, 2, 0)).reshape(blocks * samples, owned)
-
-    gauges = jnp.concatenate(
-        [
-            by_gauge(gauge_times).astype(jnp.float32), by_gauge(gauge_resid),
-            gauge_route.reshape(1, owned).astype(jnp.float32), gauge_cell.reshape(1, owned).astype(jnp.float32),
-            jnp.pad(coastal_tiles, (0, owned - coast_count)).reshape(1, owned).astype(jnp.float32),
-        ],
-        axis=0,
+    assert samples >= 3
+
+    def put(array, group, row):
+        groups, rows, lanes = array.shape
+        return jnp.pad(array, ((group, blocks + 1 - group - groups), (row, samples - row - rows), (0, owned - lanes)))
+
+    gauges = (
+        put(jnp.transpose(gauge_times, (1, 2, 0)), 0, 0)
+        + put(gauge_route.reshape(1, 1, owned), blocks, 0)
+        + put(gauge_cell.reshape(1, 1, owned), blocks, 1)
+        + put(coastal_tiles.reshape(1, 1, coast_count), blocks, 2)
     )
+    residuals = jnp.transpose(gauge_resid, (1, 2, 0))
     parcel, south, north, east, west = pl.pallas_call(
         functools.partial(prepare, halo, blocks, samples, coast_count),
         out_shape=(
             f32(tiles, parcel_rows, LANES), f32(2, halo, width), f32(2, halo, width),
             f32(height // 2, LANES), f32(height // 2, LANES),
         ),
-        in_specs=vmem(3),
+        in_specs=vmem(4),
         out_specs=tuple(vmem(5)),
         scratch_shapes=[pltpu.VMEM((24, LANES), jnp.float32)],
         compiler_params=params,
         name="prepare",
-    )(keep, gain, gauges)
+    )(keep, gain, gauges, residuals)
 
     def exchange(array, axes):
         return lax.all_to_all(array, axes, split_axis=0, concat_axis=0, tiled=True)
@@ -453,7 +459,7 @@
     wide = max(2 * LANES, owned)
     pushes = pl.pallas_call(
         functools.partial(force, steps, halo, height, width),
-        out_shape=f32(steps + 1, planes, rows_all, LANES),
+        out_shape=f32(steps + 1, planes, spaced(rows_all), LANES),
         in_specs=vmem(1),
         out_specs=vmem(1)[0],
         scratch_shapes=[
@@ -469,8 +475,8 @@
         name="force",
     )(parcel)
 
-    plane = pltpu.VMEM((planes, rows_all, LANES), jnp.float32)
-    longer = pltpu.VMEM((planes, rows_all + 16, LANES), jnp.float32)
+    plane = pltpu.VMEM((planes, spaced(rows_all), LANES), jnp.float32)
+    longer = pltpu.VMEM((planes, spaced(rows_all + 16), LANES), jnp.float32)
     grad, sums = pl.pallas_call(
         functools.partial(sweep, steps),
         out_shape=(f32(height, width), f32(lons, 8, height)),

time: 57.2 us -> 56.2 us (0.983)
  other arithmetic: 3.31 us -> 2.03 us
    convert_element_type x3 -> x0, other arithmetic: 2.02 us -> none  [the longest x1 0.69 us: local(): by_gauge(gauge_times).astype(jnp.float32)]
    add x0 -> x1, other arithmetic: none -> 0.74 us  [local(): put(jnp.transpose(gauge_times, (1, 2, 0)), 0, 0)]
    concatenate x1 -> x0, local copies, waits for them, and re-layouts: 0.71 us -> none  [local(): jnp.concatenate([by_gauge(gauge_times).astype(jnp.float32), by_gauge(gaug...]
    unnamed x0 -> x2, local copies, waits for them, and re-layouts: none -> 0.68 us
where the time goes in v5:
time: 56.2 us; the launch traced here: 55.7 us
  Pallas kernels  25.6 us (46%)
  starting transfers between devices  22.8 us (41%)
  waiting for transfers between devices  4.46 us (8%)
  other arithmetic  2.03 us (4%)
  local copies, waits for them, and re-layouts  0.68 us (1%)
    pallas_call x1, Pallas kernels, local(): pl.pallas_call(functools.partial(sweep, steps), out_shape=(f32(height, wi...  19.2 us
    all_to_all x2, starting transfers between devices, exchange(): return lax.all_to_all(array, axes, split_axis=0, concat_axis=0, tiled=True)  12.7 us
    ppermute x1, starting transfers between devices, local(): top = lax.ppermute(south, ROW_AXES, down)  3.62 us
    all_to_all x2, waiting for transfers between devices, exchange(): return lax.all_to_all(array, axes, split_axis=0, concat_axis=0, tiled=True)  3.56 us
    pallas_call x1, Pallas kernels, local(): pl.pallas_call(functools.partial(force, steps, halo, height, width), out_...  3.41 us
    ppermute x1, starting transfers between devices, local(): left = lax.ppermute(east, 'lon', [(i, i + 1) for i in range(lons - 1)])  3.28 us
    ppermute x1, starting transfers between devices, local(): bottom = lax.ppermute(north, ROW_AXES, up)  1.92 us
    ppermute x1, starting transfers between devices, local(): right = lax.ppermute(west, 'lon', [(i + 1, i) for i in range(lons - 1)])  1.29 us
  transfers between devices with their start and end apart: 6, of which 2 were waited for; matrix products, arithmetic and copies ran while one was open for 0% of the time, Pallas kernels for 8%

profile of v5, /device:TPU:1, one launch (start us, length us, event | category | flops | bytes accessed | tf_op | source)
XLA Modules:
  0.0 55.7 jit_solution(324025053122600445)
XLA Ops:
  0.0 0.7 %pad_add_fusion.gauge_ref = s32[3,4,16]{2,1,0:T(4,128)S(1)} fusion(s32[1,1,8]{2,1,0:T(1,128)} %bitcast.9, s32[1,1,16]{2,1,0:T(1,128)} %bitcast.10, s32[1,1,16]{2,1,0:T(1,128)} %bitcast.11, s32[2,4,16]{2,1,0:T(4,128)} %bitcast.8), kind=kLoop, calls=%fused_computation.2 | loop fusion | flops 576 | bytes 1440 | tf_op jit(solution)/shard_map/add | solution.py:427
  0.7 1.3 %multiply_multiply_fusion = (f32[128,512]{1,0:T(8,128)S(1)}, f32[128,512]{1,0:T(8,128)S(1)}) fusion(f32[128,512]{1,0:T(8,128)} %param.9, f32[128,512]{1,0:T(8,128)} %param.10, s32[128,512]{1,0:T(8,128)} %param.12, f32[128,512]{1,0:T(8,128)} %param.11), kind=kLoop, calls=%fused_computation | loop fusion | flops 458752 | bytes 1572864 | tf_op jit(solution)/shard_map/mul | solution.py:416
  2.0 0.0 copy-start
  2.0 0.7 %copy-done = f32[16,2,4]{0,2,1:T(4,128)S(1)} copy-done((f32[16,2,4]{0,2,1:T(4,128)S(1)}, f32[16,2,4]{0,2,1:T(4,128)}, u32[]{:S(2)}) %copy-start) | copy-done | bytes 536
  2.7 1.0 %prepare.1 = (f32[16,24,128]{2,1,0:T(8,128)}, f32[2,32,512]{2,1,0:T(8,128)S(1)}, f32[2,32,512]{2,1,0:T(8,128)S(1)}, f32[64,128]{1,0:T(8,128)S(1)}, f32[64,128]{1,0:T(8,128)S(1)}) custom-call(f32[128,512]{1,0:T(8,128)S(1)} %get-tuple-element.20.keep_ref, f32[128,512]{1,0:T(8,128)S(1)} %get-tuple-element.19.gain_ref, s32[3,4,16]{2,1,0:T(4,128)S(1)} %pad_add_fusion.gauge_ref, ...), custom_call_target="tpu_custom_call" | custom-call | tf_op jit(solution)/shard_map/prepare/pallas_call | solution.py:433
  3.7 7.3 %all-to-all-start = ((f32[16,24,128]{2,1,0:T(8,128)}), f32[16,24,128]{2,1,0:T(8,128)S(1)}, u32[]{:S(2)}, u32[]{:S(2)}) async-start(f32[16,24,128]{2,1,0:T(8,128)} %get-tuple-element.16), calls=%async_computation | async-start | bytes 393216 | tf_op jit(solution)/shard_map/all_to_all | solution.py:447
  11.0 3.3 %collective-permute-start.2 = (f32[64,128]{1,0:T(8,128)S(1)}, f32[64,128]{1,0:T(8,128)S(1)}, u32[]{:S(2)}, u32[]{:S(2)}) collective-permute-start(f32[64,128]{1,0:T(8,128)S(1)} %get-tuple-element.14), channel_id=1, source_target_pairs={{0,4},{4,8},{8,12},{1,5},{5,9},{9,13},{2,6},{6,10},{10,14},{3,7},{... | collective-permute-start | bytes 98312 | tf_op jit(solution)/shard_map/ppermute | solution.py:454
  14.3 1.3 %collective-permute-start.3 = (f32[64,128]{1,0:T(8,128)S(1)}, f32[64,128]{1,0:T(8,128)S(1)}, u32[]{:S(2)}, u32[]{:S(2)}) collective-permute-start(f32[64,128]{1,0:T(8,128)S(1)} %get-tuple-element.15), channel_id=1, source_target_pairs={{4,0},{8,4},{12,8},{5,1},{9,5},{13,9},{6,2},{10,6},{14,10},{7,3},{... | collective-permute-start | bytes 98312 | tf_op jit(solution)/shard_map/ppermute | solution.py:455
  15.6 3.6 %collective-permute-start = (f32[2,32,512]{2,1,0:T(8,128)S(1)}, f32[2,32,512]{2,1,0:T(8,128)S(1)}, u32[]{:S(2)}, u32[]{:S(2)}) collective-permute-start(f32[2,32,512]{2,1,0:T(8,128)S(1)} %get-tuple-element.12), channel_id=1, source_target_pairs={{0,1},{1,2},{2,3},{4,5},{5,6},{6,7},{8,9},{9,10},{10,11},{12,13},{... | collective-permute-start | bytes 393224 | tf_op jit(solution)/shard_map/ppermute | solution.py:452
  19.2 1.9 %collective-permute-start.1 = (f32[2,32,512]{2,1,0:T(8,128)S(1)}, f32[2,32,512]{2,1,0:T(8,128)S(1)}, u32[]{:S(2)}, u32[]{:S(2)}) collective-permute-start(f32[2,32,512]{2,1,0:T(8,128)S(1)} %get-tuple-element.13), channel_id=1, source_target_pairs={{1,0},{2,1},{3,2},{5,4},{6,5},{7,6},{9,8},{10,9},{11,10},{13,12},{... | collective-permute-start | bytes 393224 | tf_op jit(solution)/shard_map/ppermute | solution.py:453
  21.1 0.0 all-to-all-done.parcel_ref
  21.1 3.4 %force.1.force_ref = f32[17,5,200,128]{3,2,1,0:T(8,128)S(1)} custom-call(f32[16,24,128]{2,1,0:T(8,128)S(1)} %all-to-all-done.parcel_ref), custom_call_target="tpu_custom_call" | custom-call | flops 2013265920 | bytes 7864320 | tf_op jit(solution)/shard_map/force/pallas_call | solution.py:460
  24.6 0.0 collective-permute-done.2.left_ref
  24.6 0.0 collective-permute-done.3.right_ref
  24.6 0.0 collective-permute-done.top_ref
  24.6 0.9 %collective-permute-done.1.bottom_ref = f32[2,32,512]{2,1,0:T(8,128)S(1)} collective-permute-done((f32[2,32,512]{2,1,0:T(8,128)S(1)}, f32[2,32,512]{2,1,0:T(8,128)S(1)}, u32[]{:S(2)}, u32[]{:S(2)}) %collective-permute-start.1) | collective-permute-done | bytes 131104 | tf_op jit(solution)/shard_map/ppermute | solution.py:453
  25.5 19.2 %sweep.1 = (f32[128,512]{1,0:T(8,128)S(1)}, f32[4,8,128]{2,1,0:T(8,128)}) custom-call(f32[128,512]{1,0:T(8,128)S(1)} %get-tuple-element.20.keep_ref, f32[128,512]{1,0:T(8,128)S(1)} %get-tuple-element.19.gain_ref, f32[2,32,512]{2,1,0:T(8,128)S(1)} %collective-permute-done.top_ref, f32[2,32,512]{2,1,0:T(8,128)S(1)} %collective-permute-done.1.bottom_ref, ...), custom_call_target="tpu_custom_call" | custom-call | tf_op jit(solution)/shard_map/sweep/pallas_call | solution.py:480
  44.7 5.4 %all-to-all-start.1 = ((f32[4,8,128]{2,1,0:T(8,128)}), f32[4,8,128]{2,1,0:T(8,128)S(1)}, u32[]{:S(2)}, u32[]{:S(2)}) async-start(f32[4,8,128]{2,1,0:T(8,128)} %get-tuple-element.18), calls=%async_computation.1 | async-start | bytes 32768 | tf_op jit(solution)/shard_map/all_to_all | solution.py:447
  50.1 0.9 %smooth.1.own_ref = f32[128,512]{1,0:T(8,128)S(1)} custom-call(f32[128,512]{1,0:T(8,128)S(1)} %get-tuple-element.17.grad_ref), custom_call_target="tpu_custom_call" | custom-call | flops 402653184 | bytes 524288 | tf_op jit(solution)/shard_map/smooth/pallas_call | solution.py:491
  51.0 3.6 %all-to-all-done.1 = f32[4,8,128]{2,1,0:T(8,128)S(1)} async-done(((f32[4,8,128]{2,1,0:T(8,128)}), f32[4,8,128]{2,1,0:T(8,128)S(1)}, u32[]{:S(2)}, u32[]{:S(2)}) %all-to-all-start.1) | async-done | bytes 16416 | tf_op jit(solution)/shard_map/all_to_all | solution.py:447
  54.6 1.1 %finish.1 = f32[128,512]{1,0:T(8,128)} custom-call(f32[128,512]{1,0:T(8,128)S(1)} %smooth.1.own_ref, f32[32,128]{1,0:T(8,128)S(1)} %bitcast.6), custom_call_target="tpu_custom_call" | custom-call | tf_op jit(solution)/shard_map/finish/pallas_call | solution.py:498
Async XLA Ops:
  2.0 0.7 %copy-start = (f32[16,2,4]{0,2,1:T(4,128)S(1)}, f32[16,2,4]{0,2,1:T(4,128)}, u32[]{:S(2)}) copy-start(f32[16,2,4]{0,2,1:T(4,128)} %param.17) | copy-start | bytes 1540
  3.7 17.4 %all-to-all-start = ((f32[16,24,128]{2,1,0:T(8,128)}), f32[16,24,128]{2,1,0:T(8,128)S(1)}, u32[]{:S(2)}, u32[]{:S(2)}) async-start(f32[16,24,128]{2,1,0:T(8,128)} %get-tuple-element.16), calls=%async_computation | async-start | bytes 393216 | tf_op jit(solution)/shard_map/all_to_all | solution.py:447
  11.0 13.6 %collective-permute-start.2 = (f32[64,128]{1,0:T(8,128)S(1)}, f32[64,128]{1,0:T(8,128)S(1)}, u32[]{:S(2)}, u32[]{:S(2)}) collective-permute-start(f32[64,128]{1,0:T(8,128)S(1)} %get-tuple-element.14), channel_id=1, source_target_pairs={{0,4},{4,8},{8,12},{1,5},{5,9},{9,13},{2,6},{6,10},{10,14},{3,7},{... | collective-permute-start | bytes 98312 | tf_op jit(solution)/shard_map/ppermute | solution.py:454
  14.3 10.3 %collective-permute-start.3 = (f32[64,128]{1,0:T(8,128)S(1)}, f32[64,128]{1,0:T(8,128)S(1)}, u32[]{:S(2)}, u32[]{:S(2)}) collective-permute-start(f32[64,128]{1,0:T(8,128)S(1)} %get-tuple-element.15), channel_id=1, source_target_pairs={{4,0},{8,4},{12,8},{5,1},{9,5},{13,9},{6,2},{10,6},{14,10},{7,3},{... | collective-permute-start | bytes 98312 | tf_op jit(solution)/shard_map/ppermute | solution.py:455
  15.6 9.0 %collective-permute-start = (f32[2,32,512]{2,1,0:T(8,128)S(1)}, f32[2,32,512]{2,1,0:T(8,128)S(1)}, u32[]{:S(2)}, u32[]{:S(2)}) collective-permute-start(f32[2,32,512]{2,1,0:T(8,128)S(1)} %get-tuple-element.12), channel_id=1, source_target_pairs={{0,1},{1,2},{2,3},{4,5},{5,6},{6,7},{8,9},{9,10},{10,11},{12,13},{... | collective-permute-start | bytes 393224 | tf_op jit(solution)/shard_map/ppermute | solution.py:452
  19.2 6.3 %collective-permute-start.1 = (f32[2,32,512]{2,1,0:T(8,128)S(1)}, f32[2,32,512]{2,1,0:T(8,128)S(1)}, u32[]{:S(2)}, u32[]{:S(2)}) collective-permute-start(f32[2,32,512]{2,1,0:T(8,128)S(1)} %get-tuple-element.13), channel_id=1, source_target_pairs={{1,0},{2,1},{3,2},{5,4},{6,5},{7,6},{9,8},{10,9},{11,10},{13,12},{... | collective-permute-start | bytes 393224 | tf_op jit(solution)/shard_map/ppermute | solution.py:453
  44.7 9.9 %all-to-all-start.1 = ((f32[4,8,128]{2,1,0:T(8,128)}), f32[4,8,128]{2,1,0:T(8,128)S(1)}, u32[]{:S(2)}, u32[]{:S(2)}) async-start(f32[4,8,128]{2,1,0:T(8,128)} %get-tuple-element.18), calls=%async_computation.1 | async-start | bytes 32768 | tf_op jit(solution)/shard_map/all_to_all | solution.py:447

commit v6 on v5

--- a/solution.py
+++ b/solution.py
@@ -120,6 +120,22 @@
         )
 
 
+def natural_rows(shape, axis, blocks):
+    place = lax.broadcasted_iota(jnp.int32, shape, axis)
+    return (place & 7) * blocks + (place >> 3)
+
+
+def thirds(value):
+    high = value.astype(jnp.bfloat16)
+    rest = value - high.astype(jnp.float32)
+    middle = rest.astype(jnp.bfloat16)
+    return high, middle, (rest - middle.astype(jnp.float32)).astype(jnp.bfloat16)
+
+
+def pick_rows(onehot, value):
+    return sum(jnp.dot(onehot, part, preferred_element_type=jnp.float32) for part in thirds(value))
+
+
 def shift_from(planes, shift, lanes):
     count = len(planes)
     rolled = [roll_lanes(plane, -shift) for plane in planes]
@@ -142,8 +158,7 @@
     blocks = rows_all // 8
     row_shift = (halo - my_row * height).astype(jnp.float32)
     col_shift = (-my_lon * width).astype(jnp.float32)
-    place = lax.broadcasted_iota(jnp.int32, (rows_all, LANES), 0)
-    at = ((place & 7) * blocks + (place >> 3)).astype(jnp.float32)
+    at = natural_rows((rows_all, LANES), 0, blocks).astype(jnp.float32)
 
     def gather_gauges(index):
         lanes = lane_iota(STEPS_BLOCK)
@@ -214,7 +229,7 @@
 def sweep(
     steps, keep_ref, gain_ref, top_ref, bottom_ref, left_ref, right_ref, parcel_ref, force_ref,
     grad_ref, sums_ref,
-    a, fx, fy, keep_x, gain_x, keep_y, gain_y, plain,
+    a, fx, fy, keep_x, gain_x, keep_y, gain_y, plain, wet,
 ):
     height, width = keep_ref.shape
     halo = 2 * steps
@@ -239,6 +254,11 @@
 
     def down(value):
         return pltpu.roll(value, 1, 0)
+
+    square = (rows_all, rows_all)
+    spread = natural_rows(square, 0, blocks) == lax.broadcasted_iota(jnp.int32, square, 1)
+    spread = spread.astype(jnp.float32).astype(jnp.bfloat16)
+    every = range(planes)
 
     half = height // 2
     for kind, (source, by_x, by_y) in enumerate(((keep_ref, keep_x, keep_y), (gain_ref, gain_x, gain_y))):
@@ -264,13 +284,17 @@
                     jnp.where(segment == LANES // SEG - 1, roll_lanes(by_left, end - i * SEG), 0.0),
                 )
                 plain[inner, at + 8 * i : at + 8 * i + 8, :] = both
+        placed = [pick_rows(spread, plain[c, 0:rows_all, :]) for c in every]
         for q in range(blocks):
-            values = [plain[c, pl.ds(q, 8, stride=blocks), :] for c in range(planes)]
+            values = [placed[c][8 * q : 8 * q + 8] for c in every]
             shifted = shift_from(values, 1, lanes8)
             to = (q - 1) % blocks * 8
-            for c in range(planes):
+            for c in every:
                 by_x[c, 8 * q : 8 * q + 8, :] = shifted[c]
                 by_y[c, to : to + 8, :] = up(values[c]) if q == 0 else values[c]
+        if kind == 0:
+            for c in range(inner):
+                wet[c, 0:rows_all, :] = placed[c]
 
     fx[...] = jnp.zeros_like(fx)
     fy[...] = jnp.zeros_like(fy)
@@ -281,7 +305,6 @@
     sublane = lax.broadcasted_iota(jnp.int32, (8, LANES), 0)
     top_mask = jnp.where(sublane == (halo - 1) // blocks, jnp.where(has_top, 1.0, 0.0), 1.0)
     bottom_mask = jnp.where(sublane == (halo + height) // blocks, jnp.where(has_bottom, 1.0, 0.0), 1.0)
-    every = range(planes)
 
     def step(index, carry):
         after = jnp.where(index == steps - 1, steps, steps - 2 - index)
@@ -339,33 +362,38 @@
 
     lax.fori_loop(0, steps, step, 0)
 
-    for r in range(0, height, 8):
-        s, q = divmod(halo + r, blocks)
-        for c in range(inner):
-            cols = slice(c * LANES, (c + 1) * LANES)
-            value = a[c, pl.ds(8 * q + s, 8, stride=8), :]
-            grad_ref[r : r + 8, cols] = jnp.where(keep_ref[r : r + 8, cols] > 0.0, value, 0.0)
+    grad = jnp.concatenate(
+        [jnp.where(wet[c, 0:rows_all, :] > 0.0, a[c, 0:rows_all, :], 0.0) for c in range(inner)], axis=1
+    )
+    grad_ref[...] = grad
     length = 2.0 * width
     kind = lax.broadcasted_iota(jnp.int32, (8, width), 0)
     column = lax.broadcasted_iota(jnp.int32, (8, width), 1)
     steps_off = jnp.where(kind == 0, column, width - 1 - column).astype(jnp.float32)
     weights = jnp.where(kind < 2, jnp.exp(-steps_off / length), 0.0)
     sums = lax.dot_general(
-        weights, grad_ref[...], (((1,), (1,)), ((), ())), precision=lax.Precision.HIGHEST,
-        preferred_element_type=jnp.float32,
+        weights, grad, (((1,), (1,)), ((), ())), precision=lax.Precision.HIGHEST, preferred_element_type=jnp.float32
+    )
+    tall = (rows_all, height)
+    gather = natural_rows(tall, 0, blocks) == lax.broadcasted_iota(jnp.int32, tall, 1) + halo
+    sums = jnp.dot(
+        sums, gather.astype(jnp.float32), precision=lax.Precision.HIGHEST, preferred_element_type=jnp.float32
     )
     for i in range(sums_ref.shape[0]):
         sums_ref[i] = sums
 
 
-def smooth(grad_ref, out_ref):
-    width = grad_ref.shape[1]
+def smooth(halo, grad_ref, out_ref):
+    width, (height, rows_all) = grad_ref.shape[1], (out_ref.shape[0], grad_ref.shape[0])
+    wide = (height, rows_all)
+    gather = natural_rows(wide, 1, rows_all // 8) == lax.broadcasted_iota(jnp.int32, wide, 0) + halo
+    grad = pick_rows(gather.astype(jnp.float32).astype(jnp.bfloat16), grad_ref[...])
     length = 2.0 * width
     row = lax.broadcasted_iota(jnp.int32, (width, width), 0)
     column = lax.broadcasted_iota(jnp.int32, (width, width), 1)
     kernel = jnp.exp(-jnp.abs(row - column).astype(jnp.float32) / length)
     out_ref[...] = jnp.dot(
-        grad_ref[...], kernel, precision=lax.Precision.HIGHEST, preferred_element_type=jnp.float32
+        grad, kernel, precision=lax.Precision.HIGHEST, preferred_element_type=jnp.float32
     )
 
 
@@ -479,17 +507,17 @@
     longer = pltpu.VMEM((planes, spaced(rows_all + 16), LANES), jnp.float32)
     grad, sums = pl.pallas_call(
         functools.partial(sweep, steps),
-        out_shape=(f32(height, width), f32(lons, 8, height)),
+        out_shape=(f32(rows_all, width), f32(lons, 8, height)),
         in_specs=vmem(8),
         out_specs=tuple(vmem(2)),
-        scratch_shapes=[longer, plane, longer] + [plane] * 5,
+        scratch_shapes=[longer, plane, longer] + [plane] * 6,
         compiler_params=params,
         name="sweep",
     )(keep, gain, top, bottom, left, right, parcel, pushes)
 
     sums = exchange(sums, "lon")
     own = pl.pallas_call(
-        smooth, out_shape=f32(height, width), in_specs=vmem(1), out_specs=vmem(1)[0], compiler_params=params,
+        functools.partial(smooth, halo), out_shape=f32(height, width), in_specs=vmem(1), out_specs=vmem(1)[0], compiler_params=params,
         cost_estimate=pl.CostEstimate(
             flops=6 * 2 * height * width * width, bytes_accessed=2 * 4 * height * width, transcendentals=width * width
         ),

time: 56.2 us -> 57.6 us (1.025)
  Pallas kernels: 25.6 us -> 27.1 us
    pallas_call x2, Pallas kernels: 20.1 us -> 21.6 us  [the longest x1 20.6 us: local(): pl.pallas_call(functools.partial(sweep, steps), out_shape=(f32(rows_all,...]
where the time goes in v6:
time: 57.6 us; the launch traced here: 57.1 us
  Pallas kernels  27.1 us (47%)
  starting transfers between devices  22.8 us (40%)
  waiting for transfers between devices  4.31 us (7%)
  other arithmetic  2.03 us (4%)
  local copies, waits for them, and re-layouts  0.68 us (1%)
    pallas_call x1, Pallas kernels, local(): pl.pallas_call(functools.partial(sweep, steps), out_shape=(f32(rows_all,...  20.6 us
    all_to_all x2, starting transfers between devices, exchange(): return lax.all_to_all(array, axes, split_axis=0, concat_axis=0, tiled=True)  12.7 us
    ppermute x1, starting transfers between devices, local(): top = lax.ppermute(south, ROW_AXES, down)  3.62 us
    pallas_call x1, Pallas kernels, local(): pl.pallas_call(functools.partial(force, steps, halo, height, width), out_...  3.41 us
    all_to_all x2, waiting for transfers between devices, exchange(): return lax.all_to_all(array, axes, split_axis=0, concat_axis=0, tiled=True)  3.4 us
    ppermute x1, starting transfers between devices, local(): left = lax.ppermute(east, 'lon', [(i, i + 1) for i in range(lons - 1)])  3.28 us
    ppermute x1, starting transfers between devices, local(): bottom = lax.ppermute(north, ROW_AXES, up)  1.92 us
    ppermute x1, starting transfers between devices, local(): right = lax.ppermute(west, 'lon', [(i + 1, i) for i in range(lons - 1)])  1.29 us
  transfers between devices with their start and end apart: 6, of which 2 were waited for; matrix products, arithmetic and copies ran while one was open for 0% of the time, Pallas kernels for 8%

profile of v6, /device:TPU:1, one launch (start us, length us, event | category | flops | bytes accessed | tf_op | source)
XLA Modules:
  0.0 57.1 jit_solution(2960753912410080518)
XLA Ops:
  0.0 0.7 %pad_add_fusion.gauge_ref = s32[3,4,16]{2,1,0:T(4,128)S(1)} fusion(s32[1,1,8]{2,1,0:T(1,128)} %bitcast.9, s32[1,1,16]{2,1,0:T(1,128)} %bitcast.10, s32[1,1,16]{2,1,0:T(1,128)} %bitcast.11, s32[2,4,16]{2,1,0:T(4,128)} %bitcast.8), kind=kLoop, calls=%fused_computation.2 | loop fusion | flops 576 | bytes 1440 | tf_op jit(solution)/shard_map/add | solution.py:455
  0.7 1.3 %multiply_multiply_fusion = (f32[128,512]{1,0:T(8,128)S(1)}, f32[128,512]{1,0:T(8,128)S(1)}) fusion(f32[128,512]{1,0:T(8,128)} %param.9, f32[128,512]{1,0:T(8,128)} %param.10, s32[128,512]{1,0:T(8,128)} %param.12, f32[128,512]{1,0:T(8,128)} %param.11), kind=kLoop, calls=%fused_computation | loop fusion | flops 458752 | bytes 1572864 | tf_op jit(solution)/shard_map/mul | solution.py:444
  2.0 0.0 copy-start
  2.0 0.7 %copy-done = f32[16,2,4]{0,2,1:T(4,128)S(1)} copy-done((f32[16,2,4]{0,2,1:T(4,128)S(1)}, f32[16,2,4]{0,2,1:T(4,128)}, u32[]{:S(2)}) %copy-start) | copy-done | bytes 536
  2.7 1.0 %prepare.1 = (f32[16,24,128]{2,1,0:T(8,128)}, f32[2,32,512]{2,1,0:T(8,128)S(1)}, f32[2,32,512]{2,1,0:T(8,128)S(1)}, f32[64,128]{1,0:T(8,128)S(1)}, f32[64,128]{1,0:T(8,128)S(1)}) custom-call(f32[128,512]{1,0:T(8,128)S(1)} %get-tuple-element.20.keep_ref, f32[128,512]{1,0:T(8,128)S(1)} %get-tuple-element.19.gain_ref, s32[3,4,16]{2,1,0:T(4,128)S(1)} %pad_add_fusion.gauge_ref, ...), custom_call_target="tpu_custom_call" | custom-call | tf_op jit(solution)/shard_map/prepare/pallas_call | solution.py:461
  3.7 7.3 %all-to-all-start = ((f32[16,24,128]{2,1,0:T(8,128)}), f32[16,24,128]{2,1,0:T(8,128)S(1)}, u32[]{:S(2)}, u32[]{:S(2)}) async-start(f32[16,24,128]{2,1,0:T(8,128)} %get-tuple-element.16), calls=%async_computation | async-start | bytes 393216 | tf_op jit(solution)/shard_map/all_to_all | solution.py:475
  11.0 3.3 %collective-permute-start.2 = (f32[64,128]{1,0:T(8,128)S(1)}, f32[64,128]{1,0:T(8,128)S(1)}, u32[]{:S(2)}, u32[]{:S(2)}) collective-permute-start(f32[64,128]{1,0:T(8,128)S(1)} %get-tuple-element.14), channel_id=1, source_target_pairs={{0,4},{4,8},{8,12},{1,5},{5,9},{9,13},{2,6},{6,10},{10,14},{3,7},{... | collective-permute-start | bytes 98312 | tf_op jit(solution)/shard_map/ppermute | solution.py:482
  14.3 1.3 %collective-permute-start.3 = (f32[64,128]{1,0:T(8,128)S(1)}, f32[64,128]{1,0:T(8,128)S(1)}, u32[]{:S(2)}, u32[]{:S(2)}) collective-permute-start(f32[64,128]{1,0:T(8,128)S(1)} %get-tuple-element.15), channel_id=1, source_target_pairs={{4,0},{8,4},{12,8},{5,1},{9,5},{13,9},{6,2},{10,6},{14,10},{7,3},{... | collective-permute-start | bytes 98312 | tf_op jit(solution)/shard_map/ppermute | solution.py:483
  15.6 3.6 %collective-permute-start = (f32[2,32,512]{2,1,0:T(8,128)S(1)}, f32[2,32,512]{2,1,0:T(8,128)S(1)}, u32[]{:S(2)}, u32[]{:S(2)}) collective-permute-start(f32[2,32,512]{2,1,0:T(8,128)S(1)} %get-tuple-element.12), channel_id=1, source_target_pairs={{0,1},{1,2},{2,3},{4,5},{5,6},{6,7},{8,9},{9,10},{10,11},{12,13},{... | collective-permute-start | bytes 393224 | tf_op jit(solution)/shard_map/ppermute | solution.py:480
  19.2 1.9 %collective-permute-start.1 = (f32[2,32,512]{2,1,0:T(8,128)S(1)}, f32[2,32,512]{2,1,0:T(8,128)S(1)}, u32[]{:S(2)}, u32[]{:S(2)}) collective-permute-start(f32[2,32,512]{2,1,0:T(8,128)S(1)} %get-tuple-element.13), channel_id=1, source_target_pairs={{1,0},{2,1},{3,2},{5,4},{6,5},{7,6},{9,8},{10,9},{11,10},{13,12},{... | collective-permute-start | bytes 393224 | tf_op jit(solution)/shard_map/ppermute | solution.py:481
  21.1 0.0 all-to-all-done.parcel_ref
  21.1 3.4 %force.1.force_ref = f32[17,5,200,128]{3,2,1,0:T(8,128)S(1)} custom-call(f32[16,24,128]{2,1,0:T(8,128)S(1)} %all-to-all-done.parcel_ref), custom_call_target="tpu_custom_call" | custom-call | flops 2013265920 | bytes 7864320 | tf_op jit(solution)/shard_map/force/pallas_call | solution.py:488
  24.6 0.0 collective-permute-done.2.left_ref
  24.6 0.0 collective-permute-done.3.right_ref
  24.6 0.0 collective-permute-done.top_ref
  24.6 0.9 %collective-permute-done.1.bottom_ref = f32[2,32,512]{2,1,0:T(8,128)S(1)} collective-permute-done((f32[2,32,512]{2,1,0:T(8,128)S(1)}, f32[2,32,512]{2,1,0:T(8,128)S(1)}, u32[]{:S(2)}, u32[]{:S(2)}) %collective-permute-start.1) | collective-permute-done | bytes 131104 | tf_op jit(solution)/shard_map/ppermute | solution.py:481
  25.5 20.6 %sweep.1 = (f32[192,512]{1,0:T(8,128)S(1)}, f32[4,8,128]{2,1,0:T(8,128)}) custom-call(f32[128,512]{1,0:T(8,128)S(1)} %get-tuple-element.20.keep_ref, f32[128,512]{1,0:T(8,128)S(1)} %get-tuple-element.19.gain_ref, f32[2,32,512]{2,1,0:T(8,128)S(1)} %collective-permute-done.top_ref, f32[2,32,512]{2,1,0:T(8,128)S(1)} %collective-permute-done.1.bottom_ref, ...), custom_call_target="tpu_custom_call" | custom-call | tf_op jit(solution)/shard_map/sweep/pallas_call | solution.py:508
  46.0 5.4 %all-to-all-start.1 = ((f32[4,8,128]{2,1,0:T(8,128)}), f32[4,8,128]{2,1,0:T(8,128)S(1)}, u32[]{:S(2)}, u32[]{:S(2)}) async-start(f32[4,8,128]{2,1,0:T(8,128)} %get-tuple-element.18), calls=%async_computation.1 | async-start | bytes 32768 | tf_op jit(solution)/shard_map/all_to_all | solution.py:475
  51.5 1.1 %smooth.1.own_ref = f32[128,512]{1,0:T(8,128)S(1)} custom-call(f32[192,512]{1,0:T(8,128)S(1)} %get-tuple-element.17.grad_ref), custom_call_target="tpu_custom_call" | custom-call | flops 402653184 | bytes 524288 | tf_op jit(solution)/shard_map/smooth/pallas_call | solution.py:519
  52.5 3.4 %all-to-all-done.1 = f32[4,8,128]{2,1,0:T(8,128)S(1)} async-done(((f32[4,8,128]{2,1,0:T(8,128)}), f32[4,8,128]{2,1,0:T(8,128)S(1)}, u32[]{:S(2)}, u32[]{:S(2)}) %all-to-all-start.1) | async-done | bytes 16416 | tf_op jit(solution)/shard_map/all_to_all | solution.py:475
  55.9 1.1 %finish.1 = f32[128,512]{1,0:T(8,128)} custom-call(f32[128,512]{1,0:T(8,128)S(1)} %smooth.1.own_ref, f32[32,128]{1,0:T(8,128)S(1)} %bitcast.6), custom_call_target="tpu_custom_call" | custom-call | tf_op jit(solution)/shard_map/finish/pallas_call | solution.py:526
Async XLA Ops:
  2.0 0.7 %copy-start = (f32[16,2,4]{0,2,1:T(4,128)S(1)}, f32[16,2,4]{0,2,1:T(4,128)}, u32[]{:S(2)}) copy-start(f32[16,2,4]{0,2,1:T(4,128)} %param.17) | copy-start | bytes 1540
  3.7 17.4 %all-to-all-start = ((f32[16,24,128]{2,1,0:T(8,128)}), f32[16,24,128]{2,1,0:T(8,128)S(1)}, u32[]{:S(2)}, u32[]{:S(2)}) async-start(f32[16,24,128]{2,1,0:T(8,128)} %get-tuple-element.16), calls=%async_computation | async-start | bytes 393216 | tf_op jit(solution)/shard_map/all_to_all | solution.py:475
  11.0 13.6 %collective-permute-start.2 = (f32[64,128]{1,0:T(8,128)S(1)}, f32[64,128]{1,0:T(8,128)S(1)}, u32[]{:S(2)}, u32[]{:S(2)}) collective-permute-start(f32[64,128]{1,0:T(8,128)S(1)} %get-tuple-element.14), channel_id=1, source_target_pairs={{0,4},{4,8},{8,12},{1,5},{5,9},{9,13},{2,6},{6,10},{10,14},{3,7},{... | collective-permute-start | bytes 98312 | tf_op jit(solution)/shard_map/ppermute | solution.py:482
  14.3 10.3 %collective-permute-start.3 = (f32[64,128]{1,0:T(8,128)S(1)}, f32[64,128]{1,0:T(8,128)S(1)}, u32[]{:S(2)}, u32[]{:S(2)}) collective-permute-start(f32[64,128]{1,0:T(8,128)S(1)} %get-tuple-element.15), channel_id=1, source_target_pairs={{4,0},{8,4},{12,8},{5,1},{9,5},{13,9},{6,2},{10,6},{14,10},{7,3},{... | collective-permute-start | bytes 98312 | tf_op jit(solution)/shard_map/ppermute | solution.py:483
  15.6 9.0 %collective-permute-start = (f32[2,32,512]{2,1,0:T(8,128)S(1)}, f32[2,32,512]{2,1,0:T(8,128)S(1)}, u32[]{:S(2)}, u32[]{:S(2)}) collective-permute-start(f32[2,32,512]{2,1,0:T(8,128)S(1)} %get-tuple-element.12), channel_id=1, source_target_pairs={{0,1},{1,2},{2,3},{4,5},{5,6},{6,7},{8,9},{9,10},{10,11},{12,13},{... | collective-permute-start | bytes 393224 | tf_op jit(solution)/shard_map/ppermute | solution.py:480
  19.2 6.3 %collective-permute-start.1 = (f32[2,32,512]{2,1,0:T(8,128)S(1)}, f32[2,32,512]{2,1,0:T(8,128)S(1)}, u32[]{:S(2)}, u32[]{:S(2)}) collective-permute-start(f32[2,32,512]{2,1,0:T(8,128)S(1)} %get-tuple-element.13), channel_id=1, source_target_pairs={{1,0},{2,1},{3,2},{5,4},{6,5},{7,6},{9,8},{10,9},{11,10},{13,12},{... | collective-permute-start | bytes 393224 | tf_op jit(solution)/shard_map/ppermute | solution.py:481
  46.0 9.9 %all-to-all-start.1 = ((f32[4,8,128]{2,1,0:T(8,128)}), f32[4,8,128]{2,1,0:T(8,128)S(1)}, u32[]{:S(2)}, u32[]{:S(2)}) async-start(f32[4,8,128]{2,1,0:T(8,128)} %get-tuple-element.18), calls=%async_computation.1 | async-start | bytes 32768 | tf_op jit(solution)/shard_map/all_to_all | solution.py:475

commit v7 on v5

--- a/solution.py
+++ b/solution.py
@@ -12,7 +12,6 @@
 LANES = 128
 SEG = 32
 LEVELS = 4
-CHUNK = 4
 
 courant = 0.45
 depth_floor = 0.1
@@ -214,7 +213,7 @@
 def sweep(
     steps, keep_ref, gain_ref, top_ref, bottom_ref, left_ref, right_ref, parcel_ref, force_ref,
     grad_ref, sums_ref,
-    a, fx, fy, keep_x, gain_x, keep_y, gain_y, plain,
+    a, fx, fy, keep_x, gain_x, keep_y, gain_y, plain, pushes, arrived,
 ):
     height, width = keep_ref.shape
     halo = 2 * steps
@@ -272,72 +271,97 @@
                 by_x[c, 8 * q : 8 * q + 8, :] = shifted[c]
                 by_y[c, to : to + 8, :] = up(values[c]) if q == 0 else values[c]
 
+    col_valid = jnp.where(lanes8 < LANES // 2, jnp.where(has_right, 1.0, 0.0), jnp.where(has_left, 1.0, 0.0))
+    col_mask = jnp.where((lanes8 < halo) | (lanes8 >= end), col_valid, 0.0)
+    sublane = lax.broadcasted_iota(jnp.int32, (8, LANES), 0)
+    row_mask = {}
+    for row, there in ((halo - 1, has_top), (halo + height, has_bottom)):
+        row_mask[row % blocks] = jnp.where(sublane == row // blocks, jnp.where(there, 1.0, 0.0), 1.0)
+    every = range(planes)
+
+    def level_of(order):
+        return jnp.where(order < steps, steps - 1 - order, steps)
+
+    def fetch(order, odd):
+        return pltpu.make_async_copy(force_ref.at[level_of(order)], pushes.at[odd], arrived.at[odd])
+
+    fetch(1, 1).start()
+    fetch(2, 0).start()
     fx[...] = jnp.zeros_like(fx)
     fy[...] = jnp.zeros_like(fy)
     a[:, 0:rows_all, :] = force_ref[steps - 1, :, 0:rows_all, :]
 
-    col_valid = jnp.where(lanes8 < LANES // 2, jnp.where(has_right, 1.0, 0.0), jnp.where(has_left, 1.0, 0.0))
-    col_mask = jnp.where((lanes8 < halo) | (lanes8 >= end), col_valid, 0.0)
-    sublane = lax.broadcasted_iota(jnp.int32, (8, LANES), 0)
-    top_mask = jnp.where(sublane == (halo - 1) // blocks, jnp.where(has_top, 1.0, 0.0), 1.0)
-    bottom_mask = jnp.where(sublane == (halo + height) // blocks, jnp.where(has_bottom, 1.0, 0.0), 1.0)
-    every = range(planes)
-
-    def step(index, carry):
-        after = jnp.where(index == steps - 1, steps, steps - 2 - index)
+    def step(odd):
+        near, ahead, new_y, total, behind = {}, {}, {}, {}, {}
+
+        def rows(q):
+            return slice(8 * q, 8 * q + 8)
+
+        def first(q):
+            near[q] = [a[c, rows(q % blocks), :] for c in every]
+            if q < blocks:
+                ahead[q] = shift_from(near[q], 2, lanes8)
+            else:
+                near[q] = [up(value) for value in near[q]]
+
+        def second_y(q):
+            new_y[q] = [
+                keep_y[c, rows(q), :] * fy[c, rows(q), :] + gain_y[c, rows(q), :] * (near[q + 2][c] - near[q][c])
+                for c in every
+            ]
+            for c in every:
+                fy[c, rows(q), :] = new_y[q][c]
+
+        def second_x(q):
+            new_x = [
+                keep_x[c, rows(q), :] * fx[c, rows(q), :] + gain_x[c, rows(q), :] * (ahead[q][c] - near[q][c])
+                for c in every
+            ]
+            before = new_y[q - 2] if q >= 2 else [down(fy[c, rows(q - 2 + blocks), :]) for c in every]
+            total[q] = [near[q][c] + (new_y[q][c] - before[c]) + new_x[c] for c in every]
+            behind[q] = shift_from(new_x, -2, lanes8)
+            for c in every:
+                fx[c, rows(q), :] = new_x[c]
+
+        def third(q):
+            for c in every:
+                value = total[q][c] - behind[q][c]
+                if c == inner:
+                    value = value * col_mask
+                if q in row_mask:
+                    value = value * row_mask[q]
+                a[c, rows(q), :] = value + pushes[odd, c, rows(q), :]
+
+        for q in range(4):
+            first(q)
+        second_y(0)
+        second_y(1)
+        for q in range(2, blocks):
+            first(q + 2)
+            second_y(q)
+            second_x(q)
+            if q > 2:
+                third(q - 1)
         for q in range(2):
-            for c in every:
-                a[c, rows_all + 8 * q : rows_all + 8 * q + 8, :] = up(a[c, 8 * q : 8 * q + 8, :])
-
-        def chunk(number, inner_carry):
-            start = pl.multiple_of(number * (8 * CHUNK), 8 * CHUNK)
-
-            def at(q):
-                return pl.ds(start + 8 * q, 8)
-
-            near = [[a[c, at(q), :] for c in every] for q in range(CHUNK + 2)]
-            new_y = [[fy[c, at(q), :] for c in every] for q in range(2)]
-            total, new_x = [], []
-            for q in range(CHUNK):
-                new_y.append(
-                    [
-                        keep_y[c, at(q), :] * fy[c, at(q + 2), :] + gain_y[c, at(q), :] * (near[q + 2][c] - near[q][c])
-                        for c in every
-                    ]
-                )
-                ahead = shift_from(near[q], 2, lanes8)
-                new_x.append(
-                    [keep_x[c, at(q), :] * fx[c, at(q), :] + gain_x[c, at(q), :] * (ahead[c] - near[q][c]) for c in every]
-                )
-                total.append([near[q][c] + (new_y[q + 2][c] - new_y[q][c]) for c in every])
-            behind = [shift_from(new_x[q], -2, lanes8) for q in range(CHUNK)]
-            for q in range(CHUNK):
-                for c in every:
-                    value = total[q][c] + (new_x[q][c] - behind[q][c])
-                    if c == inner:
-                        value = value * col_mask
-                    total[q][c] = value + force_ref[after, c, at(q), :]
-            for q in range(CHUNK):
-                for c in every:
-                    fx[c, at(q), :] = new_x[q][c]
-                    fy[c, at(q + 2), :] = new_y[q + 2][c]
-                    a[c, at(q), :] = total[q][c]
-            return inner_carry
-
-        fy[:, 0:16, :] = jnp.zeros((planes, 16, LANES), jnp.float32)
-        lax.fori_loop(0, blocks // CHUNK, chunk, 0)
-        for q in range(2):
-            for c in every:
-                rows = slice(8 * q, 8 * q + 8)
-                past = down(fy[c, rows_all + 8 * q : rows_all + 8 * q + 8, :])
-                a[c, rows, :] = a[c, rows, :] - (past * col_mask if c == inner else past)
-        for row, mask in ((halo - 1, top_mask), (halo + height, bottom_mask)):
-            rows = slice(row % blocks * 8, row % blocks * 8 + 8)
-            for c in every:
-                a[c, rows, :] = a[c, rows, :] * mask
+            first(q)
+            new_y[q] = [fy[c, rows(q), :] for c in every]
+            second_x(q)
+            third(q - 1 if q else blocks - 1)
+        third(1)
+
+    def pair(index, carry):
+        for odd in (1, 0):
+            order = 2 * index + 2 - odd
+            fetch(order, odd).wait()
+            step(odd)
+
+            @pl.when(index < steps // 2 - 1)
+            def _():
+                fetch(order + 2, odd).start()
+
         return carry
 
-    lax.fori_loop(0, steps, step, 0)
+    lax.fori_loop(0, steps // 2, pair, 0)
 
     for r in range(0, height, 8):
         s, q = divmod(halo + r, blocks)
@@ -476,13 +500,14 @@
     )(parcel)
 
     plane = pltpu.VMEM((planes, spaced(rows_all), LANES), jnp.float32)
-    longer = pltpu.VMEM((planes, spaced(rows_all + 16), LANES), jnp.float32)
     grad, sums = pl.pallas_call(
         functools.partial(sweep, steps),
         out_shape=(f32(height, width), f32(lons, 8, height)),
         in_specs=vmem(8),
         out_specs=tuple(vmem(2)),
-        scratch_shapes=[longer, plane, longer] + [plane] * 5,
+        scratch_shapes=[plane] * 8 + [
+            pltpu.VMEM((2, planes, spaced(rows_all), LANES), jnp.float32), pltpu.SemaphoreType.DMA((2,)),
+        ],
         compiler_params=params,
         name="sweep",
     )(keep, gain, top, bottom, left, right, parcel, pushes)

time: 56.2 us -> 52.7 us (0.938)
  Pallas kernels: 25.6 us -> 22.1 us
    pallas_call x1, Pallas kernels: 19.2 us -> 15.7 us  [local(): pl.pallas_call(functools.partial(sweep, steps), out_shape=(f32(height, wi...]
where the time goes in v7:
time: 52.7 us; the launch traced here: 52.2 us
  starting transfers between devices  22.8 us (43%)
  Pallas kernels  22.1 us (42%)
  waiting for transfers between devices  4.46 us (8%)
  other arithmetic  2.03 us (4%)
  local copies, waits for them, and re-layouts  0.68 us (1%)
    pallas_call x1, Pallas kernels, local(): pl.pallas_call(functools.partial(sweep, steps), out_shape=(f32(height, wi...  15.7 us
    all_to_all x2, starting transfers between devices, exchange(): return lax.all_to_all(array, axes, split_axis=0, concat_axis=0, tiled=True)  12.7 us
    ppermute x1, starting transfers between devices, local(): top = lax.ppermute(south, ROW_AXES, down)  3.62 us
    all_to_all x2, waiting for transfers between devices, exchange(): return lax.all_to_all(array, axes, split_axis=0, concat_axis=0, tiled=True)  3.56 us
    pallas_call x1, Pallas kernels, local(): pl.pallas_call(functools.partial(force, steps, halo, height, width), out_...  3.41 us
    ppermute x1, starting transfers between devices, local(): left = lax.ppermute(east, 'lon', [(i, i + 1) for i in range(lons - 1)])  3.28 us
    ppermute x1, starting transfers between devices, local(): bottom = lax.ppermute(north, ROW_AXES, up)  1.92 us
    ppermute x1, starting transfers between devices, local(): right = lax.ppermute(west, 'lon', [(i + 1, i) for i in range(lons - 1)])  1.29 us
  transfers between devices with their start and end apart: 6, of which 2 were waited for; matrix products, arithmetic and copies ran while one was open for 0% of the time, Pallas kernels for 8%

profile of v7, /device:TPU:1, one launch (start us, length us, event | category | flops | bytes accessed | tf_op | source)
XLA Modules:
  0.0 52.2 jit_solution(10096908136070760843)
XLA Ops:
  0.0 0.7 %pad_add_fusion.gauge_ref = s32[3,4,16]{2,1,0:T(4,128)S(1)} fusion(s32[1,1,8]{2,1,0:T(1,128)} %bitcast.9, s32[1,1,16]{2,1,0:T(1,128)} %bitcast.10, s32[1,1,16]{2,1,0:T(1,128)} %bitcast.11, s32[2,4,16]{2,1,0:T(4,128)} %bitcast.8), kind=kLoop, calls=%fused_computation.2 | loop fusion | flops 576 | bytes 1440 | tf_op jit(solution)/shard_map/add | solution.py:451
  0.7 1.3 %multiply_multiply_fusion = (f32[128,512]{1,0:T(8,128)S(1)}, f32[128,512]{1,0:T(8,128)S(1)}) fusion(f32[128,512]{1,0:T(8,128)} %param.9, f32[128,512]{1,0:T(8,128)} %param.10, s32[128,512]{1,0:T(8,128)} %param.12, f32[128,512]{1,0:T(8,128)} %param.11), kind=kLoop, calls=%fused_computation | loop fusion | flops 458752 | bytes 1572864 | tf_op jit(solution)/shard_map/mul | solution.py:440
  2.0 0.0 copy-start
  2.0 0.7 %copy-done = f32[16,2,4]{0,2,1:T(4,128)S(1)} copy-done((f32[16,2,4]{0,2,1:T(4,128)S(1)}, f32[16,2,4]{0,2,1:T(4,128)}, u32[]{:S(2)}) %copy-start) | copy-done | bytes 536
  2.7 1.0 %prepare.1 = (f32[16,24,128]{2,1,0:T(8,128)}, f32[2,32,512]{2,1,0:T(8,128)S(1)}, f32[2,32,512]{2,1,0:T(8,128)S(1)}, f32[64,128]{1,0:T(8,128)S(1)}, f32[64,128]{1,0:T(8,128)S(1)}) custom-call(f32[128,512]{1,0:T(8,128)S(1)} %get-tuple-element.20.keep_ref, f32[128,512]{1,0:T(8,128)S(1)} %get-tuple-element.19.gain_ref, s32[3,4,16]{2,1,0:T(4,128)S(1)} %pad_add_fusion.gauge_ref, ...), custom_call_target="tpu_custom_call" | custom-call | tf_op jit(solution)/shard_map/prepare/pallas_call | solution.py:457
  3.7 7.3 %all-to-all-start = ((f32[16,24,128]{2,1,0:T(8,128)}), f32[16,24,128]{2,1,0:T(8,128)S(1)}, u32[]{:S(2)}, u32[]{:S(2)}) async-start(f32[16,24,128]{2,1,0:T(8,128)} %get-tuple-element.16), calls=%async_computation | async-start | bytes 393216 | tf_op jit(solution)/shard_map/all_to_all | solution.py:471
  11.0 3.3 %collective-permute-start.2 = (f32[64,128]{1,0:T(8,128)S(1)}, f32[64,128]{1,0:T(8,128)S(1)}, u32[]{:S(2)}, u32[]{:S(2)}) collective-permute-start(f32[64,128]{1,0:T(8,128)S(1)} %get-tuple-element.14), channel_id=1, source_target_pairs={{0,4},{4,8},{8,12},{1,5},{5,9},{9,13},{2,6},{6,10},{10,14},{3,7},{... | collective-permute-start | bytes 98312 | tf_op jit(solution)/shard_map/ppermute | solution.py:478
  14.3 1.3 %collective-permute-start.3 = (f32[64,128]{1,0:T(8,128)S(1)}, f32[64,128]{1,0:T(8,128)S(1)}, u32[]{:S(2)}, u32[]{:S(2)}) collective-permute-start(f32[64,128]{1,0:T(8,128)S(1)} %get-tuple-element.15), channel_id=1, source_target_pairs={{4,0},{8,4},{12,8},{5,1},{9,5},{13,9},{6,2},{10,6},{14,10},{7,3},{... | collective-permute-start | bytes 98312 | tf_op jit(solution)/shard_map/ppermute | solution.py:479
  15.6 3.6 %collective-permute-start = (f32[2,32,512]{2,1,0:T(8,128)S(1)}, f32[2,32,512]{2,1,0:T(8,128)S(1)}, u32[]{:S(2)}, u32[]{:S(2)}) collective-permute-start(f32[2,32,512]{2,1,0:T(8,128)S(1)} %get-tuple-element.12), channel_id=1, source_target_pairs={{0,1},{1,2},{2,3},{4,5},{5,6},{6,7},{8,9},{9,10},{10,11},{12,13},{... | collective-permute-start | bytes 393224 | tf_op jit(solution)/shard_map/ppermute | solution.py:476
  19.2 1.9 %collective-permute-start.1 = (f32[2,32,512]{2,1,0:T(8,128)S(1)}, f32[2,32,512]{2,1,0:T(8,128)S(1)}, u32[]{:S(2)}, u32[]{:S(2)}) collective-permute-start(f32[2,32,512]{2,1,0:T(8,128)S(1)} %get-tuple-element.13), channel_id=1, source_target_pairs={{1,0},{2,1},{3,2},{5,4},{6,5},{7,6},{9,8},{10,9},{11,10},{13,12},{... | collective-permute-start | bytes 393224 | tf_op jit(solution)/shard_map/ppermute | solution.py:477
  21.1 0.0 all-to-all-done.parcel_ref
  21.1 3.4 %force.1.force_ref = f32[17,5,200,128]{3,2,1,0:T(8,128)S(1)} custom-call(f32[16,24,128]{2,1,0:T(8,128)S(1)} %all-to-all-done.parcel_ref), custom_call_target="tpu_custom_call" | custom-call | flops 2013265920 | bytes 7864320 | tf_op jit(solution)/shard_map/force/pallas_call | solution.py:484
  24.6 0.0 collective-permute-done.2.left_ref
  24.6 0.0 collective-permute-done.3.right_ref
  24.6 0.0 collective-permute-done.top_ref
  24.6 0.9 %collective-permute-done.1.bottom_ref = f32[2,32,512]{2,1,0:T(8,128)S(1)} collective-permute-done((f32[2,32,512]{2,1,0:T(8,128)S(1)}, f32[2,32,512]{2,1,0:T(8,128)S(1)}, u32[]{:S(2)}, u32[]{:S(2)}) %collective-permute-start.1) | collective-permute-done | bytes 131104 | tf_op jit(solution)/shard_map/ppermute | solution.py:477
  25.5 15.7 %sweep.1 = (f32[128,512]{1,0:T(8,128)S(1)}, f32[4,8,128]{2,1,0:T(8,128)}) custom-call(f32[128,512]{1,0:T(8,128)S(1)} %get-tuple-element.20.keep_ref, f32[128,512]{1,0:T(8,128)S(1)} %get-tuple-element.19.gain_ref, f32[2,32,512]{2,1,0:T(8,128)S(1)} %collective-permute-done.top_ref, f32[2,32,512]{2,1,0:T(8,128)S(1)} %collective-permute-done.1.bottom_ref, ...), custom_call_target="tpu_custom_call" | custom-call | tf_op jit(solution)/shard_map/sweep/pallas_call | solution.py:503
  41.2 5.4 %all-to-all-start.1 = ((f32[4,8,128]{2,1,0:T(8,128)}), f32[4,8,128]{2,1,0:T(8,128)S(1)}, u32[]{:S(2)}, u32[]{:S(2)}) async-start(f32[4,8,128]{2,1,0:T(8,128)} %get-tuple-element.18), calls=%async_computation.1 | async-start | bytes 32768 | tf_op jit(solution)/shard_map/all_to_all | solution.py:471
  46.6 0.9 %smooth.1.own_ref = f32[128,512]{1,0:T(8,128)S(1)} custom-call(f32[128,512]{1,0:T(8,128)S(1)} %get-tuple-element.17.grad_ref), custom_call_target="tpu_custom_call" | custom-call | flops 402653184 | bytes 524288 | tf_op jit(solution)/shard_map/smooth/pallas_call | solution.py:516
  47.5 3.6 %all-to-all-done.1 = f32[4,8,128]{2,1,0:T(8,128)S(1)} async-done(((f32[4,8,128]{2,1,0:T(8,128)}), f32[4,8,128]{2,1,0:T(8,128)S(1)}, u32[]{:S(2)}, u32[]{:S(2)}) %all-to-all-start.1) | async-done | bytes 16416 | tf_op jit(solution)/shard_map/all_to_all | solution.py:471
  51.1 1.1 %finish.1 = f32[128,512]{1,0:T(8,128)} custom-call(f32[128,512]{1,0:T(8,128)S(1)} %smooth.1.own_ref, f32[32,128]{1,0:T(8,128)S(1)} %bitcast.6), custom_call_target="tpu_custom_call" | custom-call | tf_op jit(solution)/shard_map/finish/pallas_call | solution.py:523
Async XLA Ops:
  2.0 0.7 %copy-start = (f32[16,2,4]{0,2,1:T(4,128)S(1)}, f32[16,2,4]{0,2,1:T(4,128)}, u32[]{:S(2)}) copy-start(f32[16,2,4]{0,2,1:T(4,128)} %param.17) | copy-start | bytes 1540
  3.7 17.4 %all-to-all-start = ((f32[16,24,128]{2,1,0:T(8,128)}), f32[16,24,128]{2,1,0:T(8,128)S(1)}, u32[]{:S(2)}, u32[]{:S(2)}) async-start(f32[16,24,128]{2,1,0:T(8,128)} %get-tuple-element.16), calls=%async_computation | async-start | bytes 393216 | tf_op jit(solution)/shard_map/all_to_all | solution.py:471
  11.0 13.6 %collective-permute-start.2 = (f32[64,128]{1,0:T(8,128)S(1)}, f32[64,128]{1,0:T(8,128)S(1)}, u32[]{:S(2)}, u32[]{:S(2)}) collective-permute-start(f32[64,128]{1,0:T(8,128)S(1)} %get-tuple-element.14), channel_id=1, source_target_pairs={{0,4},{4,8},{8,12},{1,5},{5,9},{9,13},{2,6},{6,10},{10,14},{3,7},{... | collective-permute-start | bytes 98312 | tf_op jit(solution)/shard_map/ppermute | solution.py:478
  14.3 10.3 %collective-permute-start.3 = (f32[64,128]{1,0:T(8,128)S(1)}, f32[64,128]{1,0:T(8,128)S(1)}, u32[]{:S(2)}, u32[]{:S(2)}) collective-permute-start(f32[64,128]{1,0:T(8,128)S(1)} %get-tuple-element.15), channel_id=1, source_target_pairs={{4,0},{8,4},{12,8},{5,1},{9,5},{13,9},{6,2},{10,6},{14,10},{7,3},{... | collective-permute-start | bytes 98312 | tf_op jit(solution)/shard_map/ppermute | solution.py:479
  15.6 9.0 %collective-permute-start = (f32[2,32,512]{2,1,0:T(8,128)S(1)}, f32[2,32,512]{2,1,0:T(8,128)S(1)}, u32[]{:S(2)}, u32[]{:S(2)}) collective-permute-start(f32[2,32,512]{2,1,0:T(8,128)S(1)} %get-tuple-element.12), channel_id=1, source_target_pairs={{0,1},{1,2},{2,3},{4,5},{5,6},{6,7},{8,9},{9,10},{10,11},{12,13},{... | collective-permute-start | bytes 393224 | tf_op jit(solution)/shard_map/ppermute | solution.py:476
  19.2 6.3 %collective-permute-start.1 = (f32[2,32,512]{2,1,0:T(8,128)S(1)}, f32[2,32,512]{2,1,0:T(8,128)S(1)}, u32[]{:S(2)}, u32[]{:S(2)}) collective-permute-start(f32[2,32,512]{2,1,0:T(8,128)S(1)} %get-tuple-element.13), channel_id=1, source_target_pairs={{1,0},{2,1},{3,2},{5,4},{6,5},{7,6},{9,8},{10,9},{11,10},{13,12},{... | collective-permute-start | bytes 393224 | tf_op jit(solution)/shard_map/ppermute | solution.py:477
  41.2 9.9 %all-to-all-start.1 = ((f32[4,8,128]{2,1,0:T(8,128)}), f32[4,8,128]{2,1,0:T(8,128)S(1)}, u32[]{:S(2)}, u32[]{:S(2)}) async-start(f32[4,8,128]{2,1,0:T(8,128)} %get-tuple-element.18), calls=%async_computation.1 | async-start | bytes 32768 | tf_op jit(solution)/shard_map/all_to_all | solution.py:471

commit v8 on v7

--- a/solution.py
+++ b/solution.py
@@ -119,12 +119,15 @@
         )
 
 
-def shift_from(planes, shift, lanes):
-    count = len(planes)
-    rolled = [roll_lanes(plane, -shift) for plane in planes]
+def from_rolled(rolled, shift, lanes):
+    count = len(rolled)
     if shift > 0:
         return [jnp.where(lanes >= LANES - shift, rolled[(c + 1) % count], rolled[c]) for c in range(count)]
     return [jnp.where(lanes < -shift, rolled[(c - 1) % count], rolled[c]) for c in range(count)]
+
+
+def shift_from(planes, shift, lanes):
+    return from_rolled([roll_lanes(plane, -shift) for plane in planes], shift, lanes)
 
 
 def force(steps, halo, height, width, parcel_ref, force_ref, series_ref, rows_hot, cols_hot):
@@ -213,7 +216,7 @@
 def sweep(
     steps, keep_ref, gain_ref, top_ref, bottom_ref, left_ref, right_ref, parcel_ref, force_ref,
     grad_ref, sums_ref,
-    a, fx, fy, keep_x, gain_x, keep_y, gain_y, plain, pushes, arrived,
+    a, fx, fy, keep_x, gain_x, keep_y, gain_y, plain,
 ):
     height, width = keep_ref.shape
     halo = 2 * steps
@@ -279,20 +282,13 @@
         row_mask[row % blocks] = jnp.where(sublane == row // blocks, jnp.where(there, 1.0, 0.0), 1.0)
     every = range(planes)
 
-    def level_of(order):
-        return jnp.where(order < steps, steps - 1 - order, steps)
-
-    def fetch(order, odd):
-        return pltpu.make_async_copy(force_ref.at[level_of(order)], pushes.at[odd], arrived.at[odd])
-
-    fetch(1, 1).start()
-    fetch(2, 0).start()
     fx[...] = jnp.zeros_like(fx)
     fy[...] = jnp.zeros_like(fy)
     a[:, 0:rows_all, :] = force_ref[steps - 1, :, 0:rows_all, :]
 
-    def step(odd):
-        near, ahead, new_y, total, behind = {}, {}, {}, {}, {}
+    def step(index, carry):
+        level = jnp.where(index < steps - 1, steps - 2 - index, steps)
+        near, ahead, new_y, total, behind, push = {}, {}, {}, {}, {}, {}
 
         def rows(q):
             return slice(8 * q, 8 * q + 8)
@@ -300,7 +296,8 @@
         def first(q):
             near[q] = [a[c, rows(q % blocks), :] for c in every]
             if q < blocks:
-                ahead[q] = shift_from(near[q], 2, lanes8)
+                ahead[q] = [roll_lanes(value, -2) for value in near[q]]
+                push[q] = [force_ref[level, c, rows(q), :] for c in every]
             else:
                 near[q] = [up(value) for value in near[q]]
 
@@ -313,24 +310,25 @@
                 fy[c, rows(q), :] = new_y[q][c]
 
         def second_x(q):
+            far = from_rolled(ahead[q], 2, lanes8)
             new_x = [
-                keep_x[c, rows(q), :] * fx[c, rows(q), :] + gain_x[c, rows(q), :] * (ahead[q][c] - near[q][c])
-                for c in every
+                keep_x[c, rows(q), :] * fx[c, rows(q), :] + gain_x[c, rows(q), :] * (far[c] - near[q][c]) for c in every
             ]
+            behind[q] = [roll_lanes(value, 2) for value in new_x]
             before = new_y[q - 2] if q >= 2 else [down(fy[c, rows(q - 2 + blocks), :]) for c in every]
-            total[q] = [near[q][c] + (new_y[q][c] - before[c]) + new_x[c] for c in every]
-            behind[q] = shift_from(new_x, -2, lanes8)
+            total[q] = [(near[q][c] + push[q][c]) + (new_y[q][c] - before[c]) + new_x[c] for c in every]
             for c in every:
                 fx[c, rows(q), :] = new_x[c]
 
         def third(q):
+            far = from_rolled(behind[q], -2, lanes8)
             for c in every:
-                value = total[q][c] - behind[q][c]
+                value = total[q][c] - far[c]
                 if c == inner:
                     value = value * col_mask
                 if q in row_mask:
                     value = value * row_mask[q]
-                a[c, rows(q), :] = value + pushes[odd, c, rows(q), :]
+                a[c, rows(q), :] = value
 
         for q in range(4):
             first(q)
@@ -345,23 +343,13 @@
         for q in range(2):
             first(q)
             new_y[q] = [fy[c, rows(q), :] for c in every]
+        for q in range(2):
             second_x(q)
             third(q - 1 if q else blocks - 1)
         third(1)
-
-    def pair(index, carry):
-        for odd in (1, 0):
-            order = 2 * index + 2 - odd
-            fetch(order, odd).wait()
-            step(odd)
-
-            @pl.when(index < steps // 2 - 1)
-            def _():
-                fetch(order + 2, odd).start()
-
         return carry
 
-    lax.fori_loop(0, steps // 2, pair, 0)
+    lax.fori_loop(0, steps, step, 0)
 
     for r in range(0, height, 8):
         s, q = divmod(halo + r, blocks)
@@ -505,9 +493,7 @@
         out_shape=(f32(height, width), f32(lons, 8, height)),
         in_specs=vmem(8),
         out_specs=tuple(vmem(2)),
-        scratch_shapes=[plane] * 8 + [
-            pltpu.VMEM((2, planes, spaced(rows_all), LANES), jnp.float32), pltpu.SemaphoreType.DMA((2,)),
-        ],
+        scratch_shapes=[plane] * 8,
         compiler_params=params,
         name="sweep",
     )(keep, gain, top, bottom, left, right, parcel, pushes)

time: 52.7 us -> 47.5 us (0.901)
  Pallas kernels: 22.1 us -> 16.9 us
    pallas_call x1, Pallas kernels: 15.7 us -> 10.5 us  [local(): pl.pallas_call(functools.partial(sweep, steps), out_shape=(f32(height, wi...]
  transfers between devices with their start and end apart: 6 -> 6, of which waited for: 2 -> 2; matrix products, arithmetic and copies ran while one was open for 0% -> 0% of each run, Pallas kernels for 8% -> 9%
where the time goes in v8:
time: 47.5 us; the launch traced here: 47 us
  starting transfers between devices  22.8 us (48%)
  Pallas kernels  16.9 us (36%)
  waiting for transfers between devices  4.46 us (9%)
  other arithmetic  2.03 us (4%)
  local copies, waits for them, and re-layouts  0.68 us (1%)
    all_to_all x2, starting transfers between devices, exchange(): return lax.all_to_all(array, axes, split_axis=0, concat_axis=0, tiled=True)  12.7 us
    pallas_call x1, Pallas kernels, local(): pl.pallas_call(functools.partial(sweep, steps), out_shape=(f32(height, wi...  10.5 us
    ppermute x1, starting transfers between devices, local(): top = lax.ppermute(south, ROW_AXES, down)  3.62 us
    all_to_all x2, waiting for transfers between devices, exchange(): return lax.all_to_all(array, axes, split_axis=0, concat_axis=0, tiled=True)  3.56 us
    pallas_call x1, Pallas kernels, local(): pl.pallas_call(functools.partial(force, steps, halo, height, width), out_...  3.41 us
    ppermute x1, starting transfers between devices, local(): left = lax.ppermute(east, 'lon', [(i, i + 1) for i in range(lons - 1)])  3.28 us
    ppermute x1, starting transfers between devices, local(): bottom = lax.ppermute(north, ROW_AXES, up)  1.92 us
    ppermute x1, starting transfers between devices, local(): right = lax.ppermute(west, 'lon', [(i + 1, i) for i in range(lons - 1)])  1.29 us
  transfers between devices with their start and end apart: 6, of which 2 were waited for; matrix products, arithmetic and copies ran while one was open for 0% of the time, Pallas kernels for 9%

profile of v8, /device:TPU:1, one launch (start us, length us, event | category | flops | bytes accessed | tf_op | source)
XLA Modules:
  0.0 47.0 jit_solution(10769679945321779813)
XLA Ops:
  0.0 0.7 %pad_add_fusion.gauge_ref = s32[3,4,16]{2,1,0:T(4,128)S(1)} fusion(s32[1,1,8]{2,1,0:T(1,128)} %bitcast.9, s32[1,1,16]{2,1,0:T(1,128)} %bitcast.10, s32[1,1,16]{2,1,0:T(1,128)} %bitcast.11, s32[2,4,16]{2,1,0:T(4,128)} %bitcast.8), kind=kLoop, calls=%fused_computation.2 | loop fusion | flops 576 | bytes 1440 | tf_op jit(solution)/shard_map/add | solution.py:439
  0.7 1.3 %multiply_multiply_fusion = (f32[128,512]{1,0:T(8,128)S(1)}, f32[128,512]{1,0:T(8,128)S(1)}) fusion(f32[128,512]{1,0:T(8,128)} %param.9, f32[128,512]{1,0:T(8,128)} %param.10, s32[128,512]{1,0:T(8,128)} %param.12, f32[128,512]{1,0:T(8,128)} %param.11), kind=kLoop, calls=%fused_computation | loop fusion | flops 458752 | bytes 1572864 | tf_op jit(solution)/shard_map/mul | solution.py:428
  2.0 0.0 copy-start
  2.0 0.7 %copy-done = f32[16,2,4]{0,2,1:T(4,128)S(1)} copy-done((f32[16,2,4]{0,2,1:T(4,128)S(1)}, f32[16,2,4]{0,2,1:T(4,128)}, u32[]{:S(2)}) %copy-start) | copy-done | bytes 536
  2.7 1.0 %prepare.1 = (f32[16,24,128]{2,1,0:T(8,128)}, f32[2,32,512]{2,1,0:T(8,128)S(1)}, f32[2,32,512]{2,1,0:T(8,128)S(1)}, f32[64,128]{1,0:T(8,128)S(1)}, f32[64,128]{1,0:T(8,128)S(1)}) custom-call(f32[128,512]{1,0:T(8,128)S(1)} %get-tuple-element.20.keep_ref, f32[128,512]{1,0:T(8,128)S(1)} %get-tuple-element.19.gain_ref, s32[3,4,16]{2,1,0:T(4,128)S(1)} %pad_add_fusion.gauge_ref, ...), custom_call_target="tpu_custom_call" | custom-call | tf_op jit(solution)/shard_map/prepare/pallas_call | solution.py:445
  3.7 7.3 %all-to-all-start = ((f32[16,24,128]{2,1,0:T(8,128)}), f32[16,24,128]{2,1,0:T(8,128)S(1)}, u32[]{:S(2)}, u32[]{:S(2)}) async-start(f32[16,24,128]{2,1,0:T(8,128)} %get-tuple-element.16), calls=%async_computation | async-start | bytes 393216 | tf_op jit(solution)/shard_map/all_to_all | solution.py:459
  11.0 3.3 %collective-permute-start.2 = (f32[64,128]{1,0:T(8,128)S(1)}, f32[64,128]{1,0:T(8,128)S(1)}, u32[]{:S(2)}, u32[]{:S(2)}) collective-permute-start(f32[64,128]{1,0:T(8,128)S(1)} %get-tuple-element.14), channel_id=1, source_target_pairs={{0,4},{4,8},{8,12},{1,5},{5,9},{9,13},{2,6},{6,10},{10,14},{3,7},{... | collective-permute-start | bytes 98312 | tf_op jit(solution)/shard_map/ppermute | solution.py:466
  14.3 1.3 %collective-permute-start.3 = (f32[64,128]{1,0:T(8,128)S(1)}, f32[64,128]{1,0:T(8,128)S(1)}, u32[]{:S(2)}, u32[]{:S(2)}) collective-permute-start(f32[64,128]{1,0:T(8,128)S(1)} %get-tuple-element.15), channel_id=1, source_target_pairs={{4,0},{8,4},{12,8},{5,1},{9,5},{13,9},{6,2},{10,6},{14,10},{7,3},{... | collective-permute-start | bytes 98312 | tf_op jit(solution)/shard_map/ppermute | solution.py:467
  15.6 3.6 %collective-permute-start = (f32[2,32,512]{2,1,0:T(8,128)S(1)}, f32[2,32,512]{2,1,0:T(8,128)S(1)}, u32[]{:S(2)}, u32[]{:S(2)}) collective-permute-start(f32[2,32,512]{2,1,0:T(8,128)S(1)} %get-tuple-element.12), channel_id=1, source_target_pairs={{0,1},{1,2},{2,3},{4,5},{5,6},{6,7},{8,9},{9,10},{10,11},{12,13},{... | collective-permute-start | bytes 393224 | tf_op jit(solution)/shard_map/ppermute | solution.py:464
  19.2 1.9 %collective-permute-start.1 = (f32[2,32,512]{2,1,0:T(8,128)S(1)}, f32[2,32,512]{2,1,0:T(8,128)S(1)}, u32[]{:S(2)}, u32[]{:S(2)}) collective-permute-start(f32[2,32,512]{2,1,0:T(8,128)S(1)} %get-tuple-element.13), channel_id=1, source_target_pairs={{1,0},{2,1},{3,2},{5,4},{6,5},{7,6},{9,8},{10,9},{11,10},{13,12},{... | collective-permute-start | bytes 393224 | tf_op jit(solution)/shard_map/ppermute | solution.py:465
  21.1 0.0 all-to-all-done.parcel_ref
  21.1 3.4 %force.1.force_ref = f32[17,5,200,128]{3,2,1,0:T(8,128)S(1)} custom-call(f32[16,24,128]{2,1,0:T(8,128)S(1)} %all-to-all-done.parcel_ref), custom_call_target="tpu_custom_call" | custom-call | flops 2013265920 | bytes 7864320 | tf_op jit(solution)/shard_map/force/pallas_call | solution.py:472
  24.6 0.0 collective-permute-done.2.left_ref
  24.6 0.0 collective-permute-done.3.right_ref
  24.6 0.0 collective-permute-done.top_ref
  24.6 0.9 %collective-permute-done.1.bottom_ref = f32[2,32,512]{2,1,0:T(8,128)S(1)} collective-permute-done((f32[2,32,512]{2,1,0:T(8,128)S(1)}, f32[2,32,512]{2,1,0:T(8,128)S(1)}, u32[]{:S(2)}, u32[]{:S(2)}) %collective-permute-start.1) | collective-permute-done | bytes 131104 | tf_op jit(solution)/shard_map/ppermute | solution.py:465
  25.5 10.5 %sweep.1 = (f32[128,512]{1,0:T(8,128)S(1)}, f32[4,8,128]{2,1,0:T(8,128)}) custom-call(f32[128,512]{1,0:T(8,128)S(1)} %get-tuple-element.20.keep_ref, f32[128,512]{1,0:T(8,128)S(1)} %get-tuple-element.19.gain_ref, f32[2,32,512]{2,1,0:T(8,128)S(1)} %collective-permute-done.top_ref, f32[2,32,512]{2,1,0:T(8,128)S(1)} %collective-permute-done.1.bottom_ref, ...), custom_call_target="tpu_custom_call" | custom-call | tf_op jit(solution)/shard_map/sweep/pallas_call | solution.py:491
  36.0 5.4 %all-to-all-start.1 = ((f32[4,8,128]{2,1,0:T(8,128)}), f32[4,8,128]{2,1,0:T(8,128)S(1)}, u32[]{:S(2)}, u32[]{:S(2)}) async-start(f32[4,8,128]{2,1,0:T(8,128)} %get-tuple-element.18), calls=%async_computation.1 | async-start | bytes 32768 | tf_op jit(solution)/shard_map/all_to_all | solution.py:459
  41.4 0.9 %smooth.1.own_ref = f32[128,512]{1,0:T(8,128)S(1)} custom-call(f32[128,512]{1,0:T(8,128)S(1)} %get-tuple-element.17.grad_ref), custom_call_target="tpu_custom_call" | custom-call | flops 402653184 | bytes 524288 | tf_op jit(solution)/shard_map/smooth/pallas_call | solution.py:502
  42.3 3.6 %all-to-all-done.1 = f32[4,8,128]{2,1,0:T(8,128)S(1)} async-done(((f32[4,8,128]{2,1,0:T(8,128)}), f32[4,8,128]{2,1,0:T(8,128)S(1)}, u32[]{:S(2)}, u32[]{:S(2)}) %all-to-all-start.1) | async-done | bytes 16416 | tf_op jit(solution)/shard_map/all_to_all | solution.py:459
  45.8 1.1 %finish.1 = f32[128,512]{1,0:T(8,128)} custom-call(f32[128,512]{1,0:T(8,128)S(1)} %smooth.1.own_ref, f32[32,128]{1,0:T(8,128)S(1)} %bitcast.6), custom_call_target="tpu_custom_call" | custom-call | tf_op jit(solution)/shard_map/finish/pallas_call | solution.py:509
Async XLA Ops:
  2.0 0.7 %copy-start = (f32[16,2,4]{0,2,1:T(4,128)S(1)}, f32[16,2,4]{0,2,1:T(4,128)}, u32[]{:S(2)}) copy-start(f32[16,2,4]{0,2,1:T(4,128)} %param.17) | copy-start | bytes 1540
  3.7 17.4 %all-to-all-start = ((f32[16,24,128]{2,1,0:T(8,128)}), f32[16,24,128]{2,1,0:T(8,128)S(1)}, u32[]{:S(2)}, u32[]{:S(2)}) async-start(f32[16,24,128]{2,1,0:T(8,128)} %get-tuple-element.16), calls=%async_computation | async-start | bytes 393216 | tf_op jit(solution)/shard_map/all_to_all | solution.py:459
  11.0 13.6 %collective-permute-start.2 = (f32[64,128]{1,0:T(8,128)S(1)}, f32[64,128]{1,0:T(8,128)S(1)}, u32[]{:S(2)}, u32[]{:S(2)}) collective-permute-start(f32[64,128]{1,0:T(8,128)S(1)} %get-tuple-element.14), channel_id=1, source_target_pairs={{0,4},{4,8},{8,12},{1,5},{5,9},{9,13},{2,6},{6,10},{10,14},{3,7},{... | collective-permute-start | bytes 98312 | tf_op jit(solution)/shard_map/ppermute | solution.py:466
  14.3 10.3 %collective-permute-start.3 = (f32[64,128]{1,0:T(8,128)S(1)}, f32[64,128]{1,0:T(8,128)S(1)}, u32[]{:S(2)}, u32[]{:S(2)}) collective-permute-start(f32[64,128]{1,0:T(8,128)S(1)} %get-tuple-element.15), channel_id=1, source_target_pairs={{4,0},{8,4},{12,8},{5,1},{9,5},{13,9},{6,2},{10,6},{14,10},{7,3},{... | collective-permute-start | bytes 98312 | tf_op jit(solution)/shard_map/ppermute | solution.py:467
  15.6 9.0 %collective-permute-start = (f32[2,32,512]{2,1,0:T(8,128)S(1)}, f32[2,32,512]{2,1,0:T(8,128)S(1)}, u32[]{:S(2)}, u32[]{:S(2)}) collective-permute-start(f32[2,32,512]{2,1,0:T(8,128)S(1)} %get-tuple-element.12), channel_id=1, source_target_pairs={{0,1},{1,2},{2,3},{4,5},{5,6},{6,7},{8,9},{9,10},{10,11},{12,13},{... | collective-permute-start | bytes 393224 | tf_op jit(solution)/shard_map/ppermute | solution.py:464
  19.2 6.3 %collective-permute-start.1 = (f32[2,32,512]{2,1,0:T(8,128)S(1)}, f32[2,32,512]{2,1,0:T(8,128)S(1)}, u32[]{:S(2)}, u32[]{:S(2)}) collective-permute-start(f32[2,32,512]{2,1,0:T(8,128)S(1)} %get-tuple-element.13), channel_id=1, source_target_pairs={{1,0},{2,1},{3,2},{5,4},{6,5},{7,6},{9,8},{10,9},{11,10},{13,12},{... | collective-permute-start | bytes 393224 | tf_op jit(solution)/shard_map/ppermute | solution.py:465
  36.0 9.9 %all-to-all-start.1 = ((f32[4,8,128]{2,1,0:T(8,128)}), f32[4,8,128]{2,1,0:T(8,128)S(1)}, u32[]{:S(2)}, u32[]{:S(2)}) async-start(f32[4,8,128]{2,1,0:T(8,128)} %get-tuple-element.18), calls=%async_computation.1 | async-start | bytes 32768 | tf_op jit(solution)/shard_map/all_to_all | solution.py:459

commit v9 on v8

--- a/solution.py
+++ b/solution.py
@@ -53,7 +53,7 @@
 
 def prepare(
     halo, blocks, samples, coast_count, keep_ref, gain_ref, gauge_ref, resid_ref,
-    parcel_ref, south_ref, north_ref, east_ref, west_ref, block_ref,
+    parcel_ref, south_ref, north_ref, strips_ref, block_ref,
 ):
     height, width = keep_ref.shape
     my_row, my_lon, row_tiles, lons = my_place()
@@ -113,10 +113,14 @@
 
     south_ref[0], south_ref[1] = keep[height - halo :], gain[height - halo :]
     north_ref[0], north_ref[1] = keep[:halo], gain[:halo]
-    for goal, cols, start in ((east_ref, last, end), (west_ref, first, 0)):
-        goal[...] = pack_lanes(
-            [(keep[:half, cols], start), (gain[:half, cols], start), (keep[half:, cols], start), (gain[half:, cols], start)]
-        )
+    for d_lon, cols, start in ((1, last, end), (-1, first, 0)):
+        there = (my_lon + d_lon >= 0) & (my_lon + d_lon < lons)
+
+        @pl.when(there)
+        def _():
+            strips_ref[my_lon + d_lon] = pack_lanes(
+                [(keep[:half, cols], start), (gain[:half, cols], start), (keep[half:, cols], start), (gain[half:, cols], start)]
+            )
 
 
 def from_rolled(rolled, shift, lanes):
@@ -214,7 +218,7 @@
 
 
 def sweep(
-    steps, keep_ref, gain_ref, top_ref, bottom_ref, left_ref, right_ref, parcel_ref, force_ref,
+    steps, keep_ref, gain_ref, top_ref, bottom_ref, strips_ref, parcel_ref, force_ref,
     grad_ref, sums_ref,
     a, fx, fy, keep_x, gain_x, keep_y, gain_y, plain,
 ):
@@ -252,8 +256,8 @@
         segment = lane_iota(half) // SEG
         for part in range(2):
             piece = 2 * part + kind
-            by_left = roll_lanes(left_ref[...], end - piece * SEG)
-            by_right = roll_lanes(right_ref[...], -piece * SEG)
+            by_left = known(has_left, roll_lanes(strips_ref[left], end - piece * SEG))
+            by_right = known(has_right, roll_lanes(strips_ref[right], -piece * SEG))
             both = jnp.where(segment == 0, by_right, jnp.where(segment == LANES // SEG - 1, by_left, 0.0))
             plain[inner, halo + part * half : halo + (part + 1) * half, :] = both
         segment = lane_iota(8) // SEG
@@ -288,7 +292,7 @@
 
     def step(index, carry):
         level = jnp.where(index < steps - 1, steps - 2 - index, steps)
-        near, ahead, new_y, total, behind, push = {}, {}, {}, {}, {}, {}
+        near, ahead, new_y, total, behind = {}, {}, {}, {}, {}
 
         def rows(q):
             return slice(8 * q, 8 * q + 8)
@@ -297,7 +301,6 @@
             near[q] = [a[c, rows(q % blocks), :] for c in every]
             if q < blocks:
                 ahead[q] = [roll_lanes(value, -2) for value in near[q]]
-                push[q] = [force_ref[level, c, rows(q), :] for c in every]
             else:
                 near[q] = [up(value) for value in near[q]]
 
@@ -316,7 +319,8 @@
             ]
             behind[q] = [roll_lanes(value, 2) for value in new_x]
             before = new_y[q - 2] if q >= 2 else [down(fy[c, rows(q - 2 + blocks), :]) for c in every]
-            total[q] = [(near[q][c] + push[q][c]) + (new_y[q][c] - before[c]) + new_x[c] for c in every]
+            push = [force_ref[level, c, rows(q), :] for c in every]
+            total[q] = [(near[q][c] + push[c]) + (new_y[q][c] - before[c]) + new_x[c] for c in every]
             for c in every:
                 fx[c, rows(q), :] = new_x[c]
 
@@ -330,23 +334,35 @@
                     value = value * row_mask[q]
                 a[c, rows(q), :] = value
 
-        for q in range(4):
-            first(q)
-        second_y(0)
-        second_y(1)
-        for q in range(2, blocks):
-            first(q + 2)
-            second_y(q)
-            second_x(q)
-            if q > 2:
-                third(q - 1)
-        for q in range(2):
-            first(q)
-            new_y[q] = [fy[c, rows(q), :] for c in every]
-        for q in range(2):
-            second_x(q)
-            third(q - 1 if q else blocks - 1)
-        third(1)
+        tasks = []
+        for odd in range(2):
+            tasks += [(odd, True, False)] + [(q, True, True) for q in range(odd + 2, blocks, 2)] + [(odd, False, True)]
+
+        def begin(task):
+            q, with_y, with_x = task
+            if with_y and not with_x:
+                first(q)
+                first(q + 2)
+            elif with_y:
+                first(q + 2)
+            else:
+                first(q)
+                new_y[q] = [fy[c, rows(q), :] for c in every]
+
+        waiting = None
+        begin(tasks[0])
+        for task, following in zip(tasks, tasks[1:] + [None]):
+            q, with_y, with_x = task
+            if following is not None:
+                begin(following)
+            if with_y:
+                second_y(q)
+            if with_x:
+                second_x(q)
+            if waiting is not None:
+                third(waiting)
+            waiting = q if with_x else None
+        third(waiting)
         return carry
 
     lax.fori_loop(0, steps, step, 0)
@@ -442,14 +458,14 @@
         + put(coastal_tiles.reshape(1, 1, coast_count), blocks, 2)
     )
     residuals = jnp.transpose(gauge_resid, (1, 2, 0))
-    parcel, south, north, east, west = pl.pallas_call(
+    parcel, south, north, strips = pl.pallas_call(
         functools.partial(prepare, halo, blocks, samples, coast_count),
         out_shape=(
             f32(tiles, parcel_rows, LANES), f32(2, halo, width), f32(2, halo, width),
-            f32(height // 2, LANES), f32(height // 2, LANES),
+            f32(lons, height // 2, LANES),
         ),
         in_specs=vmem(4),
-        out_specs=tuple(vmem(5)),
+        out_specs=tuple(vmem(4)),
         scratch_shapes=[pltpu.VMEM((24, LANES), jnp.float32)],
         compiler_params=params,
         name="prepare",
@@ -463,8 +479,7 @@
     up = [(i + 1, i) for i in range(row_tiles - 1)]
     top = lax.ppermute(south, ROW_AXES, down)
     bottom = lax.ppermute(north, ROW_AXES, up)
-    left = lax.ppermute(east, "lon", [(i, i + 1) for i in range(lons - 1)])
-    right = lax.ppermute(west, "lon", [(i + 1, i) for i in range(lons - 1)])
+    strips = exchange(strips, "lon")
 
     planes = width // LANES + 1
     rows_all = height + 2 * halo
@@ -491,12 +506,12 @@
     grad, sums = pl.pallas_call(
         functools.partial(sweep, steps),
         out_shape=(f32(height, width), f32(lons, 8, height)),
-        in_specs=vmem(8),
+        in_specs=vmem(7),
         out_specs=tuple(vmem(2)),
         scratch_shapes=[plane] * 8,
         compiler_params=params,
         name="sweep",
-    )(keep, gain, top, bottom, left, right, parcel, pushes)
+    )(keep, gain, top, bottom, strips, parcel, pushes)
 
     sums = exchange(sums, "lon")
     own = pl.pallas_call(

time: 47.5 us -> 59.2 us (1.25)
  the two profiles are of different devices: /device:TPU:1 before, /device:TPU:0 now
where the time goes in v9:
time: 59.2 us; the launch traced here: 58.7 us
  Pallas kernels  17.2 us (29%)
  blocking collectives  16.2 us (27%)
  starting transfers between devices  11 us (19%)
  local copies, waits for them, and re-layouts  7.51 us (13%)
  waiting for transfers between devices  4.73 us (8%)
  other arithmetic  2.03 us (3%)
    all_to_all x1, blocking collectives, exchange(): return lax.all_to_all(array, axes, split_axis=0, concat_axis=0, tiled=True)  16.2 us
    pallas_call x1, Pallas kernels, local(): pl.pallas_call(functools.partial(sweep, steps), out_shape=(f32(height, wi...  10.8 us
    all_to_all x2, starting transfers between devices, exchange(): return lax.all_to_all(array, axes, split_axis=0, concat_axis=0, tiled=True)  8.08 us
    unnamed x6, local copies, waits for them, and re-layouts  7.51 us
    all_to_all x2, waiting for transfers between devices, exchange(): return lax.all_to_all(array, axes, split_axis=0, concat_axis=0, tiled=True)  4.72 us
    pallas_call x1, Pallas kernels, local(): pl.pallas_call(functools.partial(force, steps, halo, height, width), out_...  3.41 us
    ppermute x1, starting transfers between devices, local(): top = lax.ppermute(south, ROW_AXES, down)  1.65 us
    ppermute x1, starting transfers between devices, local(): bottom = lax.ppermute(north, ROW_AXES, up)  1.29 us
  transfers between devices with their start and end apart: 4, of which 1 were waited for; matrix products, arithmetic and copies ran while one was open for 0% of the time, Pallas kernels for 7%

profile of v9, /device:TPU:0, one launch (start us, length us, event | category | flops | bytes accessed | tf_op | source)
XLA Modules:
  0.0 58.7 jit_solution(6798071342356963427)
XLA Ops:
  0.0 0.7 %pad_add_fusion.gauge_ref = s32[3,4,16]{2,1,0:T(4,128)S(1)} fusion(s32[1,1,8]{2,1,0:T(1,128)} %bitcast.9, s32[1,1,16]{2,1,0:T(1,128)} %bitcast.10, s32[1,1,16]{2,1,0:T(1,128)} %bitcast.11, s32[2,4,16]{2,1,0:T(4,128)} %bitcast.8), kind=kLoop, calls=%fused_computation.2 | loop fusion | flops 576 | bytes 1440 | tf_op jit(solution)/shard_map/add | solution.py:455
  0.7 1.3 %multiply_multiply_fusion = (f32[128,512]{1,0:T(8,128)S(1)}, f32[128,512]{1,0:T(8,128)S(1)}) fusion(f32[128,512]{1,0:T(8,128)} %param.9, f32[128,512]{1,0:T(8,128)} %param.10, s32[128,512]{1,0:T(8,128)} %param.12, f32[128,512]{1,0:T(8,128)} %param.11), kind=kLoop, calls=%fused_computation | loop fusion | flops 458752 | bytes 1572864 | tf_op jit(solution)/shard_map/mul | solution.py:444
  2.0 0.0 copy-start.2
  2.0 0.7 %copy-done.2 = f32[16,2,4]{0,2,1:T(4,128)S(1)} copy-done((f32[16,2,4]{0,2,1:T(4,128)S(1)}, f32[16,2,4]{0,2,1:T(4,128)}, u32[]{:S(2)}) %copy-start.2) | copy-done | bytes 536
  2.7 1.0 %prepare.1 = (f32[16,24,128]{2,1,0:T(8,128)S(1)}, f32[2,32,512]{2,1,0:T(8,128)S(1)}, f32[2,32,512]{2,1,0:T(8,128)S(1)}, f32[4,64,128]{2,1,0:T(8,128)}) custom-call(f32[128,512]{1,0:T(8,128)S(1)} %get-tuple-element.18.keep_ref, f32[128,512]{1,0:T(8,128)S(1)} %get-tuple-element.17.gain_ref, s32[3,4,16]{2,1,0:T(4,128)S(1)} %pad_add_fusion.gauge_ref, ...), custom_call_target="tpu_custom_call" | custom-call | tf_op jit(solution)/shard_map/prepare/pallas_call | solution.py:461
  3.7 16.2 %all_to_all.15.parcel_ref = f32[16,24,128]{2,1,0:T(8,128)S(1)} all-to-all(f32[16,24,128]{2,1,0:T(8,128)S(1)} %get-tuple-element.14), channel_id=1, replica_groups=mesh['scen'=2,'lon'=4,'lat'=2,'gau'=2] {'lon','lat','gau'}, dimensions={0} | all-to-all | bytes 393216 | tf_op jit(solution)/shard_map/all_to_all | solution.py:475
  19.9 3.3 %all-to-all-start = ((f32[4,64,128]{2,1,0:T(8,128)}), f32[4,64,128]{2,1,0:T(8,128)S(1)}, u32[]{:S(2)}, u32[]{:S(2)}) async-start(f32[4,64,128]{2,1,0:T(8,128)} %get-tuple-element.13), calls=%async_computation | async-start | bytes 262144 | tf_op jit(solution)/shard_map/all_to_all | solution.py:475
  23.2 1.6 %collective-permute-start = (f32[2,32,512]{2,1,0:T(8,128)S(1)}, f32[2,32,512]{2,1,0:T(8,128)S(1)}, u32[]{:S(2)}, u32[]{:S(2)}) collective-permute-start(f32[2,32,512]{2,1,0:T(8,128)S(1)} %get-tuple-element.11), channel_id=1, source_target_pairs={{0,1},{1,2},{2,3},{4,5},{5,6},{6,7},{8,9},{9,10},{10,11},{12,13},{... | collective-permute-start | bytes 393224 | tf_op jit(solution)/shard_map/ppermute | solution.py:480
  24.9 1.3 %collective-permute-start.1 = (f32[2,32,512]{2,1,0:T(8,128)S(1)}, f32[2,32,512]{2,1,0:T(8,128)S(1)}, u32[]{:S(2)}, u32[]{:S(2)}) collective-permute-start(f32[2,32,512]{2,1,0:T(8,128)S(1)} %get-tuple-element.12), channel_id=1, source_target_pairs={{1,0},{2,1},{3,2},{5,4},{6,5},{7,6},{9,8},{10,9},{11,10},{13,12},{... | collective-permute-start | bytes 393224 | tf_op jit(solution)/shard_map/ppermute | solution.py:481
  26.2 3.4 %force.1.force_ref = f32[17,5,200,128]{3,2,1,0:T(8,128)S(1)} custom-call(f32[16,24,128]{2,1,0:T(8,128)S(1)} %all_to_all.15.parcel_ref), custom_call_target="tpu_custom_call" | custom-call | flops 2013265920 | bytes 7864320 | tf_op jit(solution)/shard_map/force/pallas_call | solution.py:487
  29.6 0.0 copy-start
  29.6 3.4 %copy-done = f32[17,5,200,128]{3,2,1,0:T(8,128)} copy-done((f32[17,5,200,128]{3,2,1,0:T(8,128)}, f32[17,5,200,128]{3,2,1,0:T(8,128)S(1)}, u32[]{:S(2)}) %copy-start) | copy-done | bytes 8704024
  32.9 0.0 collective-permute-done.top_ref
  32.9 0.0 collective-permute-done.1.bottom_ref
  33.0 0.0 all-to-all-done.strips_ref
  33.0 0.0 copy-start.1
  33.0 3.5 %copy-done.1 = f32[17,5,200,128]{3,2,1,0:T(8,128)S(1)} copy-done((f32[17,5,200,128]{3,2,1,0:T(8,128)S(1)}, f32[17,5,200,128]{3,2,1,0:T(8,128)}, u32[]{:S(2)}) %copy-start.1) | copy-done | bytes 8704024
  36.4 10.8 %sweep.1 = (f32[128,512]{1,0:T(8,128)S(1)}, f32[4,8,128]{2,1,0:T(8,128)}) custom-call(f32[128,512]{1,0:T(8,128)S(1)} %get-tuple-element.18.keep_ref, f32[128,512]{1,0:T(8,128)S(1)} %get-tuple-element.17.gain_ref, f32[2,32,512]{2,1,0:T(8,128)S(1)} %collective-permute-done.top_ref, f32[2,32,512]{2,1,0:T(8,128)S(1)} %collective-permute-done.1.bottom_ref, ...), custom_call_target="tpu_custom_call" | custom-call | tf_op jit(solution)/shard_map/sweep/pallas_call | solution.py:506
  47.2 4.8 %all-to-all-start.2 = ((f32[4,8,128]{2,1,0:T(8,128)}), f32[4,8,128]{2,1,0:T(8,128)S(1)}, u32[]{:S(2)}, u32[]{:S(2)}) async-start(f32[4,8,128]{2,1,0:T(8,128)} %get-tuple-element.16), calls=%async_computation.2 | async-start | bytes 32768 | tf_op jit(solution)/shard_map/all_to_all | solution.py:475
  52.0 0.9 %smooth.1.own_ref = f32[128,512]{1,0:T(8,128)S(1)} custom-call(f32[128,512]{1,0:T(8,128)S(1)} %get-tuple-element.15.grad_ref), custom_call_target="tpu_custom_call" | custom-call | flops 402653184 | bytes 524288 | tf_op jit(solution)/shard_map/smooth/pallas_call | solution.py:517
  52.9 4.7 %all-to-all-done.2 = f32[4,8,128]{2,1,0:T(8,128)S(1)} async-done(((f32[4,8,128]{2,1,0:T(8,128)}), f32[4,8,128]{2,1,0:T(8,128)S(1)}, u32[]{:S(2)}, u32[]{:S(2)}) %all-to-all-start.2) | async-done | bytes 16416 | tf_op jit(solution)/shard_map/all_to_all | solution.py:475
  57.6 1.1 %finish.1 = f32[128,512]{1,0:T(8,128)} custom-call(f32[128,512]{1,0:T(8,128)S(1)} %smooth.1.own_ref, f32[32,128]{1,0:T(8,128)S(1)} %bitcast.6), custom_call_target="tpu_custom_call" | custom-call | tf_op jit(solution)/shard_map/finish/pallas_call | solution.py:524
Async XLA Ops:
  2.0 0.7 %copy-start.2 = (f32[16,2,4]{0,2,1:T(4,128)S(1)}, f32[16,2,4]{0,2,1:T(4,128)}, u32[]{:S(2)}) copy-start(f32[16,2,4]{0,2,1:T(4,128)} %param.17) | copy-start | bytes 1540
  19.9 13.1 %all-to-all-start = ((f32[4,64,128]{2,1,0:T(8,128)}), f32[4,64,128]{2,1,0:T(8,128)S(1)}, u32[]{:S(2)}, u32[]{:S(2)}) async-start(f32[4,64,128]{2,1,0:T(8,128)} %get-tuple-element.13), calls=%async_computation | async-start | bytes 262144 | tf_op jit(solution)/shard_map/all_to_all | solution.py:475
  23.2 9.7 %collective-permute-start = (f32[2,32,512]{2,1,0:T(8,128)S(1)}, f32[2,32,512]{2,1,0:T(8,128)S(1)}, u32[]{:S(2)}, u32[]{:S(2)}) collective-permute-start(f32[2,32,512]{2,1,0:T(8,128)S(1)} %get-tuple-element.11), channel_id=1, source_target_pairs={{0,1},{1,2},{2,3},{4,5},{5,6},{6,7},{8,9},{9,10},{10,11},{12,13},{... | collective-permute-start | bytes 393224 | tf_op jit(solution)/shard_map/ppermute | solution.py:480
  24.9 8.1 %collective-permute-start.1 = (f32[2,32,512]{2,1,0:T(8,128)S(1)}, f32[2,32,512]{2,1,0:T(8,128)S(1)}, u32[]{:S(2)}, u32[]{:S(2)}) collective-permute-start(f32[2,32,512]{2,1,0:T(8,128)S(1)} %get-tuple-element.12), channel_id=1, source_target_pairs={{1,0},{2,1},{3,2},{5,4},{6,5},{7,6},{9,8},{10,9},{11,10},{13,12},{... | collective-permute-start | bytes 393224 | tf_op jit(solution)/shard_map/ppermute | solution.py:481
  29.6 3.4 %copy-start = (f32[17,5,200,128]{3,2,1,0:T(8,128)}, f32[17,5,200,128]{3,2,1,0:T(8,128)S(1)}, u32[]{:S(2)}) copy-start(f32[17,5,200,128]{3,2,1,0:T(8,128)S(1)} %force.1.force_ref) | copy-start | bytes 26112004
  33.0 3.5 %copy-start.1 = (f32[17,5,200,128]{3,2,1,0:T(8,128)S(1)}, f32[17,5,200,128]{3,2,1,0:T(8,128)}, u32[]{:S(2)}) copy-start(f32[17,5,200,128]{3,2,1,0:T(8,128)} %copy-done) | copy-start | bytes 26112004
  47.2 10.4 %all-to-all-start.2 = ((f32[4,8,128]{2,1,0:T(8,128)}), f32[4,8,128]{2,1,0:T(8,128)S(1)}, u32[]{:S(2)}, u32[]{:S(2)}) async-start(f32[4,8,128]{2,1,0:T(8,128)} %get-tuple-element.16), calls=%async_computation.2 | async-start | bytes 32768 | tf_op jit(solution)/shard_map/all_to_all | solution.py:475

commit v10 on v8

--- a/solution.py
+++ b/solution.py
@@ -30,15 +30,6 @@
     return lax.broadcasted_iota(jnp.int32, (rows, LANES), 1)
 
 
-def pack_lanes(pieces):
-    rows = pieces[0][0].shape[0]
-    segment = lane_iota(rows) // SEG
-    packed = jnp.zeros((rows, LANES), jnp.float32)
-    for place, (array, first) in enumerate(pieces):
-        packed = jnp.where(segment == place, roll_lanes(array, place * SEG - first), packed)
-    return packed
-
-
 def gauge_rows(owned):
     if 3 * owned <= LANES:
         return STEPS_BLOCK, owned
@@ -52,19 +43,15 @@
 
 
 def prepare(
-    halo, blocks, samples, coast_count, keep_ref, gain_ref, gauge_ref, resid_ref,
-    parcel_ref, south_ref, north_ref, east_ref, west_ref, block_ref,
+    halo, blocks, samples, coast_count, keep_ref, gain_ref, gauge_ref,
+    parcel_ref, south_ref, north_ref, west_ref, block_ref,
 ):
     height, width = keep_ref.shape
     my_row, my_lon, row_tiles, lons = my_place()
     keep, gain = keep_ref[...], gain_ref[...]
-    half = height // 2
-    first, last = slice(0, LANES), slice(width - LANES, width)
-    end = LANES - halo
-
     owned = gauge_ref.shape[2]
     assert blocks == 2
-    route, cell, coast = (gauge_ref[blocks, i : i + 1, :] for i in range(3))
+    route, cell, coast = (gauge_ref[2 * blocks, i : i + 1, :].astype(jnp.int32) for i in range(3))
     target = jnp.zeros_like(route)
     for entry in range(coast_count):
         target = jnp.where(route == entry, jnp.broadcast_to(coast[:, entry : entry + 1], route.shape), target)
@@ -73,12 +60,12 @@
     grid_row = (target & (row_tiles - 1)) * height + (cell >> width_bits)
     grid_col = (target >> row_bits) * width + (cell & (width - 1))
     block_ref[...] = jnp.zeros_like(block_ref)
-    levels = lax.broadcasted_iota(jnp.int32, (STEPS_BLOCK, owned), 0)
+    levels = lax.broadcasted_iota(jnp.int32, (STEPS_BLOCK, owned), 0).astype(jnp.float32)
     for block in range(blocks):
         series = jnp.zeros((STEPS_BLOCK, owned), jnp.float32)
         for sample in range(samples):
             times = gauge_ref[block, sample : sample + 1, :]
-            resid = resid_ref[block, sample : sample + 1, :]
+            resid = gauge_ref[blocks + block, sample : sample + 1, :]
             series = series + jnp.where(times == levels, resid, 0.0)
         block_ref[block * STEPS_BLOCK : (block + 1) * STEPS_BLOCK, :owned] = series
     at = blocks * STEPS_BLOCK
@@ -98,25 +85,20 @@
 
     lax.fori_loop(0, tiles, put, 0, unroll=tiles <= 16)
 
+    reach = 2 * halo
+    lower = lane_iota(height) < reach
+    west = jnp.where(lower, keep[:, :LANES], roll_lanes(gain[:, :LANES], reach))
+    west_ref[...] = west
     for d_row in (-1, 1):
         top = 0 if d_row < 0 else height - halo
-        for d_lon in (-1, 1):
-            cols, start = (first, 0) if d_lon < 0 else (last, end)
-            to_row, to_lon = my_row + d_row, my_lon + d_lon
-            there = (to_row >= 0) & (to_row < row_tiles) & (to_lon >= 0) & (to_lon < lons)
-
-            @pl.when(there)
-            def _():
-                for kind, source in enumerate((keep, gain)):
-                    corner = pack_lanes([(source[top + 8 * i : top + 8 * i + 8, cols], start) for i in range(4)])
-                    parcel_ref[to_lon * row_tiles + to_row, size + 8 * kind : size + 8 * kind + 8, :] = corner
+        to_row, to_lon = my_row + d_row, my_lon - 1
+
+        @pl.when((to_row >= 0) & (to_row < row_tiles) & (to_lon >= 0))
+        def _():
+            parcel_ref[to_lon * row_tiles + to_row, size : size + halo, :] = west[top : top + halo]
 
     south_ref[0], south_ref[1] = keep[height - halo :], gain[height - halo :]
     north_ref[0], north_ref[1] = keep[:halo], gain[:halo]
-    for goal, cols, start in ((east_ref, last, end), (west_ref, first, 0)):
-        goal[...] = pack_lanes(
-            [(keep[:half, cols], start), (gain[:half, cols], start), (keep[half:, cols], start), (gain[half:, cols], start)]
-        )
 
 
 def from_rolled(rolled, shift, lanes):
@@ -135,7 +117,7 @@
     my_row, my_lon, row_tiles, lons = my_place()
     wide = rows_hot.shape[1]
     tiles, parcel_rows = parcel_ref.shape[:2]
-    size = parcel_rows - 16
+    size = parcel_rows - halo
     apart = wide // tiles if size == STEPS_BLOCK else 0
     owned = apart if apart else LANES
     group = wide // owned
@@ -164,7 +146,7 @@
             series_ref[8:16, cols] = fields[1]
             row = fields[2][0:1] + row_shift
             col = fields[2][1:2] + col_shift
-            col = jnp.where((col >= -halo) & (col < 0), col + float(planes * LANES), jnp.where(col < width + halo, col, -1.0))
+            col = jnp.where(col < width + 2 * halo, col, -1.0)
             rows_hot[:, cols] = (at == row).astype(jnp.float32).astype(jnp.bfloat16)
             by_gauge = jnp.transpose(jnp.broadcast_to(col, (LANES, LANES)))
             for c in range(planes):
@@ -214,7 +196,7 @@
 
 
 def sweep(
-    steps, keep_ref, gain_ref, top_ref, bottom_ref, left_ref, right_ref, parcel_ref, force_ref,
+    steps, keep_ref, gain_ref, top_ref, bottom_ref, right_ref, parcel_ref, force_ref,
     grad_ref, sums_ref,
     a, fx, fy, keep_x, gain_x, keep_y, gain_y, plain,
 ):
@@ -225,12 +207,12 @@
     rows_all = height + 2 * halo
     blocks = rows_all // 8
     my_row, my_lon, row_tiles, lons = my_place()
-    end = LANES - halo
-    size = parcel_ref.shape[1] - 16
+    reach = 2 * halo
+    size = parcel_ref.shape[1] - halo
     has_top, has_bottom = my_row > 0, my_row < row_tiles - 1
-    has_left, has_right = my_lon > 0, my_lon < lons - 1
+    has_right = my_lon < lons - 1
     above, below = jnp.maximum(my_row - 1, 0), jnp.minimum(my_row + 1, row_tiles - 1)
-    left, right = jnp.maximum(my_lon - 1, 0), jnp.minimum(my_lon + 1, lons - 1)
+    right = jnp.minimum(my_lon + 1, lons - 1)
     lanes8 = lane_iota(8)
 
     def known(condition, value):
@@ -242,30 +224,18 @@
     def down(value):
         return pltpu.roll(value, 1, 0)
 
-    half = height // 2
     for kind, (source, by_x, by_y) in enumerate(((keep_ref, keep_x, keep_y), (gain_ref, gain_x, gain_y))):
         for c in range(inner):
             cols = slice(c * LANES, (c + 1) * LANES)
             plain[c, halo : halo + height, :] = source[:, cols]
             plain[c, 0:halo, :] = top_ref[kind, :, cols]
             plain[c, halo + height : rows_all, :] = bottom_ref[kind, :, cols]
-        segment = lane_iota(half) // SEG
-        for part in range(2):
-            piece = 2 * part + kind
-            by_left = roll_lanes(left_ref[...], end - piece * SEG)
-            by_right = roll_lanes(right_ref[...], -piece * SEG)
-            both = jnp.where(segment == 0, by_right, jnp.where(segment == LANES // SEG - 1, by_left, 0.0))
-            plain[inner, halo + part * half : halo + (part + 1) * half, :] = both
-        segment = lane_iota(8) // SEG
+        lower = lane_iota(height) < reach
+        plain[inner, halo : halo + height, :] = jnp.where(lower, roll_lanes(right_ref[...], -reach * kind), 0.0)
+        lower = lane_iota(halo) < reach
         for has_row, row, at in ((has_top, above, 0), (has_bottom, below, halo + height)):
-            by_left = known(has_row & has_left, parcel_ref[left * row_tiles + row, size + 8 * kind : size + 8 * kind + 8, :])
-            by_right = known(has_row & has_right, parcel_ref[right * row_tiles + row, size + 8 * kind : size + 8 * kind + 8, :])
-            for i in range(4):
-                both = jnp.where(
-                    segment == 0, roll_lanes(by_right, -i * SEG),
-                    jnp.where(segment == LANES // SEG - 1, roll_lanes(by_left, end - i * SEG), 0.0),
-                )
-                plain[inner, at + 8 * i : at + 8 * i + 8, :] = both
+            corner = roll_lanes(parcel_ref[right * row_tiles + row, size : size + halo, :], -reach * kind)
+            plain[inner, at : at + halo, :] = known(has_row & has_right, jnp.where(lower, corner, 0.0))
         for q in range(blocks):
             values = [plain[c, pl.ds(q, 8, stride=blocks), :] for c in range(planes)]
             shifted = shift_from(values, 1, lanes8)
@@ -274,8 +244,7 @@
                 by_x[c, 8 * q : 8 * q + 8, :] = shifted[c]
                 by_y[c, to : to + 8, :] = up(values[c]) if q == 0 else values[c]
 
-    col_valid = jnp.where(lanes8 < LANES // 2, jnp.where(has_right, 1.0, 0.0), jnp.where(has_left, 1.0, 0.0))
-    col_mask = jnp.where((lanes8 < halo) | (lanes8 >= end), col_valid, 0.0)
+    col_mask = jnp.where(lanes8 < reach, jnp.where(has_right, 1.0, 0.0), 0.0)
     sublane = lax.broadcasted_iota(jnp.int32, (8, LANES), 0)
     row_mask = {}
     for row, there in ((halo - 1, has_top), (halo + height, has_bottom)):
@@ -351,17 +320,26 @@
 
     lax.fori_loop(0, steps, step, 0)
 
+    start = jnp.where(my_lon > 0, halo, 0)
     for r in range(0, height, 8):
         s, q = divmod(halo + r, blocks)
-        for c in range(inner):
+        for c in every:
             cols = slice(c * LANES, (c + 1) * LANES)
             value = a[c, pl.ds(8 * q + s, 8, stride=8), :]
-            grad_ref[r : r + 8, cols] = jnp.where(keep_ref[r : r + 8, cols] > 0.0, value, 0.0)
+            wet = keep_ref[r : r + 8, cols] if c < inner else right_ref[r : r + 8, :]
+            if c == 0:
+                wet = jnp.where(lanes8 >= start, wet, 0.0)
+            if c == inner:
+                wet = jnp.where(lanes8 < halo, wet, 0.0)
+            grad_ref[r : r + 8, cols] = jnp.where(wet > 0.0, value, 0.0)
     length = 2.0 * width
-    kind = lax.broadcasted_iota(jnp.int32, (8, width), 0)
-    column = lax.broadcasted_iota(jnp.int32, (8, width), 1)
-    steps_off = jnp.where(kind == 0, column, width - 1 - column).astype(jnp.float32)
-    weights = jnp.where(kind < 2, jnp.exp(-steps_off / length), 0.0)
+    shape = (8 + halo, planes * LANES)
+    kind, column = lax.broadcasted_iota(jnp.int32, shape, 0), lax.broadcasted_iota(jnp.int32, shape, 1)
+    beyond = column - width
+    off = jnp.where(kind == 0, column, jnp.where(kind == 1, -1 - beyond, jnp.where(kind == 2, beyond, width - 1 - beyond)))
+    mine = ((kind < 2) & (beyond < 0)) | ((kind >= 2) & (kind < 4) & (beyond >= 0))
+    weights = jnp.where(mine, jnp.exp(-jnp.maximum(off, 0).astype(jnp.float32) / length), 0.0)
+    weights = jnp.where((kind >= 8) & (beyond == kind - 8), 1.0, weights)
     sums = lax.dot_general(
         weights, grad_ref[...], (((1,), (1,)), ((), ())), precision=lax.Precision.HIGHEST,
         preferred_element_type=jnp.float32,
@@ -370,31 +348,32 @@
         sums_ref[i] = sums
 
 
-def smooth(grad_ref, out_ref):
-    width = grad_ref.shape[1]
+def smooth(halo, lons, grad_ref, out_ref, weights_ref):
+    width = out_ref.shape[1]
     length = 2.0 * width
     row = lax.broadcasted_iota(jnp.int32, (width, width), 0)
     column = lax.broadcasted_iota(jnp.int32, (width, width), 1)
     kernel = jnp.exp(-jnp.abs(row - column).astype(jnp.float32) / length)
     out_ref[...] = jnp.dot(
-        grad_ref[...], kernel, precision=lax.Precision.HIGHEST, preferred_element_type=jnp.float32
+        grad_ref[:, :width], kernel, precision=lax.Precision.HIGHEST, preferred_element_type=jnp.float32
     )
-
-
-def finish(own_ref, sums_ref, out_ref):
-    width = own_ref.shape[1]
-    length = 2.0 * width
-    count = sums_ref.shape[0]
     me = lax.axis_index("lon")
-    row = lax.broadcasted_iota(jnp.int32, (count, width), 0)
-    column = lax.broadcasted_iota(jnp.int32, (count, width), 1)
-    strip, kind = row >> 3, row & 7
-    left = (kind == 0) & (strip > me)
-    right = (kind == 1) & (strip < me)
-    away = jnp.where(left, (strip - me) * width - column, (me - strip - 1) * width + column + 1)
-    weights = jnp.where(left | right, jnp.exp(-jnp.maximum(away, 0).astype(jnp.float32) / length), 0.0)
+    shape = (8 + halo, width)
+    kind, column = lax.broadcasted_iota(jnp.int32, shape, 0), lax.broadcasted_iota(jnp.int32, shape, 1)
+    for source in range(lons):
+        strip = jnp.where(kind < 2, source, source + 1)
+        left = ((kind == 0) | (kind == 2)) & (strip > me)
+        right = ((kind == 1) | (kind == 3)) & (strip < me)
+        near = (kind >= 8) & (source + 1 == me)
+        away = jnp.where(left, (strip - me) * width - column, (me - strip - 1) * width + column + 1)
+        away = jnp.where(near, jnp.abs(kind - 8 - column), away)
+        weights = jnp.where(left | right | near, jnp.exp(-jnp.maximum(away, 0).astype(jnp.float32) / length), 0.0)
+        weights_ref[source * shape[0] : (source + 1) * shape[0], :] = weights
+
+
+def finish(own_ref, weights_ref, sums_ref, out_ref):
     out_ref[...] = own_ref[...] + lax.dot_general(
-        sums_ref[...], weights, (((0,), (0,)), ((), ())), precision=lax.Precision.HIGHEST,
+        sums_ref[...], weights_ref[...], (((0,), (0,)), ((), ())), precision=lax.Precision.HIGHEST,
         preferred_element_type=jnp.float32,
     )
 
@@ -421,7 +400,7 @@
     tiles = lax.axis_size(GRID_AXES)
     lons = lax.axis_size("lon")
     row_tiles = lax.axis_size(ROW_AXES)
-    parcel_rows = gauge_rows(owned)[0] + 16
+    parcel_rows = gauge_rows(owned)[0] + halo
     params = pltpu.CompilerParams(vmem_limit_bytes=VMEM_LIMIT)
 
     keep = (1.0 - friction) * wet.astype(jnp.float32)
@@ -433,27 +412,26 @@
 
     def put(array, group, row):
         groups, rows, lanes = array.shape
-        return jnp.pad(array, ((group, blocks + 1 - group - groups), (row, samples - row - rows), (0, owned - lanes)))
+        return jnp.pad(array, ((group, 2 * blocks + 1 - group - groups), (row, samples - row - rows), (0, owned - lanes)))
 
     gauges = (
         put(jnp.transpose(gauge_times, (1, 2, 0)), 0, 0)
-        + put(gauge_route.reshape(1, 1, owned), blocks, 0)
-        + put(gauge_cell.reshape(1, 1, owned), blocks, 1)
-        + put(coastal_tiles.reshape(1, 1, coast_count), blocks, 2)
-    )
-    residuals = jnp.transpose(gauge_resid, (1, 2, 0))
-    parcel, south, north, east, west = pl.pallas_call(
+        + put(gauge_route.reshape(1, 1, owned), 2 * blocks, 0)
+        + put(gauge_cell.reshape(1, 1, owned), 2 * blocks, 1)
+        + put(coastal_tiles.reshape(1, 1, coast_count), 2 * blocks, 2)
+    ).astype(jnp.float32) + put(jnp.transpose(gauge_resid, (1, 2, 0)), blocks, 0)
+    parcel, south, north, west = pl.pallas_call(
         functools.partial(prepare, halo, blocks, samples, coast_count),
         out_shape=(
             f32(tiles, parcel_rows, LANES), f32(2, halo, width), f32(2, halo, width),
-            f32(height // 2, LANES), f32(height // 2, LANES),
+            f32(height, LANES),
         ),
-        in_specs=vmem(4),
-        out_specs=tuple(vmem(5)),
+        in_specs=vmem(3),
+        out_specs=tuple(vmem(4)),
         scratch_shapes=[pltpu.VMEM((24, LANES), jnp.float32)],
         compiler_params=params,
         name="prepare",
-    )(keep, gain, gauges, residuals)
+    )(keep, gain, gauges)
 
     def exchange(array, axes):
         return lax.all_to_all(array, axes, split_axis=0, concat_axis=0, tiled=True)
@@ -463,7 +441,6 @@
     up = [(i + 1, i) for i in range(row_tiles - 1)]
     top = lax.ppermute(south, ROW_AXES, down)
     bottom = lax.ppermute(north, ROW_AXES, up)
-    left = lax.ppermute(east, "lon", [(i, i + 1) for i in range(lons - 1)])
     right = lax.ppermute(west, "lon", [(i + 1, i) for i in range(lons - 1)])
 
     planes = width // LANES + 1
@@ -490,25 +467,29 @@
     plane = pltpu.VMEM((planes, spaced(rows_all), LANES), jnp.float32)
     grad, sums = pl.pallas_call(
         functools.partial(sweep, steps),
-        out_shape=(f32(height, width), f32(lons, 8, height)),
-        in_specs=vmem(8),
+        out_shape=(f32(height, planes * LANES), f32(lons, 8 + halo, height)),
+        in_specs=vmem(7),
         out_specs=tuple(vmem(2)),
         scratch_shapes=[plane] * 8,
         compiler_params=params,
         name="sweep",
-    )(keep, gain, top, bottom, left, right, parcel, pushes)
+    )(keep, gain, top, bottom, right, parcel, pushes)
 
     sums = exchange(sums, "lon")
-    own = pl.pallas_call(
-        smooth, out_shape=f32(height, width), in_specs=vmem(1), out_specs=vmem(1)[0], compiler_params=params,
+    own, weights = pl.pallas_call(
+        functools.partial(smooth, halo, lons),
+        out_shape=(f32(height, width), f32(lons * (8 + halo), width)),
+        in_specs=vmem(1),
+        out_specs=tuple(vmem(2)),
+        compiler_params=params,
         cost_estimate=pl.CostEstimate(
             flops=6 * 2 * height * width * width, bytes_accessed=2 * 4 * height * width, transcendentals=width * width
         ),
         name="smooth",
     )(grad)
     return pl.pallas_call(
-        finish, out_shape=f32(height, width), in_specs=vmem(2), out_specs=vmem(1)[0], compiler_params=params, name="finish",
-    )(own, sums.reshape(lons * 8, height))
+        finish, out_shape=f32(height, width), in_specs=vmem(3), out_specs=vmem(1)[0], compiler_params=params, name="finish",
+    )(own, weights, sums.reshape(lons * (8 + halo), height))
 
 
 def solution(mesh):

time: 47.5 us -> 46.5 us (0.979)
  the two profiles are of different devices: /device:TPU:1 before, /device:TPU:0 now
where the time goes in v10:
time: 46.5 us; the launch traced here: 46.1 us
  Pallas kernels  17 us (37%)
  starting transfers between devices  15.5 us (33%)
  waiting for transfers between devices  11.4 us (25%)
  other arithmetic  2.05 us (4%)
    all_to_all x2, waiting for transfers between devices, exchange(): return lax.all_to_all(array, axes, split_axis=0, concat_axis=0, tiled=True)  11.4 us
    all_to_all x2, starting transfers between devices, exchange(): return lax.all_to_all(array, axes, split_axis=0, concat_axis=0, tiled=True)  10.7 us
    pallas_call x1, Pallas kernels, local(): pl.pallas_call(functools.partial(sweep, steps), out_shape=(f32(height, pl...  10.6 us
    pallas_call x1, Pallas kernels, local(): pl.pallas_call(functools.partial(force, steps, halo, height, width), out_...  3.4 us
    ppermute x1, starting transfers between devices, local(): top = lax.ppermute(south, ROW_AXES, down)  2.31 us
    ppermute x1, starting transfers between devices, local(): right = lax.ppermute(west, 'lon', [(i + 1, i) for i in range(lons - 1)])  1.29 us
    ppermute x1, starting transfers between devices, local(): bottom = lax.ppermute(north, ROW_AXES, up)  1.29 us
    mul x1, other arithmetic, local(): (courant * 0.5) ** 2 * jnp.maximum(depth + surface, depth_floor) * keep  1.29 us
  transfers between devices with their start and end apart: 5, of which 2 were waited for; matrix products, arithmetic and copies ran while one was open for 0% of the time, Pallas kernels for 10%

profile of v10, /device:TPU:0, one launch (start us, length us, event | category | flops | bytes accessed | tf_op | source)
XLA Modules:
  0.0 46.1 jit_solution(16500119076117336689)
XLA Ops:
  0.0 1.3 %multiply_multiply_fusion = (f32[128,512]{1,0:T(8,128)S(1)}, f32[128,512]{1,0:T(8,128)S(1)}) fusion(f32[128,512]{1,0:T(8,128)} %param.9, f32[128,512]{1,0:T(8,128)} %param.10, s32[128,512]{1,0:T(8,128)} %param.12, f32[128,512]{1,0:T(8,128)} %param.11), kind=kLoop, calls=%fused_computation | loop fusion | flops 458752 | bytes 1572864 | tf_op jit(solution)/shard_map/mul | solution.py:407
  1.3 0.8 %pad_add_fusion.gauge_ref = f32[5,4,16]{2,1,0:T(4,128)S(1)} fusion(f32[2,4,16]{2,1,0:T(4,128)} %bitcast.7, s32[1,1,8]{2,1,0:T(1,128)} %bitcast.9, s32[1,1,16]{2,1,0:T(1,128)} %bitcast.10, s32[1,1,16]{2,1,0:T(1,128)} %bitcast.11, s32[2,4,16]{2,1,0:T(4,128)} %bitcast.8), kind=kLoop, calls=%fused_computation.2 | loop fusion | flops 1600 | bytes 2464 | tf_op jit(solution)/shard_map/add | solution.py:417
  2.1 0.9 %prepare.1 = (f32[16,40,128]{2,1,0:T(8,128)}, f32[2,32,512]{2,1,0:T(8,128)S(1)}, f32[2,32,512]{2,1,0:T(8,128)S(1)}, f32[128,128]{1,0:T(8,128)S(1)}) custom-call(f32[128,512]{1,0:T(8,128)S(1)} %get-tuple-element.22.keep_ref, f32[128,512]{1,0:T(8,128)S(1)} %get-tuple-element.21.gain_ref, f32[5,4,16]{2,1,0:T(4,128)S(1)} %pad_add_fusion.gauge_ref), custom_call_target="tpu_custom_call" | custom-call | tf_op jit(solution)/shard_map/prepare/pallas_call | solution.py:423
  3.0 7.4 %all-to-all-start = ((f32[16,40,128]{2,1,0:T(8,128)}), f32[16,40,128]{2,1,0:T(8,128)S(1)}, u32[]{:S(2)}, u32[]{:S(2)}) async-start(f32[16,40,128]{2,1,0:T(8,128)} %get-tuple-element.16), calls=%async_computation | async-start | bytes 655360 | tf_op jit(solution)/shard_map/all_to_all | solution.py:437
  10.3 1.3 %collective-permute-start.2 = (f32[128,128]{1,0:T(8,128)S(1)}, f32[128,128]{1,0:T(8,128)S(1)}, u32[]{:S(2)}, u32[]{:S(2)}) collective-permute-start(f32[128,128]{1,0:T(8,128)S(1)} %get-tuple-element.15), channel_id=1, source_target_pairs={{4,0},{8,4},{12,8},{5,1},{9,5},{13,9},{6,2},{10,6},{14,10},{7,3},{... | collective-permute-start | bytes 196616 | tf_op jit(solution)/shard_map/ppermute | solution.py:444
  11.6 2.3 %collective-permute-start = (f32[2,32,512]{2,1,0:T(8,128)S(1)}, f32[2,32,512]{2,1,0:T(8,128)S(1)}, u32[]{:S(2)}, u32[]{:S(2)}) collective-permute-start(f32[2,32,512]{2,1,0:T(8,128)S(1)} %get-tuple-element.13), channel_id=1, source_target_pairs={{0,1},{1,2},{2,3},{4,5},{5,6},{6,7},{8,9},{9,10},{10,11},{12,13},{... | collective-permute-start | bytes 393224 | tf_op jit(solution)/shard_map/ppermute | solution.py:442
  14.0 1.3 %collective-permute-start.1 = (f32[2,32,512]{2,1,0:T(8,128)S(1)}, f32[2,32,512]{2,1,0:T(8,128)S(1)}, u32[]{:S(2)}, u32[]{:S(2)}) collective-permute-start(f32[2,32,512]{2,1,0:T(8,128)S(1)} %get-tuple-element.14), channel_id=1, source_target_pairs={{1,0},{2,1},{3,2},{5,4},{6,5},{7,6},{9,8},{10,9},{11,10},{13,12},{... | collective-permute-start | bytes 393224 | tf_op jit(solution)/shard_map/ppermute | solution.py:443
  15.3 6.7 %all-to-all-done.parcel_ref = f32[16,40,128]{2,1,0:T(8,128)S(1)} async-done(((f32[16,40,128]{2,1,0:T(8,128)}), f32[16,40,128]{2,1,0:T(8,128)S(1)}, u32[]{:S(2)}, u32[]{:S(2)}) %all-to-all-start) | async-done | bytes 327712 | tf_op jit(solution)/shard_map/all_to_all | solution.py:437
  21.9 3.4 %force.1.force_ref = f32[17,5,200,128]{3,2,1,0:T(8,128)S(1)} custom-call(f32[16,40,128]{2,1,0:T(8,128)S(1)} %all-to-all-done.parcel_ref), custom_call_target="tpu_custom_call" | custom-call | flops 2013265920 | bytes 7864320 | tf_op jit(solution)/shard_map/force/pallas_call | solution.py:449
  25.3 0.0 collective-permute-done.2.right_ref
  25.3 0.0 collective-permute-done.top_ref
  25.3 0.0 collective-permute-done.1.bottom_ref
  25.3 10.6 %sweep.1 = (f32[128,640]{1,0:T(8,128)S(1)}, f32[4,40,128]{2,1,0:T(8,128)}) custom-call(f32[128,512]{1,0:T(8,128)S(1)} %get-tuple-element.22.keep_ref, f32[128,512]{1,0:T(8,128)S(1)} %get-tuple-element.21.gain_ref, f32[2,32,512]{2,1,0:T(8,128)S(1)} %collective-permute-done.top_ref, f32[2,32,512]{2,1,0:T(8,128)S(1)} %collective-permute-done.1.bottom_ref, ...), custom_call_target="tpu_custom_call" | custom-call | tf_op jit(solution)/shard_map/sweep/pallas_call | solution.py:468
  35.9 3.3 %all-to-all-start.1 = ((f32[4,40,128]{2,1,0:T(8,128)}), f32[4,40,128]{2,1,0:T(8,128)S(1)}, u32[]{:S(2)}, u32[]{:S(2)}) async-start(f32[4,40,128]{2,1,0:T(8,128)} %get-tuple-element.20), calls=%async_computation.1 | async-start | bytes 163840 | tf_op jit(solution)/shard_map/all_to_all | solution.py:437
  39.2 1.0 %smooth.1 = (f32[128,512]{1,0:T(8,128)S(1)}, f32[160,512]{1,0:T(8,128)S(1)}) custom-call(f32[128,640]{1,0:T(8,128)S(1)} %get-tuple-element.17.grad_ref), custom_call_target="tpu_custom_call" | custom-call | flops 402653184 | bytes 524288 | tf_op jit(solution)/shard_map/smooth/pallas_call | solution.py:479
  40.2 4.7 %all-to-all-done.1 = f32[4,40,128]{2,1,0:T(8,128)S(1)} async-done(((f32[4,40,128]{2,1,0:T(8,128)}), f32[4,40,128]{2,1,0:T(8,128)S(1)}, u32[]{:S(2)}, u32[]{:S(2)}) %all-to-all-start.1) | async-done | bytes 81952 | tf_op jit(solution)/shard_map/all_to_all | solution.py:437
  45.0 1.1 %finish.1 = f32[128,512]{1,0:T(8,128)} custom-call(f32[128,512]{1,0:T(8,128)S(1)} %get-tuple-element.18.own_ref, f32[160,512]{1,0:T(8,128)S(1)} %get-tuple-element.19.weights_ref, f32[160,128]{1,0:T(8,128)S(1)} %bitcast.6), custom_call_target="tpu_custom_call" | custom-call | tf_op jit(solution)/shard_map/finish/pallas_call | solution.py:490
Async XLA Ops:
  3.0 18.9 %all-to-all-start = ((f32[16,40,128]{2,1,0:T(8,128)}), f32[16,40,128]{2,1,0:T(8,128)S(1)}, u32[]{:S(2)}, u32[]{:S(2)}) async-start(f32[16,40,128]{2,1,0:T(8,128)} %get-tuple-element.16), calls=%async_computation | async-start | bytes 655360 | tf_op jit(solution)/shard_map/all_to_all | solution.py:437
  10.3 15.0 %collective-permute-start.2 = (f32[128,128]{1,0:T(8,128)S(1)}, f32[128,128]{1,0:T(8,128)S(1)}, u32[]{:S(2)}, u32[]{:S(2)}) collective-permute-start(f32[128,128]{1,0:T(8,128)S(1)} %get-tuple-element.15), channel_id=1, source_target_pairs={{4,0},{8,4},{12,8},{5,1},{9,5},{13,9},{6,2},{10,6},{14,10},{7,3},{... | collective-permute-start | bytes 196616 | tf_op jit(solution)/shard_map/ppermute | solution.py:444
  11.6 13.7 %collective-permute-start = (f32[2,32,512]{2,1,0:T(8,128)S(1)}, f32[2,32,512]{2,1,0:T(8,128)S(1)}, u32[]{:S(2)}, u32[]{:S(2)}) collective-permute-start(f32[2,32,512]{2,1,0:T(8,128)S(1)} %get-tuple-element.13), channel_id=1, source_target_pairs={{0,1},{1,2},{2,3},{4,5},{5,6},{6,7},{8,9},{9,10},{10,11},{12,13},{... | collective-permute-start | bytes 393224 | tf_op jit(solution)/shard_map/ppermute | solution.py:442
  14.0 11.4 %collective-permute-start.1 = (f32[2,32,512]{2,1,0:T(8,128)S(1)}, f32[2,32,512]{2,1,0:T(8,128)S(1)}, u32[]{:S(2)}, u32[]{:S(2)}) collective-permute-start(f32[2,32,512]{2,1,0:T(8,128)S(1)} %get-tuple-element.14), channel_id=1, source_target_pairs={{1,0},{2,1},{3,2},{5,4},{6,5},{7,6},{9,8},{10,9},{11,10},{13,12},{... | collective-permute-start | bytes 393224 | tf_op jit(solution)/shard_map/ppermute | solution.py:443
  35.9 9.1 %all-to-all-start.1 = ((f32[4,40,128]{2,1,0:T(8,128)}), f32[4,40,128]{2,1,0:T(8,128)S(1)}, u32[]{:S(2)}, u32[]{:S(2)}) async-start(f32[4,40,128]{2,1,0:T(8,128)} %get-tuple-element.20), calls=%async_computation.1 | async-start | bytes 163840 | tf_op jit(solution)/shard_map/all_to_all | solution.py:437

commit v11 on v10

--- a/solution.py
+++ b/solution.py
@@ -42,13 +42,22 @@
     return row, lax.axis_index("lon"), lax.axis_size("lat") * lax.axis_size("gau"), lax.axis_size("lon")
 
 
-def prepare(
-    halo, blocks, samples, coast_count, keep_ref, gain_ref, gauge_ref,
-    parcel_ref, south_ref, north_ref, west_ref, block_ref,
-):
+def give_west(reach, keep_ref, gain_ref, west_ref):
+    lower = lane_iota(west_ref.shape[0]) < reach
+    west_ref[...] = jnp.where(lower, keep_ref[:, :LANES], roll_lanes(gain_ref[:, :LANES], reach))
+
+
+def give_rows(halo, keep_ref, gain_ref, right_ref, south_ref, north_ref):
     height, width = keep_ref.shape
-    my_row, my_lon, row_tiles, lons = my_place()
-    keep, gain = keep_ref[...], gain_ref[...]
+    lower = lane_iota(halo) < 2 * halo
+    for goal, rows in ((south_ref, slice(height - halo, height)), (north_ref, slice(0, halo))):
+        for kind, source in enumerate((keep_ref, gain_ref)):
+            goal[kind, :, :width] = source[rows, :]
+            goal[kind, :, width:] = jnp.where(lower, roll_lanes(right_ref[rows, :], -2 * halo * kind), 0.0)
+
+
+def give_gauges(height, width, blocks, samples, coast_count, gauge_ref, after_ref, parcel_ref, block_ref):
+    row_tiles = lax.axis_size("lat") * lax.axis_size("gau")
     owned = gauge_ref.shape[2]
     assert blocks == 2
     route, cell, coast = (gauge_ref[2 * blocks, i : i + 1, :].astype(jnp.int32) for i in range(3))
@@ -85,21 +94,6 @@
 
     lax.fori_loop(0, tiles, put, 0, unroll=tiles <= 16)
 
-    reach = 2 * halo
-    lower = lane_iota(height) < reach
-    west = jnp.where(lower, keep[:, :LANES], roll_lanes(gain[:, :LANES], reach))
-    west_ref[...] = west
-    for d_row in (-1, 1):
-        top = 0 if d_row < 0 else height - halo
-        to_row, to_lon = my_row + d_row, my_lon - 1
-
-        @pl.when((to_row >= 0) & (to_row < row_tiles) & (to_lon >= 0))
-        def _():
-            parcel_ref[to_lon * row_tiles + to_row, size : size + halo, :] = west[top : top + halo]
-
-    south_ref[0], south_ref[1] = keep[height - halo :], gain[height - halo :]
-    north_ref[0], north_ref[1] = keep[:halo], gain[:halo]
-
 
 def from_rolled(rolled, shift, lanes):
     count = len(rolled)
@@ -117,7 +111,7 @@
     my_row, my_lon, row_tiles, lons = my_place()
     wide = rows_hot.shape[1]
     tiles, parcel_rows = parcel_ref.shape[:2]
-    size = parcel_rows - halo
+    size = parcel_rows
     apart = wide // tiles if size == STEPS_BLOCK else 0
     owned = apart if apart else LANES
     group = wide // owned
@@ -196,7 +190,7 @@
 
 
 def sweep(
-    steps, keep_ref, gain_ref, top_ref, bottom_ref, right_ref, parcel_ref, force_ref,
+    steps, keep_ref, gain_ref, top_ref, bottom_ref, right_ref, force_ref,
     grad_ref, sums_ref,
     a, fx, fy, keep_x, gain_x, keep_y, gain_y, plain,
 ):
@@ -208,15 +202,9 @@
     blocks = rows_all // 8
     my_row, my_lon, row_tiles, lons = my_place()
     reach = 2 * halo
-    size = parcel_ref.shape[1] - halo
     has_top, has_bottom = my_row > 0, my_row < row_tiles - 1
     has_right = my_lon < lons - 1
-    above, below = jnp.maximum(my_row - 1, 0), jnp.minimum(my_row + 1, row_tiles - 1)
-    right = jnp.minimum(my_lon + 1, lons - 1)
     lanes8 = lane_iota(8)
-
-    def known(condition, value):
-        return jnp.where(jnp.where(condition, 1, 0) == 1, value, 0.0)
 
     def up(value):
         return pltpu.roll(value, 7, 0)
@@ -225,17 +213,14 @@
         return pltpu.roll(value, 1, 0)
 
     for kind, (source, by_x, by_y) in enumerate(((keep_ref, keep_x, keep_y), (gain_ref, gain_x, gain_y))):
-        for c in range(inner):
+        for c in range(planes):
             cols = slice(c * LANES, (c + 1) * LANES)
-            plain[c, halo : halo + height, :] = source[:, cols]
             plain[c, 0:halo, :] = top_ref[kind, :, cols]
             plain[c, halo + height : rows_all, :] = bottom_ref[kind, :, cols]
+            if c < inner:
+                plain[c, halo : halo + height, :] = source[:, cols]
         lower = lane_iota(height) < reach
         plain[inner, halo : halo + height, :] = jnp.where(lower, roll_lanes(right_ref[...], -reach * kind), 0.0)
-        lower = lane_iota(halo) < reach
-        for has_row, row, at in ((has_top, above, 0), (has_bottom, below, halo + height)):
-            corner = roll_lanes(parcel_ref[right * row_tiles + row, size : size + halo, :], -reach * kind)
-            plain[inner, at : at + halo, :] = known(has_row & has_right, jnp.where(lower, corner, 0.0))
         for q in range(blocks):
             values = [plain[c, pl.ds(q, 8, stride=blocks), :] for c in range(planes)]
             shifted = shift_from(values, 1, lanes8)
@@ -400,7 +385,8 @@
     tiles = lax.axis_size(GRID_AXES)
     lons = lax.axis_size("lon")
     row_tiles = lax.axis_size(ROW_AXES)
-    parcel_rows = gauge_rows(owned)[0] + halo
+    planes = width // LANES + 1
+    rows_all = height + 2 * halo
     params = pltpu.CompilerParams(vmem_limit_bytes=VMEM_LIMIT)
 
     keep = (1.0 - friction) * wet.astype(jnp.float32)
@@ -420,31 +406,34 @@
         + put(gauge_cell.reshape(1, 1, owned), 2 * blocks, 1)
         + put(coastal_tiles.reshape(1, 1, coast_count), 2 * blocks, 2)
     ).astype(jnp.float32) + put(jnp.transpose(gauge_resid, (1, 2, 0)), blocks, 0)
-    parcel, south, north, west = pl.pallas_call(
-        functools.partial(prepare, halo, blocks, samples, coast_count),
-        out_shape=(
-            f32(tiles, parcel_rows, LANES), f32(2, halo, width), f32(2, halo, width),
-            f32(height, LANES),
-        ),
-        in_specs=vmem(3),
-        out_specs=tuple(vmem(4)),
+    west = pl.pallas_call(
+        functools.partial(give_west, 2 * halo), out_shape=f32(height, LANES), in_specs=vmem(2), out_specs=vmem(1)[0],
+        compiler_params=params, name="give_west",
+    )(keep, gain)
+    right = lax.ppermute(west, "lon", [(i + 1, i) for i in range(lons - 1)])
+
+    parcel = pl.pallas_call(
+        functools.partial(give_gauges, height, width, blocks, samples, coast_count),
+        out_shape=f32(tiles, gauge_rows(owned)[0], LANES),
+        in_specs=vmem(1) + [pl.BlockSpec(memory_space=pl.ANY)],
+        out_specs=vmem(1)[0],
         scratch_shapes=[pltpu.VMEM((24, LANES), jnp.float32)],
         compiler_params=params,
-        name="prepare",
-    )(keep, gain, gauges)
+        name="give_gauges",
+    )(gauges, west)
 
     def exchange(array, axes):
         return lax.all_to_all(array, axes, split_axis=0, concat_axis=0, tiled=True)
 
     parcel = exchange(parcel, GRID_AXES)
-    down = [(i, i + 1) for i in range(row_tiles - 1)]
-    up = [(i + 1, i) for i in range(row_tiles - 1)]
-    top = lax.ppermute(south, ROW_AXES, down)
-    bottom = lax.ppermute(north, ROW_AXES, up)
-    right = lax.ppermute(west, "lon", [(i + 1, i) for i in range(lons - 1)])
-
-    planes = width // LANES + 1
-    rows_all = height + 2 * halo
+
+    south, north = pl.pallas_call(
+        functools.partial(give_rows, halo), out_shape=(f32(2, halo, planes * LANES),) * 2, in_specs=vmem(3),
+        out_specs=tuple(vmem(2)), compiler_params=params, name="give_rows",
+    )(keep, gain, right)
+    top = lax.ppermute(south, ROW_AXES, [(i, i + 1) for i in range(row_tiles - 1)])
+    bottom = lax.ppermute(north, ROW_AXES, [(i + 1, i) for i in range(row_tiles - 1)])
+
     wide = max(2 * LANES, owned)
     pushes = pl.pallas_call(
         functools.partial(force, steps, halo, height, width),
@@ -468,12 +457,12 @@
     grad, sums = pl.pallas_call(
         functools.partial(sweep, steps),
         out_shape=(f32(height, planes * LANES), f32(lons, 8 + halo, height)),
-        in_specs=vmem(7),
+        in_specs=vmem(6),
         out_specs=tuple(vmem(2)),
         scratch_shapes=[plane] * 8,
         compiler_params=params,
         name="sweep",
-    )(keep, gain, top, bottom, right, parcel, pushes)
+    )(keep, gain, top, bottom, right, pushes)
 
     sums = exchange(sums, "lon")
     own, weights = pl.pallas_call(

time: 46.5 us -> 46.8 us (level)
  the two profiles are of different devices: /device:TPU:0 before, /device:TPU:1 now
where the time goes in v11:
time: 46.8 us; the launch traced here: 46.4 us
  starting transfers between devices  17.6 us (38%)
  Pallas kernels  17.1 us (37%)
  waiting for transfers between devices  9.63 us (21%)
  other arithmetic  2.05 us (4%)
    all_to_all x2, starting transfers between devices, exchange(): return lax.all_to_all(array, axes, split_axis=0, concat_axis=0, tiled=True)  10.6 us
    pallas_call x1, Pallas kernels, local(): pl.pallas_call(functools.partial(sweep, steps), out_shape=(f32(height, pl...  10.5 us
    ppermute x1, waiting for transfers between devices, local(): right = lax.ppermute(west, 'lon', [(i + 1, i) for i in range(lons - 1)])  4.79 us
    ppermute x1, starting transfers between devices, local(): lax.ppermute(south, ROW_AXES, [(i, i + 1) for i in range(row_tiles - 1)])  3.8 us
    all_to_all x2, waiting for transfers between devices, exchange(): return lax.all_to_all(array, axes, split_axis=0, concat_axis=0, tiled=True)  3.57 us
    pallas_call x1, Pallas kernels, local(): pl.pallas_call(functools.partial(force, steps, halo, height, width), out_...  3.41 us
    ppermute x1, starting transfers between devices, local(): lax.ppermute(north, ROW_AXES, [(i + 1, i) for i in range(row_tiles - 1)])  1.92 us
    mul x1, other arithmetic, local(): (courant * 0.5) ** 2 * jnp.maximum(depth + surface, depth_floor) * keep  1.29 us
  transfers between devices with their start and end apart: 5, of which 3 were waited for; matrix products, arithmetic and copies ran while one was open for 0% of the time, Pallas kernels for 10%

profile of v11, /device:TPU:1, one launch (start us, length us, event | category | flops | bytes accessed | tf_op | source)
XLA Modules:
  0.0 46.4 jit_solution(11393134636773739936)
XLA Ops:
  0.0 1.3 %multiply_multiply_fusion = (f32[128,512]{1,0:T(8,128)S(1)}, f32[128,512]{1,0:T(8,128)S(1)}) fusion(f32[128,512]{1,0:T(8,128)} %param.9, f32[128,512]{1,0:T(8,128)} %param.10, s32[128,512]{1,0:T(8,128)} %param.12, f32[128,512]{1,0:T(8,128)} %param.11), kind=kLoop, calls=%fused_computation | loop fusion | flops 458752 | bytes 1572864 | tf_op jit(solution)/shard_map/mul | solution.py:393
  1.3 0.1 give_west.1.after_ref
  1.4 0.8 %pad_add_fusion.gauge_ref = f32[5,4,16]{2,1,0:T(4,128)S(1)} fusion(f32[2,4,16]{2,1,0:T(4,128)} %bitcast.7, s32[1,1,8]{2,1,0:T(1,128)} %bitcast.9, s32[1,1,16]{2,1,0:T(1,128)} %bitcast.10, s32[1,1,16]{2,1,0:T(1,128)} %bitcast.11, s32[2,4,16]{2,1,0:T(4,128)} %bitcast.8), kind=kLoop, calls=%fused_computation.2 | loop fusion | flops 1600 | bytes 2464 | tf_op jit(solution)/shard_map/add | solution.py:403
  2.1 0.8 %give_gauges.1 = f32[16,8,128]{2,1,0:T(8,128)} custom-call(f32[5,4,16]{2,1,0:T(4,128)S(1)} %pad_add_fusion.gauge_ref, f32[128,128]{1,0:T(8,128)S(1)} %give_west.1.after_ref), custom_call_target="tpu_custom_call" | custom-call | tf_op jit(solution)/shard_map/give_gauges/pallas_call | solution.py:415
  2.9 7.3 %all-to-all-start = ((f32[16,8,128]{2,1,0:T(8,128)}), f32[16,8,128]{2,1,0:T(8,128)S(1)}, u32[]{:S(2)}, u32[]{:S(2)}) async-start(f32[16,8,128]{2,1,0:T(8,128)} %give_gauges.1), calls=%async_computation | async-start | bytes 131072 | tf_op jit(solution)/shard_map/all_to_all | solution.py:426
  10.3 1.3 %collective-permute-start = (f32[128,128]{1,0:T(8,128)S(1)}, f32[128,128]{1,0:T(8,128)S(1)}, u32[]{:S(2)}, u32[]{:S(2)}) collective-permute-start(f32[128,128]{1,0:T(8,128)S(1)} %give_west.1.after_ref), channel_id=1, source_target_pairs={{4,0},{8,4},{12,8},{5,1},{9,5},{13,9},{6,2},{10,6},{14,10},{7,3},{... | collective-permute-start | bytes 196616 | tf_op jit(solution)/shard_map/ppermute | solution.py:413
  11.6 4.8 %collective-permute-done.right_ref = f32[128,128]{1,0:T(8,128)S(1)} collective-permute-done((f32[128,128]{1,0:T(8,128)S(1)}, f32[128,128]{1,0:T(8,128)S(1)}, u32[]{:S(2)}, u32[]{:S(2)}) %collective-permute-start) | collective-permute-done | bytes 65568 | tf_op jit(solution)/shard_map/ppermute | solution.py:413
  16.3 0.1 give_rows.1
  16.4 3.8 %collective-permute-start.1 = (f32[2,32,640]{2,1,0:T(8,128)S(1)}, f32[2,32,640]{2,1,0:T(8,128)S(1)}, u32[]{:S(2)}, u32[]{:S(2)}) collective-permute-start(f32[2,32,640]{2,1,0:T(8,128)S(1)} %get-tuple-element.11), channel_id=1, source_target_pairs={{0,1},{1,2},{2,3},{4,5},{5,6},{6,7},{8,9},{9,10},{10,11},{12,13},{... | collective-permute-start | bytes 491528 | tf_op jit(solution)/shard_map/ppermute | solution.py:434
  20.2 1.9 %collective-permute-start.2 = (f32[2,32,640]{2,1,0:T(8,128)S(1)}, f32[2,32,640]{2,1,0:T(8,128)S(1)}, u32[]{:S(2)}, u32[]{:S(2)}) collective-permute-start(f32[2,32,640]{2,1,0:T(8,128)S(1)} %get-tuple-element.12), channel_id=1, source_target_pairs={{1,0},{2,1},{3,2},{5,4},{6,5},{7,6},{9,8},{10,9},{11,10},{13,12},{... | collective-permute-start | bytes 491528 | tf_op jit(solution)/shard_map/ppermute | solution.py:435
  22.2 0.0 all-to-all-done.parcel_ref
  22.2 3.4 %force.1.force_ref = f32[17,5,200,128]{3,2,1,0:T(8,128)S(1)} custom-call(f32[16,8,128]{2,1,0:T(8,128)S(1)} %all-to-all-done.parcel_ref), custom_call_target="tpu_custom_call" | custom-call | flops 2013265920 | bytes 7864320 | tf_op jit(solution)/shard_map/force/pallas_call | solution.py:438
  25.6 0.0 collective-permute-done.1.top_ref
  25.6 1.3 %collective-permute-done.2.bottom_ref = f32[2,32,640]{2,1,0:T(8,128)S(1)} collective-permute-done((f32[2,32,640]{2,1,0:T(8,128)S(1)}, f32[2,32,640]{2,1,0:T(8,128)S(1)}, u32[]{:S(2)}, u32[]{:S(2)}) %collective-permute-start.2) | collective-permute-done | bytes 163872 | tf_op jit(solution)/shard_map/ppermute | solution.py:435
  26.9 10.5 %sweep.1 = (f32[128,640]{1,0:T(8,128)S(1)}, f32[4,40,128]{2,1,0:T(8,128)}) custom-call(f32[128,512]{1,0:T(8,128)S(1)} %get-tuple-element.18.keep_ref, f32[128,512]{1,0:T(8,128)S(1)} %get-tuple-element.17.gain_ref, f32[2,32,640]{2,1,0:T(8,128)S(1)} %collective-permute-done.1.top_ref, f32[2,32,640]{2,1,0:T(8,128)S(1)} %collective-permute-done.2.bottom_ref, ...), custom_call_target="tpu_custom_call" | custom-call | tf_op jit(solution)/shard_map/sweep/pallas_call | solution.py:457
  37.4 3.3 %all-to-all-start.1 = ((f32[4,40,128]{2,1,0:T(8,128)}), f32[4,40,128]{2,1,0:T(8,128)S(1)}, u32[]{:S(2)}, u32[]{:S(2)}) async-start(f32[4,40,128]{2,1,0:T(8,128)} %get-tuple-element.16), calls=%async_computation.1 | async-start | bytes 163840 | tf_op jit(solution)/shard_map/all_to_all | solution.py:426
  40.7 1.0 %smooth.1 = (f32[128,512]{1,0:T(8,128)S(1)}, f32[160,512]{1,0:T(8,128)S(1)}) custom-call(f32[128,640]{1,0:T(8,128)S(1)} %get-tuple-element.13.grad_ref), custom_call_target="tpu_custom_call" | custom-call | flops 402653184 | bytes 524288 | tf_op jit(solution)/shard_map/smooth/pallas_call | solution.py:468
  41.8 3.6 %all-to-all-done.1 = f32[4,40,128]{2,1,0:T(8,128)S(1)} async-done(((f32[4,40,128]{2,1,0:T(8,128)}), f32[4,40,128]{2,1,0:T(8,128)S(1)}, u32[]{:S(2)}, u32[]{:S(2)}) %all-to-all-start.1) | async-done | bytes 81952 | tf_op jit(solution)/shard_map/all_to_all | solution.py:426
  45.3 1.1 %finish.1 = f32[128,512]{1,0:T(8,128)} custom-call(f32[128,512]{1,0:T(8,128)S(1)} %get-tuple-element.14.own_ref, f32[160,512]{1,0:T(8,128)S(1)} %get-tuple-element.15.weights_ref, f32[160,128]{1,0:T(8,128)S(1)} %bitcast.6), custom_call_target="tpu_custom_call" | custom-call | tf_op jit(solution)/shard_map/finish/pallas_call | solution.py:479
Async XLA Ops:
  2.9 19.2 %all-to-all-start = ((f32[16,8,128]{2,1,0:T(8,128)}), f32[16,8,128]{2,1,0:T(8,128)S(1)}, u32[]{:S(2)}, u32[]{:S(2)}) async-start(f32[16,8,128]{2,1,0:T(8,128)} %give_gauges.1), calls=%async_computation | async-start | bytes 131072 | tf_op jit(solution)/shard_map/all_to_all | solution.py:426
  10.3 6.1 %collective-permute-start = (f32[128,128]{1,0:T(8,128)S(1)}, f32[128,128]{1,0:T(8,128)S(1)}, u32[]{:S(2)}, u32[]{:S(2)}) collective-permute-start(f32[128,128]{1,0:T(8,128)S(1)} %give_west.1.after_ref), channel_id=1, source_target_pairs={{4,0},{8,4},{12,8},{5,1},{9,5},{13,9},{6,2},{10,6},{14,10},{7,3},{... | collective-permute-start | bytes 196616 | tf_op jit(solution)/shard_map/ppermute | solution.py:413
  16.4 9.2 %collective-permute-start.1 = (f32[2,32,640]{2,1,0:T(8,128)S(1)}, f32[2,32,640]{2,1,0:T(8,128)S(1)}, u32[]{:S(2)}, u32[]{:S(2)}) collective-permute-start(f32[2,32,640]{2,1,0:T(8,128)S(1)} %get-tuple-element.11), channel_id=1, source_target_pairs={{0,1},{1,2},{2,3},{4,5},{5,6},{6,7},{8,9},{9,10},{10,11},{12,13},{... | collective-permute-start | bytes 491528 | tf_op jit(solution)/shard_map/ppermute | solution.py:434
  20.2 6.6 %collective-permute-start.2 = (f32[2,32,640]{2,1,0:T(8,128)S(1)}, f32[2,32,640]{2,1,0:T(8,128)S(1)}, u32[]{:S(2)}, u32[]{:S(2)}) collective-permute-start(f32[2,32,640]{2,1,0:T(8,128)S(1)} %get-tuple-element.12), channel_id=1, source_target_pairs={{1,0},{2,1},{3,2},{5,4},{6,5},{7,6},{9,8},{10,9},{11,10},{13,12},{... | collective-permute-start | bytes 491528 | tf_op jit(solution)/shard_map/ppermute | solution.py:435
  37.4 7.9 %all-to-all-start.1 = ((f32[4,40,128]{2,1,0:T(8,128)}), f32[4,40,128]{2,1,0:T(8,128)S(1)}, u32[]{:S(2)}, u32[]{:S(2)}) async-start(f32[4,40,128]{2,1,0:T(8,128)} %get-tuple-element.16), calls=%async_computation.1 | async-start | bytes 163840 | tf_op jit(solution)/shard_map/all_to_all | solution.py:426

commit v12 on v11

--- a/solution.py
+++ b/solution.py
@@ -367,6 +367,10 @@
     return jax.ShapeDtypeStruct(shape, jnp.float32)
 
 
+def hint(megabytes):
+    return pl.CostEstimate(flops=0, bytes_accessed=megabytes * 1000 * 1000, transcendentals=0)
+
+
 def spaced(rows):
     return 8 * (rows // 8 | 1)
 
@@ -419,6 +423,7 @@
         out_specs=vmem(1)[0],
         scratch_shapes=[pltpu.VMEM((24, LANES), jnp.float32)],
         compiler_params=params,
+        cost_estimate=hint(10),
         name="give_gauges",
     )(gauges, west)
 
@@ -429,7 +434,7 @@
 
     south, north = pl.pallas_call(
         functools.partial(give_rows, halo), out_shape=(f32(2, halo, planes * LANES),) * 2, in_specs=vmem(3),
-        out_specs=tuple(vmem(2)), compiler_params=params, name="give_rows",
+        out_specs=tuple(vmem(2)), compiler_params=params, cost_estimate=hint(40), name="give_rows",
     )(keep, gain, right)
     top = lax.ppermute(south, ROW_AXES, [(i, i + 1) for i in range(row_tiles - 1)])
     bottom = lax.ppermute(north, ROW_AXES, [(i + 1, i) for i in range(row_tiles - 1)])

time: 46.8 us -> 46.8 us (level)
  no operation moved by 1% of the time
where the time goes in v12:
time: 46.8 us; the launch traced here: 46.4 us
  starting transfers between devices  17.6 us (38%)
  Pallas kernels  17.1 us (37%)
  waiting for transfers between devices  9.63 us (21%)
  other arithmetic  2.05 us (4%)
    all_to_all x2, starting transfers between devices, exchange(): return lax.all_to_all(array, axes, split_axis=0, concat_axis=0, tiled=True)  10.6 us
    pallas_call x1, Pallas kernels, local(): pl.pallas_call(functools.partial(sweep, steps), out_shape=(f32(height, pl...  10.5 us
    ppermute x1, waiting for transfers between devices, local(): right = lax.ppermute(west, 'lon', [(i + 1, i) for i in range(lons - 1)])  4.79 us
    ppermute x1, starting transfers between devices, local(): lax.ppermute(south, ROW_AXES, [(i, i + 1) for i in range(row_tiles - 1)])  3.8 us
    all_to_all x2, waiting for transfers between devices, exchange(): return lax.all_to_all(array, axes, split_axis=0, concat_axis=0, tiled=True)  3.57 us
    pallas_call x1, Pallas kernels, local(): pl.pallas_call(functools.partial(force, steps, halo, height, width), out_...  3.41 us
    ppermute x1, starting transfers between devices, local(): lax.ppermute(north, ROW_AXES, [(i + 1, i) for i in range(row_tiles - 1)])  1.92 us
    mul x1, other arithmetic, local(): (courant * 0.5) ** 2 * jnp.maximum(depth + surface, depth_floor) * keep  1.29 us
  transfers between devices with their start and end apart: 5, of which 3 were waited for; matrix products, arithmetic and copies ran while one was open for 0% of the time, Pallas kernels for 10%

profile of v12, /device:TPU:1, one launch (start us, length us, event | category | flops | bytes accessed | tf_op | source)
XLA Modules:
  0.0 46.4 jit_solution(11393134636773739936)
XLA Ops:
  0.0 1.3 %multiply_multiply_fusion = (f32[128,512]{1,0:T(8,128)S(1)}, f32[128,512]{1,0:T(8,128)S(1)}) fusion(f32[128,512]{1,0:T(8,128)} %param.9, f32[128,512]{1,0:T(8,128)} %param.10, s32[128,512]{1,0:T(8,128)} %param.12, f32[128,512]{1,0:T(8,128)} %param.11), kind=kLoop, calls=%fused_computation | loop fusion | flops 458752 | bytes 1572864 | tf_op jit(solution)/shard_map/mul | solution.py:397
  1.3 0.1 give_west.1.after_ref
  1.4 0.8 %pad_add_fusion.gauge_ref = f32[5,4,16]{2,1,0:T(4,128)S(1)} fusion(f32[2,4,16]{2,1,0:T(4,128)} %bitcast.7, s32[1,1,8]{2,1,0:T(1,128)} %bitcast.9, s32[1,1,16]{2,1,0:T(1,128)} %bitcast.10, s32[1,1,16]{2,1,0:T(1,128)} %bitcast.11, s32[2,4,16]{2,1,0:T(4,128)} %bitcast.8), kind=kLoop, calls=%fused_computation.2 | loop fusion | flops 1600 | bytes 2464 | tf_op jit(solution)/shard_map/add | solution.py:407
  2.1 0.8 %give_gauges.1 = f32[16,8,128]{2,1,0:T(8,128)} custom-call(f32[5,4,16]{2,1,0:T(4,128)S(1)} %pad_add_fusion.gauge_ref, f32[128,128]{1,0:T(8,128)S(1)} %give_west.1.after_ref), custom_call_target="tpu_custom_call" | custom-call | bytes 10000000 | tf_op jit(solution)/shard_map/give_gauges/pallas_call | solution.py:419
  2.9 7.3 %all-to-all-start = ((f32[16,8,128]{2,1,0:T(8,128)}), f32[16,8,128]{2,1,0:T(8,128)S(1)}, u32[]{:S(2)}, u32[]{:S(2)}) async-start(f32[16,8,128]{2,1,0:T(8,128)} %give_gauges.1), calls=%async_computation | async-start | bytes 131072 | tf_op jit(solution)/shard_map/all_to_all | solution.py:431
  10.3 1.3 %collective-permute-start = (f32[128,128]{1,0:T(8,128)S(1)}, f32[128,128]{1,0:T(8,128)S(1)}, u32[]{:S(2)}, u32[]{:S(2)}) collective-permute-start(f32[128,128]{1,0:T(8,128)S(1)} %give_west.1.after_ref), channel_id=1, source_target_pairs={{4,0},{8,4},{12,8},{5,1},{9,5},{13,9},{6,2},{10,6},{14,10},{7,3},{... | collective-permute-start | bytes 196616 | tf_op jit(solution)/shard_map/ppermute | solution.py:417
  11.6 4.8 %collective-permute-done.right_ref = f32[128,128]{1,0:T(8,128)S(1)} collective-permute-done((f32[128,128]{1,0:T(8,128)S(1)}, f32[128,128]{1,0:T(8,128)S(1)}, u32[]{:S(2)}, u32[]{:S(2)}) %collective-permute-start) | collective-permute-done | bytes 65568 | tf_op jit(solution)/shard_map/ppermute | solution.py:417
  16.3 0.1 give_rows.1
  16.4 3.8 %collective-permute-start.1 = (f32[2,32,640]{2,1,0:T(8,128)S(1)}, f32[2,32,640]{2,1,0:T(8,128)S(1)}, u32[]{:S(2)}, u32[]{:S(2)}) collective-permute-start(f32[2,32,640]{2,1,0:T(8,128)S(1)} %get-tuple-element.11), channel_id=1, source_target_pairs={{0,1},{1,2},{2,3},{4,5},{5,6},{6,7},{8,9},{9,10},{10,11},{12,13},{... | collective-permute-start | bytes 491528 | tf_op jit(solution)/shard_map/ppermute | solution.py:439
  20.2 1.9 %collective-permute-start.2 = (f32[2,32,640]{2,1,0:T(8,128)S(1)}, f32[2,32,640]{2,1,0:T(8,128)S(1)}, u32[]{:S(2)}, u32[]{:S(2)}) collective-permute-start(f32[2,32,640]{2,1,0:T(8,128)S(1)} %get-tuple-element.12), channel_id=1, source_target_pairs={{1,0},{2,1},{3,2},{5,4},{6,5},{7,6},{9,8},{10,9},{11,10},{13,12},{... | collective-permute-start | bytes 491528 | tf_op jit(solution)/shard_map/ppermute | solution.py:440
  22.2 0.0 all-to-all-done.parcel_ref
  22.2 3.4 %force.1.force_ref = f32[17,5,200,128]{3,2,1,0:T(8,128)S(1)} custom-call(f32[16,8,128]{2,1,0:T(8,128)S(1)} %all-to-all-done.parcel_ref), custom_call_target="tpu_custom_call" | custom-call | flops 2013265920 | bytes 7864320 | tf_op jit(solution)/shard_map/force/pallas_call | solution.py:443
  25.6 0.0 collective-permute-done.1.top_ref
  25.6 1.3 %collective-permute-done.2.bottom_ref = f32[2,32,640]{2,1,0:T(8,128)S(1)} collective-permute-done((f32[2,32,640]{2,1,0:T(8,128)S(1)}, f32[2,32,640]{2,1,0:T(8,128)S(1)}, u32[]{:S(2)}, u32[]{:S(2)}) %collective-permute-start.2) | collective-permute-done | bytes 163872 | tf_op jit(solution)/shard_map/ppermute | solution.py:440
  26.9 10.5 %sweep.1 = (f32[128,640]{1,0:T(8,128)S(1)}, f32[4,40,128]{2,1,0:T(8,128)}) custom-call(f32[128,512]{1,0:T(8,128)S(1)} %get-tuple-element.18.keep_ref, f32[128,512]{1,0:T(8,128)S(1)} %get-tuple-element.17.gain_ref, f32[2,32,640]{2,1,0:T(8,128)S(1)} %collective-permute-done.1.top_ref, f32[2,32,640]{2,1,0:T(8,128)S(1)} %collective-permute-done.2.bottom_ref, ...), custom_call_target="tpu_custom_call" | custom-call | tf_op jit(solution)/shard_map/sweep/pallas_call | solution.py:462
  37.4 3.3 %all-to-all-start.1 = ((f32[4,40,128]{2,1,0:T(8,128)}), f32[4,40,128]{2,1,0:T(8,128)S(1)}, u32[]{:S(2)}, u32[]{:S(2)}) async-start(f32[4,40,128]{2,1,0:T(8,128)} %get-tuple-element.16), calls=%async_computation.1 | async-start | bytes 163840 | tf_op jit(solution)/shard_map/all_to_all | solution.py:431
  40.7 1.0 %smooth.1 = (f32[128,512]{1,0:T(8,128)S(1)}, f32[160,512]{1,0:T(8,128)S(1)}) custom-call(f32[128,640]{1,0:T(8,128)S(1)} %get-tuple-element.13.grad_ref), custom_call_target="tpu_custom_call" | custom-call | flops 402653184 | bytes 524288 | tf_op jit(solution)/shard_map/smooth/pallas_call | solution.py:473
  41.8 3.6 %all-to-all-done.1 = f32[4,40,128]{2,1,0:T(8,128)S(1)} async-done(((f32[4,40,128]{2,1,0:T(8,128)}), f32[4,40,128]{2,1,0:T(8,128)S(1)}, u32[]{:S(2)}, u32[]{:S(2)}) %all-to-all-start.1) | async-done | bytes 81952 | tf_op jit(solution)/shard_map/all_to_all | solution.py:431
  45.3 1.1 %finish.1 = f32[128,512]{1,0:T(8,128)} custom-call(f32[128,512]{1,0:T(8,128)S(1)} %get-tuple-element.14.own_ref, f32[160,512]{1,0:T(8,128)S(1)} %get-tuple-element.15.weights_ref, f32[160,128]{1,0:T(8,128)S(1)} %bitcast.6), custom_call_target="tpu_custom_call" | custom-call | tf_op jit(solution)/shard_map/finish/pallas_call | solution.py:484
Async XLA Ops:
  2.9 19.2 %all-to-all-start = ((f32[16,8,128]{2,1,0:T(8,128)}), f32[16,8,128]{2,1,0:T(8,128)S(1)}, u32[]{:S(2)}, u32[]{:S(2)}) async-start(f32[16,8,128]{2,1,0:T(8,128)} %give_gauges.1), calls=%async_computation | async-start | bytes 131072 | tf_op jit(solution)/shard_map/all_to_all | solution.py:431
  10.3 6.1 %collective-permute-start = (f32[128,128]{1,0:T(8,128)S(1)}, f32[128,128]{1,0:T(8,128)S(1)}, u32[]{:S(2)}, u32[]{:S(2)}) collective-permute-start(f32[128,128]{1,0:T(8,128)S(1)} %give_west.1.after_ref), channel_id=1, source_target_pairs={{4,0},{8,4},{12,8},{5,1},{9,5},{13,9},{6,2},{10,6},{14,10},{7,3},{... | collective-permute-start | bytes 196616 | tf_op jit(solution)/shard_map/ppermute | solution.py:417
  16.4 9.2 %collective-permute-start.1 = (f32[2,32,640]{2,1,0:T(8,128)S(1)}, f32[2,32,640]{2,1,0:T(8,128)S(1)}, u32[]{:S(2)}, u32[]{:S(2)}) collective-permute-start(f32[2,32,640]{2,1,0:T(8,128)S(1)} %get-tuple-element.11), channel_id=1, source_target_pairs={{0,1},{1,2},{2,3},{4,5},{5,6},{6,7},{8,9},{9,10},{10,11},{12,13},{... | collective-permute-start | bytes 491528 | tf_op jit(solution)/shard_map/ppermute | solution.py:439
  20.2 6.6 %collective-permute-start.2 = (f32[2,32,640]{2,1,0:T(8,128)S(1)}, f32[2,32,640]{2,1,0:T(8,128)S(1)}, u32[]{:S(2)}, u32[]{:S(2)}) collective-permute-start(f32[2,32,640]{2,1,0:T(8,128)S(1)} %get-tuple-element.12), channel_id=1, source_target_pairs={{1,0},{2,1},{3,2},{5,4},{6,5},{7,6},{9,8},{10,9},{11,10},{13,12},{... | collective-permute-start | bytes 491528 | tf_op jit(solution)/shard_map/ppermute | solution.py:440
  37.4 7.9 %all-to-all-start.1 = ((f32[4,40,128]{2,1,0:T(8,128)}), f32[4,40,128]{2,1,0:T(8,128)S(1)}, u32[]{:S(2)}, u32[]{:S(2)}) async-start(f32[4,40,128]{2,1,0:T(8,128)} %get-tuple-element.16), calls=%async_computation.1 | async-start | bytes 163840 | tf_op jit(solution)/shard_map/all_to_all | solution.py:431

commit v13 on v12

--- a/solution.py
+++ b/solution.py
@@ -43,8 +43,10 @@
 
 
 def give_west(reach, keep_ref, gain_ref, west_ref):
-    lower = lane_iota(west_ref.shape[0]) < reach
-    west_ref[...] = jnp.where(lower, keep_ref[:, :LANES], roll_lanes(gain_ref[:, :LANES], reach))
+    lower = lane_iota(west_ref.shape[1]) < reach
+    west_ref[0] = jnp.where(lower, keep_ref[:, :LANES], roll_lanes(gain_ref[:, :LANES], reach))
+    for spare in range(1, west_ref.shape[0]):
+        west_ref[spare] = jnp.zeros(west_ref.shape[1:], jnp.float32)
 
 
 def give_rows(halo, keep_ref, gain_ref, right_ref, south_ref, north_ref):
@@ -53,7 +55,7 @@
     for goal, rows in ((south_ref, slice(height - halo, height)), (north_ref, slice(0, halo))):
         for kind, source in enumerate((keep_ref, gain_ref)):
             goal[kind, :, :width] = source[rows, :]
-            goal[kind, :, width:] = jnp.where(lower, roll_lanes(right_ref[rows, :], -2 * halo * kind), 0.0)
+            goal[kind, :, width:] = jnp.where(lower, roll_lanes(right_ref[0, rows, :], -2 * halo * kind), 0.0)
 
 
 def give_gauges(height, width, blocks, samples, coast_count, gauge_ref, after_ref, parcel_ref, block_ref):
@@ -220,7 +222,7 @@
             if c < inner:
                 plain[c, halo : halo + height, :] = source[:, cols]
         lower = lane_iota(height) < reach
-        plain[inner, halo : halo + height, :] = jnp.where(lower, roll_lanes(right_ref[...], -reach * kind), 0.0)
+        plain[inner, halo : halo + height, :] = jnp.where(lower, roll_lanes(right_ref[0], -reach * kind), 0.0)
         for q in range(blocks):
             values = [plain[c, pl.ds(q, 8, stride=blocks), :] for c in range(planes)]
             shifted = shift_from(values, 1, lanes8)
@@ -311,7 +313,7 @@
         for c in every:
             cols = slice(c * LANES, (c + 1) * LANES)
             value = a[c, pl.ds(8 * q + s, 8, stride=8), :]
-            wet = keep_ref[r : r + 8, cols] if c < inner else right_ref[r : r + 8, :]
+            wet = keep_ref[r : r + 8, cols] if c < inner else right_ref[0, r : r + 8, :]
             if c == 0:
                 wet = jnp.where(lanes8 >= start, wet, 0.0)
             if c == inner:
@@ -411,7 +413,7 @@
         + put(coastal_tiles.reshape(1, 1, coast_count), 2 * blocks, 2)
     ).astype(jnp.float32) + put(jnp.transpose(gauge_resid, (1, 2, 0)), blocks, 0)
     west = pl.pallas_call(
-        functools.partial(give_west, 2 * halo), out_shape=f32(height, LANES), in_specs=vmem(2), out_specs=vmem(1)[0],
+        functools.partial(give_west, 2 * halo), out_shape=f32(4, height, LANES), in_specs=vmem(2), out_specs=vmem(1)[0],
         compiler_params=params, name="give_west",
     )(keep, gain)
     right = lax.ppermute(west, "lon", [(i + 1, i) for i in range(lons - 1)])

time: 46.8 us -> 44.1 us (0.942)
  the two profiles are of different devices: /device:TPU:1 before, /device:TPU:0 now
where the time goes in v13:
time: 44.1 us; the launch traced here: 43.8 us
  Pallas kernels  17.1 us (39%)
  starting transfers between devices  16.6 us (38%)
  waiting for transfers between devices  7.9 us (18%)
  other arithmetic  2.05 us (5%)
    all_to_all x2, starting transfers between devices, exchange(): return lax.all_to_all(array, axes, split_axis=0, concat_axis=0, tiled=True)  11.7 us
    pallas_call x1, Pallas kernels, local(): pl.pallas_call(functools.partial(sweep, steps), out_shape=(f32(height, pl...  10.5 us
    all_to_all x2, waiting for transfers between devices, exchange(): return lax.all_to_all(array, axes, split_axis=0, concat_axis=0, tiled=True)  7.89 us
    pallas_call x1, Pallas kernels, local(): pl.pallas_call(functools.partial(force, steps, halo, height, width), out_...  3.41 us
    ppermute x1, starting transfers between devices, local(): lax.ppermute(south, ROW_AXES, [(i, i + 1) for i in range(row_tiles - 1)])  2.32 us
    ppermute x1, starting transfers between devices, local(): right = lax.ppermute(west, 'lon', [(i + 1, i) for i in range(lons - 1)])  1.29 us
    ppermute x1, starting transfers between devices, local(): lax.ppermute(north, ROW_AXES, [(i + 1, i) for i in range(row_tiles - 1)])  1.29 us
    mul x1, other arithmetic, local(): (courant * 0.5) ** 2 * jnp.maximum(depth + surface, depth_floor) * keep  1.29 us
  transfers between devices with their start and end apart: 5, of which 2 were waited for; matrix products, arithmetic and copies ran while one was open for 2% of the time, Pallas kernels for 12%

profile of v13, /device:TPU:0, one launch (start us, length us, event | category | flops | bytes accessed | tf_op | source)
XLA Modules:
  0.0 43.8 jit_solution(807297789111007792)
XLA Ops:
  0.0 1.3 %multiply_multiply_fusion = (f32[128,512]{1,0:T(8,128)S(1)}, f32[128,512]{1,0:T(8,128)S(1)}) fusion(f32[128,512]{1,0:T(8,128)} %param.9, f32[128,512]{1,0:T(8,128)} %param.10, s32[128,512]{1,0:T(8,128)} %param.12, f32[128,512]{1,0:T(8,128)} %param.11), kind=kLoop, calls=%fused_computation | loop fusion | flops 458752 | bytes 1572864 | tf_op jit(solution)/shard_map/mul | solution.py:399
  1.3 0.1 give_west.1.after_ref
  1.4 1.3 %collective-permute-start = (f32[4,128,128]{2,1,0:T(8,128)S(1)}, f32[4,128,128]{2,1,0:T(8,128)S(1)}, u32[]{:S(2)}, u32[]{:S(2)}) collective-permute-start(f32[4,128,128]{2,1,0:T(8,128)S(1)} %give_west.1.after_ref), channel_id=1, source_target_pairs={{4,0},{8,4},{12,8},{5,1},{9,5},{13,9},{6,2},{10,6},{14,10},{7,3},{... | collective-permute-start | bytes 786440 | tf_op jit(solution)/shard_map/ppermute | solution.py:419
  2.7 0.8 %pad_add_fusion.gauge_ref = f32[5,4,16]{2,1,0:T(4,128)S(1)} fusion(f32[2,4,16]{2,1,0:T(4,128)} %bitcast.7, s32[1,1,8]{2,1,0:T(1,128)} %bitcast.9, s32[1,1,16]{2,1,0:T(1,128)} %bitcast.10, s32[1,1,16]{2,1,0:T(1,128)} %bitcast.11, s32[2,4,16]{2,1,0:T(4,128)} %bitcast.8), kind=kLoop, calls=%fused_computation.2 | loop fusion | flops 1600 | bytes 2464 | tf_op jit(solution)/shard_map/add | solution.py:409
  3.4 0.8 %give_gauges.1 = f32[16,8,128]{2,1,0:T(8,128)} custom-call(f32[5,4,16]{2,1,0:T(4,128)S(1)} %pad_add_fusion.gauge_ref, f32[4,128,128]{2,1,0:T(8,128)S(1)} %give_west.1.after_ref), custom_call_target="tpu_custom_call" | custom-call | bytes 10000000 | tf_op jit(solution)/shard_map/give_gauges/pallas_call | solution.py:421
  4.2 8.4 %all-to-all-start = ((f32[16,8,128]{2,1,0:T(8,128)}), f32[16,8,128]{2,1,0:T(8,128)S(1)}, u32[]{:S(2)}, u32[]{:S(2)}) async-start(f32[16,8,128]{2,1,0:T(8,128)} %give_gauges.1), calls=%async_computation | async-start | bytes 131072 | tf_op jit(solution)/shard_map/all_to_all | solution.py:433
  12.7 0.0 collective-permute-done.right_ref
  12.7 0.1 give_rows.1
  12.8 2.3 %collective-permute-start.1 = (f32[2,32,640]{2,1,0:T(8,128)S(1)}, f32[2,32,640]{2,1,0:T(8,128)S(1)}, u32[]{:S(2)}, u32[]{:S(2)}) collective-permute-start(f32[2,32,640]{2,1,0:T(8,128)S(1)} %get-tuple-element.11), channel_id=1, source_target_pairs={{0,1},{1,2},{2,3},{4,5},{5,6},{6,7},{8,9},{9,10},{10,11},{12,13},{... | collective-permute-start | bytes 491528 | tf_op jit(solution)/shard_map/ppermute | solution.py:441
  15.1 1.3 %collective-permute-start.2 = (f32[2,32,640]{2,1,0:T(8,128)S(1)}, f32[2,32,640]{2,1,0:T(8,128)S(1)}, u32[]{:S(2)}, u32[]{:S(2)}) collective-permute-start(f32[2,32,640]{2,1,0:T(8,128)S(1)} %get-tuple-element.12), channel_id=1, source_target_pairs={{1,0},{2,1},{3,2},{5,4},{6,5},{7,6},{9,8},{10,9},{11,10},{13,12},{... | collective-permute-start | bytes 491528 | tf_op jit(solution)/shard_map/ppermute | solution.py:442
  16.4 3.2 %all-to-all-done.parcel_ref = f32[16,8,128]{2,1,0:T(8,128)S(1)} async-done(((f32[16,8,128]{2,1,0:T(8,128)}), f32[16,8,128]{2,1,0:T(8,128)S(1)}, u32[]{:S(2)}, u32[]{:S(2)}) %all-to-all-start) | async-done | bytes 65568 | tf_op jit(solution)/shard_map/all_to_all | solution.py:433
  19.6 3.4 %force.1.force_ref = f32[17,5,200,128]{3,2,1,0:T(8,128)S(1)} custom-call(f32[16,8,128]{2,1,0:T(8,128)S(1)} %all-to-all-done.parcel_ref), custom_call_target="tpu_custom_call" | custom-call | flops 2013265920 | bytes 7864320 | tf_op jit(solution)/shard_map/force/pallas_call | solution.py:445
  23.0 0.0 collective-permute-done.1.top_ref
  23.0 0.0 collective-permute-done.2.bottom_ref
  23.0 10.5 %sweep.1 = (f32[128,640]{1,0:T(8,128)S(1)}, f32[4,40,128]{2,1,0:T(8,128)}) custom-call(f32[128,512]{1,0:T(8,128)S(1)} %get-tuple-element.18.keep_ref, f32[128,512]{1,0:T(8,128)S(1)} %get-tuple-element.17.gain_ref, f32[2,32,640]{2,1,0:T(8,128)S(1)} %collective-permute-done.1.top_ref, f32[2,32,640]{2,1,0:T(8,128)S(1)} %collective-permute-done.2.bottom_ref, ...), custom_call_target="tpu_custom_call" | custom-call | tf_op jit(solution)/shard_map/sweep/pallas_call | solution.py:464
  33.6 3.3 %all-to-all-start.1 = ((f32[4,40,128]{2,1,0:T(8,128)}), f32[4,40,128]{2,1,0:T(8,128)S(1)}, u32[]{:S(2)}, u32[]{:S(2)}) async-start(f32[4,40,128]{2,1,0:T(8,128)} %get-tuple-element.16), calls=%async_computation.1 | async-start | bytes 163840 | tf_op jit(solution)/shard_map/all_to_all | solution.py:433
  36.9 1.0 %smooth.1 = (f32[128,512]{1,0:T(8,128)S(1)}, f32[160,512]{1,0:T(8,128)S(1)}) custom-call(f32[128,640]{1,0:T(8,128)S(1)} %get-tuple-element.13.grad_ref), custom_call_target="tpu_custom_call" | custom-call | flops 402653184 | bytes 524288 | tf_op jit(solution)/shard_map/smooth/pallas_call | solution.py:475
  37.9 4.7 %all-to-all-done.1 = f32[4,40,128]{2,1,0:T(8,128)S(1)} async-done(((f32[4,40,128]{2,1,0:T(8,128)}), f32[4,40,128]{2,1,0:T(8,128)S(1)}, u32[]{:S(2)}, u32[]{:S(2)}) %all-to-all-start.1) | async-done | bytes 81952 | tf_op jit(solution)/shard_map/all_to_all | solution.py:433
  42.6 1.1 %finish.1 = f32[128,512]{1,0:T(8,128)} custom-call(f32[128,512]{1,0:T(8,128)S(1)} %get-tuple-element.14.own_ref, f32[160,512]{1,0:T(8,128)S(1)} %get-tuple-element.15.weights_ref, f32[160,128]{1,0:T(8,128)S(1)} %bitcast.6), custom_call_target="tpu_custom_call" | custom-call | tf_op jit(solution)/shard_map/finish/pallas_call | solution.py:486
Async XLA Ops:
  1.4 11.3 %collective-permute-start = (f32[4,128,128]{2,1,0:T(8,128)S(1)}, f32[4,128,128]{2,1,0:T(8,128)S(1)}, u32[]{:S(2)}, u32[]{:S(2)}) collective-permute-start(f32[4,128,128]{2,1,0:T(8,128)S(1)} %give_west.1.after_ref), channel_id=1, source_target_pairs={{4,0},{8,4},{12,8},{5,1},{9,5},{13,9},{6,2},{10,6},{14,10},{7,3},{... | collective-permute-start | bytes 786440 | tf_op jit(solution)/shard_map/ppermute | solution.py:419
  4.2 15.3 %all-to-all-start = ((f32[16,8,128]{2,1,0:T(8,128)}), f32[16,8,128]{2,1,0:T(8,128)S(1)}, u32[]{:S(2)}, u32[]{:S(2)}) async-start(f32[16,8,128]{2,1,0:T(8,128)} %give_gauges.1), calls=%async_computation | async-start | bytes 131072 | tf_op jit(solution)/shard_map/all_to_all | solution.py:433
  12.8 10.2 %collective-permute-start.1 = (f32[2,32,640]{2,1,0:T(8,128)S(1)}, f32[2,32,640]{2,1,0:T(8,128)S(1)}, u32[]{:S(2)}, u32[]{:S(2)}) collective-permute-start(f32[2,32,640]{2,1,0:T(8,128)S(1)} %get-tuple-element.11), channel_id=1, source_target_pairs={{0,1},{1,2},{2,3},{4,5},{5,6},{6,7},{8,9},{9,10},{10,11},{12,13},{... | collective-permute-start | bytes 491528 | tf_op jit(solution)/shard_map/ppermute | solution.py:441
  15.1 7.9 %collective-permute-start.2 = (f32[2,32,640]{2,1,0:T(8,128)S(1)}, f32[2,32,640]{2,1,0:T(8,128)S(1)}, u32[]{:S(2)}, u32[]{:S(2)}) collective-permute-start(f32[2,32,640]{2,1,0:T(8,128)S(1)} %get-tuple-element.12), channel_id=1, source_target_pairs={{1,0},{2,1},{3,2},{5,4},{6,5},{7,6},{9,8},{10,9},{11,10},{13,12},{... | collective-permute-start | bytes 491528 | tf_op jit(solution)/shard_map/ppermute | solution.py:442
  33.6 9.1 %all-to-all-start.1 = ((f32[4,40,128]{2,1,0:T(8,128)}), f32[4,40,128]{2,1,0:T(8,128)S(1)}, u32[]{:S(2)}, u32[]{:S(2)}) async-start(f32[4,40,128]{2,1,0:T(8,128)} %get-tuple-element.16), calls=%async_computation.1 | async-start | bytes 163840 | tf_op jit(solution)/shard_map/all_to_all | solution.py:433

commit v14 on v13

--- a/solution.py
+++ b/solution.py
@@ -12,6 +12,7 @@
 LANES = 128
 SEG = 32
 LEVELS = 4
+BEHIND = 2
 
 courant = 0.45
 depth_floor = 0.1
@@ -49,10 +50,12 @@
         west_ref[spare] = jnp.zeros(west_ref.shape[1:], jnp.float32)
 
 
-def give_rows(halo, keep_ref, gain_ref, right_ref, south_ref, north_ref):
+def give_rows(halo, keep_ref, gain_ref, right_ref, far_ref, near_ref):
     height, width = keep_ref.shape
     lower = lane_iota(halo) < 2 * halo
-    for goal, rows in ((south_ref, slice(height - halo, height)), (north_ref, slice(0, halo))):
+    odd = my_place()[0] & 1
+    for goal, south in ((far_ref, odd), (near_ref, 1 - odd)):
+        rows = pl.ds(pl.multiple_of(south * (height - halo), halo), halo)
         for kind, source in enumerate((keep_ref, gain_ref)):
             goal[kind, :, :width] = source[rows, :]
             goal[kind, :, width:] = jnp.where(lower, roll_lanes(right_ref[0, rows, :], -2 * halo * kind), 0.0)
@@ -192,7 +195,7 @@
 
 
 def sweep(
-    steps, keep_ref, gain_ref, top_ref, bottom_ref, right_ref, force_ref,
+    steps, keep_ref, gain_ref, far_ref, near_ref, right_ref, force_ref,
     grad_ref, sums_ref,
     a, fx, fy, keep_x, gain_x, keep_y, gain_y, plain,
 ):
@@ -206,6 +209,7 @@
     reach = 2 * halo
     has_top, has_bottom = my_row > 0, my_row < row_tiles - 1
     has_right = my_lon < lons - 1
+    odd = (jnp.zeros((halo, LANES), jnp.int32) + (my_row & 1)) == 1
     lanes8 = lane_iota(8)
 
     def up(value):
@@ -217,8 +221,9 @@
     for kind, (source, by_x, by_y) in enumerate(((keep_ref, keep_x, keep_y), (gain_ref, gain_x, gain_y))):
         for c in range(planes):
             cols = slice(c * LANES, (c + 1) * LANES)
-            plain[c, 0:halo, :] = top_ref[kind, :, cols]
-            plain[c, halo + height : rows_all, :] = bottom_ref[kind, :, cols]
+            far, near = far_ref[kind, :, cols], near_ref[kind, :, cols]
+            plain[c, 0:halo, :] = jnp.where(odd, near, far)
+            plain[c, halo + height : rows_all, :] = jnp.where(odd, far, near)
             if c < inner:
                 plain[c, halo : halo + height, :] = source[:, cols]
         lower = lane_iota(height) < reach
@@ -244,7 +249,7 @@
 
     def step(index, carry):
         level = jnp.where(index < steps - 1, steps - 2 - index, steps)
-        near, ahead, new_y, total, behind, push = {}, {}, {}, {}, {}, {}
+        near, ahead, new_y, total, behind = {}, {}, {}, {}, {}
 
         def rows(q):
             return slice(8 * q, 8 * q + 8)
@@ -253,7 +258,6 @@
             near[q] = [a[c, rows(q % blocks), :] for c in every]
             if q < blocks:
                 ahead[q] = [roll_lanes(value, -2) for value in near[q]]
-                push[q] = [force_ref[level, c, rows(q), :] for c in every]
             else:
                 near[q] = [up(value) for value in near[q]]
 
@@ -272,7 +276,8 @@
             ]
             behind[q] = [roll_lanes(value, 2) for value in new_x]
             before = new_y[q - 2] if q >= 2 else [down(fy[c, rows(q - 2 + blocks), :]) for c in every]
-            total[q] = [(near[q][c] + push[q][c]) + (new_y[q][c] - before[c]) + new_x[c] for c in every]
+            push = [force_ref[level, c, rows(q), :] for c in every]
+            total[q] = [(near[q][c] + push[c]) + (new_y[q][c] - before[c]) + new_x[c] for c in every]
             for c in every:
                 fx[c, rows(q), :] = new_x[c]
 
@@ -286,23 +291,36 @@
                     value = value * row_mask[q]
                 a[c, rows(q), :] = value
 
-        for q in range(4):
-            first(q)
-        second_y(0)
-        second_y(1)
-        for q in range(2, blocks):
-            first(q + 2)
-            second_y(q)
-            second_x(q)
-            if q > 2:
-                third(q - 1)
-        for q in range(2):
-            first(q)
-            new_y[q] = [fy[c, rows(q), :] for c in every]
-        for q in range(2):
-            second_x(q)
-            third(q - 1 if q else blocks - 1)
-        third(1)
+        tasks = []
+        for odd in range(2):
+            tasks += [(odd, True, False)] + [(q, True, True) for q in range(odd + 2, blocks, 2)] + [(odd, False, True)]
+
+        def begin(task):
+            q, with_y, with_x = task
+            if with_y and not with_x:
+                first(q)
+                first(q + 2)
+            elif with_y:
+                first(q + 2)
+            else:
+                first(q)
+                new_y[q] = [fy[c, rows(q), :] for c in every]
+
+        waiting = []
+        begin(tasks[0])
+        for task, following in zip(tasks, tasks[1:] + [None]):
+            q, with_y, with_x = task
+            if following is not None:
+                begin(following)
+            if with_y:
+                second_y(q)
+            if with_x:
+                second_x(q)
+                waiting.append(q)
+            if len(waiting) > BEHIND:
+                third(waiting.pop(0))
+        for q in waiting:
+            third(q)
         return carry
 
     lax.fori_loop(0, steps, step, 0)
@@ -429,17 +447,18 @@
         name="give_gauges",
     )(gauges, west)
 
-    def exchange(array, axes):
-        return lax.all_to_all(array, axes, split_axis=0, concat_axis=0, tiled=True)
-
-    parcel = exchange(parcel, GRID_AXES)
-
-    south, north = pl.pallas_call(
+    def exchange(array, axes, groups=None):
+        return lax.all_to_all(array, axes, split_axis=0, concat_axis=0, axis_index_groups=groups, tiled=True)
+
+    group = sorted(range(tiles), key=lambda tile: (tile % row_tiles in (0, row_tiles - 1), -(tile // row_tiles)))
+    parcel = exchange(parcel, GRID_AXES, [group])
+
+    far, near = pl.pallas_call(
         functools.partial(give_rows, halo), out_shape=(f32(2, halo, planes * LANES),) * 2, in_specs=vmem(3),
         out_specs=tuple(vmem(2)), compiler_params=params, cost_estimate=hint(40), name="give_rows",
     )(keep, gain, right)
-    top = lax.ppermute(south, ROW_AXES, [(i, i + 1) for i in range(row_tiles - 1)])
-    bottom = lax.ppermute(north, ROW_AXES, [(i + 1, i) for i in range(row_tiles - 1)])
+    far = lax.ppermute(far, ROW_AXES, [pair for i in range(1, row_tiles - 1, 2) for pair in ((i, i + 1), (i + 1, i))])
+    near = lax.ppermute(near, ROW_AXES, [pair for i in range(0, row_tiles, 2) for pair in ((i, i + 1), (i + 1, i))])
 
     wide = max(2 * LANES, owned)
     pushes = pl.pallas_call(
@@ -469,7 +488,7 @@
         scratch_shapes=[plane] * 8,
         compiler_params=params,
         name="sweep",
-    )(keep, gain, top, bottom, right, pushes)
+    )(keep, gain, far, near, right, pushes)
 
     sums = exchange(sums, "lon")
     own, weights = pl.pallas_call(

time: 44.1 us -> 42.6 us (0.966)
  waiting for transfers between devices: 7.9 us -> 5.12 us
  starting transfers between devices: 16.6 us -> 17.5 us
    all_to_all x2, waiting for transfers between devices: 7.89 us -> 5.11 us  [exchange(): lax.all_to_all(array, axes, split_axis=0, concat_axis=0, axis_index_group...]
    all_to_all x2, starting transfers between devices: 11.7 us -> 12.8 us  [exchange(): lax.all_to_all(array, axes, split_axis=0, concat_axis=0, axis_index_group...]
  transfers between devices with their start and end apart: 5 -> 5, of which waited for: 2 -> 2; matrix products, arithmetic and copies ran while one was open for 2% -> 2% of each run, Pallas kernels for 12% -> 13%
where the time goes in v14:
time: 42.6 us; the launch traced here: 42.3 us
  Pallas kernels  17.5 us (41%)
  starting transfers between devices  17.5 us (41%)
  waiting for transfers between devices  5.12 us (12%)
  other arithmetic  2.05 us (5%)
    all_to_all x2, starting transfers between devices, exchange(): lax.all_to_all(array, axes, split_axis=0, concat_axis=0, axis_index_group...  12.8 us
    pallas_call x1, Pallas kernels, local(): pl.pallas_call(functools.partial(sweep, steps), out_shape=(f32(height, pl...  10.9 us
    all_to_all x2, waiting for transfers between devices, exchange(): lax.all_to_all(array, axes, split_axis=0, concat_axis=0, axis_index_group...  5.11 us
    pallas_call x1, Pallas kernels, local(): pl.pallas_call(functools.partial(force, steps, halo, height, width), out_...  3.4 us
    ppermute x1, starting transfers between devices, local(): lax.ppermute(near, ROW_AXES, [pair for i in range(0, row_tiles, 2) for pa...  2.83 us
    ppermute x1, starting transfers between devices, local(): right = lax.ppermute(west, 'lon', [(i + 1, i) for i in range(lons - 1)])  1.29 us
    mul x1, other arithmetic, local(): (courant * 0.5) ** 2 * jnp.maximum(depth + surface, depth_floor) * keep  1.29 us
    pallas_call x1, Pallas kernels, local(): pl.pallas_call(finish, out_shape=f32(height, width), in_specs=vmem(3), ou...  1.12 us
  transfers between devices with their start and end apart: 5, of which 2 were waited for; matrix products, arithmetic and copies ran while one was open for 2% of the time, Pallas kernels for 13%

profile of v14, /device:TPU:0, one launch (start us, length us, event | category | flops | bytes accessed | tf_op | source)
XLA Modules:
  0.0 42.3 jit_solution(16931559401481917300)
XLA Ops:
  0.0 1.3 %multiply_multiply_fusion = (f32[128,512]{1,0:T(8,128)S(1)}, f32[128,512]{1,0:T(8,128)S(1)}) fusion(f32[128,512]{1,0:T(8,128)} %param.9, f32[128,512]{1,0:T(8,128)} %param.10, s32[128,512]{1,0:T(8,128)} %param.12, f32[128,512]{1,0:T(8,128)} %param.11), kind=kLoop, calls=%fused_computation | loop fusion | flops 458752 | bytes 1572864 | tf_op jit(solution)/shard_map/mul | solution.py:417
  1.3 0.1 give_west.1.after_ref
  1.4 1.3 %collective-permute-start = (f32[4,128,128]{2,1,0:T(8,128)S(1)}, f32[4,128,128]{2,1,0:T(8,128)S(1)}, u32[]{:S(2)}, u32[]{:S(2)}) collective-permute-start(f32[4,128,128]{2,1,0:T(8,128)S(1)} %give_west.1.after_ref), channel_id=1, source_target_pairs={{4,0},{8,4},{12,8},{5,1},{9,5},{13,9},{6,2},{10,6},{14,10},{7,3},{... | collective-permute-start | bytes 786440 | tf_op jit(solution)/shard_map/ppermute | solution.py:437
  2.7 0.8 %pad_add_fusion.gauge_ref = f32[5,4,16]{2,1,0:T(4,128)S(1)} fusion(f32[2,4,16]{2,1,0:T(4,128)} %bitcast.7, s32[1,1,8]{2,1,0:T(1,128)} %bitcast.9, s32[1,1,16]{2,1,0:T(1,128)} %bitcast.10, s32[1,1,16]{2,1,0:T(1,128)} %bitcast.11, s32[2,4,16]{2,1,0:T(4,128)} %bitcast.8), kind=kLoop, calls=%fused_computation.2 | loop fusion | flops 1600 | bytes 2464 | tf_op jit(solution)/shard_map/add | solution.py:427
  3.4 0.8 %give_gauges.1 = f32[16,8,128]{2,1,0:T(8,128)} custom-call(f32[5,4,16]{2,1,0:T(4,128)S(1)} %pad_add_fusion.gauge_ref, f32[4,128,128]{2,1,0:T(8,128)S(1)} %give_west.1.after_ref), custom_call_target="tpu_custom_call" | custom-call | bytes 10000000 | tf_op jit(solution)/shard_map/give_gauges/pallas_call | solution.py:439
  4.2 8.7 %all-to-all-start = ((f32[16,8,128]{2,1,0:T(8,128)}), f32[16,8,128]{2,1,0:T(8,128)S(1)}, u32[]{:S(2)}, u32[]{:S(2)}) async-start(f32[16,8,128]{2,1,0:T(8,128)} %give_gauges.1), calls=%async_computation | async-start | bytes 131072 | tf_op jit(solution)/shard_map/all_to_all | solution.py:451
  12.9 0.0 collective-permute-done.right_ref
  12.9 0.1 give_rows.1
  13.0 0.7 %collective-permute-start.1 = (f32[2,32,640]{2,1,0:T(8,128)S(1)}, f32[2,32,640]{2,1,0:T(8,128)S(1)}, u32[]{:S(2)}, u32[]{:S(2)}) collective-permute-start(f32[2,32,640]{2,1,0:T(8,128)S(1)} %get-tuple-element.11), channel_id=1, source_target_pairs={{1,2},{2,1},{5,6},{6,5},{9,10},{10,9},{13,14},{14,13},{17,18},{18,... | collective-permute-start | bytes 491528 | tf_op jit(solution)/shard_map/ppermute | solution.py:460
  13.7 2.8 %collective-permute-start.2 = (f32[2,32,640]{2,1,0:T(8,128)S(1)}, f32[2,32,640]{2,1,0:T(8,128)S(1)}, u32[]{:S(2)}, u32[]{:S(2)}) collective-permute-start(f32[2,32,640]{2,1,0:T(8,128)S(1)} %get-tuple-element.12), channel_id=1, source_target_pairs={{0,1},{1,0},{2,3},{3,2},{4,5},{5,4},{6,7},{7,6},{8,9},{9,8},{10,11... | collective-permute-start | bytes 491528 | tf_op jit(solution)/shard_map/ppermute | solution.py:461
  16.5 0.4 all-to-all-done.parcel_ref
  16.9 3.4 %force.1.force_ref = f32[17,5,200,128]{3,2,1,0:T(8,128)S(1)} custom-call(f32[16,8,128]{2,1,0:T(8,128)S(1)} %all-to-all-done.parcel_ref), custom_call_target="tpu_custom_call" | custom-call | flops 2013265920 | bytes 7864320 | tf_op jit(solution)/shard_map/force/pallas_call | solution.py:464
  20.3 0.0 collective-permute-done.1.far_ref
  20.3 0.0 collective-permute-done.2.near_ref
  20.3 10.9 %sweep.1 = (f32[128,640]{1,0:T(8,128)S(1)}, f32[4,40,128]{2,1,0:T(8,128)}) custom-call(f32[128,512]{1,0:T(8,128)S(1)} %get-tuple-element.18.keep_ref, f32[128,512]{1,0:T(8,128)S(1)} %get-tuple-element.17.gain_ref, f32[2,32,640]{2,1,0:T(8,128)S(1)} %collective-permute-done.1.far_ref, f32[2,32,640]{2,1,0:T(8,128)S(1)} %collective-permute-done.2.near_ref, ...), custom_call_target="tpu_custom_call" | custom-call | tf_op jit(solution)/shard_map/sweep/pallas_call | solution.py:483
  31.3 4.1 %all-to-all-start.1 = ((f32[4,40,128]{2,1,0:T(8,128)}), f32[4,40,128]{2,1,0:T(8,128)S(1)}, u32[]{:S(2)}, u32[]{:S(2)}) async-start(f32[4,40,128]{2,1,0:T(8,128)} %get-tuple-element.16), calls=%async_computation.1 | async-start | bytes 163840 | tf_op jit(solution)/shard_map/all_to_all | solution.py:451
  35.3 1.0 %smooth.1 = (f32[128,512]{1,0:T(8,128)S(1)}, f32[160,512]{1,0:T(8,128)S(1)}) custom-call(f32[128,640]{1,0:T(8,128)S(1)} %get-tuple-element.13.grad_ref), custom_call_target="tpu_custom_call" | custom-call | flops 402653184 | bytes 524288 | tf_op jit(solution)/shard_map/smooth/pallas_call | solution.py:494
  36.4 4.7 %all-to-all-done.1 = f32[4,40,128]{2,1,0:T(8,128)S(1)} async-done(((f32[4,40,128]{2,1,0:T(8,128)}), f32[4,40,128]{2,1,0:T(8,128)S(1)}, u32[]{:S(2)}, u32[]{:S(2)}) %all-to-all-start.1) | async-done | bytes 81952 | tf_op jit(solution)/shard_map/all_to_all | solution.py:451
  41.1 1.1 %finish.1 = f32[128,512]{1,0:T(8,128)} custom-call(f32[128,512]{1,0:T(8,128)S(1)} %get-tuple-element.14.own_ref, f32[160,512]{1,0:T(8,128)S(1)} %get-tuple-element.15.weights_ref, f32[160,128]{1,0:T(8,128)S(1)} %bitcast.6), custom_call_target="tpu_custom_call" | custom-call | tf_op jit(solution)/shard_map/finish/pallas_call | solution.py:505
Async XLA Ops:
  1.4 11.5 %collective-permute-start = (f32[4,128,128]{2,1,0:T(8,128)S(1)}, f32[4,128,128]{2,1,0:T(8,128)S(1)}, u32[]{:S(2)}, u32[]{:S(2)}) collective-permute-start(f32[4,128,128]{2,1,0:T(8,128)S(1)} %give_west.1.after_ref), channel_id=1, source_target_pairs={{4,0},{8,4},{12,8},{5,1},{9,5},{13,9},{6,2},{10,6},{14,10},{7,3},{... | collective-permute-start | bytes 786440 | tf_op jit(solution)/shard_map/ppermute | solution.py:437
  4.2 12.6 %all-to-all-start = ((f32[16,8,128]{2,1,0:T(8,128)}), f32[16,8,128]{2,1,0:T(8,128)S(1)}, u32[]{:S(2)}, u32[]{:S(2)}) async-start(f32[16,8,128]{2,1,0:T(8,128)} %give_gauges.1), calls=%async_computation | async-start | bytes 131072 | tf_op jit(solution)/shard_map/all_to_all | solution.py:451
  13.0 7.3 %collective-permute-start.1 = (f32[2,32,640]{2,1,0:T(8,128)S(1)}, f32[2,32,640]{2,1,0:T(8,128)S(1)}, u32[]{:S(2)}, u32[]{:S(2)}) collective-permute-start(f32[2,32,640]{2,1,0:T(8,128)S(1)} %get-tuple-element.11), channel_id=1, source_target_pairs={{1,2},{2,1},{5,6},{6,5},{9,10},{10,9},{13,14},{14,13},{17,18},{18,... | collective-permute-start | bytes 491528 | tf_op jit(solution)/shard_map/ppermute | solution.py:460
  13.7 6.6 %collective-permute-start.2 = (f32[2,32,640]{2,1,0:T(8,128)S(1)}, f32[2,32,640]{2,1,0:T(8,128)S(1)}, u32[]{:S(2)}, u32[]{:S(2)}) collective-permute-start(f32[2,32,640]{2,1,0:T(8,128)S(1)} %get-tuple-element.12), channel_id=1, source_target_pairs={{0,1},{1,0},{2,3},{3,2},{4,5},{5,4},{6,7},{7,6},{8,9},{9,8},{10,11... | collective-permute-start | bytes 491528 | tf_op jit(solution)/shard_map/ppermute | solution.py:461
  31.3 9.9 %all-to-all-start.1 = ((f32[4,40,128]{2,1,0:T(8,128)}), f32[4,40,128]{2,1,0:T(8,128)S(1)}, u32[]{:S(2)}, u32[]{:S(2)}) async-start(f32[4,40,128]{2,1,0:T(8,128)} %get-tuple-element.16), calls=%async_computation.1 | async-start | bytes 163840 | tf_op jit(solution)/shard_map/all_to_all | solution.py:451

commit v15 on v13

--- a/solution.py
+++ b/solution.py
@@ -49,10 +49,12 @@
         west_ref[spare] = jnp.zeros(west_ref.shape[1:], jnp.float32)
 
 
-def give_rows(halo, keep_ref, gain_ref, right_ref, south_ref, north_ref):
+def give_rows(halo, keep_ref, gain_ref, right_ref, far_ref, near_ref):
     height, width = keep_ref.shape
     lower = lane_iota(halo) < 2 * halo
-    for goal, rows in ((south_ref, slice(height - halo, height)), (north_ref, slice(0, halo))):
+    odd = my_place()[0] & 1
+    for goal, south in ((far_ref, odd), (near_ref, 1 - odd)):
+        rows = pl.ds(pl.multiple_of(south * (height - halo), halo), halo)
         for kind, source in enumerate((keep_ref, gain_ref)):
             goal[kind, :, :width] = source[rows, :]
             goal[kind, :, width:] = jnp.where(lower, roll_lanes(right_ref[0, rows, :], -2 * halo * kind), 0.0)
@@ -192,9 +194,9 @@
 
 
 def sweep(
-    steps, keep_ref, gain_ref, top_ref, bottom_ref, right_ref, force_ref,
+    steps, keep_ref, gain_ref, far_ref, near_ref, right_ref, force_ref,
     grad_ref, sums_ref,
-    a, fx, fy, keep_x, gain_x, keep_y, gain_y, plain,
+    a, fx, fy, keep_y, gain_y, plain,
 ):
     height, width = keep_ref.shape
     halo = 2 * steps
@@ -206,6 +208,7 @@
     reach = 2 * halo
     has_top, has_bottom = my_row > 0, my_row < row_tiles - 1
     has_right = my_lon < lons - 1
+    odd = (jnp.zeros((halo, LANES), jnp.int32) + (my_row & 1)) == 1
     lanes8 = lane_iota(8)
 
     def up(value):
@@ -214,22 +217,21 @@
     def down(value):
         return pltpu.roll(value, 1, 0)
 
-    for kind, (source, by_x, by_y) in enumerate(((keep_ref, keep_x, keep_y), (gain_ref, gain_x, gain_y))):
+    for kind, (source, by_y) in enumerate(((keep_ref, keep_y), (gain_ref, gain_y))):
         for c in range(planes):
             cols = slice(c * LANES, (c + 1) * LANES)
-            plain[c, 0:halo, :] = top_ref[kind, :, cols]
-            plain[c, halo + height : rows_all, :] = bottom_ref[kind, :, cols]
+            far, near = far_ref[kind, :, cols], near_ref[kind, :, cols]
+            plain[c, 0:halo, :] = jnp.where(odd, near, far)
+            plain[c, halo + height : rows_all, :] = jnp.where(odd, far, near)
             if c < inner:
                 plain[c, halo : halo + height, :] = source[:, cols]
         lower = lane_iota(height) < reach
         plain[inner, halo : halo + height, :] = jnp.where(lower, roll_lanes(right_ref[0], -reach * kind), 0.0)
         for q in range(blocks):
-            values = [plain[c, pl.ds(q, 8, stride=blocks), :] for c in range(planes)]
-            shifted = shift_from(values, 1, lanes8)
             to = (q - 1) % blocks * 8
             for c in range(planes):
-                by_x[c, 8 * q : 8 * q + 8, :] = shifted[c]
-                by_y[c, to : to + 8, :] = up(values[c]) if q == 0 else values[c]
+                value = plain[c, pl.ds(q, 8, stride=blocks), :]
+                by_y[c, to : to + 8, :] = up(value) if q == 0 else value
 
     col_mask = jnp.where(lanes8 < reach, jnp.where(has_right, 1.0, 0.0), 0.0)
     sublane = lax.broadcasted_iota(jnp.int32, (8, LANES), 0)
@@ -244,7 +246,7 @@
 
     def step(index, carry):
         level = jnp.where(index < steps - 1, steps - 2 - index, steps)
-        near, ahead, new_y, total, behind, push = {}, {}, {}, {}, {}, {}
+        near, ahead, new_y, beside, total, behind = {}, {}, {}, {}, {}, {}
 
         def rows(q):
             return slice(8 * q, 8 * q + 8)
@@ -253,26 +255,24 @@
             near[q] = [a[c, rows(q % blocks), :] for c in every]
             if q < blocks:
                 ahead[q] = [roll_lanes(value, -2) for value in near[q]]
-                push[q] = [force_ref[level, c, rows(q), :] for c in every]
             else:
                 near[q] = [up(value) for value in near[q]]
 
         def second_y(q):
-            new_y[q] = [
-                keep_y[c, rows(q), :] * fy[c, rows(q), :] + gain_y[c, rows(q), :] * (near[q + 2][c] - near[q][c])
-                for c in every
-            ]
+            keep, gain = ([ref[c, rows(q), :] for c in every] for ref in (keep_y, gain_y))
+            new_y[q] = [keep[c] * fy[c, rows(q), :] + gain[c] * (near[q + 2][c] - near[q][c]) for c in every]
             for c in every:
                 fy[c, rows(q), :] = new_y[q][c]
+            beside[q + 1] = [[roll_lanes(value, -1) for value in part] for part in (keep, gain)]
 
         def second_x(q):
+            keep, gain = (from_rolled(part, 1, lanes8) for part in beside[q])
             far = from_rolled(ahead[q], 2, lanes8)
-            new_x = [
-                keep_x[c, rows(q), :] * fx[c, rows(q), :] + gain_x[c, rows(q), :] * (far[c] - near[q][c]) for c in every
-            ]
+            new_x = [keep[c] * fx[c, rows(q), :] + gain[c] * (far[c] - near[q][c]) for c in every]
             behind[q] = [roll_lanes(value, 2) for value in new_x]
             before = new_y[q - 2] if q >= 2 else [down(fy[c, rows(q - 2 + blocks), :]) for c in every]
-            total[q] = [(near[q][c] + push[q][c]) + (new_y[q][c] - before[c]) + new_x[c] for c in every]
+            push = [force_ref[level, c, rows(q), :] for c in every]
+            total[q] = [(near[q][c] + push[c]) + (new_y[q][c] - before[c]) + new_x[c] for c in every]
             for c in every:
                 fx[c, rows(q), :] = new_x[c]
 
@@ -299,6 +299,10 @@
         for q in range(2):
             first(q)
             new_y[q] = [fy[c, rows(q), :] for c in every]
+            keep, gain = ([ref[c, rows((q - 1) % blocks), :] for c in every] for ref in (keep_y, gain_y))
+            if q == 0:
+                keep, gain = ([down(value) for value in part] for part in (keep, gain))
+            beside[q] = [[roll_lanes(value, -1) for value in part] for part in (keep, gain)]
         for q in range(2):
             second_x(q)
             third(q - 1 if q else blocks - 1)
@@ -429,17 +433,18 @@
         name="give_gauges",
     )(gauges, west)
 
-    def exchange(array, axes):
-        return lax.all_to_all(array, axes, split_axis=0, concat_axis=0, tiled=True)
-
-    parcel = exchange(parcel, GRID_AXES)
-
-    south, north = pl.pallas_call(
+    def exchange(array, axes, groups=None):
+        return lax.all_to_all(array, axes, split_axis=0, concat_axis=0, axis_index_groups=groups, tiled=True)
+
+    group = sorted(range(tiles), key=lambda tile: (tile % row_tiles in (0, row_tiles - 1), -(tile // row_tiles)))
+    parcel = exchange(parcel, GRID_AXES, [group])
+
+    far, near = pl.pallas_call(
         functools.partial(give_rows, halo), out_shape=(f32(2, halo, planes * LANES),) * 2, in_specs=vmem(3),
         out_specs=tuple(vmem(2)), compiler_params=params, cost_estimate=hint(40), name="give_rows",
     )(keep, gain, right)
-    top = lax.ppermute(south, ROW_AXES, [(i, i + 1) for i in range(row_tiles - 1)])
-    bottom = lax.ppermute(north, ROW_AXES, [(i + 1, i) for i in range(row_tiles - 1)])
+    far = lax.ppermute(far, ROW_AXES, [pair for i in range(1, row_tiles - 1, 2) for pair in ((i, i + 1), (i + 1, i))])
+    near = lax.ppermute(near, ROW_AXES, [pair for i in range(0, row_tiles, 2) for pair in ((i, i + 1), (i + 1, i))])
 
     wide = max(2 * LANES, owned)
     pushes = pl.pallas_call(
@@ -466,10 +471,10 @@
         out_shape=(f32(height, planes * LANES), f32(lons, 8 + halo, height)),
         in_specs=vmem(6),
         out_specs=tuple(vmem(2)),
-        scratch_shapes=[plane] * 8,
+        scratch_shapes=[plane] * 6,
         compiler_params=params,
         name="sweep",
-    )(keep, gain, top, bottom, right, pushes)
+    )(keep, gain, far, near, right, pushes)
 
     sums = exchange(sums, "lon")
     own, weights = pl.pallas_call(

time: 44.1 us -> 49.5 us (1.12)
  Pallas kernels: 17.1 us -> 24.4 us
  waiting for transfers between devices: 7.9 us -> 5.12 us
  starting transfers between devices: 16.6 us -> 17.5 us
    pallas_call x1, Pallas kernels: 10.5 us -> 17.8 us  [local(): pl.pallas_call(functools.partial(sweep, steps), out_shape=(f32(height, pl...]
    all_to_all x2, waiting for transfers between devices: 7.89 us -> 5.12 us  [exchange(): lax.all_to_all(array, axes, split_axis=0, concat_axis=0, axis_index_group...]
    all_to_all x2, starting transfers between devices: 11.7 us -> 12.8 us  [exchange(): lax.all_to_all(array, axes, split_axis=0, concat_axis=0, axis_index_group...]
  transfers between devices with their start and end apart: 5 -> 5, of which waited for: 2 -> 2; matrix products, arithmetic and copies ran while one was open for 2% -> 2% of each run, Pallas kernels for 12% -> 11%
where the time goes in v15:
time: 49.5 us; the launch traced here: 49.1 us
  Pallas kernels  24.4 us (49%)
  starting transfers between devices  17.5 us (35%)
  waiting for transfers between devices  5.12 us (10%)
  other arithmetic  2.05 us (4%)
    pallas_call x1, Pallas kernels, local(): pl.pallas_call(functools.partial(sweep, steps), out_shape=(f32(height, pl...  17.8 us
    all_to_all x2, starting transfers between devices, exchange(): lax.all_to_all(array, axes, split_axis=0, concat_axis=0, axis_index_group...  12.8 us
    all_to_all x2, waiting for transfers between devices, exchange(): lax.all_to_all(array, axes, split_axis=0, concat_axis=0, axis_index_group...  5.12 us
    pallas_call x1, Pallas kernels, local(): pl.pallas_call(functools.partial(force, steps, halo, height, width), out_...  3.4 us
    ppermute x1, starting transfers between devices, local(): lax.ppermute(near, ROW_AXES, [pair for i in range(0, row_tiles, 2) for pa...  2.83 us
    ppermute x1, starting transfers between devices, local(): right = lax.ppermute(west, 'lon', [(i + 1, i) for i in range(lons - 1)])  1.29 us
    mul x1, other arithmetic, local(): (courant * 0.5) ** 2 * jnp.maximum(depth + surface, depth_floor) * keep  1.29 us
    pallas_call x1, Pallas kernels, local(): pl.pallas_call(finish, out_shape=f32(height, width), in_specs=vmem(3), ou...  1.13 us
  transfers between devices with their start and end apart: 5, of which 2 were waited for; matrix products, arithmetic and copies ran while one was open for 2% of the time, Pallas kernels for 11%

profile of v15, /device:TPU:0, one launch (start us, length us, event | category | flops | bytes accessed | tf_op | source)
XLA Modules:
  0.0 49.1 jit_solution(15139916511272454936)
XLA Ops:
  0.0 1.3 %multiply_multiply_fusion = (f32[128,512]{1,0:T(8,128)S(1)}, f32[128,512]{1,0:T(8,128)S(1)}) fusion(f32[128,512]{1,0:T(8,128)} %param.9, f32[128,512]{1,0:T(8,128)} %param.10, s32[128,512]{1,0:T(8,128)} %param.12, f32[128,512]{1,0:T(8,128)} %param.11), kind=kLoop, calls=%fused_computation | loop fusion | flops 458752 | bytes 1572864 | tf_op jit(solution)/shard_map/mul | solution.py:403
  1.3 0.1 give_west.1.after_ref
  1.4 1.3 %collective-permute-start = (f32[4,128,128]{2,1,0:T(8,128)S(1)}, f32[4,128,128]{2,1,0:T(8,128)S(1)}, u32[]{:S(2)}, u32[]{:S(2)}) collective-permute-start(f32[4,128,128]{2,1,0:T(8,128)S(1)} %give_west.1.after_ref), channel_id=1, source_target_pairs={{4,0},{8,4},{12,8},{5,1},{9,5},{13,9},{6,2},{10,6},{14,10},{7,3},{... | collective-permute-start | bytes 786440 | tf_op jit(solution)/shard_map/ppermute | solution.py:423
  2.7 0.8 %pad_add_fusion.gauge_ref = f32[5,4,16]{2,1,0:T(4,128)S(1)} fusion(f32[2,4,16]{2,1,0:T(4,128)} %bitcast.7, s32[1,1,8]{2,1,0:T(1,128)} %bitcast.9, s32[1,1,16]{2,1,0:T(1,128)} %bitcast.10, s32[1,1,16]{2,1,0:T(1,128)} %bitcast.11, s32[2,4,16]{2,1,0:T(4,128)} %bitcast.8), kind=kLoop, calls=%fused_computation.2 | loop fusion | flops 1600 | bytes 2464 | tf_op jit(solution)/shard_map/add | solution.py:413
  3.4 0.8 %give_gauges.1 = f32[16,8,128]{2,1,0:T(8,128)} custom-call(f32[5,4,16]{2,1,0:T(4,128)S(1)} %pad_add_fusion.gauge_ref, f32[4,128,128]{2,1,0:T(8,128)S(1)} %give_west.1.after_ref), custom_call_target="tpu_custom_call" | custom-call | bytes 10000000 | tf_op jit(solution)/shard_map/give_gauges/pallas_call | solution.py:425
  4.2 8.7 %all-to-all-start = ((f32[16,8,128]{2,1,0:T(8,128)}), f32[16,8,128]{2,1,0:T(8,128)S(1)}, u32[]{:S(2)}, u32[]{:S(2)}) async-start(f32[16,8,128]{2,1,0:T(8,128)} %give_gauges.1), calls=%async_computation | async-start | bytes 131072 | tf_op jit(solution)/shard_map/all_to_all | solution.py:437
  12.9 0.0 collective-permute-done.right_ref
  12.9 0.1 give_rows.1
  13.0 0.7 %collective-permute-start.1 = (f32[2,32,640]{2,1,0:T(8,128)S(1)}, f32[2,32,640]{2,1,0:T(8,128)S(1)}, u32[]{:S(2)}, u32[]{:S(2)}) collective-permute-start(f32[2,32,640]{2,1,0:T(8,128)S(1)} %get-tuple-element.11), channel_id=1, source_target_pairs={{1,2},{2,1},{5,6},{6,5},{9,10},{10,9},{13,14},{14,13},{17,18},{18,... | collective-permute-start | bytes 491528 | tf_op jit(solution)/shard_map/ppermute | solution.py:446
  13.7 2.8 %collective-permute-start.2 = (f32[2,32,640]{2,1,0:T(8,128)S(1)}, f32[2,32,640]{2,1,0:T(8,128)S(1)}, u32[]{:S(2)}, u32[]{:S(2)}) collective-permute-start(f32[2,32,640]{2,1,0:T(8,128)S(1)} %get-tuple-element.12), channel_id=1, source_target_pairs={{0,1},{1,0},{2,3},{3,2},{4,5},{5,4},{6,7},{7,6},{8,9},{9,8},{10,11... | collective-permute-start | bytes 491528 | tf_op jit(solution)/shard_map/ppermute | solution.py:447
  16.5 0.4 all-to-all-done.parcel_ref
  16.9 3.4 %force.1.force_ref = f32[17,5,200,128]{3,2,1,0:T(8,128)S(1)} custom-call(f32[16,8,128]{2,1,0:T(8,128)S(1)} %all-to-all-done.parcel_ref), custom_call_target="tpu_custom_call" | custom-call | flops 2013265920 | bytes 7864320 | tf_op jit(solution)/shard_map/force/pallas_call | solution.py:450
  20.3 0.0 collective-permute-done.1.far_ref
  20.3 0.0 collective-permute-done.2.near_ref
  20.3 17.8 %sweep.1 = (f32[128,640]{1,0:T(8,128)S(1)}, f32[4,40,128]{2,1,0:T(8,128)}) custom-call(f32[128,512]{1,0:T(8,128)S(1)} %get-tuple-element.18.keep_ref, f32[128,512]{1,0:T(8,128)S(1)} %get-tuple-element.17.gain_ref, f32[2,32,640]{2,1,0:T(8,128)S(1)} %collective-permute-done.1.far_ref, f32[2,32,640]{2,1,0:T(8,128)S(1)} %collective-permute-done.2.near_ref, ...), custom_call_target="tpu_custom_call" | custom-call | tf_op jit(solution)/shard_map/sweep/pallas_call | solution.py:469
  38.2 4.1 %all-to-all-start.1 = ((f32[4,40,128]{2,1,0:T(8,128)}), f32[4,40,128]{2,1,0:T(8,128)S(1)}, u32[]{:S(2)}, u32[]{:S(2)}) async-start(f32[4,40,128]{2,1,0:T(8,128)} %get-tuple-element.16), calls=%async_computation.1 | async-start | bytes 163840 | tf_op jit(solution)/shard_map/all_to_all | solution.py:437
  42.2 1.0 %smooth.1 = (f32[128,512]{1,0:T(8,128)S(1)}, f32[160,512]{1,0:T(8,128)S(1)}) custom-call(f32[128,640]{1,0:T(8,128)S(1)} %get-tuple-element.13.grad_ref), custom_call_target="tpu_custom_call" | custom-call | flops 402653184 | bytes 524288 | tf_op jit(solution)/shard_map/smooth/pallas_call | solution.py:480
  43.3 4.7 %all-to-all-done.1 = f32[4,40,128]{2,1,0:T(8,128)S(1)} async-done(((f32[4,40,128]{2,1,0:T(8,128)}), f32[4,40,128]{2,1,0:T(8,128)S(1)}, u32[]{:S(2)}, u32[]{:S(2)}) %all-to-all-start.1) | async-done | bytes 81952 | tf_op jit(solution)/shard_map/all_to_all | solution.py:437
  48.0 1.1 %finish.1 = f32[128,512]{1,0:T(8,128)} custom-call(f32[128,512]{1,0:T(8,128)S(1)} %get-tuple-element.14.own_ref, f32[160,512]{1,0:T(8,128)S(1)} %get-tuple-element.15.weights_ref, f32[160,128]{1,0:T(8,128)S(1)} %bitcast.6), custom_call_target="tpu_custom_call" | custom-call | tf_op jit(solution)/shard_map/finish/pallas_call | solution.py:491
Async XLA Ops:
  1.4 11.5 %collective-permute-start = (f32[4,128,128]{2,1,0:T(8,128)S(1)}, f32[4,128,128]{2,1,0:T(8,128)S(1)}, u32[]{:S(2)}, u32[]{:S(2)}) collective-permute-start(f32[4,128,128]{2,1,0:T(8,128)S(1)} %give_west.1.after_ref), channel_id=1, source_target_pairs={{4,0},{8,4},{12,8},{5,1},{9,5},{13,9},{6,2},{10,6},{14,10},{7,3},{... | collective-permute-start | bytes 786440 | tf_op jit(solution)/shard_map/ppermute | solution.py:423
  4.2 12.6 %all-to-all-start = ((f32[16,8,128]{2,1,0:T(8,128)}), f32[16,8,128]{2,1,0:T(8,128)S(1)}, u32[]{:S(2)}, u32[]{:S(2)}) async-start(f32[16,8,128]{2,1,0:T(8,128)} %give_gauges.1), calls=%async_computation | async-start | bytes 131072 | tf_op jit(solution)/shard_map/all_to_all | solution.py:437
  13.0 7.3 %collective-permute-start.1 = (f32[2,32,640]{2,1,0:T(8,128)S(1)}, f32[2,32,640]{2,1,0:T(8,128)S(1)}, u32[]{:S(2)}, u32[]{:S(2)}) collective-permute-start(f32[2,32,640]{2,1,0:T(8,128)S(1)} %get-tuple-element.11), channel_id=1, source_target_pairs={{1,2},{2,1},{5,6},{6,5},{9,10},{10,9},{13,14},{14,13},{17,18},{18,... | collective-permute-start | bytes 491528 | tf_op jit(solution)/shard_map/ppermute | solution.py:446
  13.7 6.6 %collective-permute-start.2 = (f32[2,32,640]{2,1,0:T(8,128)S(1)}, f32[2,32,640]{2,1,0:T(8,128)S(1)}, u32[]{:S(2)}, u32[]{:S(2)}) collective-permute-start(f32[2,32,640]{2,1,0:T(8,128)S(1)} %get-tuple-element.12), channel_id=1, source_target_pairs={{0,1},{1,0},{2,3},{3,2},{4,5},{5,4},{6,7},{7,6},{8,9},{9,8},{10,11... | collective-permute-start | bytes 491528 | tf_op jit(solution)/shard_map/ppermute | solution.py:447
  38.2 9.9 %all-to-all-start.1 = ((f32[4,40,128]{2,1,0:T(8,128)}), f32[4,40,128]{2,1,0:T(8,128)S(1)}, u32[]{:S(2)}, u32[]{:S(2)}) async-start(f32[4,40,128]{2,1,0:T(8,128)} %get-tuple-element.16), calls=%async_computation.1 | async-start | bytes 163840 | tf_op jit(solution)/shard_map/all_to_all | solution.py:437

commit v16 on v15

--- a/solution.py
+++ b/solution.py
@@ -99,15 +99,8 @@
     lax.fori_loop(0, tiles, put, 0, unroll=tiles <= 16)
 
 
-def from_rolled(rolled, shift, lanes):
-    count = len(rolled)
-    if shift > 0:
-        return [jnp.where(lanes >= LANES - shift, rolled[(c + 1) % count], rolled[c]) for c in range(count)]
-    return [jnp.where(lanes < -shift, rolled[(c - 1) % count], rolled[c]) for c in range(count)]
-
-
-def shift_from(planes, shift, lanes):
-    return from_rolled([roll_lanes(plane, -shift) for plane in planes], shift, lanes)
+def dealt_column(place, planes):
+    return (place & (LANES - 1)) * planes + place // LANES
 
 
 def force(steps, halo, height, width, parcel_ref, force_ref, series_ref, rows_hot, cols_hot):
@@ -148,7 +141,7 @@
             rows_hot[:, cols] = (at == row).astype(jnp.float32).astype(jnp.bfloat16)
             by_gauge = jnp.transpose(jnp.broadcast_to(col, (LANES, LANES)))
             for c in range(planes):
-                spot = (lane_iota(LANES) + c * LANES).astype(jnp.float32)
+                spot = (lane_iota(LANES) * planes + c).astype(jnp.float32)
                 hot = (by_gauge == spot).astype(jnp.float32).astype(jnp.bfloat16)
                 cols_hot[part * LANES : (part + 1) * LANES, c * LANES : (c + 1) * LANES] = hot
                 cols_hot[wide + part * LANES : wide + (part + 1) * LANES, c * LANES : (c + 1) * LANES] = hot
@@ -196,7 +189,7 @@
 def sweep(
     steps, keep_ref, gain_ref, far_ref, near_ref, right_ref, force_ref,
     grad_ref, sums_ref,
-    a, fx, fy, keep_y, gain_y, plain,
+    a, fx, fy, keeps, gains, plain,
 ):
     height, width = keep_ref.shape
     halo = 2 * steps
@@ -208,7 +201,7 @@
     reach = 2 * halo
     has_top, has_bottom = my_row > 0, my_row < row_tiles - 1
     has_right = my_lon < lons - 1
-    odd = (jnp.zeros((halo, LANES), jnp.int32) + (my_row & 1)) == 1
+    odd = (jnp.zeros((halo, planes * LANES), jnp.int32) + (my_row & 1)) == 1
     lanes8 = lane_iota(8)
 
     def up(value):
@@ -217,28 +210,52 @@
     def down(value):
         return pltpu.roll(value, 1, 0)
 
-    for kind, (source, by_y) in enumerate(((keep_ref, keep_y), (gain_ref, gain_y))):
-        for c in range(planes):
-            cols = slice(c * LANES, (c + 1) * LANES)
-            far, near = far_ref[kind, :, cols], near_ref[kind, :, cols]
-            plain[c, 0:halo, :] = jnp.where(odd, near, far)
-            plain[c, halo + height : rows_all, :] = jnp.where(odd, far, near)
-            if c < inner:
-                plain[c, halo : halo + height, :] = source[:, cols]
-        lower = lane_iota(height) < reach
-        plain[inner, halo : halo + height, :] = jnp.where(lower, roll_lanes(right_ref[0], -reach * kind), 0.0)
+    every = range(planes)
+    columns = planes * LANES
+
+    parts = []
+    for kind, source in enumerate((keep_ref, gain_ref)):
+        far, near = far_ref[kind], near_ref[kind]
+        beside = jnp.where(lane_iota(height) < reach, roll_lanes(right_ref[0], -reach * kind), 0.0)
+        whole = jnp.concatenate(
+            [
+                jnp.where(odd, near, far),
+                jnp.concatenate([source[...], beside], axis=1),
+                jnp.where(odd, far, near),
+            ],
+            axis=0,
+        )
+        high = whole.astype(jnp.bfloat16)
+        parts += [high, (whole - high.astype(jnp.float32)).astype(jnp.bfloat16)]
+    parts = jnp.concatenate(parts, axis=0)
+    shape = (columns, LANES)
+    column = lax.broadcasted_iota(jnp.int32, shape, 0)
+    for c in every:
+        deal = (column == lax.broadcasted_iota(jnp.int32, shape, 1) * planes + c).astype(jnp.float32)
+        dealt = jnp.dot(parts, deal.astype(jnp.bfloat16), preferred_element_type=jnp.float32)
+        for kind in range(2):
+            at = 2 * kind * rows_all
+            plain[kind, c, 0:rows_all, :] = dealt[at : at + rows_all] + dealt[at + rows_all : at + 2 * rows_all]
+    for kind, goal in enumerate((keeps, gains)):
         for q in range(blocks):
-            to = (q - 1) % blocks * 8
-            for c in range(planes):
-                value = plain[c, pl.ds(q, 8, stride=blocks), :]
-                by_y[c, to : to + 8, :] = up(value) if q == 0 else value
-
-    col_mask = jnp.where(lanes8 < reach, jnp.where(has_right, 1.0, 0.0), 0.0)
+            for c in every:
+                value = plain[kind, c, pl.ds(q, 8, stride=blocks), :]
+                goal[c, 8 * q : 8 * q + 8, :] = value
+                if q == 0:
+                    goal[c, 8 * blocks : 8 * blocks + 8, :] = up(value)
+                if c == 0:
+                    goal[planes, 8 * q : 8 * q + 8, :] = roll_lanes(value, -1)
+
+    def cell_mask(column, there):
+        lane, plane = column // planes, column % planes
+        return plane, jnp.where(lanes8 == lane, there, 1.0)
+
+    column_mask = dict([cell_mask(width, jnp.where(has_right, 1.0, 0.0)), cell_mask(columns - 1, 0.0)])
+    assert len(column_mask) == 2
     sublane = lax.broadcasted_iota(jnp.int32, (8, LANES), 0)
     row_mask = {}
     for row, there in ((halo - 1, has_top), (halo + height, has_bottom)):
         row_mask[row % blocks] = jnp.where(sublane == row // blocks, jnp.where(there, 1.0, 0.0), 1.0)
-    every = range(planes)
 
     fx[...] = jnp.zeros_like(fx)
     fy[...] = jnp.zeros_like(fy)
@@ -254,22 +271,25 @@
         def first(q):
             near[q] = [a[c, rows(q % blocks), :] for c in every]
             if q < blocks:
-                ahead[q] = [roll_lanes(value, -2) for value in near[q]]
+                ahead[q] = near[q][2:] + [roll_lanes(value, -1) for value in near[q][:2]]
             else:
                 near[q] = [up(value) for value in near[q]]
 
+        def coefficients(q):
+            return [[ref[c, rows(q), :] for c in range(planes + 1)] for ref in (keeps, gains)]
+
         def second_y(q):
-            keep, gain = ([ref[c, rows(q), :] for c in every] for ref in (keep_y, gain_y))
+            beside[q + 1] = keep, gain = coefficients(q + 1)
             new_y[q] = [keep[c] * fy[c, rows(q), :] + gain[c] * (near[q + 2][c] - near[q][c]) for c in every]
             for c in every:
                 fy[c, rows(q), :] = new_y[q][c]
-            beside[q + 1] = [[roll_lanes(value, -1) for value in part] for part in (keep, gain)]
 
         def second_x(q):
-            keep, gain = (from_rolled(part, 1, lanes8) for part in beside[q])
-            far = from_rolled(ahead[q], 2, lanes8)
-            new_x = [keep[c] * fx[c, rows(q), :] + gain[c] * (far[c] - near[q][c]) for c in every]
-            behind[q] = [roll_lanes(value, 2) for value in new_x]
+            keep, gain = beside[q]
+            new_x = [
+                keep[c + 1] * fx[c, rows(q), :] + gain[c + 1] * (ahead[q][c] - near[q][c]) for c in every
+            ]
+            behind[q] = [roll_lanes(value, 1) for value in new_x[-2:]] + new_x[:-2]
             before = new_y[q - 2] if q >= 2 else [down(fy[c, rows(q - 2 + blocks), :]) for c in every]
             push = [force_ref[level, c, rows(q), :] for c in every]
             total[q] = [(near[q][c] + push[c]) + (new_y[q][c] - before[c]) + new_x[c] for c in every]
@@ -277,11 +297,10 @@
                 fx[c, rows(q), :] = new_x[c]
 
         def third(q):
-            far = from_rolled(behind[q], -2, lanes8)
             for c in every:
-                value = total[q][c] - far[c]
-                if c == inner:
-                    value = value * col_mask
+                value = total[q][c] - behind[q][c]
+                if c in column_mask:
+                    value = value * column_mask[c]
                 if q in row_mask:
                     value = value * row_mask[q]
                 a[c, rows(q), :] = value
@@ -299,10 +318,7 @@
         for q in range(2):
             first(q)
             new_y[q] = [fy[c, rows(q), :] for c in every]
-            keep, gain = ([ref[c, rows((q - 1) % blocks), :] for c in every] for ref in (keep_y, gain_y))
-            if q == 0:
-                keep, gain = ([down(value) for value in part] for part in (keep, gain))
-            beside[q] = [[roll_lanes(value, -1) for value in part] for part in (keep, gain)]
+            beside[q] = coefficients(q)
         for q in range(2):
             second_x(q)
             third(q - 1 if q else blocks - 1)
@@ -312,20 +328,18 @@
     lax.fori_loop(0, steps, step, 0)
 
     start = jnp.where(my_lon > 0, halo, 0)
-    for r in range(0, height, 8):
-        s, q = divmod(halo + r, blocks)
-        for c in every:
-            cols = slice(c * LANES, (c + 1) * LANES)
-            value = a[c, pl.ds(8 * q + s, 8, stride=8), :]
-            wet = keep_ref[r : r + 8, cols] if c < inner else right_ref[0, r : r + 8, :]
-            if c == 0:
-                wet = jnp.where(lanes8 >= start, wet, 0.0)
-            if c == inner:
-                wet = jnp.where(lanes8 < halo, wet, 0.0)
-            grad_ref[r : r + 8, cols] = jnp.where(wet > 0.0, value, 0.0)
+    for c in every:
+        column = lanes8 * planes + c
+        known = (column >= start) & (column < width + halo)
+        for r in range(0, height, 8):
+            s, q = divmod(halo + r, blocks)
+            strided = pl.ds(8 * q + s, 8, stride=8)
+            value = jnp.where(known & (keeps[c, strided, :] > 0.0), a[c, strided, :], 0.0)
+            grad_ref[r : r + 8, c * LANES : (c + 1) * LANES] = value
     length = 2.0 * width
     shape = (8 + halo, planes * LANES)
-    kind, column = lax.broadcasted_iota(jnp.int32, shape, 0), lax.broadcasted_iota(jnp.int32, shape, 1)
+    kind = lax.broadcasted_iota(jnp.int32, shape, 0)
+    column = dealt_column(lax.broadcasted_iota(jnp.int32, shape, 1), planes)
     beyond = column - width
     off = jnp.where(kind == 0, column, jnp.where(kind == 1, -1 - beyond, jnp.where(kind == 2, beyond, width - 1 - beyond)))
     mine = ((kind < 2) & (beyond < 0)) | ((kind >= 2) & (kind < 4) & (beyond >= 0))
@@ -342,11 +356,15 @@
 def smooth(halo, lons, grad_ref, out_ref, weights_ref):
     width = out_ref.shape[1]
     length = 2.0 * width
-    row = lax.broadcasted_iota(jnp.int32, (width, width), 0)
-    column = lax.broadcasted_iota(jnp.int32, (width, width), 1)
-    kernel = jnp.exp(-jnp.abs(row - column).astype(jnp.float32) / length)
+    planes = grad_ref.shape[1] // LANES
+    column = lax.broadcasted_iota(jnp.int32, (LANES, width), 1)
+    lane = lax.broadcasted_iota(jnp.int32, (LANES, width), 0)
+    sources = [lane * planes + c for c in range(planes)]
+    kernel = jnp.concatenate(
+        [jnp.where(x < width, jnp.exp(-jnp.abs(x - column).astype(jnp.float32) / length), 0.0) for x in sources], axis=0
+    )
     out_ref[...] = jnp.dot(
-        grad_ref[:, :width], kernel, precision=lax.Precision.HIGHEST, preferred_element_type=jnp.float32
+        grad_ref[...], kernel, precision=lax.Precision.HIGHEST, preferred_element_type=jnp.float32
     )
     me = lax.axis_index("lon")
     shape = (8 + halo, width)
@@ -471,7 +489,11 @@
         out_shape=(f32(height, planes * LANES), f32(lons, 8 + halo, height)),
         in_specs=vmem(6),
         out_specs=tuple(vmem(2)),
-        scratch_shapes=[plane] * 6,
+        scratch_shapes=[plane] * 3 + [
+            pltpu.VMEM((planes + 1, spaced(rows_all + 8), LANES), jnp.float32),
+            pltpu.VMEM((planes + 1, spaced(rows_all + 8), LANES), jnp.float32),
+            pltpu.VMEM((2, planes, spaced(rows_all), LANES), jnp.float32),
+        ],
         compiler_params=params,
         name="sweep",
     )(keep, gain, far, near, right, pushes)

time: 49.5 us -> 39.5 us (0.80)
  Pallas kernels: 24.4 us -> 14.7 us
    pallas_call x1, Pallas kernels: 17.8 us -> 7.84 us  [local(): pl.pallas_call(functools.partial(sweep, steps), out_shape=(f32(height, pl...]
  transfers between devices with their start and end apart: 5 -> 5, of which waited for: 2 -> 2; matrix products, arithmetic and copies ran while one was open for 2% -> 2% of each run, Pallas kernels for 11% -> 14%
where the time goes in v16:
time: 39.5 us; the launch traced here: 39.2 us
  starting transfers between devices  17.5 us (44%)
  Pallas kernels  14.7 us (37%)
  waiting for transfers between devices  4.78 us (12%)
  other arithmetic  2.05 us (5%)
    all_to_all x2, starting transfers between devices, exchange(): lax.all_to_all(array, axes, split_axis=0, concat_axis=0, axis_index_group...  12.8 us
    pallas_call x1, Pallas kernels, local(): pl.pallas_call(functools.partial(sweep, steps), out_shape=(f32(height, pl...  7.84 us
    all_to_all x2, waiting for transfers between devices, exchange(): lax.all_to_all(array, axes, split_axis=0, concat_axis=0, axis_index_group...  4.78 us
    pallas_call x1, Pallas kernels, local(): pl.pallas_call(functools.partial(force, steps, halo, height, width), out_...  3.4 us
    ppermute x1, starting transfers between devices, local(): lax.ppermute(near, ROW_AXES, [pair for i in range(0, row_tiles, 2) for pa...  2.83 us
    pallas_call x1, Pallas kernels, local(): pl.pallas_call(functools.partial(smooth, halo, lons), out_shape=(f32(heig...  1.37 us
    ppermute x1, starting transfers between devices, local(): right = lax.ppermute(west, 'lon', [(i + 1, i) for i in range(lons - 1)])  1.29 us
    mul x1, other arithmetic, local(): (courant * 0.5) ** 2 * jnp.maximum(depth + surface, depth_floor) * keep  1.29 us
  transfers between devices with their start and end apart: 5, of which 2 were waited for; matrix products, arithmetic and copies ran while one was open for 2% of the time, Pallas kernels for 14%

profile of v16, /device:TPU:0, one launch (start us, length us, event | category | flops | bytes accessed | tf_op | source)
XLA Modules:
  0.0 39.2 jit_solution(10369789313174495103)
XLA Ops:
  0.0 1.3 %multiply_multiply_fusion = (f32[128,512]{1,0:T(8,128)S(1)}, f32[128,512]{1,0:T(8,128)S(1)}) fusion(f32[128,512]{1,0:T(8,128)} %param.9, f32[128,512]{1,0:T(8,128)} %param.10, s32[128,512]{1,0:T(8,128)} %param.12, f32[128,512]{1,0:T(8,128)} %param.11), kind=kLoop, calls=%fused_computation | loop fusion | flops 458752 | bytes 1572864 | tf_op jit(solution)/shard_map/mul | solution.py:421
  1.3 0.1 give_west.1.after_ref
  1.4 1.3 %collective-permute-start = (f32[4,128,128]{2,1,0:T(8,128)S(1)}, f32[4,128,128]{2,1,0:T(8,128)S(1)}, u32[]{:S(2)}, u32[]{:S(2)}) collective-permute-start(f32[4,128,128]{2,1,0:T(8,128)S(1)} %give_west.1.after_ref), channel_id=1, source_target_pairs={{4,0},{8,4},{12,8},{5,1},{9,5},{13,9},{6,2},{10,6},{14,10},{7,3},{... | collective-permute-start | bytes 786440 | tf_op jit(solution)/shard_map/ppermute | solution.py:441
  2.7 0.8 %pad_add_fusion.gauge_ref = f32[5,4,16]{2,1,0:T(4,128)S(1)} fusion(f32[2,4,16]{2,1,0:T(4,128)} %bitcast.7, s32[1,1,8]{2,1,0:T(1,128)} %bitcast.9, s32[1,1,16]{2,1,0:T(1,128)} %bitcast.10, s32[1,1,16]{2,1,0:T(1,128)} %bitcast.11, s32[2,4,16]{2,1,0:T(4,128)} %bitcast.8), kind=kLoop, calls=%fused_computation.2 | loop fusion | flops 1600 | bytes 2464 | tf_op jit(solution)/shard_map/add | solution.py:431
  3.4 0.8 %give_gauges.1 = f32[16,8,128]{2,1,0:T(8,128)} custom-call(f32[5,4,16]{2,1,0:T(4,128)S(1)} %pad_add_fusion.gauge_ref, f32[4,128,128]{2,1,0:T(8,128)S(1)} %give_west.1.after_ref), custom_call_target="tpu_custom_call" | custom-call | bytes 10000000 | tf_op jit(solution)/shard_map/give_gauges/pallas_call | solution.py:443
  4.2 8.7 %all-to-all-start = ((f32[16,8,128]{2,1,0:T(8,128)}), f32[16,8,128]{2,1,0:T(8,128)S(1)}, u32[]{:S(2)}, u32[]{:S(2)}) async-start(f32[16,8,128]{2,1,0:T(8,128)} %give_gauges.1), calls=%async_computation | async-start | bytes 131072 | tf_op jit(solution)/shard_map/all_to_all | solution.py:455
  12.9 0.0 collective-permute-done.right_ref
  12.9 0.1 give_rows.1
  13.0 0.7 %collective-permute-start.1 = (f32[2,32,640]{2,1,0:T(8,128)S(1)}, f32[2,32,640]{2,1,0:T(8,128)S(1)}, u32[]{:S(2)}, u32[]{:S(2)}) collective-permute-start(f32[2,32,640]{2,1,0:T(8,128)S(1)} %get-tuple-element.11), channel_id=1, source_target_pairs={{1,2},{2,1},{5,6},{6,5},{9,10},{10,9},{13,14},{14,13},{17,18},{18,... | collective-permute-start | bytes 491528 | tf_op jit(solution)/shard_map/ppermute | solution.py:464
  13.7 2.8 %collective-permute-start.2 = (f32[2,32,640]{2,1,0:T(8,128)S(1)}, f32[2,32,640]{2,1,0:T(8,128)S(1)}, u32[]{:S(2)}, u32[]{:S(2)}) collective-permute-start(f32[2,32,640]{2,1,0:T(8,128)S(1)} %get-tuple-element.12), channel_id=1, source_target_pairs={{0,1},{1,0},{2,3},{3,2},{4,5},{5,4},{6,7},{7,6},{8,9},{9,8},{10,11... | collective-permute-start | bytes 491528 | tf_op jit(solution)/shard_map/ppermute | solution.py:465
  16.5 0.4 all-to-all-done.parcel_ref
  16.9 3.4 %force.1.force_ref = f32[17,5,200,128]{3,2,1,0:T(8,128)S(1)} custom-call(f32[16,8,128]{2,1,0:T(8,128)S(1)} %all-to-all-done.parcel_ref), custom_call_target="tpu_custom_call" | custom-call | flops 2013265920 | bytes 7864320 | tf_op jit(solution)/shard_map/force/pallas_call | solution.py:468
  20.3 0.0 collective-permute-done.1.far_ref
  20.3 0.0 collective-permute-done.2.near_ref
  20.3 7.8 %sweep.1 = (f32[128,640]{1,0:T(8,128)S(1)}, f32[4,40,128]{2,1,0:T(8,128)}) custom-call(f32[128,512]{1,0:T(8,128)S(1)} %get-tuple-element.18.keep_ref, f32[128,512]{1,0:T(8,128)S(1)} %get-tuple-element.17.gain_ref, f32[2,32,640]{2,1,0:T(8,128)S(1)} %collective-permute-done.1.far_ref, f32[2,32,640]{2,1,0:T(8,128)S(1)} %collective-permute-done.2.near_ref, ...), custom_call_target="tpu_custom_call" | custom-call | tf_op jit(solution)/shard_map/sweep/pallas_call | solution.py:487
  28.2 4.1 %all-to-all-start.1 = ((f32[4,40,128]{2,1,0:T(8,128)}), f32[4,40,128]{2,1,0:T(8,128)S(1)}, u32[]{:S(2)}, u32[]{:S(2)}) async-start(f32[4,40,128]{2,1,0:T(8,128)} %get-tuple-element.16), calls=%async_computation.1 | async-start | bytes 163840 | tf_op jit(solution)/shard_map/all_to_all | solution.py:455
  32.2 1.4 %smooth.1 = (f32[128,512]{1,0:T(8,128)S(1)}, f32[160,512]{1,0:T(8,128)S(1)}) custom-call(f32[128,640]{1,0:T(8,128)S(1)} %get-tuple-element.13.grad_ref), custom_call_target="tpu_custom_call" | custom-call | flops 402653184 | bytes 524288 | tf_op jit(solution)/shard_map/smooth/pallas_call | solution.py:502
  33.6 4.4 %all-to-all-done.1 = f32[4,40,128]{2,1,0:T(8,128)S(1)} async-done(((f32[4,40,128]{2,1,0:T(8,128)}), f32[4,40,128]{2,1,0:T(8,128)S(1)}, u32[]{:S(2)}, u32[]{:S(2)}) %all-to-all-start.1) | async-done | bytes 81952 | tf_op jit(solution)/shard_map/all_to_all | solution.py:455
  38.0 1.1 %finish.1 = f32[128,512]{1,0:T(8,128)} custom-call(f32[128,512]{1,0:T(8,128)S(1)} %get-tuple-element.14.own_ref, f32[160,512]{1,0:T(8,128)S(1)} %get-tuple-element.15.weights_ref, f32[160,128]{1,0:T(8,128)S(1)} %bitcast.6), custom_call_target="tpu_custom_call" | custom-call | tf_op jit(solution)/shard_map/finish/pallas_call | solution.py:513
Async XLA Ops:
  1.4 11.5 %collective-permute-start = (f32[4,128,128]{2,1,0:T(8,128)S(1)}, f32[4,128,128]{2,1,0:T(8,128)S(1)}, u32[]{:S(2)}, u32[]{:S(2)}) collective-permute-start(f32[4,128,128]{2,1,0:T(8,128)S(1)} %give_west.1.after_ref), channel_id=1, source_target_pairs={{4,0},{8,4},{12,8},{5,1},{9,5},{13,9},{6,2},{10,6},{14,10},{7,3},{... | collective-permute-start | bytes 786440 | tf_op jit(solution)/shard_map/ppermute | solution.py:441
  4.2 12.6 %all-to-all-start = ((f32[16,8,128]{2,1,0:T(8,128)}), f32[16,8,128]{2,1,0:T(8,128)S(1)}, u32[]{:S(2)}, u32[]{:S(2)}) async-start(f32[16,8,128]{2,1,0:T(8,128)} %give_gauges.1), calls=%async_computation | async-start | bytes 131072 | tf_op jit(solution)/shard_map/all_to_all | solution.py:455
  13.0 7.3 %collective-permute-start.1 = (f32[2,32,640]{2,1,0:T(8,128)S(1)}, f32[2,32,640]{2,1,0:T(8,128)S(1)}, u32[]{:S(2)}, u32[]{:S(2)}) collective-permute-start(f32[2,32,640]{2,1,0:T(8,128)S(1)} %get-tuple-element.11), channel_id=1, source_target_pairs={{1,2},{2,1},{5,6},{6,5},{9,10},{10,9},{13,14},{14,13},{17,18},{18,... | collective-permute-start | bytes 491528 | tf_op jit(solution)/shard_map/ppermute | solution.py:464
  13.7 6.6 %collective-permute-start.2 = (f32[2,32,640]{2,1,0:T(8,128)S(1)}, f32[2,32,640]{2,1,0:T(8,128)S(1)}, u32[]{:S(2)}, u32[]{:S(2)}) collective-permute-start(f32[2,32,640]{2,1,0:T(8,128)S(1)} %get-tuple-element.12), channel_id=1, source_target_pairs={{0,1},{1,0},{2,3},{3,2},{4,5},{5,4},{6,7},{7,6},{8,9},{9,8},{10,11... | collective-permute-start | bytes 491528 | tf_op jit(solution)/shard_map/ppermute | solution.py:465
  28.2 9.9 %all-to-all-start.1 = ((f32[4,40,128]{2,1,0:T(8,128)}), f32[4,40,128]{2,1,0:T(8,128)S(1)}, u32[]{:S(2)}, u32[]{:S(2)}) async-start(f32[4,40,128]{2,1,0:T(8,128)} %get-tuple-element.16), calls=%async_computation.1 | async-start | bytes 163840 | tf_op jit(solution)/shard_map/all_to_all | solution.py:455

commit v17 on v16

--- a/solution.py
+++ b/solution.py
@@ -353,7 +353,7 @@
         sums_ref[i] = sums
 
 
-def smooth(halo, lons, grad_ref, out_ref, weights_ref):
+def smooth(halo, order, grad_ref, out_ref, weights_ref):
     width = out_ref.shape[1]
     length = 2.0 * width
     planes = grad_ref.shape[1] // LANES
@@ -369,7 +369,7 @@
     me = lax.axis_index("lon")
     shape = (8 + halo, width)
     kind, column = lax.broadcasted_iota(jnp.int32, shape, 0), lax.broadcasted_iota(jnp.int32, shape, 1)
-    for source in range(lons):
+    for place, source in enumerate(order):
         strip = jnp.where(kind < 2, source, source + 1)
         left = ((kind == 0) | (kind == 2)) & (strip > me)
         right = ((kind == 1) | (kind == 3)) & (strip < me)
@@ -377,7 +377,7 @@
         away = jnp.where(left, (strip - me) * width - column, (me - strip - 1) * width + column + 1)
         away = jnp.where(near, jnp.abs(kind - 8 - column), away)
         weights = jnp.where(left | right | near, jnp.exp(-jnp.maximum(away, 0).astype(jnp.float32) / length), 0.0)
-        weights_ref[source * shape[0] : (source + 1) * shape[0], :] = weights
+        weights_ref[place * shape[0] : (place + 1) * shape[0], :] = weights
 
 
 def finish(own_ref, weights_ref, sums_ref, out_ref):
@@ -435,7 +435,7 @@
         + put(coastal_tiles.reshape(1, 1, coast_count), 2 * blocks, 2)
     ).astype(jnp.float32) + put(jnp.transpose(gauge_resid, (1, 2, 0)), blocks, 0)
     west = pl.pallas_call(
-        functools.partial(give_west, 2 * halo), out_shape=f32(4, height, LANES), in_specs=vmem(2), out_specs=vmem(1)[0],
+        functools.partial(give_west, 2 * halo), out_shape=f32(2, height, LANES), in_specs=vmem(2), out_specs=vmem(1)[0],
         compiler_params=params, name="give_west",
     )(keep, gain)
     right = lax.ppermute(west, "lon", [(i + 1, i) for i in range(lons - 1)])
@@ -498,9 +498,10 @@
         name="sweep",
     )(keep, gain, far, near, right, pushes)
 
-    sums = exchange(sums, "lon")
+    order = list(range(lons // 2, lons)) + list(range(lons // 2))[::-1]
+    sums = exchange(sums, "lon", [order])
     own, weights = pl.pallas_call(
-        functools.partial(smooth, halo, lons),
+        functools.partial(smooth, halo, order),
         out_shape=(f32(height, width), f32(lons * (8 + halo), width)),
         in_specs=vmem(1),
         out_specs=tuple(vmem(2)),

time: 39.5 us -> 38.6 us (0.977)
  waiting for transfers between devices: 4.78 us -> 2.85 us
  starting transfers between devices: 17.5 us -> 18.6 us
    all_to_all x2, waiting for transfers between devices: 4.78 us -> 2.85 us  [exchange(): lax.all_to_all(array, axes, split_axis=0, concat_axis=0, axis_index_group...]
    all_to_all x2, starting transfers between devices: 12.8 us -> 13.8 us  [exchange(): lax.all_to_all(array, axes, split_axis=0, concat_axis=0, axis_index_group...]
  transfers between devices with their start and end apart: 5 -> 5, of which waited for: 2 -> 2; matrix products, arithmetic and copies ran while one was open for 2% -> 2% of each run, Pallas kernels for 14% -> 15%
where the time goes in v17:
time: 38.6 us; the launch traced here: 38.3 us
  starting transfers between devices  18.6 us (48%)
  Pallas kernels  14.7 us (38%)
  waiting for transfers between devices  2.85 us (7%)
  other arithmetic  2.05 us (5%)
    all_to_all x2, starting transfers between devices, exchange(): lax.all_to_all(array, axes, split_axis=0, concat_axis=0, axis_index_group...  13.8 us
    pallas_call x1, Pallas kernels, local(): pl.pallas_call(functools.partial(sweep, steps), out_shape=(f32(height, pl...  7.84 us
    pallas_call x1, Pallas kernels, local(): pl.pallas_call(functools.partial(force, steps, halo, height, width), out_...  3.4 us
    all_to_all x2, waiting for transfers between devices, exchange(): lax.all_to_all(array, axes, split_axis=0, concat_axis=0, axis_index_group...  2.85 us
    ppermute x1, starting transfers between devices, local(): lax.ppermute(near, ROW_AXES, [pair for i in range(0, row_tiles, 2) for pa...  2.83 us
    pallas_call x1, Pallas kernels, local(): pl.pallas_call(functools.partial(smooth, halo, order), out_shape=(f32(hei...  1.37 us
    ppermute x1, starting transfers between devices, local(): right = lax.ppermute(west, 'lon', [(i + 1, i) for i in range(lons - 1)])  1.29 us
    mul x1, other arithmetic, local(): (courant * 0.5) ** 2 * jnp.maximum(depth + surface, depth_floor) * keep  1.29 us
  transfers between devices with their start and end apart: 5, of which 2 were waited for; matrix products, arithmetic and copies ran while one was open for 2% of the time, Pallas kernels for 15%

profile of v17, /device:TPU:0, one launch (start us, length us, event | category | flops | bytes accessed | tf_op | source)
XLA Modules:
  0.0 38.3 jit_solution(15220035217138289658)
XLA Ops:
  0.0 1.3 %multiply_multiply_fusion = (f32[128,512]{1,0:T(8,128)S(1)}, f32[128,512]{1,0:T(8,128)S(1)}) fusion(f32[128,512]{1,0:T(8,128)} %param.9, f32[128,512]{1,0:T(8,128)} %param.10, s32[128,512]{1,0:T(8,128)} %param.12, f32[128,512]{1,0:T(8,128)} %param.11), kind=kLoop, calls=%fused_computation | loop fusion | flops 458752 | bytes 1572864 | tf_op jit(solution)/shard_map/mul | solution.py:421
  1.3 0.1 give_west.1.after_ref
  1.4 1.3 %collective-permute-start = (f32[2,128,128]{2,1,0:T(8,128)S(1)}, f32[2,128,128]{2,1,0:T(8,128)S(1)}, u32[]{:S(2)}, u32[]{:S(2)}) collective-permute-start(f32[2,128,128]{2,1,0:T(8,128)S(1)} %give_west.1.after_ref), channel_id=1, source_target_pairs={{4,0},{8,4},{12,8},{5,1},{9,5},{13,9},{6,2},{10,6},{14,10},{7,3},{... | collective-permute-start | bytes 393224 | tf_op jit(solution)/shard_map/ppermute | solution.py:441
  2.7 0.8 %pad_add_fusion.gauge_ref = f32[5,4,16]{2,1,0:T(4,128)S(1)} fusion(f32[2,4,16]{2,1,0:T(4,128)} %bitcast.7, s32[1,1,8]{2,1,0:T(1,128)} %bitcast.9, s32[1,1,16]{2,1,0:T(1,128)} %bitcast.10, s32[1,1,16]{2,1,0:T(1,128)} %bitcast.11, s32[2,4,16]{2,1,0:T(4,128)} %bitcast.8), kind=kLoop, calls=%fused_computation.2 | loop fusion | flops 1600 | bytes 2464 | tf_op jit(solution)/shard_map/add | solution.py:431
  3.4 0.8 %give_gauges.1 = f32[16,8,128]{2,1,0:T(8,128)} custom-call(f32[5,4,16]{2,1,0:T(4,128)S(1)} %pad_add_fusion.gauge_ref, f32[2,128,128]{2,1,0:T(8,128)S(1)} %give_west.1.after_ref), custom_call_target="tpu_custom_call" | custom-call | bytes 10000000 | tf_op jit(solution)/shard_map/give_gauges/pallas_call | solution.py:443
  4.2 8.7 %all-to-all-start = ((f32[16,8,128]{2,1,0:T(8,128)}), f32[16,8,128]{2,1,0:T(8,128)S(1)}, u32[]{:S(2)}, u32[]{:S(2)}) async-start(f32[16,8,128]{2,1,0:T(8,128)} %give_gauges.1), calls=%async_computation | async-start | bytes 131072 | tf_op jit(solution)/shard_map/all_to_all | solution.py:455
  12.9 0.0 collective-permute-done.right_ref
  12.9 0.1 give_rows.1
  13.0 0.7 %collective-permute-start.1 = (f32[2,32,640]{2,1,0:T(8,128)S(1)}, f32[2,32,640]{2,1,0:T(8,128)S(1)}, u32[]{:S(2)}, u32[]{:S(2)}) collective-permute-start(f32[2,32,640]{2,1,0:T(8,128)S(1)} %get-tuple-element.11), channel_id=1, source_target_pairs={{1,2},{2,1},{5,6},{6,5},{9,10},{10,9},{13,14},{14,13},{17,18},{18,... | collective-permute-start | bytes 491528 | tf_op jit(solution)/shard_map/ppermute | solution.py:464
  13.7 2.8 %collective-permute-start.2 = (f32[2,32,640]{2,1,0:T(8,128)S(1)}, f32[2,32,640]{2,1,0:T(8,128)S(1)}, u32[]{:S(2)}, u32[]{:S(2)}) collective-permute-start(f32[2,32,640]{2,1,0:T(8,128)S(1)} %get-tuple-element.12), channel_id=1, source_target_pairs={{0,1},{1,0},{2,3},{3,2},{4,5},{5,4},{6,7},{7,6},{8,9},{9,8},{10,11... | collective-permute-start | bytes 491528 | tf_op jit(solution)/shard_map/ppermute | solution.py:465
  16.5 0.4 all-to-all-done.parcel_ref
  16.9 3.4 %force.1.force_ref = f32[17,5,200,128]{3,2,1,0:T(8,128)S(1)} custom-call(f32[16,8,128]{2,1,0:T(8,128)S(1)} %all-to-all-done.parcel_ref), custom_call_target="tpu_custom_call" | custom-call | flops 2013265920 | bytes 7864320 | tf_op jit(solution)/shard_map/force/pallas_call | solution.py:468
  20.3 0.0 collective-permute-done.1.far_ref
  20.3 0.0 collective-permute-done.2.near_ref
  20.3 7.8 %sweep.1 = (f32[128,640]{1,0:T(8,128)S(1)}, f32[4,40,128]{2,1,0:T(8,128)}) custom-call(f32[128,512]{1,0:T(8,128)S(1)} %get-tuple-element.18.keep_ref, f32[128,512]{1,0:T(8,128)S(1)} %get-tuple-element.17.gain_ref, f32[2,32,640]{2,1,0:T(8,128)S(1)} %collective-permute-done.1.far_ref, f32[2,32,640]{2,1,0:T(8,128)S(1)} %collective-permute-done.2.near_ref, ...), custom_call_target="tpu_custom_call" | custom-call | tf_op jit(solution)/shard_map/sweep/pallas_call | solution.py:487
  28.2 5.1 %all-to-all-start.1 = ((f32[4,40,128]{2,1,0:T(8,128)}), f32[4,40,128]{2,1,0:T(8,128)S(1)}, u32[]{:S(2)}, u32[]{:S(2)}) async-start(f32[4,40,128]{2,1,0:T(8,128)} %get-tuple-element.16), calls=%async_computation.1 | async-start | bytes 163840 | tf_op jit(solution)/shard_map/all_to_all | solution.py:455
  33.3 1.4 %smooth.1 = (f32[128,512]{1,0:T(8,128)S(1)}, f32[160,512]{1,0:T(8,128)S(1)}) custom-call(f32[128,640]{1,0:T(8,128)S(1)} %get-tuple-element.13.grad_ref), custom_call_target="tpu_custom_call" | custom-call | flops 402653184 | bytes 524288 | tf_op jit(solution)/shard_map/smooth/pallas_call | solution.py:503
  34.7 2.5 %all-to-all-done.1 = f32[4,40,128]{2,1,0:T(8,128)S(1)} async-done(((f32[4,40,128]{2,1,0:T(8,128)}), f32[4,40,128]{2,1,0:T(8,128)S(1)}, u32[]{:S(2)}, u32[]{:S(2)}) %all-to-all-start.1) | async-done | bytes 81952 | tf_op jit(solution)/shard_map/all_to_all | solution.py:455
  37.1 1.1 %finish.1 = f32[128,512]{1,0:T(8,128)} custom-call(f32[128,512]{1,0:T(8,128)S(1)} %get-tuple-element.14.own_ref, f32[160,512]{1,0:T(8,128)S(1)} %get-tuple-element.15.weights_ref, f32[160,128]{1,0:T(8,128)S(1)} %bitcast.6), custom_call_target="tpu_custom_call" | custom-call | tf_op jit(solution)/shard_map/finish/pallas_call | solution.py:514
Async XLA Ops:
  1.4 11.5 %collective-permute-start = (f32[2,128,128]{2,1,0:T(8,128)S(1)}, f32[2,128,128]{2,1,0:T(8,128)S(1)}, u32[]{:S(2)}, u32[]{:S(2)}) collective-permute-start(f32[2,128,128]{2,1,0:T(8,128)S(1)} %give_west.1.after_ref), channel_id=1, source_target_pairs={{4,0},{8,4},{12,8},{5,1},{9,5},{13,9},{6,2},{10,6},{14,10},{7,3},{... | collective-permute-start | bytes 393224 | tf_op jit(solution)/shard_map/ppermute | solution.py:441
  4.2 12.6 %all-to-all-start = ((f32[16,8,128]{2,1,0:T(8,128)}), f32[16,8,128]{2,1,0:T(8,128)S(1)}, u32[]{:S(2)}, u32[]{:S(2)}) async-start(f32[16,8,128]{2,1,0:T(8,128)} %give_gauges.1), calls=%async_computation | async-start | bytes 131072 | tf_op jit(solution)/shard_map/all_to_all | solution.py:455
  13.0 7.3 %collective-permute-start.1 = (f32[2,32,640]{2,1,0:T(8,128)S(1)}, f32[2,32,640]{2,1,0:T(8,128)S(1)}, u32[]{:S(2)}, u32[]{:S(2)}) collective-permute-start(f32[2,32,640]{2,1,0:T(8,128)S(1)} %get-tuple-element.11), channel_id=1, source_target_pairs={{1,2},{2,1},{5,6},{6,5},{9,10},{10,9},{13,14},{14,13},{17,18},{18,... | collective-permute-start | bytes 491528 | tf_op jit(solution)/shard_map/ppermute | solution.py:464
  13.7 6.6 %collective-permute-start.2 = (f32[2,32,640]{2,1,0:T(8,128)S(1)}, f32[2,32,640]{2,1,0:T(8,128)S(1)}, u32[]{:S(2)}, u32[]{:S(2)}) collective-permute-start(f32[2,32,640]{2,1,0:T(8,128)S(1)} %get-tuple-element.12), channel_id=1, source_target_pairs={{0,1},{1,0},{2,3},{3,2},{4,5},{5,4},{6,7},{7,6},{8,9},{9,8},{10,11... | collective-permute-start | bytes 491528 | tf_op jit(solution)/shard_map/ppermute | solution.py:465
  28.2 9.0 %all-to-all-start.1 = ((f32[4,40,128]{2,1,0:T(8,128)}), f32[4,40,128]{2,1,0:T(8,128)S(1)}, u32[]{:S(2)}, u32[]{:S(2)}) async-start(f32[4,40,128]{2,1,0:T(8,128)} %get-tuple-element.16), calls=%async_computation.1 | async-start | bytes 163840 | tf_op jit(solution)/shard_map/all_to_all | solution.py:455

commit v18 on v17

--- a/solution.py
+++ b/solution.py
@@ -229,13 +229,16 @@
         parts += [high, (whole - high.astype(jnp.float32)).astype(jnp.bfloat16)]
     parts = jnp.concatenate(parts, axis=0)
     shape = (columns, LANES)
-    column = lax.broadcasted_iota(jnp.int32, shape, 0)
-    for c in every:
-        deal = (column == lax.broadcasted_iota(jnp.int32, shape, 1) * planes + c).astype(jnp.float32)
-        dealt = jnp.dot(parts, deal.astype(jnp.bfloat16), preferred_element_type=jnp.float32)
-        for kind in range(2):
-            at = 2 * kind * rows_all
-            plain[kind, c, 0:rows_all, :] = dealt[at : at + rows_all] + dealt[at + rows_all : at + 2 * rows_all]
+    ahead = lax.broadcasted_iota(jnp.int32, shape, 0) - lax.broadcasted_iota(jnp.int32, shape, 1) * planes
+    for first in range(0, planes, 2):
+        pair = range(first, min(first + 2, planes))
+        deal = jnp.concatenate([(ahead == c).astype(jnp.float32).astype(jnp.bfloat16) for c in pair], axis=1)
+        dealt = jnp.dot(parts, deal, preferred_element_type=jnp.float32)
+        for i, c in enumerate(pair):
+            piece = dealt[:, i * LANES : (i + 1) * LANES]
+            for kind in range(2):
+                at = 2 * kind * rows_all
+                plain[kind, c, 0:rows_all, :] = piece[at : at + rows_all] + piece[at + rows_all : at + 2 * rows_all]
     for kind, goal in enumerate((keeps, gains)):
         for q in range(blocks):
             for c in every:
@@ -454,7 +457,8 @@
     def exchange(array, axes, groups=None):
         return lax.all_to_all(array, axes, split_axis=0, concat_axis=0, axis_index_groups=groups, tiled=True)
 
-    group = sorted(range(tiles), key=lambda tile: (tile % row_tiles in (0, row_tiles - 1), -(tile // row_tiles)))
+    order = list(range(lons // 2, lons)) + list(range(lons // 2))[::-1]
+    group = sorted(range(tiles), key=lambda tile: (tile % row_tiles in (0, row_tiles - 1), order.index(tile // row_tiles)))
     parcel = exchange(parcel, GRID_AXES, [group])
 
     far, near = pl.pallas_call(
@@ -498,7 +502,6 @@
         name="sweep",
     )(keep, gain, far, near, right, pushes)
 
-    order = list(range(lons // 2, lons)) + list(range(lons // 2))[::-1]
     sums = exchange(sums, "lon", [order])
     own, weights = pl.pallas_call(
         functools.partial(smooth, halo, order),

time: 38.6 us -> 38.3 us (level)
  waiting for transfers between devices: 2.85 us -> 3.37 us
  starting transfers between devices: 18.6 us -> 18.1 us
  Pallas kernels: 14.7 us -> 14.3 us
    all_to_all x2, waiting for transfers between devices: 2.85 us -> 3.36 us  [exchange(): lax.all_to_all(array, axes, split_axis=0, concat_axis=0, axis_index_group...]
    all_to_all x2, starting transfers between devices: 13.8 us -> 13.3 us  [exchange(): lax.all_to_all(array, axes, split_axis=0, concat_axis=0, axis_index_group...]
    pallas_call x1, Pallas kernels: 7.84 us -> 7.44 us  [local(): pl.pallas_call(functools.partial(sweep, steps), out_shape=(f32(height, pl...]
where the time goes in v18:
time: 38.3 us; the launch traced here: 37.9 us
  starting transfers between devices  18.1 us (47%)
  Pallas kernels  14.3 us (37%)
  waiting for transfers between devices  3.37 us (9%)
  other arithmetic  2.05 us (5%)
    all_to_all x2, starting transfers between devices, exchange(): lax.all_to_all(array, axes, split_axis=0, concat_axis=0, axis_index_group...  13.3 us
    pallas_call x1, Pallas kernels, local(): pl.pallas_call(functools.partial(sweep, steps), out_shape=(f32(height, pl...  7.44 us
    pallas_call x1, Pallas kernels, local(): pl.pallas_call(functools.partial(force, steps, halo, height, width), out_...  3.4 us
    all_to_all x2, waiting for transfers between devices, exchange(): lax.all_to_all(array, axes, split_axis=0, concat_axis=0, axis_index_group...  3.36 us
    ppermute x1, starting transfers between devices, local(): lax.ppermute(near, ROW_AXES, [pair for i in range(0, row_tiles, 2) for pa...  2.85 us
    pallas_call x1, Pallas kernels, local(): pl.pallas_call(functools.partial(smooth, halo, order), out_shape=(f32(hei...  1.37 us
    ppermute x1, starting transfers between devices, local(): right = lax.ppermute(west, 'lon', [(i + 1, i) for i in range(lons - 1)])  1.29 us
    mul x1, other arithmetic, local(): (courant * 0.5) ** 2 * jnp.maximum(depth + surface, depth_floor) * keep  1.29 us
  transfers between devices with their start and end apart: 5, of which 2 were waited for; matrix products, arithmetic and copies ran while one was open for 2% of the time, Pallas kernels for 15%

profile of v18, /device:TPU:0, one launch (start us, length us, event | category | flops | bytes accessed | tf_op | source)
XLA Modules:
  0.0 37.9 jit_solution(14625371974852652636)
XLA Ops:
  0.0 1.3 %multiply_multiply_fusion = (f32[128,512]{1,0:T(8,128)S(1)}, f32[128,512]{1,0:T(8,128)S(1)}) fusion(f32[128,512]{1,0:T(8,128)} %param.9, f32[128,512]{1,0:T(8,128)} %param.10, s32[128,512]{1,0:T(8,128)} %param.12, f32[128,512]{1,0:T(8,128)} %param.11), kind=kLoop, calls=%fused_computation | loop fusion | flops 458752 | bytes 1572864 | tf_op jit(solution)/shard_map/mul | solution.py:424
  1.3 0.1 give_west.1.after_ref
  1.4 1.3 %collective-permute-start = (f32[2,128,128]{2,1,0:T(8,128)S(1)}, f32[2,128,128]{2,1,0:T(8,128)S(1)}, u32[]{:S(2)}, u32[]{:S(2)}) collective-permute-start(f32[2,128,128]{2,1,0:T(8,128)S(1)} %give_west.1.after_ref), channel_id=1, source_target_pairs={{4,0},{8,4},{12,8},{5,1},{9,5},{13,9},{6,2},{10,6},{14,10},{7,3},{... | collective-permute-start | bytes 393224 | tf_op jit(solution)/shard_map/ppermute | solution.py:444
  2.7 0.8 %pad_add_fusion.gauge_ref = f32[5,4,16]{2,1,0:T(4,128)S(1)} fusion(f32[2,4,16]{2,1,0:T(4,128)} %bitcast.7, s32[1,1,8]{2,1,0:T(1,128)} %bitcast.9, s32[1,1,16]{2,1,0:T(1,128)} %bitcast.10, s32[1,1,16]{2,1,0:T(1,128)} %bitcast.11, s32[2,4,16]{2,1,0:T(4,128)} %bitcast.8), kind=kLoop, calls=%fused_computation.2 | loop fusion | flops 1600 | bytes 2464 | tf_op jit(solution)/shard_map/add | solution.py:434
  3.4 0.8 %give_gauges.1 = f32[16,8,128]{2,1,0:T(8,128)} custom-call(f32[5,4,16]{2,1,0:T(4,128)S(1)} %pad_add_fusion.gauge_ref, f32[2,128,128]{2,1,0:T(8,128)S(1)} %give_west.1.after_ref), custom_call_target="tpu_custom_call" | custom-call | bytes 10000000 | tf_op jit(solution)/shard_map/give_gauges/pallas_call | solution.py:446
  4.2 8.7 %all-to-all-start = ((f32[16,8,128]{2,1,0:T(8,128)}), f32[16,8,128]{2,1,0:T(8,128)S(1)}, u32[]{:S(2)}, u32[]{:S(2)}) async-start(f32[16,8,128]{2,1,0:T(8,128)} %give_gauges.1), calls=%async_computation | async-start | bytes 131072 | tf_op jit(solution)/shard_map/all_to_all | solution.py:458
  12.9 0.0 collective-permute-done.right_ref
  12.9 0.1 give_rows.1
  13.0 0.7 %collective-permute-start.1 = (f32[2,32,640]{2,1,0:T(8,128)S(1)}, f32[2,32,640]{2,1,0:T(8,128)S(1)}, u32[]{:S(2)}, u32[]{:S(2)}) collective-permute-start(f32[2,32,640]{2,1,0:T(8,128)S(1)} %get-tuple-element.11), channel_id=1, source_target_pairs={{1,2},{2,1},{5,6},{6,5},{9,10},{10,9},{13,14},{14,13},{17,18},{18,... | collective-permute-start | bytes 491528 | tf_op jit(solution)/shard_map/ppermute | solution.py:468
  13.7 2.8 %collective-permute-start.2 = (f32[2,32,640]{2,1,0:T(8,128)S(1)}, f32[2,32,640]{2,1,0:T(8,128)S(1)}, u32[]{:S(2)}, u32[]{:S(2)}) collective-permute-start(f32[2,32,640]{2,1,0:T(8,128)S(1)} %get-tuple-element.12), channel_id=1, source_target_pairs={{0,1},{1,0},{2,3},{3,2},{4,5},{5,4},{6,7},{7,6},{8,9},{9,8},{10,11... | collective-permute-start | bytes 491528 | tf_op jit(solution)/shard_map/ppermute | solution.py:469
  16.5 0.9 %all-to-all-done.parcel_ref = f32[16,8,128]{2,1,0:T(8,128)S(1)} async-done(((f32[16,8,128]{2,1,0:T(8,128)}), f32[16,8,128]{2,1,0:T(8,128)S(1)}, u32[]{:S(2)}, u32[]{:S(2)}) %all-to-all-start) | async-done | bytes 65568 | tf_op jit(solution)/shard_map/all_to_all | solution.py:458
  17.4 3.4 %force.1.force_ref = f32[17,5,200,128]{3,2,1,0:T(8,128)S(1)} custom-call(f32[16,8,128]{2,1,0:T(8,128)S(1)} %all-to-all-done.parcel_ref), custom_call_target="tpu_custom_call" | custom-call | flops 2013265920 | bytes 7864320 | tf_op jit(solution)/shard_map/force/pallas_call | solution.py:472
  20.8 0.0 collective-permute-done.1.far_ref
  20.8 0.0 collective-permute-done.2.near_ref
  20.8 7.4 %sweep.1 = (f32[128,640]{1,0:T(8,128)S(1)}, f32[4,40,128]{2,1,0:T(8,128)}) custom-call(f32[128,512]{1,0:T(8,128)S(1)} %get-tuple-element.18.keep_ref, f32[128,512]{1,0:T(8,128)S(1)} %get-tuple-element.17.gain_ref, f32[2,32,640]{2,1,0:T(8,128)S(1)} %collective-permute-done.1.far_ref, f32[2,32,640]{2,1,0:T(8,128)S(1)} %collective-permute-done.2.near_ref, ...), custom_call_target="tpu_custom_call" | custom-call | tf_op jit(solution)/shard_map/sweep/pallas_call | solution.py:491
  28.3 4.7 %all-to-all-start.1 = ((f32[4,40,128]{2,1,0:T(8,128)}), f32[4,40,128]{2,1,0:T(8,128)S(1)}, u32[]{:S(2)}, u32[]{:S(2)}) async-start(f32[4,40,128]{2,1,0:T(8,128)} %get-tuple-element.16), calls=%async_computation.1 | async-start | bytes 163840 | tf_op jit(solution)/shard_map/all_to_all | solution.py:458
  32.9 1.4 %smooth.1 = (f32[128,512]{1,0:T(8,128)S(1)}, f32[160,512]{1,0:T(8,128)S(1)}) custom-call(f32[128,640]{1,0:T(8,128)S(1)} %get-tuple-element.13.grad_ref), custom_call_target="tpu_custom_call" | custom-call | flops 402653184 | bytes 524288 | tf_op jit(solution)/shard_map/smooth/pallas_call | solution.py:506
  34.3 2.5 %all-to-all-done.1 = f32[4,40,128]{2,1,0:T(8,128)S(1)} async-done(((f32[4,40,128]{2,1,0:T(8,128)}), f32[4,40,128]{2,1,0:T(8,128)S(1)}, u32[]{:S(2)}, u32[]{:S(2)}) %all-to-all-start.1) | async-done | bytes 81952 | tf_op jit(solution)/shard_map/all_to_all | solution.py:458
  36.8 1.1 %finish.1 = f32[128,512]{1,0:T(8,128)} custom-call(f32[128,512]{1,0:T(8,128)S(1)} %get-tuple-element.14.own_ref, f32[160,512]{1,0:T(8,128)S(1)} %get-tuple-element.15.weights_ref, f32[160,128]{1,0:T(8,128)S(1)} %bitcast.6), custom_call_target="tpu_custom_call" | custom-call | tf_op jit(solution)/shard_map/finish/pallas_call | solution.py:517
Async XLA Ops:
  1.4 11.5 %collective-permute-start = (f32[2,128,128]{2,1,0:T(8,128)S(1)}, f32[2,128,128]{2,1,0:T(8,128)S(1)}, u32[]{:S(2)}, u32[]{:S(2)}) collective-permute-start(f32[2,128,128]{2,1,0:T(8,128)S(1)} %give_west.1.after_ref), channel_id=1, source_target_pairs={{4,0},{8,4},{12,8},{5,1},{9,5},{13,9},{6,2},{10,6},{14,10},{7,3},{... | collective-permute-start | bytes 393224 | tf_op jit(solution)/shard_map/ppermute | solution.py:444
  4.2 13.2 %all-to-all-start = ((f32[16,8,128]{2,1,0:T(8,128)}), f32[16,8,128]{2,1,0:T(8,128)S(1)}, u32[]{:S(2)}, u32[]{:S(2)}) async-start(f32[16,8,128]{2,1,0:T(8,128)} %give_gauges.1), calls=%async_computation | async-start | bytes 131072 | tf_op jit(solution)/shard_map/all_to_all | solution.py:458
  13.0 7.8 %collective-permute-start.1 = (f32[2,32,640]{2,1,0:T(8,128)S(1)}, f32[2,32,640]{2,1,0:T(8,128)S(1)}, u32[]{:S(2)}, u32[]{:S(2)}) collective-permute-start(f32[2,32,640]{2,1,0:T(8,128)S(1)} %get-tuple-element.11), channel_id=1, source_target_pairs={{1,2},{2,1},{5,6},{6,5},{9,10},{10,9},{13,14},{14,13},{17,18},{18,... | collective-permute-start | bytes 491528 | tf_op jit(solution)/shard_map/ppermute | solution.py:468
  13.7 7.1 %collective-permute-start.2 = (f32[2,32,640]{2,1,0:T(8,128)S(1)}, f32[2,32,640]{2,1,0:T(8,128)S(1)}, u32[]{:S(2)}, u32[]{:S(2)}) collective-permute-start(f32[2,32,640]{2,1,0:T(8,128)S(1)} %get-tuple-element.12), channel_id=1, source_target_pairs={{0,1},{1,0},{2,3},{3,2},{4,5},{5,4},{6,7},{7,6},{8,9},{9,8},{10,11... | collective-permute-start | bytes 491528 | tf_op jit(solution)/shard_map/ppermute | solution.py:469
  28.3 8.5 %all-to-all-start.1 = ((f32[4,40,128]{2,1,0:T(8,128)}), f32[4,40,128]{2,1,0:T(8,128)S(1)}, u32[]{:S(2)}, u32[]{:S(2)}) async-start(f32[4,40,128]{2,1,0:T(8,128)} %get-tuple-element.16), calls=%async_computation.1 | async-start | bytes 163840 | tf_op jit(solution)/shard_map/all_to_all | solution.py:458

commit v19 on v18

--- a/solution.py
+++ b/solution.py
@@ -11,7 +11,7 @@
 STEPS_BLOCK = 8
 LANES = 128
 SEG = 32
-LEVELS = 4
+LEVELS = 16
 
 courant = 0.45
 depth_floor = 0.1
@@ -43,10 +43,10 @@
 
 
 def give_west(reach, keep_ref, gain_ref, west_ref):
-    lower = lane_iota(west_ref.shape[1]) < reach
-    west_ref[0] = jnp.where(lower, keep_ref[:, :LANES], roll_lanes(gain_ref[:, :LANES], reach))
-    for spare in range(1, west_ref.shape[0]):
-        west_ref[spare] = jnp.zeros(west_ref.shape[1:], jnp.float32)
+    height = keep_ref.shape[0]
+    lower = lane_iota(height) < reach
+    west_ref[:height] = jnp.where(lower, keep_ref[:, :LANES], roll_lanes(gain_ref[:, :LANES], reach))
+    west_ref[height:] = jnp.zeros((west_ref.shape[0] - height, LANES), jnp.float32)
 
 
 def give_rows(halo, keep_ref, gain_ref, right_ref, far_ref, near_ref):
@@ -57,7 +57,7 @@
         rows = pl.ds(pl.multiple_of(south * (height - halo), halo), halo)
         for kind, source in enumerate((keep_ref, gain_ref)):
             goal[kind, :, :width] = source[rows, :]
-            goal[kind, :, width:] = jnp.where(lower, roll_lanes(right_ref[0, rows, :], -2 * halo * kind), 0.0)
+            goal[kind, :, width:] = jnp.where(lower, roll_lanes(right_ref[rows, :], -2 * halo * kind), 0.0)
 
 
 def give_gauges(height, width, blocks, samples, coast_count, gauge_ref, after_ref, parcel_ref, block_ref):
@@ -99,6 +99,11 @@
     lax.fori_loop(0, tiles, put, 0, unroll=tiles <= 16)
 
 
+def halves(value):
+    high = value.astype(jnp.bfloat16)
+    return high, (value - high.astype(jnp.float32)).astype(jnp.bfloat16)
+
+
 def dealt_column(place, planes):
     return (place & (LANES - 1)) * planes + place // LANES
 
@@ -151,8 +156,7 @@
         both = []
         for level in range(LEVELS):
             value = series_ref[pl.ds(start + level, 1), :]
-            high = value.astype(jnp.bfloat16)
-            low = (value - high.astype(jnp.float32)).astype(jnp.bfloat16)
+            high, low = halves(value)
             both.append(jnp.concatenate([hot * high, hot * low], axis=1))
         both = jnp.concatenate(both, axis=0)
         for first in range(0, planes, 2):
@@ -216,7 +220,7 @@
     parts = []
     for kind, source in enumerate((keep_ref, gain_ref)):
         far, near = far_ref[kind], near_ref[kind]
-        beside = jnp.where(lane_iota(height) < reach, roll_lanes(right_ref[0], -reach * kind), 0.0)
+        beside = jnp.where(lane_iota(height) < reach, roll_lanes(right_ref[:height], -reach * kind), 0.0)
         whole = jnp.concatenate(
             [
                 jnp.where(odd, near, far),
@@ -225,8 +229,7 @@
             ],
             axis=0,
         )
-        high = whole.astype(jnp.bfloat16)
-        parts += [high, (whole - high.astype(jnp.float32)).astype(jnp.bfloat16)]
+        parts += halves(whole)
     parts = jnp.concatenate(parts, axis=0)
     shape = (columns, LANES)
     ahead = lax.broadcasted_iota(jnp.int32, shape, 0) - lax.broadcasted_iota(jnp.int32, shape, 1) * planes
@@ -356,7 +359,7 @@
         sums_ref[i] = sums
 
 
-def smooth(halo, order, grad_ref, out_ref, weights_ref):
+def smooth(halo, order, grad_ref, out_ref, weights_ref, exact_ref):
     width = out_ref.shape[1]
     length = 2.0 * width
     planes = grad_ref.shape[1] // LANES
@@ -380,12 +383,17 @@
         away = jnp.where(left, (strip - me) * width - column, (me - strip - 1) * width + column + 1)
         away = jnp.where(near, jnp.abs(kind - 8 - column), away)
         weights = jnp.where(left | right | near, jnp.exp(-jnp.maximum(away, 0).astype(jnp.float32) / length), 0.0)
-        weights_ref[place * shape[0] : (place + 1) * shape[0], :] = weights
+        exact_ref[place * shape[0] : (place + 1) * shape[0], :] = weights
+    high, low = halves(exact_ref[...])
+    count = high.shape[0]
+    for place, part in enumerate((high, high, low)):
+        weights_ref[place * count : (place + 1) * count, :] = part
 
 
 def finish(own_ref, weights_ref, sums_ref, out_ref):
+    high, low = halves(sums_ref[...])
     out_ref[...] = own_ref[...] + lax.dot_general(
-        sums_ref[...], weights_ref[...], (((0,), (0,)), ((), ())), precision=lax.Precision.HIGHEST,
+        jnp.concatenate([high, low, high], axis=0), weights_ref[...], (((0,), (0,)), ((), ())),
         preferred_element_type=jnp.float32,
     )
 
@@ -438,7 +446,7 @@
         + put(coastal_tiles.reshape(1, 1, coast_count), 2 * blocks, 2)
     ).astype(jnp.float32) + put(jnp.transpose(gauge_resid, (1, 2, 0)), blocks, 0)
     west = pl.pallas_call(
-        functools.partial(give_west, 2 * halo), out_shape=f32(2, height, LANES), in_specs=vmem(2), out_specs=vmem(1)[0],
+        functools.partial(give_west, 2 * halo), out_shape=f32(height + 16, LANES), in_specs=vmem(2), out_specs=vmem(1)[0],
         compiler_params=params, name="give_west",
     )(keep, gain)
     right = lax.ppermute(west, "lon", [(i + 1, i) for i in range(lons - 1)])
@@ -505,9 +513,10 @@
     sums = exchange(sums, "lon", [order])
     own, weights = pl.pallas_call(
         functools.partial(smooth, halo, order),
-        out_shape=(f32(height, width), f32(lons * (8 + halo), width)),
+        out_shape=(f32(height, width), jax.ShapeDtypeStruct((3 * lons * (8 + halo), width), jnp.bfloat16)),
         in_specs=vmem(1),
         out_specs=tuple(vmem(2)),
+        scratch_shapes=[pltpu.VMEM((lons * (8 + halo), width), jnp.float32)],
         compiler_params=params,
         cost_estimate=pl.CostEstimate(
             flops=6 * 2 * height * width * width, bytes_accessed=2 * 4 * height * width, transcendentals=width * width

time: 38.3 us -> 40.1 us (1.047)
  waiting for transfers between devices: 3.37 us -> 7.39 us
  starting transfers between devices: 18.1 us -> 16.6 us
  Pallas kernels: 14.3 us -> 13.7 us
    ppermute x1, waiting for transfers between devices: 0.01 us -> 4.95 us  [local(): right = lax.ppermute(west, 'lon', [(i + 1, i) for i in range(lons - 1)])]
    all_to_all x2, starting transfers between devices: 13.3 us -> 11.8 us  [exchange(): lax.all_to_all(array, axes, split_axis=0, concat_axis=0, axis_index_group...]
    all_to_all x2, waiting for transfers between devices: 3.36 us -> 2.44 us  [exchange(): lax.all_to_all(array, axes, split_axis=0, concat_axis=0, axis_index_group...]
    pallas_call x1, Pallas kernels: 3.4 us -> 2.9 us  [local(): pl.pallas_call(functools.partial(force, steps, halo, height, width), out_...]
  transfers between devices with their start and end apart: 5 -> 5, of which waited for: 2 -> 2; matrix products, arithmetic and copies ran while one was open for 2% -> 0% of each run, Pallas kernels for 15% -> 11%
where the time goes in v19:
time: 40.1 us; the launch traced here: 39.8 us
  starting transfers between devices  16.6 us (41%)
  Pallas kernels  13.7 us (34%)
  waiting for transfers between devices  7.39 us (18%)
  other arithmetic  2.05 us (5%)
    all_to_all x2, starting transfers between devices, exchange(): lax.all_to_all(array, axes, split_axis=0, concat_axis=0, axis_index_group...  11.8 us
    pallas_call x1, Pallas kernels, local(): pl.pallas_call(functools.partial(sweep, steps), out_shape=(f32(height, pl...  7.48 us
    ppermute x1, waiting for transfers between devices, local(): right = lax.ppermute(west, 'lon', [(i + 1, i) for i in range(lons - 1)])  4.95 us
    pallas_call x1, Pallas kernels, local(): pl.pallas_call(functools.partial(force, steps, halo, height, width), out_...  2.9 us
    ppermute x1, starting transfers between devices, local(): lax.ppermute(near, ROW_AXES, [pair for i in range(0, row_tiles, 2) for pa...  2.85 us
    all_to_all x2, waiting for transfers between devices, exchange(): lax.all_to_all(array, axes, split_axis=0, concat_axis=0, axis_index_group...  2.44 us
    pallas_call x1, Pallas kernels, local(): pl.pallas_call(functools.partial(smooth, halo, order), out_shape=(f32(hei...  1.42 us
    mul x1, other arithmetic, local(): (courant * 0.5) ** 2 * jnp.maximum(depth + surface, depth_floor) * keep  1.29 us
  transfers between devices with their start and end apart: 5, of which 2 were waited for; matrix products, arithmetic and copies ran while one was open for 0% of the time, Pallas kernels for 11%

profile of v19, /device:TPU:0, one launch (start us, length us, event | category | flops | bytes accessed | tf_op | source)
XLA Modules:
  0.0 39.8 jit_solution(6565681689164806390)
XLA Ops:
  0.0 1.3 %multiply_multiply_fusion = (f32[128,512]{1,0:T(8,128)S(1)}, f32[128,512]{1,0:T(8,128)S(1)}) fusion(f32[128,512]{1,0:T(8,128)} %param.9, f32[128,512]{1,0:T(8,128)} %param.10, s32[128,512]{1,0:T(8,128)} %param.12, f32[128,512]{1,0:T(8,128)} %param.11), kind=kLoop, calls=%fused_computation | loop fusion | flops 458752 | bytes 1572864 | tf_op jit(solution)/shard_map/mul | solution.py:432
  1.3 0.1 give_west.1.after_ref
  1.4 0.8 %pad_add_fusion.gauge_ref = f32[5,4,16]{2,1,0:T(4,128)S(1)} fusion(f32[2,4,16]{2,1,0:T(4,128)} %bitcast.7, s32[1,1,8]{2,1,0:T(1,128)} %bitcast.9, s32[1,1,16]{2,1,0:T(1,128)} %bitcast.10, s32[1,1,16]{2,1,0:T(1,128)} %bitcast.11, s32[2,4,16]{2,1,0:T(4,128)} %bitcast.8), kind=kLoop, calls=%fused_computation.2 | loop fusion | flops 1600 | bytes 2464 | tf_op jit(solution)/shard_map/add | solution.py:442
  2.1 0.8 %give_gauges.1 = f32[16,8,128]{2,1,0:T(8,128)} custom-call(f32[5,4,16]{2,1,0:T(4,128)S(1)} %pad_add_fusion.gauge_ref, f32[144,128]{1,0:T(8,128)S(1)} %give_west.1.after_ref), custom_call_target="tpu_custom_call" | custom-call | bytes 10000000 | tf_op jit(solution)/shard_map/give_gauges/pallas_call | solution.py:454
  2.9 7.6 %all-to-all-start = ((f32[16,8,128]{2,1,0:T(8,128)}), f32[16,8,128]{2,1,0:T(8,128)S(1)}, u32[]{:S(2)}, u32[]{:S(2)}) async-start(f32[16,8,128]{2,1,0:T(8,128)} %give_gauges.1), calls=%async_computation | async-start | bytes 131072 | tf_op jit(solution)/shard_map/all_to_all | solution.py:466
  10.5 1.3 %collective-permute-start = (f32[144,128]{1,0:T(8,128)S(1)}, f32[144,128]{1,0:T(8,128)S(1)}, u32[]{:S(2)}, u32[]{:S(2)}) collective-permute-start(f32[144,128]{1,0:T(8,128)S(1)} %give_west.1.after_ref), channel_id=1, source_target_pairs={{4,0},{8,4},{12,8},{5,1},{9,5},{13,9},{6,2},{10,6},{14,10},{7,3},{... | collective-permute-start | bytes 221192 | tf_op jit(solution)/shard_map/ppermute | solution.py:452
  11.8 4.9 %collective-permute-done.right_ref = f32[144,128]{1,0:T(8,128)S(1)} collective-permute-done((f32[144,128]{1,0:T(8,128)S(1)}, f32[144,128]{1,0:T(8,128)S(1)}, u32[]{:S(2)}, u32[]{:S(2)}) %collective-permute-start) | collective-permute-done | bytes 73760 | tf_op jit(solution)/shard_map/ppermute | solution.py:452
  16.8 0.1 give_rows.1
  16.9 0.7 %collective-permute-start.1 = (f32[2,32,640]{2,1,0:T(8,128)S(1)}, f32[2,32,640]{2,1,0:T(8,128)S(1)}, u32[]{:S(2)}, u32[]{:S(2)}) collective-permute-start(f32[2,32,640]{2,1,0:T(8,128)S(1)} %get-tuple-element.11), channel_id=1, source_target_pairs={{1,2},{2,1},{5,6},{6,5},{9,10},{10,9},{13,14},{14,13},{17,18},{18,... | collective-permute-start | bytes 491528 | tf_op jit(solution)/shard_map/ppermute | solution.py:476
  17.5 2.8 %collective-permute-start.2 = (f32[2,32,640]{2,1,0:T(8,128)S(1)}, f32[2,32,640]{2,1,0:T(8,128)S(1)}, u32[]{:S(2)}, u32[]{:S(2)}) collective-permute-start(f32[2,32,640]{2,1,0:T(8,128)S(1)} %get-tuple-element.12), channel_id=1, source_target_pairs={{0,1},{1,0},{2,3},{3,2},{4,5},{5,4},{6,7},{7,6},{8,9},{9,8},{10,11... | collective-permute-start | bytes 491528 | tf_op jit(solution)/shard_map/ppermute | solution.py:477
  20.4 0.0 all-to-all-done.parcel_ref
  20.4 2.9 %force.1.force_ref = f32[17,5,200,128]{3,2,1,0:T(8,128)S(1)} custom-call(f32[16,8,128]{2,1,0:T(8,128)S(1)} %all-to-all-done.parcel_ref), custom_call_target="tpu_custom_call" | custom-call | flops 2013265920 | bytes 7864320 | tf_op jit(solution)/shard_map/force/pallas_call | solution.py:480
  23.3 0.0 collective-permute-done.1.far_ref
  23.3 0.0 collective-permute-done.2.near_ref
  23.3 7.5 %sweep.1 = (f32[128,640]{1,0:T(8,128)S(1)}, f32[4,40,128]{2,1,0:T(8,128)}) custom-call(f32[128,512]{1,0:T(8,128)S(1)} %get-tuple-element.18.keep_ref, f32[128,512]{1,0:T(8,128)S(1)} %get-tuple-element.17.gain_ref, f32[2,32,640]{2,1,0:T(8,128)S(1)} %collective-permute-done.1.far_ref, f32[2,32,640]{2,1,0:T(8,128)S(1)} %collective-permute-done.2.near_ref, ...), custom_call_target="tpu_custom_call" | custom-call | tf_op jit(solution)/shard_map/sweep/pallas_call | solution.py:499
  30.8 4.2 %all-to-all-start.1 = ((f32[4,40,128]{2,1,0:T(8,128)}), f32[4,40,128]{2,1,0:T(8,128)S(1)}, u32[]{:S(2)}, u32[]{:S(2)}) async-start(f32[4,40,128]{2,1,0:T(8,128)} %get-tuple-element.16), calls=%async_computation.1 | async-start | bytes 163840 | tf_op jit(solution)/shard_map/all_to_all | solution.py:466
  35.0 1.4 %smooth.1 = (f32[128,512]{1,0:T(8,128)S(1)}, bf16[480,512]{1,0:T(8,128)(2,1)S(1)}) custom-call(f32[128,640]{1,0:T(8,128)S(1)} %get-tuple-element.13.grad_ref), custom_call_target="tpu_custom_call" | custom-call | flops 402653184 | bytes 524288 | tf_op jit(solution)/shard_map/smooth/pallas_call | solution.py:514
  36.4 2.4 %all-to-all-done.1 = f32[4,40,128]{2,1,0:T(8,128)S(1)} async-done(((f32[4,40,128]{2,1,0:T(8,128)}), f32[4,40,128]{2,1,0:T(8,128)S(1)}, u32[]{:S(2)}, u32[]{:S(2)}) %all-to-all-start.1) | async-done | bytes 81952 | tf_op jit(solution)/shard_map/all_to_all | solution.py:466
  38.8 1.0 %finish.1 = f32[128,512]{1,0:T(8,128)} custom-call(f32[128,512]{1,0:T(8,128)S(1)} %get-tuple-element.14.own_ref, bf16[480,512]{1,0:T(8,128)(2,1)S(1)} %get-tuple-element.15.weights_ref, f32[160,128]{1,0:T(8,128)S(1)} %bitcast.6), custom_call_target="tpu_custom_call" | custom-call | tf_op jit(solution)/shard_map/finish/pallas_call | solution.py:526
Async XLA Ops:
  2.9 17.4 %all-to-all-start = ((f32[16,8,128]{2,1,0:T(8,128)}), f32[16,8,128]{2,1,0:T(8,128)S(1)}, u32[]{:S(2)}, u32[]{:S(2)}) async-start(f32[16,8,128]{2,1,0:T(8,128)} %give_gauges.1), calls=%async_computation | async-start | bytes 131072 | tf_op jit(solution)/shard_map/all_to_all | solution.py:466
  10.5 6.2 %collective-permute-start = (f32[144,128]{1,0:T(8,128)S(1)}, f32[144,128]{1,0:T(8,128)S(1)}, u32[]{:S(2)}, u32[]{:S(2)}) collective-permute-start(f32[144,128]{1,0:T(8,128)S(1)} %give_west.1.after_ref), channel_id=1, source_target_pairs={{4,0},{8,4},{12,8},{5,1},{9,5},{13,9},{6,2},{10,6},{14,10},{7,3},{... | collective-permute-start | bytes 221192 | tf_op jit(solution)/shard_map/ppermute | solution.py:452
  16.9 6.4 %collective-permute-start.1 = (f32[2,32,640]{2,1,0:T(8,128)S(1)}, f32[2,32,640]{2,1,0:T(8,128)S(1)}, u32[]{:S(2)}, u32[]{:S(2)}) collective-permute-start(f32[2,32,640]{2,1,0:T(8,128)S(1)} %get-tuple-element.11), channel_id=1, source_target_pairs={{1,2},{2,1},{5,6},{6,5},{9,10},{10,9},{13,14},{14,13},{17,18},{18,... | collective-permute-start | bytes 491528 | tf_op jit(solution)/shard_map/ppermute | solution.py:476
  17.5 5.8 %collective-permute-start.2 = (f32[2,32,640]{2,1,0:T(8,128)S(1)}, f32[2,32,640]{2,1,0:T(8,128)S(1)}, u32[]{:S(2)}, u32[]{:S(2)}) collective-permute-start(f32[2,32,640]{2,1,0:T(8,128)S(1)} %get-tuple-element.12), channel_id=1, source_target_pairs={{0,1},{1,0},{2,3},{3,2},{4,5},{5,4},{6,7},{7,6},{8,9},{9,8},{10,11... | collective-permute-start | bytes 491528 | tf_op jit(solution)/shard_map/ppermute | solution.py:477
  30.8 8.1 %all-to-all-start.1 = ((f32[4,40,128]{2,1,0:T(8,128)}), f32[4,40,128]{2,1,0:T(8,128)S(1)}, u32[]{:S(2)}, u32[]{:S(2)}) async-start(f32[4,40,128]{2,1,0:T(8,128)} %get-tuple-element.16), calls=%async_computation.1 | async-start | bytes 163840 | tf_op jit(solution)/shard_map/all_to_all | solution.py:466

commit v20 on v19

--- a/solution.py
+++ b/solution.py
@@ -446,7 +446,7 @@
         + put(coastal_tiles.reshape(1, 1, coast_count), 2 * blocks, 2)
     ).astype(jnp.float32) + put(jnp.transpose(gauge_resid, (1, 2, 0)), blocks, 0)
     west = pl.pallas_call(
-        functools.partial(give_west, 2 * halo), out_shape=f32(height + 16, LANES), in_specs=vmem(2), out_specs=vmem(1)[0],
+        functools.partial(give_west, 2 * halo), out_shape=f32(2 * height, LANES), in_specs=vmem(2), out_specs=vmem(1)[0],
         compiler_params=params, name="give_west",
     )(keep, gain)
     right = lax.ppermute(west, "lon", [(i + 1, i) for i in range(lons - 1)])
@@ -466,7 +466,7 @@
         return lax.all_to_all(array, axes, split_axis=0, concat_axis=0, axis_index_groups=groups, tiled=True)
 
     order = list(range(lons // 2, lons)) + list(range(lons // 2))[::-1]
-    group = sorted(range(tiles), key=lambda tile: (tile % row_tiles in (0, row_tiles - 1), order.index(tile // row_tiles)))
+    group = sorted(range(tiles), key=lambda tile: (tile % row_tiles in (0, row_tiles - 1), (tile // row_tiles - 1) % lons))
     parcel = exchange(parcel, GRID_AXES, [group])
 
     far, near = pl.pallas_call(

time: 40.1 us -> 38 us (0.948)
  waiting for transfers between devices: 7.39 us -> 4.19 us
  starting transfers between devices: 16.6 us -> 17.6 us
    ppermute x1, waiting for transfers between devices: 4.95 us -> 0.01 us  [local(): right = lax.ppermute(west, 'lon', [(i + 1, i) for i in range(lons - 1)])]
    all_to_all x2, waiting for transfers between devices: 2.44 us -> 4.18 us  [exchange(): lax.all_to_all(array, axes, split_axis=0, concat_axis=0, axis_index_group...]
    all_to_all x2, starting transfers between devices: 11.8 us -> 12.8 us  [exchange(): lax.all_to_all(array, axes, split_axis=0, concat_axis=0, axis_index_group...]
  transfers between devices with their start and end apart: 5 -> 5, of which waited for: 2 -> 2; matrix products, arithmetic and copies ran while one was open for 0% -> 2% of each run, Pallas kernels for 11% -> 14%
where the time goes in v20:
time: 38 us; the launch traced here: 37.6 us
  starting transfers between devices  17.6 us (46%)
  Pallas kernels  13.7 us (36%)
  waiting for transfers between devices  4.19 us (11%)
  other arithmetic  2.05 us (5%)
    all_to_all x2, starting transfers between devices, exchange(): lax.all_to_all(array, axes, split_axis=0, concat_axis=0, axis_index_group...  12.8 us
    pallas_call x1, Pallas kernels, local(): pl.pallas_call(functools.partial(sweep, steps), out_shape=(f32(height, pl...  7.44 us
    all_to_all x2, waiting for transfers between devices, exchange(): lax.all_to_all(array, axes, split_axis=0, concat_axis=0, axis_index_group...  4.18 us
    pallas_call x1, Pallas kernels, local(): pl.pallas_call(functools.partial(force, steps, halo, height, width), out_...  2.9 us
    ppermute x1, starting transfers between devices, local(): lax.ppermute(near, ROW_AXES, [pair for i in range(0, row_tiles, 2) for pa...  2.85 us
    pallas_call x1, Pallas kernels, local(): pl.pallas_call(functools.partial(smooth, halo, order), out_shape=(f32(hei...  1.42 us
    ppermute x1, starting transfers between devices, local(): right = lax.ppermute(west, 'lon', [(i + 1, i) for i in range(lons - 1)])  1.29 us
    mul x1, other arithmetic, local(): (courant * 0.5) ** 2 * jnp.maximum(depth + surface, depth_floor) * keep  1.29 us
  transfers between devices with their start and end apart: 5, of which 2 were waited for; matrix products, arithmetic and copies ran while one was open for 2% of the time, Pallas kernels for 14%

profile of v20, /device:TPU:0, one launch (start us, length us, event | category | flops | bytes accessed | tf_op | source)
XLA Modules:
  0.0 37.6 jit_solution(12312748014372669531)
XLA Ops:
  0.0 1.3 %multiply_multiply_fusion = (f32[128,512]{1,0:T(8,128)S(1)}, f32[128,512]{1,0:T(8,128)S(1)}) fusion(f32[128,512]{1,0:T(8,128)} %param.9, f32[128,512]{1,0:T(8,128)} %param.10, s32[128,512]{1,0:T(8,128)} %param.12, f32[128,512]{1,0:T(8,128)} %param.11), kind=kLoop, calls=%fused_computation | loop fusion | flops 458752 | bytes 1572864 | tf_op jit(solution)/shard_map/mul | solution.py:432
  1.3 0.1 give_west.1.after_ref
  1.4 1.3 %collective-permute-start = (f32[256,128]{1,0:T(8,128)S(1)}, f32[256,128]{1,0:T(8,128)S(1)}, u32[]{:S(2)}, u32[]{:S(2)}) collective-permute-start(f32[256,128]{1,0:T(8,128)S(1)} %give_west.1.after_ref), channel_id=1, source_target_pairs={{4,0},{8,4},{12,8},{5,1},{9,5},{13,9},{6,2},{10,6},{14,10},{7,3},{... | collective-permute-start | bytes 393224 | tf_op jit(solution)/shard_map/ppermute | solution.py:452
  2.7 0.8 %pad_add_fusion.gauge_ref = f32[5,4,16]{2,1,0:T(4,128)S(1)} fusion(f32[2,4,16]{2,1,0:T(4,128)} %bitcast.7, s32[1,1,8]{2,1,0:T(1,128)} %bitcast.9, s32[1,1,16]{2,1,0:T(1,128)} %bitcast.10, s32[1,1,16]{2,1,0:T(1,128)} %bitcast.11, s32[2,4,16]{2,1,0:T(4,128)} %bitcast.8), kind=kLoop, calls=%fused_computation.2 | loop fusion | flops 1600 | bytes 2464 | tf_op jit(solution)/shard_map/add | solution.py:442
  3.4 0.8 %give_gauges.1 = f32[16,8,128]{2,1,0:T(8,128)} custom-call(f32[5,4,16]{2,1,0:T(4,128)S(1)} %pad_add_fusion.gauge_ref, f32[256,128]{1,0:T(8,128)S(1)} %give_west.1.after_ref), custom_call_target="tpu_custom_call" | custom-call | bytes 10000000 | tf_op jit(solution)/shard_map/give_gauges/pallas_call | solution.py:454
  4.2 8.7 %all-to-all-start = ((f32[16,8,128]{2,1,0:T(8,128)}), f32[16,8,128]{2,1,0:T(8,128)S(1)}, u32[]{:S(2)}, u32[]{:S(2)}) async-start(f32[16,8,128]{2,1,0:T(8,128)} %give_gauges.1), calls=%async_computation | async-start | bytes 131072 | tf_op jit(solution)/shard_map/all_to_all | solution.py:466
  12.9 0.0 collective-permute-done.right_ref
  12.9 0.1 give_rows.1
  13.0 0.7 %collective-permute-start.1 = (f32[2,32,640]{2,1,0:T(8,128)S(1)}, f32[2,32,640]{2,1,0:T(8,128)S(1)}, u32[]{:S(2)}, u32[]{:S(2)}) collective-permute-start(f32[2,32,640]{2,1,0:T(8,128)S(1)} %get-tuple-element.11), channel_id=1, source_target_pairs={{1,2},{2,1},{5,6},{6,5},{9,10},{10,9},{13,14},{14,13},{17,18},{18,... | collective-permute-start | bytes 491528 | tf_op jit(solution)/shard_map/ppermute | solution.py:476
  13.7 2.8 %collective-permute-start.2 = (f32[2,32,640]{2,1,0:T(8,128)S(1)}, f32[2,32,640]{2,1,0:T(8,128)S(1)}, u32[]{:S(2)}, u32[]{:S(2)}) collective-permute-start(f32[2,32,640]{2,1,0:T(8,128)S(1)} %get-tuple-element.12), channel_id=1, source_target_pairs={{0,1},{1,0},{2,3},{3,2},{4,5},{5,4},{6,7},{7,6},{8,9},{9,8},{10,11... | collective-permute-start | bytes 491528 | tf_op jit(solution)/shard_map/ppermute | solution.py:477
  16.5 1.7 %all-to-all-done.parcel_ref = f32[16,8,128]{2,1,0:T(8,128)S(1)} async-done(((f32[16,8,128]{2,1,0:T(8,128)}), f32[16,8,128]{2,1,0:T(8,128)S(1)}, u32[]{:S(2)}, u32[]{:S(2)}) %all-to-all-start) | async-done | bytes 65568 | tf_op jit(solution)/shard_map/all_to_all | solution.py:466
  18.3 2.9 %force.1.force_ref = f32[17,5,200,128]{3,2,1,0:T(8,128)S(1)} custom-call(f32[16,8,128]{2,1,0:T(8,128)S(1)} %all-to-all-done.parcel_ref), custom_call_target="tpu_custom_call" | custom-call | flops 2013265920 | bytes 7864320 | tf_op jit(solution)/shard_map/force/pallas_call | solution.py:480
  21.2 0.0 collective-permute-done.1.far_ref
  21.2 0.0 collective-permute-done.2.near_ref
  21.2 7.4 %sweep.1 = (f32[128,640]{1,0:T(8,128)S(1)}, f32[4,40,128]{2,1,0:T(8,128)}) custom-call(f32[128,512]{1,0:T(8,128)S(1)} %get-tuple-element.18.keep_ref, f32[128,512]{1,0:T(8,128)S(1)} %get-tuple-element.17.gain_ref, f32[2,32,640]{2,1,0:T(8,128)S(1)} %collective-permute-done.1.far_ref, f32[2,32,640]{2,1,0:T(8,128)S(1)} %collective-permute-done.2.near_ref, ...), custom_call_target="tpu_custom_call" | custom-call | tf_op jit(solution)/shard_map/sweep/pallas_call | solution.py:499
  28.6 4.2 %all-to-all-start.1 = ((f32[4,40,128]{2,1,0:T(8,128)}), f32[4,40,128]{2,1,0:T(8,128)S(1)}, u32[]{:S(2)}, u32[]{:S(2)}) async-start(f32[4,40,128]{2,1,0:T(8,128)} %get-tuple-element.16), calls=%async_computation.1 | async-start | bytes 163840 | tf_op jit(solution)/shard_map/all_to_all | solution.py:466
  32.8 1.4 %smooth.1 = (f32[128,512]{1,0:T(8,128)S(1)}, bf16[480,512]{1,0:T(8,128)(2,1)S(1)}) custom-call(f32[128,640]{1,0:T(8,128)S(1)} %get-tuple-element.13.grad_ref), custom_call_target="tpu_custom_call" | custom-call | flops 402653184 | bytes 524288 | tf_op jit(solution)/shard_map/smooth/pallas_call | solution.py:514
  34.2 2.4 %all-to-all-done.1 = f32[4,40,128]{2,1,0:T(8,128)S(1)} async-done(((f32[4,40,128]{2,1,0:T(8,128)}), f32[4,40,128]{2,1,0:T(8,128)S(1)}, u32[]{:S(2)}, u32[]{:S(2)}) %all-to-all-start.1) | async-done | bytes 81952 | tf_op jit(solution)/shard_map/all_to_all | solution.py:466
  36.7 1.0 %finish.1 = f32[128,512]{1,0:T(8,128)} custom-call(f32[128,512]{1,0:T(8,128)S(1)} %get-tuple-element.14.own_ref, bf16[480,512]{1,0:T(8,128)(2,1)S(1)} %get-tuple-element.15.weights_ref, f32[160,128]{1,0:T(8,128)S(1)} %bitcast.6), custom_call_target="tpu_custom_call" | custom-call | tf_op jit(solution)/shard_map/finish/pallas_call | solution.py:526
Async XLA Ops:
  1.4 11.5 %collective-permute-start = (f32[256,128]{1,0:T(8,128)S(1)}, f32[256,128]{1,0:T(8,128)S(1)}, u32[]{:S(2)}, u32[]{:S(2)}) collective-permute-start(f32[256,128]{1,0:T(8,128)S(1)} %give_west.1.after_ref), channel_id=1, source_target_pairs={{4,0},{8,4},{12,8},{5,1},{9,5},{13,9},{6,2},{10,6},{14,10},{7,3},{... | collective-permute-start | bytes 393224 | tf_op jit(solution)/shard_map/ppermute | solution.py:452
  4.2 14.0 %all-to-all-start = ((f32[16,8,128]{2,1,0:T(8,128)}), f32[16,8,128]{2,1,0:T(8,128)S(1)}, u32[]{:S(2)}, u32[]{:S(2)}) async-start(f32[16,8,128]{2,1,0:T(8,128)} %give_gauges.1), calls=%async_computation | async-start | bytes 131072 | tf_op jit(solution)/shard_map/all_to_all | solution.py:466
  13.0 8.2 %collective-permute-start.1 = (f32[2,32,640]{2,1,0:T(8,128)S(1)}, f32[2,32,640]{2,1,0:T(8,128)S(1)}, u32[]{:S(2)}, u32[]{:S(2)}) collective-permute-start(f32[2,32,640]{2,1,0:T(8,128)S(1)} %get-tuple-element.11), channel_id=1, source_target_pairs={{1,2},{2,1},{5,6},{6,5},{9,10},{10,9},{13,14},{14,13},{17,18},{18,... | collective-permute-start | bytes 491528 | tf_op jit(solution)/shard_map/ppermute | solution.py:476
  13.7 7.5 %collective-permute-start.2 = (f32[2,32,640]{2,1,0:T(8,128)S(1)}, f32[2,32,640]{2,1,0:T(8,128)S(1)}, u32[]{:S(2)}, u32[]{:S(2)}) collective-permute-start(f32[2,32,640]{2,1,0:T(8,128)S(1)} %get-tuple-element.12), channel_id=1, source_target_pairs={{0,1},{1,0},{2,3},{3,2},{4,5},{5,4},{6,7},{7,6},{8,9},{9,8},{10,11... | collective-permute-start | bytes 491528 | tf_op jit(solution)/shard_map/ppermute | solution.py:477
  28.6 8.1 %all-to-all-start.1 = ((f32[4,40,128]{2,1,0:T(8,128)}), f32[4,40,128]{2,1,0:T(8,128)S(1)}, u32[]{:S(2)}, u32[]{:S(2)}) async-start(f32[4,40,128]{2,1,0:T(8,128)} %get-tuple-element.16), calls=%async_computation.1 | async-start | bytes 163840 | tf_op jit(solution)/shard_map/all_to_all | solution.py:466

commit v21 on v19

--- a/solution.py
+++ b/solution.py
@@ -42,22 +42,23 @@
     return row, lax.axis_index("lon"), lax.axis_size("lat") * lax.axis_size("gau"), lax.axis_size("lon")
 
 
-def give_west(reach, keep_ref, gain_ref, west_ref):
-    height = keep_ref.shape[0]
-    lower = lane_iota(height) < reach
-    west_ref[:height] = jnp.where(lower, keep_ref[:, :LANES], roll_lanes(gain_ref[:, :LANES], reach))
-    west_ref[height:] = jnp.zeros((west_ref.shape[0] - height, LANES), jnp.float32)
-
-
-def give_rows(halo, keep_ref, gain_ref, right_ref, far_ref, near_ref):
+def give_east(reach, keep_ref, gain_ref, east_ref):
     height, width = keep_ref.shape
-    lower = lane_iota(halo) < 2 * halo
+    last = slice(width - LANES, width)
+    upper = lane_iota(height) >= LANES - reach
+    east_ref[:height] = jnp.where(upper, keep_ref[:, last], roll_lanes(gain_ref[:, last], reach))
+    east_ref[height:] = jnp.zeros((east_ref.shape[0] - height, LANES), jnp.float32)
+
+
+def give_rows(halo, keep_ref, gain_ref, left_ref, far_ref, near_ref):
+    height, width = keep_ref.shape
+    upper = lane_iota(halo) >= LANES - 2 * halo
     odd = my_place()[0] & 1
     for goal, south in ((far_ref, odd), (near_ref, 1 - odd)):
         rows = pl.ds(pl.multiple_of(south * (height - halo), halo), halo)
         for kind, source in enumerate((keep_ref, gain_ref)):
             goal[kind, :, :width] = source[rows, :]
-            goal[kind, :, width:] = jnp.where(lower, roll_lanes(right_ref[rows, :], -2 * halo * kind), 0.0)
+            goal[kind, :, width:] = jnp.where(upper, roll_lanes(left_ref[rows, :], 2 * halo * kind), 0.0)
 
 
 def give_gauges(height, width, blocks, samples, coast_count, gauge_ref, after_ref, parcel_ref, block_ref):
@@ -142,7 +143,8 @@
             series_ref[8:16, cols] = fields[1]
             row = fields[2][0:1] + row_shift
             col = fields[2][1:2] + col_shift
-            col = jnp.where(col < width + 2 * halo, col, -1.0)
+            inside = jnp.where(col < width, col, -1.0)
+            col = jnp.where(col >= 0, inside, jnp.where(col >= -2 * halo, col + float(planes * LANES), -1.0))
             rows_hot[:, cols] = (at == row).astype(jnp.float32).astype(jnp.bfloat16)
             by_gauge = jnp.transpose(jnp.broadcast_to(col, (LANES, LANES)))
             for c in range(planes):
@@ -191,7 +193,7 @@
 
 
 def sweep(
-    steps, keep_ref, gain_ref, far_ref, near_ref, right_ref, force_ref,
+    steps, keep_ref, gain_ref, far_ref, near_ref, left_ref, force_ref,
     grad_ref, sums_ref,
     a, fx, fy, keeps, gains, plain,
 ):
@@ -204,7 +206,7 @@
     my_row, my_lon, row_tiles, lons = my_place()
     reach = 2 * halo
     has_top, has_bottom = my_row > 0, my_row < row_tiles - 1
-    has_right = my_lon < lons - 1
+    has_left = my_lon > 0
     odd = (jnp.zeros((halo, planes * LANES), jnp.int32) + (my_row & 1)) == 1
     lanes8 = lane_iota(8)
 
@@ -220,7 +222,7 @@
     parts = []
     for kind, source in enumerate((keep_ref, gain_ref)):
         far, near = far_ref[kind], near_ref[kind]
-        beside = jnp.where(lane_iota(height) < reach, roll_lanes(right_ref[:height], -reach * kind), 0.0)
+        beside = jnp.where(lane_iota(height) >= LANES - reach, roll_lanes(left_ref[:height], reach * kind), 0.0)
         whole = jnp.concatenate(
             [
                 jnp.where(odd, near, far),
@@ -256,7 +258,7 @@
         lane, plane = column // planes, column % planes
         return plane, jnp.where(lanes8 == lane, there, 1.0)
 
-    column_mask = dict([cell_mask(width, jnp.where(has_right, 1.0, 0.0)), cell_mask(columns - 1, 0.0)])
+    column_mask = dict([cell_mask(width, 0.0), cell_mask(columns - 1, jnp.where(has_left, 1.0, 0.0))])
     assert len(column_mask) == 2
     sublane = lax.broadcasted_iota(jnp.int32, (8, LANES), 0)
     row_mask = {}
@@ -333,10 +335,10 @@
 
     lax.fori_loop(0, steps, step, 0)
 
-    start = jnp.where(my_lon > 0, halo, 0)
+    stop = jnp.where(my_lon < lons - 1, width - halo, width)
     for c in every:
         column = lanes8 * planes + c
-        known = (column >= start) & (column < width + halo)
+        known = (column < stop) | (column >= columns - halo)
         for r in range(0, height, 8):
             s, q = divmod(halo + r, blocks)
             strided = pl.ds(8 * q + s, 8, stride=8)
@@ -346,11 +348,11 @@
     shape = (8 + halo, planes * LANES)
     kind = lax.broadcasted_iota(jnp.int32, shape, 0)
     column = dealt_column(lax.broadcasted_iota(jnp.int32, shape, 1), planes)
-    beyond = column - width
-    off = jnp.where(kind == 0, column, jnp.where(kind == 1, -1 - beyond, jnp.where(kind == 2, beyond, width - 1 - beyond)))
-    mine = ((kind < 2) & (beyond < 0)) | ((kind >= 2) & (kind < 4) & (beyond >= 0))
+    own, back = column < width, columns - 1 - column
+    off = jnp.where(kind == 0, column, jnp.where(kind == 1, width - 1 - column, jnp.where(kind == 2, width - 1 - back, back)))
+    mine = ((kind < 2) & own) | ((kind >= 2) & (kind < 4) & ~own)
     weights = jnp.where(mine, jnp.exp(-jnp.maximum(off, 0).astype(jnp.float32) / length), 0.0)
-    weights = jnp.where((kind >= 8) & (beyond == kind - 8), 1.0, weights)
+    weights = jnp.where((kind >= 8) & (column == columns - halo - 8 + kind), 1.0, weights)
     sums = lax.dot_general(
         weights, grad_ref[...], (((1,), (1,)), ((), ())), precision=lax.Precision.HIGHEST,
         preferred_element_type=jnp.float32,
@@ -376,12 +378,12 @@
     shape = (8 + halo, width)
     kind, column = lax.broadcasted_iota(jnp.int32, shape, 0), lax.broadcasted_iota(jnp.int32, shape, 1)
     for place, source in enumerate(order):
-        strip = jnp.where(kind < 2, source, source + 1)
+        strip = jnp.where(kind < 2, source, source - 1)
         left = ((kind == 0) | (kind == 2)) & (strip > me)
         right = ((kind == 1) | (kind == 3)) & (strip < me)
-        near = (kind >= 8) & (source + 1 == me)
+        near = (kind >= 8) & (source - 1 == me)
         away = jnp.where(left, (strip - me) * width - column, (me - strip - 1) * width + column + 1)
-        away = jnp.where(near, jnp.abs(kind - 8 - column), away)
+        away = jnp.where(near, jnp.abs(width - halo - 8 + kind - column), away)
         weights = jnp.where(left | right | near, jnp.exp(-jnp.maximum(away, 0).astype(jnp.float32) / length), 0.0)
         exact_ref[place * shape[0] : (place + 1) * shape[0], :] = weights
     high, low = halves(exact_ref[...])
@@ -445,11 +447,11 @@
         + put(gauge_cell.reshape(1, 1, owned), 2 * blocks, 1)
         + put(coastal_tiles.reshape(1, 1, coast_count), 2 * blocks, 2)
     ).astype(jnp.float32) + put(jnp.transpose(gauge_resid, (1, 2, 0)), blocks, 0)
-    west = pl.pallas_call(
-        functools.partial(give_west, 2 * halo), out_shape=f32(height + 16, LANES), in_specs=vmem(2), out_specs=vmem(1)[0],
-        compiler_params=params, name="give_west",
+    east = pl.pallas_call(
+        functools.partial(give_east, 2 * halo), out_shape=f32(2 * height, LANES), in_specs=vmem(2), out_specs=vmem(1)[0],
+        compiler_params=params, name="give_east",
     )(keep, gain)
-    right = lax.ppermute(west, "lon", [(i + 1, i) for i in range(lons - 1)])
+    left = lax.ppermute(east, "lon", [(i, i + 1) for i in range(lons - 1)])
 
     parcel = pl.pallas_call(
         functools.partial(give_gauges, height, width, blocks, samples, coast_count),
@@ -460,19 +462,19 @@
         compiler_params=params,
         cost_estimate=hint(10),
         name="give_gauges",
-    )(gauges, west)
+    )(gauges, east)
 
     def exchange(array, axes, groups=None):
         return lax.all_to_all(array, axes, split_axis=0, concat_axis=0, axis_index_groups=groups, tiled=True)
 
-    order = list(range(lons // 2, lons)) + list(range(lons // 2))[::-1]
+    order = list(range(lons // 2))[::-1] + list(range(lons // 2, lons))
     group = sorted(range(tiles), key=lambda tile: (tile % row_tiles in (0, row_tiles - 1), order.index(tile // row_tiles)))
     parcel = exchange(parcel, GRID_AXES, [group])
 
     far, near = pl.pallas_call(
         functools.partial(give_rows, halo), out_shape=(f32(2, halo, planes * LANES),) * 2, in_specs=vmem(3),
         out_specs=tuple(vmem(2)), compiler_params=params, cost_estimate=hint(40), name="give_rows",
-    )(keep, gain, right)
+    )(keep, gain, left)
     far = lax.ppermute(far, ROW_AXES, [pair for i in range(1, row_tiles - 1, 2) for pair in ((i, i + 1), (i + 1, i))])
     near = lax.ppermute(near, ROW_AXES, [pair for i in range(0, row_tiles, 2) for pair in ((i, i + 1), (i + 1, i))])
 
@@ -508,8 +510,9 @@
         ],
         compiler_params=params,
         name="sweep",
-    )(keep, gain, far, near, right, pushes)
-
+    )(keep, gain, far, near, left, pushes)
+
+    order = list(range(1, lons - 1)) + [0, lons - 1]
     sums = exchange(sums, "lon", [order])
     own, weights = pl.pallas_call(
         functools.partial(smooth, halo, order),

time: 40.1 us -> 38.3 us (0.955)
  waiting for transfers between devices: 7.39 us -> 4.79 us
  starting transfers between devices: 16.6 us -> 17.4 us
    ppermute x1, waiting for transfers between devices: 4.95 us -> 0.01 us  [local(): left = lax.ppermute(east, 'lon', [(i, i + 1) for i in range(lons - 1)])]
    ppermute x1, starting transfers between devices: 1.28 us -> 4.94 us  [local(): left = lax.ppermute(east, 'lon', [(i, i + 1) for i in range(lons - 1)])]
    all_to_all x2, starting transfers between devices: 11.8 us -> 9.01 us  [exchange(): lax.all_to_all(array, axes, split_axis=0, concat_axis=0, axis_index_group...]
    all_to_all x2, waiting for transfers between devices: 2.44 us -> 4.78 us  [exchange(): lax.all_to_all(array, axes, split_axis=0, concat_axis=0, axis_index_group...]
  transfers between devices with their start and end apart: 5 -> 5, of which waited for: 2 -> 2; matrix products, arithmetic and copies ran while one was open for 0% -> 2% of each run, Pallas kernels for 11% -> 14%
where the time goes in v21:
time: 38.3 us; the launch traced here: 38 us
  starting transfers between devices  17.4 us (45%)
  Pallas kernels  13.6 us (36%)
  waiting for transfers between devices  4.79 us (13%)
  other arithmetic  2.05 us (5%)
    all_to_all x2, starting transfers between devices, exchange(): lax.all_to_all(array, axes, split_axis=0, concat_axis=0, axis_index_group...  9.01 us
    pallas_call x1, Pallas kernels, local(): pl.pallas_call(functools.partial(sweep, steps), out_shape=(f32(height, pl...  7.44 us
    ppermute x1, starting transfers between devices, local(): left = lax.ppermute(east, 'lon', [(i, i + 1) for i in range(lons - 1)])  4.94 us
    all_to_all x2, waiting for transfers between devices, exchange(): lax.all_to_all(array, axes, split_axis=0, concat_axis=0, axis_index_group...  4.78 us
    pallas_call x1, Pallas kernels, local(): pl.pallas_call(functools.partial(force, steps, halo, height, width), out_...  2.86 us
    ppermute x1, starting transfers between devices, local(): lax.ppermute(near, ROW_AXES, [pair for i in range(0, row_tiles, 2) for pa...  2.85 us
    pallas_call x1, Pallas kernels, local(): pl.pallas_call(functools.partial(smooth, halo, order), out_shape=(f32(hei...  1.41 us
    mul x1, other arithmetic, local(): (courant * 0.5) ** 2 * jnp.maximum(depth + surface, depth_floor) * keep  1.29 us
  transfers between devices with their start and end apart: 5, of which 2 were waited for; matrix products, arithmetic and copies ran while one was open for 2% of the time, Pallas kernels for 14%

profile of v21, /device:TPU:0, one launch (start us, length us, event | category | flops | bytes accessed | tf_op | source)
XLA Modules:
  0.0 38.0 jit_solution(11977752798978199827)
XLA Ops:
  0.0 1.3 %multiply_multiply_fusion = (f32[128,512]{1,0:T(8,128)S(1)}, f32[128,512]{1,0:T(8,128)S(1)}) fusion(f32[128,512]{1,0:T(8,128)} %param.9, f32[128,512]{1,0:T(8,128)} %param.10, s32[128,512]{1,0:T(8,128)} %param.12, f32[128,512]{1,0:T(8,128)} %param.11), kind=kLoop, calls=%fused_computation | loop fusion | flops 458752 | bytes 1572864 | tf_op jit(solution)/shard_map/mul | solution.py:434
  1.3 0.1 give_east.1.after_ref
  1.4 4.9 %collective-permute-start = (f32[256,128]{1,0:T(8,128)S(1)}, f32[256,128]{1,0:T(8,128)S(1)}, u32[]{:S(2)}, u32[]{:S(2)}) collective-permute-start(f32[256,128]{1,0:T(8,128)S(1)} %give_east.1.after_ref), channel_id=1, source_target_pairs={{0,4},{4,8},{8,12},{1,5},{5,9},{9,13},{2,6},{6,10},{10,14},{3,7},{... | collective-permute-start | bytes 393224 | tf_op jit(solution)/shard_map/ppermute | solution.py:454
  6.3 0.8 %pad_add_fusion.gauge_ref = f32[5,4,16]{2,1,0:T(4,128)S(1)} fusion(f32[2,4,16]{2,1,0:T(4,128)} %bitcast.7, s32[1,1,8]{2,1,0:T(1,128)} %bitcast.9, s32[1,1,16]{2,1,0:T(1,128)} %bitcast.10, s32[1,1,16]{2,1,0:T(1,128)} %bitcast.11, s32[2,4,16]{2,1,0:T(4,128)} %bitcast.8), kind=kLoop, calls=%fused_computation.2 | loop fusion | flops 1600 | bytes 2464 | tf_op jit(solution)/shard_map/add | solution.py:444
  7.1 0.8 %give_gauges.1 = f32[16,8,128]{2,1,0:T(8,128)} custom-call(f32[5,4,16]{2,1,0:T(4,128)S(1)} %pad_add_fusion.gauge_ref, f32[256,128]{1,0:T(8,128)S(1)} %give_east.1.after_ref), custom_call_target="tpu_custom_call" | custom-call | bytes 10000000 | tf_op jit(solution)/shard_map/give_gauges/pallas_call | solution.py:456
  7.9 5.1 %all-to-all-start = ((f32[16,8,128]{2,1,0:T(8,128)}), f32[16,8,128]{2,1,0:T(8,128)S(1)}, u32[]{:S(2)}, u32[]{:S(2)}) async-start(f32[16,8,128]{2,1,0:T(8,128)} %give_gauges.1), calls=%async_computation | async-start | bytes 131072 | tf_op jit(solution)/shard_map/all_to_all | solution.py:468
  13.0 0.0 collective-permute-done.left_ref
  13.0 0.1 give_rows.1
  13.1 0.7 %collective-permute-start.1 = (f32[2,32,640]{2,1,0:T(8,128)S(1)}, f32[2,32,640]{2,1,0:T(8,128)S(1)}, u32[]{:S(2)}, u32[]{:S(2)}) collective-permute-start(f32[2,32,640]{2,1,0:T(8,128)S(1)} %get-tuple-element.11), channel_id=1, source_target_pairs={{1,2},{2,1},{5,6},{6,5},{9,10},{10,9},{13,14},{14,13},{17,18},{18,... | collective-permute-start | bytes 491528 | tf_op jit(solution)/shard_map/ppermute | solution.py:478
  13.8 2.8 %collective-permute-start.2 = (f32[2,32,640]{2,1,0:T(8,128)S(1)}, f32[2,32,640]{2,1,0:T(8,128)S(1)}, u32[]{:S(2)}, u32[]{:S(2)}) collective-permute-start(f32[2,32,640]{2,1,0:T(8,128)S(1)} %get-tuple-element.12), channel_id=1, source_target_pairs={{0,1},{1,0},{2,3},{3,2},{4,5},{5,4},{6,7},{7,6},{8,9},{9,8},{10,11... | collective-permute-start | bytes 491528 | tf_op jit(solution)/shard_map/ppermute | solution.py:479
  16.6 1.7 %all-to-all-done.parcel_ref = f32[16,8,128]{2,1,0:T(8,128)S(1)} async-done(((f32[16,8,128]{2,1,0:T(8,128)}), f32[16,8,128]{2,1,0:T(8,128)S(1)}, u32[]{:S(2)}, u32[]{:S(2)}) %all-to-all-start) | async-done | bytes 65568 | tf_op jit(solution)/shard_map/all_to_all | solution.py:468
  18.3 2.9 %force.1.force_ref = f32[17,5,200,128]{3,2,1,0:T(8,128)S(1)} custom-call(f32[16,8,128]{2,1,0:T(8,128)S(1)} %all-to-all-done.parcel_ref), custom_call_target="tpu_custom_call" | custom-call | flops 2013265920 | bytes 7864320 | tf_op jit(solution)/shard_map/force/pallas_call | solution.py:482
  21.1 0.0 collective-permute-done.1.far_ref
  21.2 0.0 collective-permute-done.2.near_ref
  21.2 7.4 %sweep.1 = (f32[128,640]{1,0:T(8,128)S(1)}, f32[4,40,128]{2,1,0:T(8,128)}) custom-call(f32[128,512]{1,0:T(8,128)S(1)} %get-tuple-element.18.keep_ref, f32[128,512]{1,0:T(8,128)S(1)} %get-tuple-element.17.gain_ref, f32[2,32,640]{2,1,0:T(8,128)S(1)} %collective-permute-done.1.far_ref, f32[2,32,640]{2,1,0:T(8,128)S(1)} %collective-permute-done.2.near_ref, ...), custom_call_target="tpu_custom_call" | custom-call | tf_op jit(solution)/shard_map/sweep/pallas_call | solution.py:501
  28.6 3.9 %all-to-all-start.1 = ((f32[4,40,128]{2,1,0:T(8,128)}), f32[4,40,128]{2,1,0:T(8,128)S(1)}, u32[]{:S(2)}, u32[]{:S(2)}) async-start(f32[4,40,128]{2,1,0:T(8,128)} %get-tuple-element.16), calls=%async_computation.1 | async-start | bytes 163840 | tf_op jit(solution)/shard_map/all_to_all | solution.py:468
  32.5 1.4 %smooth.1 = (f32[128,512]{1,0:T(8,128)S(1)}, bf16[480,512]{1,0:T(8,128)(2,1)S(1)}) custom-call(f32[128,640]{1,0:T(8,128)S(1)} %get-tuple-element.13.grad_ref), custom_call_target="tpu_custom_call" | custom-call | flops 402653184 | bytes 524288 | tf_op jit(solution)/shard_map/smooth/pallas_call | solution.py:517
  33.9 3.1 %all-to-all-done.1 = f32[4,40,128]{2,1,0:T(8,128)S(1)} async-done(((f32[4,40,128]{2,1,0:T(8,128)}), f32[4,40,128]{2,1,0:T(8,128)S(1)}, u32[]{:S(2)}, u32[]{:S(2)}) %all-to-all-start.1) | async-done | bytes 81952 | tf_op jit(solution)/shard_map/all_to_all | solution.py:468
  37.0 1.0 %finish.1 = f32[128,512]{1,0:T(8,128)} custom-call(f32[128,512]{1,0:T(8,128)S(1)} %get-tuple-element.14.own_ref, bf16[480,512]{1,0:T(8,128)(2,1)S(1)} %get-tuple-element.15.weights_ref, f32[160,128]{1,0:T(8,128)S(1)} %bitcast.6), custom_call_target="tpu_custom_call" | custom-call | tf_op jit(solution)/shard_map/finish/pallas_call | solution.py:529
Async XLA Ops:
  1.4 11.6 %collective-permute-start = (f32[256,128]{1,0:T(8,128)S(1)}, f32[256,128]{1,0:T(8,128)S(1)}, u32[]{:S(2)}, u32[]{:S(2)}) collective-permute-start(f32[256,128]{1,0:T(8,128)S(1)} %give_east.1.after_ref), channel_id=1, source_target_pairs={{0,4},{4,8},{8,12},{1,5},{5,9},{9,13},{2,6},{6,10},{10,14},{3,7},{... | collective-permute-start | bytes 393224 | tf_op jit(solution)/shard_map/ppermute | solution.py:454
  7.9 10.4 %all-to-all-start = ((f32[16,8,128]{2,1,0:T(8,128)}), f32[16,8,128]{2,1,0:T(8,128)S(1)}, u32[]{:S(2)}, u32[]{:S(2)}) async-start(f32[16,8,128]{2,1,0:T(8,128)} %give_gauges.1), calls=%async_computation | async-start | bytes 131072 | tf_op jit(solution)/shard_map/all_to_all | solution.py:468
  13.1 8.0 %collective-permute-start.1 = (f32[2,32,640]{2,1,0:T(8,128)S(1)}, f32[2,32,640]{2,1,0:T(8,128)S(1)}, u32[]{:S(2)}, u32[]{:S(2)}) collective-permute-start(f32[2,32,640]{2,1,0:T(8,128)S(1)} %get-tuple-element.11), channel_id=1, source_target_pairs={{1,2},{2,1},{5,6},{6,5},{9,10},{10,9},{13,14},{14,13},{17,18},{18,... | collective-permute-start | bytes 491528 | tf_op jit(solution)/shard_map/ppermute | solution.py:478
  13.8 7.4 %collective-permute-start.2 = (f32[2,32,640]{2,1,0:T(8,128)S(1)}, f32[2,32,640]{2,1,0:T(8,128)S(1)}, u32[]{:S(2)}, u32[]{:S(2)}) collective-permute-start(f32[2,32,640]{2,1,0:T(8,128)S(1)} %get-tuple-element.12), channel_id=1, source_target_pairs={{0,1},{1,0},{2,3},{3,2},{4,5},{5,4},{6,7},{7,6},{8,9},{9,8},{10,11... | collective-permute-start | bytes 491528 | tf_op jit(solution)/shard_map/ppermute | solution.py:479
  28.6 8.4 %all-to-all-start.1 = ((f32[4,40,128]{2,1,0:T(8,128)}), f32[4,40,128]{2,1,0:T(8,128)S(1)}, u32[]{:S(2)}, u32[]{:S(2)}) async-start(f32[4,40,128]{2,1,0:T(8,128)} %get-tuple-element.16), calls=%async_computation.1 | async-start | bytes 163840 | tf_op jit(solution)/shard_map/all_to_all | solution.py:468

commit v22 on v20

--- a/solution.py
+++ b/solution.py
@@ -40,13 +40,6 @@
 def my_place():
     row = lax.axis_index("lat") * lax.axis_size("gau") + lax.axis_index("gau")
     return row, lax.axis_index("lon"), lax.axis_size("lat") * lax.axis_size("gau"), lax.axis_size("lon")
-
-
-def give_west(reach, keep_ref, gain_ref, west_ref):
-    height = keep_ref.shape[0]
-    lower = lane_iota(height) < reach
-    west_ref[:height] = jnp.where(lower, keep_ref[:, :LANES], roll_lanes(gain_ref[:, :LANES], reach))
-    west_ref[height:] = jnp.zeros((west_ref.shape[0] - height, LANES), jnp.float32)
 
 
 def give_rows(halo, keep_ref, gain_ref, right_ref, far_ref, near_ref):
@@ -60,25 +53,35 @@
             goal[kind, :, width:] = jnp.where(lower, roll_lanes(right_ref[rows, :], -2 * halo * kind), 0.0)
 
 
-def give_gauges(height, width, blocks, samples, coast_count, gauge_ref, after_ref, parcel_ref, block_ref):
+def prepare(reach, count, *refs):
+    given, (keep_ref, gain_ref, west_ref, parcel_ref) = refs[:count], refs[count : count + 4]
+    here, (block_ref, arrived) = refs[count + 4 : 2 * count + 4], refs[2 * count + 4 :]
+    copies = [pltpu.make_async_copy(given[i], here[i], arrived.at[i]) for i in range(count)]
+    for copy in copies:
+        copy.start()
+    depth_ref, surface_ref, friction_ref, wet_ref, coast_ref, route_ref, cell_ref, times_ref, resid_ref = here
+    height, width = depth_ref.shape
     row_tiles = lax.axis_size("lat") * lax.axis_size("gau")
-    owned = gauge_ref.shape[2]
+    for copy in copies[4:]:
+        copy.wait()
+    owned = route_ref.shape[1]
+    blocks, samples = times_ref.shape[:2]
     assert blocks == 2
-    route, cell, coast = (gauge_ref[2 * blocks, i : i + 1, :].astype(jnp.int32) for i in range(3))
+    route, cell, coast = route_ref[...], cell_ref[...], coast_ref[...]
     target = jnp.zeros_like(route)
-    for entry in range(coast_count):
+    for entry in range(coast.shape[1]):
         target = jnp.where(route == entry, jnp.broadcast_to(coast[:, entry : entry + 1], route.shape), target)
     row_bits, width_bits = int(math.log2(row_tiles)), int(math.log2(width))
     assert row_tiles == 1 << row_bits and width == 1 << width_bits
     grid_row = (target & (row_tiles - 1)) * height + (cell >> width_bits)
     grid_col = (target >> row_bits) * width + (cell & (width - 1))
     block_ref[...] = jnp.zeros_like(block_ref)
-    levels = lax.broadcasted_iota(jnp.int32, (STEPS_BLOCK, owned), 0).astype(jnp.float32)
+    levels = lax.broadcasted_iota(jnp.int32, (STEPS_BLOCK, owned), 0)
     for block in range(blocks):
         series = jnp.zeros((STEPS_BLOCK, owned), jnp.float32)
         for sample in range(samples):
-            times = gauge_ref[block, sample : sample + 1, :]
-            resid = gauge_ref[blocks + block, sample : sample + 1, :]
+            times = times_ref[block, sample : sample + 1, :]
+            resid = resid_ref[block, sample : sample + 1, :]
             series = series + jnp.where(times == levels, resid, 0.0)
         block_ref[block * STEPS_BLOCK : (block + 1) * STEPS_BLOCK, :owned] = series
     at = blocks * STEPS_BLOCK
@@ -97,6 +100,15 @@
         return carry
 
     lax.fori_loop(0, tiles, put, 0, unroll=tiles <= 16)
+
+    for copy in copies[:4]:
+        copy.wait()
+    keep = (1.0 - friction_ref[...]) * wet_ref[...].astype(jnp.float32)
+    gain = ((courant * 0.5) ** 2 * jnp.maximum(depth_ref[...] + surface_ref[...], depth_floor)) * keep
+    keep_ref[...], gain_ref[...] = keep, gain
+    lower = lane_iota(height) < reach
+    west_ref[:height] = jnp.where(lower, keep[:, :LANES], roll_lanes(gain[:, :LANES], reach))
+    west_ref[height:] = jnp.zeros((west_ref.shape[0] - height, LANES), jnp.float32)
 
 
 def halves(value):
@@ -428,45 +440,29 @@
     rows_all = height + 2 * halo
     params = pltpu.CompilerParams(vmem_limit_bytes=VMEM_LIMIT)
 
-    keep = (1.0 - friction) * wet.astype(jnp.float32)
-    gain = ((courant * 0.5) ** 2 * jnp.maximum(depth + surface, depth_floor)) * keep
-    samples, coast_count = gauge_resid.shape[2], coastal_tiles.shape[0]
-    assert coast_count <= owned
-
-    assert samples >= 3
-
-    def put(array, group, row):
-        groups, rows, lanes = array.shape
-        return jnp.pad(array, ((group, 2 * blocks + 1 - group - groups), (row, samples - row - rows), (0, owned - lanes)))
-
-    gauges = (
-        put(jnp.transpose(gauge_times, (1, 2, 0)), 0, 0)
-        + put(gauge_route.reshape(1, 1, owned), 2 * blocks, 0)
-        + put(gauge_cell.reshape(1, 1, owned), 2 * blocks, 1)
-        + put(coastal_tiles.reshape(1, 1, coast_count), 2 * blocks, 2)
-    ).astype(jnp.float32) + put(jnp.transpose(gauge_resid, (1, 2, 0)), blocks, 0)
-    west = pl.pallas_call(
-        functools.partial(give_west, 2 * halo), out_shape=f32(2 * height, LANES), in_specs=vmem(2), out_specs=vmem(1)[0],
-        compiler_params=params, name="give_west",
-    )(keep, gain)
+    given = (
+        depth, surface, friction, wet, coastal_tiles.reshape(1, -1), gauge_route.reshape(1, owned),
+        gauge_cell.reshape(1, owned), jnp.transpose(gauge_times, (1, 2, 0)), jnp.transpose(gauge_resid, (1, 2, 0)),
+    )
+    keep, gain, west, parcel = pl.pallas_call(
+        functools.partial(prepare, 2 * halo, len(given)),
+        out_shape=(
+            f32(height, width), f32(height, width), f32(2 * height, LANES), f32(tiles, gauge_rows(owned)[0], LANES),
+        ),
+        in_specs=[pl.BlockSpec(memory_space=pl.ANY)] * len(given),
+        out_specs=tuple(vmem(4)),
+        scratch_shapes=[pltpu.VMEM(array.shape, array.dtype) for array in given] + [
+            pltpu.VMEM((24, LANES), jnp.float32), pltpu.SemaphoreType.DMA((len(given),)),
+        ],
+        compiler_params=pltpu.CompilerParams(vmem_limit_bytes=62 * 1024 * 1024),
+        name="prepare",
+    )(*given)
     right = lax.ppermute(west, "lon", [(i + 1, i) for i in range(lons - 1)])
-
-    parcel = pl.pallas_call(
-        functools.partial(give_gauges, height, width, blocks, samples, coast_count),
-        out_shape=f32(tiles, gauge_rows(owned)[0], LANES),
-        in_specs=vmem(1) + [pl.BlockSpec(memory_space=pl.ANY)],
-        out_specs=vmem(1)[0],
-        scratch_shapes=[pltpu.VMEM((24, LANES), jnp.float32)],
-        compiler_params=params,
-        cost_estimate=hint(10),
-        name="give_gauges",
-    )(gauges, west)
 
     def exchange(array, axes, groups=None):
         return lax.all_to_all(array, axes, split_axis=0, concat_axis=0, axis_index_groups=groups, tiled=True)
 
-    order = list(range(lons // 2, lons)) + list(range(lons // 2))[::-1]
-    group = sorted(range(tiles), key=lambda tile: (tile % row_tiles in (0, row_tiles - 1), (tile // row_tiles - 1) % lons))
+    group = sorted(range(tiles), key=lambda tile: (tile % row_tiles in (0, row_tiles - 1), -(tile // row_tiles)))
     parcel = exchange(parcel, GRID_AXES, [group])
 
     far, near = pl.pallas_call(
@@ -510,6 +506,7 @@
         name="sweep",
     )(keep, gain, far, near, right, pushes)
 
+    order = list(range(lons // 2, lons)) + list(range(lons // 2))[::-1]
     sums = exchange(sums, "lon", [order])
     own, weights = pl.pallas_call(
         functools.partial(smooth, halo, order),

time: 38 us -> 38.1 us (level)
  other arithmetic: 2.05 us -> 0 us
  local copies, waits for them, and re-layouts: 0 us -> 1.9 us
  waiting for transfers between devices: 4.19 us -> 2.44 us
  Pallas kernels: 13.7 us -> 15 us
  starting transfers between devices: 17.6 us -> 18.3 us
    unnamed x0 -> x8, local copies, waits for them, and re-layouts: none -> 1.9 us
    all_to_all x2, waiting for transfers between devices: 4.18 us -> 2.43 us  [exchange(): lax.all_to_all(array, axes, split_axis=0, concat_axis=0, axis_index_group...]
    pallas_call x2 -> x1, Pallas kernels: 0.88 us -> 2.21 us  [local(): pl.pallas_call(functools.partial(prepare, 2 * halo, len(given)), out_shap...]
    mul x1 -> x0, other arithmetic: 1.29 us -> none  [local(): (courant * 0.5) ** 2 * jnp.maximum(depth + surface, depth_floor) * keep]
    add x1 -> x0, other arithmetic: 0.77 us -> none  [local(): (put(jnp.transpose(gauge_times, (1, 2, 0)), 0, 0) + put(gauge_route.resha...]
    all_to_all x2, starting transfers between devices: 12.8 us -> 13.4 us  [exchange(): lax.all_to_all(array, axes, split_axis=0, concat_axis=0, axis_index_group...]
  transfers between devices with their start and end apart: 5 -> 5, of which waited for: 2 -> 1; matrix products, arithmetic and copies ran while one was open for 2% -> 0% of each run, Pallas kernels for 14% -> 12%
where the time goes in v22:
time: 38.1 us; the launch traced here: 37.8 us
  starting transfers between devices  18.3 us (48%)
  Pallas kernels  15 us (39%)
  waiting for transfers between devices  2.44 us (6%)
  local copies, waits for them, and re-layouts  1.9 us (5%)
    all_to_all x2, starting transfers between devices, exchange(): lax.all_to_all(array, axes, split_axis=0, concat_axis=0, axis_index_group...  13.4 us
    pallas_call x1, Pallas kernels, local(): pl.pallas_call(functools.partial(sweep, steps), out_shape=(f32(height, pl...  7.44 us
    pallas_call x1, Pallas kernels, local(): pl.pallas_call(functools.partial(force, steps, halo, height, width), out_...  2.9 us
    ppermute x1, starting transfers between devices, local(): lax.ppermute(near, ROW_AXES, [pair for i in range(0, row_tiles, 2) for pa...  2.84 us
    all_to_all x2, waiting for transfers between devices, exchange(): lax.all_to_all(array, axes, split_axis=0, concat_axis=0, axis_index_group...  2.43 us
    pallas_call x1, Pallas kernels, local(): pl.pallas_call(functools.partial(prepare, 2 * halo, len(given)), out_shap...  2.21 us
    unnamed x8, local copies, waits for them, and re-layouts  1.9 us
    pallas_call x1, Pallas kernels, local(): pl.pallas_call(functools.partial(smooth, halo, order), out_shape=(f32(hei...  1.42 us
  transfers between devices with their start and end apart: 5, of which 1 were waited for; matrix products, arithmetic and copies ran while one was open for 0% of the time, Pallas kernels for 12%

profile of v22, /device:TPU:0, one launch (start us, length us, event | category | flops | bytes accessed | tf_op | source)
XLA Modules:
  0.0 37.8 jit_solution(16726881194502223945)
XLA Ops:
  0.0 2.2 %prepare.1 = (f32[128,512]{1,0:T(8,128)}, f32[128,512]{1,0:T(8,128)}, f32[256,128]{1,0:T(8,128)}, f32[16,8,128]{2,1,0:T(8,128)}) custom-call(f32[128,512]{1,0:T(8,128)} %refs_0_.1, f32[128,512]{1,0:T(8,128)} %refs_1_.1, f32[128,512]{1,0:T(8,128)} %refs_2_.1, s32[128,512]{1,0:T(8,128)} %refs_3_.1, s32[1,8]{1,0:T(1,128)} %bitcast.9, s32[1,16]{1,0:T(1,128)} %bitcast.10, ...), custom_call_target="tpu_custom_call" | custom-call | tf_op jit(solution)/shard_map/prepare/pallas_call | solution.py:447
  2.2 1.3 %collective-permute-start = (f32[256,128]{1,0:T(8,128)}, f32[256,128]{1,0:T(8,128)S(1)}, u32[]{:S(2)}, u32[]{:S(2)}) collective-permute-start(f32[256,128]{1,0:T(8,128)} %get-tuple-element.17), channel_id=1, source_target_pairs={{4,0},{8,4},{12,8},{5,1},{9,5},{13,9},{6,2},{10,6},{14,10},{7,3},{... | collective-permute-start | bytes 393224 | tf_op jit(solution)/shard_map/ppermute | solution.py:460
  3.5 8.7 %all-to-all-start = ((f32[16,8,128]{2,1,0:T(8,128)}), f32[16,8,128]{2,1,0:T(8,128)S(1)}, u32[]{:S(2)}, u32[]{:S(2)}) async-start(f32[16,8,128]{2,1,0:T(8,128)} %get-tuple-element.20), calls=%async_computation | async-start | bytes 131072 | tf_op jit(solution)/shard_map/all_to_all | solution.py:463
  12.2 0.0 collective-permute-done.right_ref
  12.2 0.0 copy-start
  12.2 0.9 %copy-done = f32[128,512]{1,0:T(8,128)S(1)} copy-done((f32[128,512]{1,0:T(8,128)S(1)}, f32[128,512]{1,0:T(8,128)}, u32[]{:S(2)}) %copy-start) | copy-done | bytes 262168
  13.1 0.0 copy-start.2
  13.1 0.9 %copy-done.2 = f32[128,512]{1,0:T(8,128)S(1)} copy-done((f32[128,512]{1,0:T(8,128)S(1)}, f32[128,512]{1,0:T(8,128)}, u32[]{:S(2)}) %copy-start.2) | copy-done | bytes 262168
  14.1 0.0 copy-start.1
  14.1 0.0 copy-start.3
  14.1 0.1 give_rows.1
  14.2 0.8 %collective-permute-start.1 = (f32[2,32,640]{2,1,0:T(8,128)S(1)}, f32[2,32,640]{2,1,0:T(8,128)S(1)}, u32[]{:S(2)}, u32[]{:S(2)}) collective-permute-start(f32[2,32,640]{2,1,0:T(8,128)S(1)} %get-tuple-element.18), channel_id=1, source_target_pairs={{1,2},{2,1},{5,6},{6,5},{9,10},{10,9},{13,14},{14,13},{17,18},{18,... | collective-permute-start | bytes 491528 | tf_op jit(solution)/shard_map/ppermute | solution.py:472
  15.0 2.8 %collective-permute-start.2 = (f32[2,32,640]{2,1,0:T(8,128)S(1)}, f32[2,32,640]{2,1,0:T(8,128)S(1)}, u32[]{:S(2)}, u32[]{:S(2)}) collective-permute-start(f32[2,32,640]{2,1,0:T(8,128)S(1)} %get-tuple-element.19), channel_id=1, source_target_pairs={{0,1},{1,0},{2,3},{3,2},{4,5},{5,4},{6,7},{7,6},{8,9},{9,8},{10,11... | collective-permute-start | bytes 491528 | tf_op jit(solution)/shard_map/ppermute | solution.py:473
  17.8 0.0 all-to-all-done.parcel_ref
  17.8 2.9 %force.1.force_ref = f32[17,5,200,128]{3,2,1,0:T(8,128)S(1)} custom-call(f32[16,8,128]{2,1,0:T(8,128)S(1)} %all-to-all-done.parcel_ref), custom_call_target="tpu_custom_call" | custom-call | flops 2013265920 | bytes 7864320 | tf_op jit(solution)/shard_map/force/pallas_call | solution.py:476
  20.7 0.0 collective-permute-done.1.far_ref
  20.7 0.0 collective-permute-done.2.near_ref
  20.8 0.0 copy-done.1
  20.8 0.0 copy-done.3
  20.8 7.4 %sweep.1 = (f32[128,640]{1,0:T(8,128)S(1)}, f32[4,40,128]{2,1,0:T(8,128)}) custom-call(f32[128,512]{1,0:T(8,128)S(1)} %copy-done.1, f32[128,512]{1,0:T(8,128)S(1)} %copy-done.3, f32[2,32,640]{2,1,0:T(8,128)S(1)} %collective-permute-done.1.far_ref, f32[2,32,640]{2,1,0:T(8,128)S(1)} %collective-permute-done.2.near_ref, ...), custom_call_target="tpu_custom_call" | custom-call | tf_op jit(solution)/shard_map/sweep/pallas_call | solution.py:495
  28.2 4.7 %all-to-all-start.1 = ((f32[4,40,128]{2,1,0:T(8,128)}), f32[4,40,128]{2,1,0:T(8,128)S(1)}, u32[]{:S(2)}, u32[]{:S(2)}) async-start(f32[4,40,128]{2,1,0:T(8,128)} %get-tuple-element.24), calls=%async_computation.1 | async-start | bytes 163840 | tf_op jit(solution)/shard_map/all_to_all | solution.py:463
  32.9 1.4 %smooth.1 = (f32[128,512]{1,0:T(8,128)S(1)}, bf16[480,512]{1,0:T(8,128)(2,1)S(1)}) custom-call(f32[128,640]{1,0:T(8,128)S(1)} %get-tuple-element.21.grad_ref), custom_call_target="tpu_custom_call" | custom-call | flops 402653184 | bytes 524288 | tf_op jit(solution)/shard_map/smooth/pallas_call | solution.py:511
  34.4 2.4 %all-to-all-done.1 = f32[4,40,128]{2,1,0:T(8,128)S(1)} async-done(((f32[4,40,128]{2,1,0:T(8,128)}), f32[4,40,128]{2,1,0:T(8,128)S(1)}, u32[]{:S(2)}, u32[]{:S(2)}) %all-to-all-start.1) | async-done | bytes 81952 | tf_op jit(solution)/shard_map/all_to_all | solution.py:463
  36.8 1.0 %finish.1 = f32[128,512]{1,0:T(8,128)} custom-call(f32[128,512]{1,0:T(8,128)S(1)} %get-tuple-element.22.own_ref, bf16[480,512]{1,0:T(8,128)(2,1)S(1)} %get-tuple-element.23.weights_ref, f32[160,128]{1,0:T(8,128)S(1)} %bitcast.6), custom_call_target="tpu_custom_call" | custom-call | tf_op jit(solution)/shard_map/finish/pallas_call | solution.py:523
Async XLA Ops:
  2.2 10.0 %collective-permute-start = (f32[256,128]{1,0:T(8,128)}, f32[256,128]{1,0:T(8,128)S(1)}, u32[]{:S(2)}, u32[]{:S(2)}) collective-permute-start(f32[256,128]{1,0:T(8,128)} %get-tuple-element.17), channel_id=1, source_target_pairs={{4,0},{8,4},{12,8},{5,1},{9,5},{13,9},{6,2},{10,6},{14,10},{7,3},{... | collective-permute-start | bytes 393224 | tf_op jit(solution)/shard_map/ppermute | solution.py:460
  3.5 14.3 %all-to-all-start = ((f32[16,8,128]{2,1,0:T(8,128)}), f32[16,8,128]{2,1,0:T(8,128)S(1)}, u32[]{:S(2)}, u32[]{:S(2)}) async-start(f32[16,8,128]{2,1,0:T(8,128)} %get-tuple-element.20), calls=%async_computation | async-start | bytes 131072 | tf_op jit(solution)/shard_map/all_to_all | solution.py:463
  12.2 1.0 %copy-start = (f32[128,512]{1,0:T(8,128)S(1)}, f32[128,512]{1,0:T(8,128)}, u32[]{:S(2)}) copy-start(f32[128,512]{1,0:T(8,128)} %get-tuple-element.15.keep_ref) | copy-start | bytes 786436
  13.1 0.9 %copy-start.2 = (f32[128,512]{1,0:T(8,128)S(1)}, f32[128,512]{1,0:T(8,128)}, u32[]{:S(2)}) copy-start(f32[128,512]{1,0:T(8,128)} %get-tuple-element.16.gain_ref) | copy-start | bytes 786436
  14.1 6.7 %copy-start.1 = (f32[128,512]{1,0:T(8,128)S(1)}, f32[128,512]{1,0:T(8,128)}, u32[]{:S(2)}) copy-start(f32[128,512]{1,0:T(8,128)} %get-tuple-element.15.keep_ref) | copy-start | bytes 786436
  14.1 6.7 %copy-start.3 = (f32[128,512]{1,0:T(8,128)S(1)}, f32[128,512]{1,0:T(8,128)}, u32[]{:S(2)}) copy-start(f32[128,512]{1,0:T(8,128)} %get-tuple-element.16.gain_ref) | copy-start | bytes 786436
  14.2 6.6 %collective-permute-start.1 = (f32[2,32,640]{2,1,0:T(8,128)S(1)}, f32[2,32,640]{2,1,0:T(8,128)S(1)}, u32[]{:S(2)}, u32[]{:S(2)}) collective-permute-start(f32[2,32,640]{2,1,0:T(8,128)S(1)} %get-tuple-element.18), channel_id=1, source_target_pairs={{1,2},{2,1},{5,6},{6,5},{9,10},{10,9},{13,14},{14,13},{17,18},{18,... | collective-permute-start | bytes 491528 | tf_op jit(solution)/shard_map/ppermute | solution.py:472
  15.0 5.8 %collective-permute-start.2 = (f32[2,32,640]{2,1,0:T(8,128)S(1)}, f32[2,32,640]{2,1,0:T(8,128)S(1)}, u32[]{:S(2)}, u32[]{:S(2)}) collective-permute-start(f32[2,32,640]{2,1,0:T(8,128)S(1)} %get-tuple-element.19), channel_id=1, source_target_pairs={{0,1},{1,0},{2,3},{3,2},{4,5},{5,4},{6,7},{7,6},{8,9},{9,8},{10,11... | collective-permute-start | bytes 491528 | tf_op jit(solution)/shard_map/ppermute | solution.py:473
  28.2 8.6 %all-to-all-start.1 = ((f32[4,40,128]{2,1,0:T(8,128)}), f32[4,40,128]{2,1,0:T(8,128)S(1)}, u32[]{:S(2)}, u32[]{:S(2)}) async-start(f32[4,40,128]{2,1,0:T(8,128)} %get-tuple-element.24), calls=%async_computation.1 | async-start | bytes 163840 | tf_op jit(solution)/shard_map/all_to_all | solution.py:463

commit v23 on v20

--- a/solution.py
+++ b/solution.py
@@ -465,8 +465,7 @@
     def exchange(array, axes, groups=None):
         return lax.all_to_all(array, axes, split_axis=0, concat_axis=0, axis_index_groups=groups, tiled=True)
 
-    order = list(range(lons // 2, lons)) + list(range(lons // 2))[::-1]
-    group = sorted(range(tiles), key=lambda tile: (tile % row_tiles in (0, row_tiles - 1), (tile // row_tiles - 1) % lons))
+    group = sorted(range(tiles), key=lambda tile: (tile % row_tiles in (0, row_tiles - 1), -(tile // row_tiles)))
     parcel = exchange(parcel, GRID_AXES, [group])
 
     far, near = pl.pallas_call(
@@ -510,6 +509,7 @@
         name="sweep",
     )(keep, gain, far, near, right, pushes)
 
+    order = list(range(lons // 2, lons)) + list(range(lons // 2))[::-1]
     sums = exchange(sums, "lon", [order])
     own, weights = pl.pallas_call(
         functools.partial(smooth, halo, order),

time: 38 us -> 37.5 us (0.987)
  waiting for transfers between devices: 4.19 us -> 2.81 us
  starting transfers between devices: 17.6 us -> 18.6 us
    all_to_all x2, waiting for transfers between devices: 4.18 us -> 2.8 us  [exchange(): lax.all_to_all(array, axes, split_axis=0, concat_axis=0, axis_index_group...]
    all_to_all x2, starting transfers between devices: 12.8 us -> 13.8 us  [exchange(): lax.all_to_all(array, axes, split_axis=0, concat_axis=0, axis_index_group...]
where the time goes in v23:
time: 37.5 us; the launch traced here: 37.2 us
  starting transfers between devices  18.6 us (50%)
  Pallas kernels  13.7 us (37%)
  waiting for transfers between devices  2.81 us (7%)
  other arithmetic  2.05 us (5%)
    all_to_all x2, starting transfers between devices, exchange(): lax.all_to_all(array, axes, split_axis=0, concat_axis=0, axis_index_group...  13.8 us
    pallas_call x1, Pallas kernels, local(): pl.pallas_call(functools.partial(sweep, steps), out_shape=(f32(height, pl...  7.44 us
    pallas_call x1, Pallas kernels, local(): pl.pallas_call(functools.partial(force, steps, halo, height, width), out_...  2.9 us
    ppermute x1, starting transfers between devices, local(): lax.ppermute(near, ROW_AXES, [pair for i in range(0, row_tiles, 2) for pa...  2.83 us
    all_to_all x2, waiting for transfers between devices, exchange(): lax.all_to_all(array, axes, split_axis=0, concat_axis=0, axis_index_group...  2.8 us
    pallas_call x1, Pallas kernels, local(): pl.pallas_call(functools.partial(smooth, halo, order), out_shape=(f32(hei...  1.42 us
    ppermute x1, starting transfers between devices, local(): right = lax.ppermute(west, 'lon', [(i + 1, i) for i in range(lons - 1)])  1.29 us
    mul x1, other arithmetic, local(): (courant * 0.5) ** 2 * jnp.maximum(depth + surface, depth_floor) * keep  1.29 us
  transfers between devices with their start and end apart: 5, of which 2 were waited for; matrix products, arithmetic and copies ran while one was open for 2% of the time, Pallas kernels for 14%

profile of v23, /device:TPU:0, one launch (start us, length us, event | category | flops | bytes accessed | tf_op | source)
XLA Modules:
  0.0 37.2 jit_solution(14792909694631671238)
XLA Ops:
  0.0 1.3 %multiply_multiply_fusion = (f32[128,512]{1,0:T(8,128)S(1)}, f32[128,512]{1,0:T(8,128)S(1)}) fusion(f32[128,512]{1,0:T(8,128)} %param.9, f32[128,512]{1,0:T(8,128)} %param.10, s32[128,512]{1,0:T(8,128)} %param.12, f32[128,512]{1,0:T(8,128)} %param.11), kind=kLoop, calls=%fused_computation | loop fusion | flops 458752 | bytes 1572864 | tf_op jit(solution)/shard_map/mul | solution.py:432
  1.3 0.1 give_west.1.after_ref
  1.4 1.3 %collective-permute-start = (f32[256,128]{1,0:T(8,128)S(1)}, f32[256,128]{1,0:T(8,128)S(1)}, u32[]{:S(2)}, u32[]{:S(2)}) collective-permute-start(f32[256,128]{1,0:T(8,128)S(1)} %give_west.1.after_ref), channel_id=1, source_target_pairs={{4,0},{8,4},{12,8},{5,1},{9,5},{13,9},{6,2},{10,6},{14,10},{7,3},{... | collective-permute-start | bytes 393224 | tf_op jit(solution)/shard_map/ppermute | solution.py:452
  2.7 0.8 %pad_add_fusion.gauge_ref = f32[5,4,16]{2,1,0:T(4,128)S(1)} fusion(f32[2,4,16]{2,1,0:T(4,128)} %bitcast.7, s32[1,1,8]{2,1,0:T(1,128)} %bitcast.9, s32[1,1,16]{2,1,0:T(1,128)} %bitcast.10, s32[1,1,16]{2,1,0:T(1,128)} %bitcast.11, s32[2,4,16]{2,1,0:T(4,128)} %bitcast.8), kind=kLoop, calls=%fused_computation.2 | loop fusion | flops 1600 | bytes 2464 | tf_op jit(solution)/shard_map/add | solution.py:442
  3.4 0.8 %give_gauges.1 = f32[16,8,128]{2,1,0:T(8,128)} custom-call(f32[5,4,16]{2,1,0:T(4,128)S(1)} %pad_add_fusion.gauge_ref, f32[256,128]{1,0:T(8,128)S(1)} %give_west.1.after_ref), custom_call_target="tpu_custom_call" | custom-call | bytes 10000000 | tf_op jit(solution)/shard_map/give_gauges/pallas_call | solution.py:454
  4.2 8.7 %all-to-all-start = ((f32[16,8,128]{2,1,0:T(8,128)}), f32[16,8,128]{2,1,0:T(8,128)S(1)}, u32[]{:S(2)}, u32[]{:S(2)}) async-start(f32[16,8,128]{2,1,0:T(8,128)} %give_gauges.1), calls=%async_computation | async-start | bytes 131072 | tf_op jit(solution)/shard_map/all_to_all | solution.py:466
  12.9 0.0 collective-permute-done.right_ref
  12.9 0.1 give_rows.1
  13.0 0.7 %collective-permute-start.1 = (f32[2,32,640]{2,1,0:T(8,128)S(1)}, f32[2,32,640]{2,1,0:T(8,128)S(1)}, u32[]{:S(2)}, u32[]{:S(2)}) collective-permute-start(f32[2,32,640]{2,1,0:T(8,128)S(1)} %get-tuple-element.11), channel_id=1, source_target_pairs={{1,2},{2,1},{5,6},{6,5},{9,10},{10,9},{13,14},{14,13},{17,18},{18,... | collective-permute-start | bytes 491528 | tf_op jit(solution)/shard_map/ppermute | solution.py:475
  13.7 2.8 %collective-permute-start.2 = (f32[2,32,640]{2,1,0:T(8,128)S(1)}, f32[2,32,640]{2,1,0:T(8,128)S(1)}, u32[]{:S(2)}, u32[]{:S(2)}) collective-permute-start(f32[2,32,640]{2,1,0:T(8,128)S(1)} %get-tuple-element.12), channel_id=1, source_target_pairs={{0,1},{1,0},{2,3},{3,2},{4,5},{5,4},{6,7},{7,6},{8,9},{9,8},{10,11... | collective-permute-start | bytes 491528 | tf_op jit(solution)/shard_map/ppermute | solution.py:476
  16.5 0.4 all-to-all-done.parcel_ref
  16.9 2.9 %force.1.force_ref = f32[17,5,200,128]{3,2,1,0:T(8,128)S(1)} custom-call(f32[16,8,128]{2,1,0:T(8,128)S(1)} %all-to-all-done.parcel_ref), custom_call_target="tpu_custom_call" | custom-call | flops 2013265920 | bytes 7864320 | tf_op jit(solution)/shard_map/force/pallas_call | solution.py:479
  19.8 0.0 collective-permute-done.1.far_ref
  19.8 0.0 collective-permute-done.2.near_ref
  19.8 7.4 %sweep.1 = (f32[128,640]{1,0:T(8,128)S(1)}, f32[4,40,128]{2,1,0:T(8,128)}) custom-call(f32[128,512]{1,0:T(8,128)S(1)} %get-tuple-element.18.keep_ref, f32[128,512]{1,0:T(8,128)S(1)} %get-tuple-element.17.gain_ref, f32[2,32,640]{2,1,0:T(8,128)S(1)} %collective-permute-done.1.far_ref, f32[2,32,640]{2,1,0:T(8,128)S(1)} %collective-permute-done.2.near_ref, ...), custom_call_target="tpu_custom_call" | custom-call | tf_op jit(solution)/shard_map/sweep/pallas_call | solution.py:498
  27.2 5.1 %all-to-all-start.1 = ((f32[4,40,128]{2,1,0:T(8,128)}), f32[4,40,128]{2,1,0:T(8,128)S(1)}, u32[]{:S(2)}, u32[]{:S(2)}) async-start(f32[4,40,128]{2,1,0:T(8,128)} %get-tuple-element.16), calls=%async_computation.1 | async-start | bytes 163840 | tf_op jit(solution)/shard_map/all_to_all | solution.py:466
  32.4 1.4 %smooth.1 = (f32[128,512]{1,0:T(8,128)S(1)}, bf16[480,512]{1,0:T(8,128)(2,1)S(1)}) custom-call(f32[128,640]{1,0:T(8,128)S(1)} %get-tuple-element.13.grad_ref), custom_call_target="tpu_custom_call" | custom-call | flops 402653184 | bytes 524288 | tf_op jit(solution)/shard_map/smooth/pallas_call | solution.py:514
  33.8 2.4 %all-to-all-done.1 = f32[4,40,128]{2,1,0:T(8,128)S(1)} async-done(((f32[4,40,128]{2,1,0:T(8,128)}), f32[4,40,128]{2,1,0:T(8,128)S(1)}, u32[]{:S(2)}, u32[]{:S(2)}) %all-to-all-start.1) | async-done | bytes 81952 | tf_op jit(solution)/shard_map/all_to_all | solution.py:466
  36.2 1.0 %finish.1 = f32[128,512]{1,0:T(8,128)} custom-call(f32[128,512]{1,0:T(8,128)S(1)} %get-tuple-element.14.own_ref, bf16[480,512]{1,0:T(8,128)(2,1)S(1)} %get-tuple-element.15.weights_ref, f32[160,128]{1,0:T(8,128)S(1)} %bitcast.6), custom_call_target="tpu_custom_call" | custom-call | tf_op jit(solution)/shard_map/finish/pallas_call | solution.py:526
Async XLA Ops:
  1.4 11.5 %collective-permute-start = (f32[256,128]{1,0:T(8,128)S(1)}, f32[256,128]{1,0:T(8,128)S(1)}, u32[]{:S(2)}, u32[]{:S(2)}) collective-permute-start(f32[256,128]{1,0:T(8,128)S(1)} %give_west.1.after_ref), channel_id=1, source_target_pairs={{4,0},{8,4},{12,8},{5,1},{9,5},{13,9},{6,2},{10,6},{14,10},{7,3},{... | collective-permute-start | bytes 393224 | tf_op jit(solution)/shard_map/ppermute | solution.py:452
  4.2 12.6 %all-to-all-start = ((f32[16,8,128]{2,1,0:T(8,128)}), f32[16,8,128]{2,1,0:T(8,128)S(1)}, u32[]{:S(2)}, u32[]{:S(2)}) async-start(f32[16,8,128]{2,1,0:T(8,128)} %give_gauges.1), calls=%async_computation | async-start | bytes 131072 | tf_op jit(solution)/shard_map/all_to_all | solution.py:466
  13.0 6.8 %collective-permute-start.1 = (f32[2,32,640]{2,1,0:T(8,128)S(1)}, f32[2,32,640]{2,1,0:T(8,128)S(1)}, u32[]{:S(2)}, u32[]{:S(2)}) collective-permute-start(f32[2,32,640]{2,1,0:T(8,128)S(1)} %get-tuple-element.11), channel_id=1, source_target_pairs={{1,2},{2,1},{5,6},{6,5},{9,10},{10,9},{13,14},{14,13},{17,18},{18,... | collective-permute-start | bytes 491528 | tf_op jit(solution)/shard_map/ppermute | solution.py:475
  13.7 6.1 %collective-permute-start.2 = (f32[2,32,640]{2,1,0:T(8,128)S(1)}, f32[2,32,640]{2,1,0:T(8,128)S(1)}, u32[]{:S(2)}, u32[]{:S(2)}) collective-permute-start(f32[2,32,640]{2,1,0:T(8,128)S(1)} %get-tuple-element.12), channel_id=1, source_target_pairs={{0,1},{1,0},{2,3},{3,2},{4,5},{5,4},{6,7},{7,6},{8,9},{9,8},{10,11... | collective-permute-start | bytes 491528 | tf_op jit(solution)/shard_map/ppermute | solution.py:476
  27.2 9.0 %all-to-all-start.1 = ((f32[4,40,128]{2,1,0:T(8,128)}), f32[4,40,128]{2,1,0:T(8,128)S(1)}, u32[]{:S(2)}, u32[]{:S(2)}) async-start(f32[4,40,128]{2,1,0:T(8,128)} %get-tuple-element.16), calls=%async_computation.1 | async-start | bytes 163840 | tf_op jit(solution)/shard_map/all_to_all | solution.py:466

commit v24 on v23

--- a/solution.py
+++ b/solution.py
@@ -108,7 +108,7 @@
     return (place & (LANES - 1)) * planes + place // LANES
 
 
-def force(steps, halo, height, width, parcel_ref, force_ref, series_ref, rows_hot, cols_hot):
+def force(steps, halo, height, width, parcel_ref, after_ref, force_ref, series_ref, rows_hot, cols_hot):
     planes, rows_all = force_ref.shape[1], height + 2 * halo
     my_row, my_lon, row_tiles, lons = my_place()
     wide = rows_hot.shape[1]
@@ -190,58 +190,72 @@
         lax.fori_loop(1, groups, more, 0)
 
 
-def sweep(
-    steps, keep_ref, gain_ref, far_ref, near_ref, right_ref, force_ref,
-    grad_ref, sums_ref,
-    a, fx, fy, keeps, gains, plain,
-):
+def deal_own(reach, keep_ref, gain_ref, right_ref, after_ref, deal_ref, own_ref):
     height, width = keep_ref.shape
-    halo = 2 * steps
-    inner = width // LANES
-    planes = inner + 1
-    rows_all = height + 2 * halo
-    blocks = rows_all // 8
-    my_row, my_lon, row_tiles, lons = my_place()
-    reach = 2 * halo
-    has_top, has_bottom = my_row > 0, my_row < row_tiles - 1
-    has_right = my_lon < lons - 1
-    odd = (jnp.zeros((halo, planes * LANES), jnp.int32) + (my_row & 1)) == 1
-    lanes8 = lane_iota(8)
-
-    def up(value):
-        return pltpu.roll(value, 7, 0)
-
-    def down(value):
-        return pltpu.roll(value, 1, 0)
-
-    every = range(planes)
+    planes = own_ref.shape[1]
     columns = planes * LANES
-
     parts = []
     for kind, source in enumerate((keep_ref, gain_ref)):
-        far, near = far_ref[kind], near_ref[kind]
         beside = jnp.where(lane_iota(height) < reach, roll_lanes(right_ref[:height], -reach * kind), 0.0)
-        whole = jnp.concatenate(
-            [
-                jnp.where(odd, near, far),
-                jnp.concatenate([source[...], beside], axis=1),
-                jnp.where(odd, far, near),
-            ],
-            axis=0,
-        )
-        parts += halves(whole)
+        parts += halves(jnp.concatenate([source[...], beside], axis=1))
     parts = jnp.concatenate(parts, axis=0)
     shape = (columns, LANES)
     ahead = lax.broadcasted_iota(jnp.int32, shape, 0) - lax.broadcasted_iota(jnp.int32, shape, 1) * planes
     for first in range(0, planes, 2):
         pair = range(first, min(first + 2, planes))
         deal = jnp.concatenate([(ahead == c).astype(jnp.float32).astype(jnp.bfloat16) for c in pair], axis=1)
+        deal_ref[:, first * LANES : (first + len(pair)) * LANES] = deal
         dealt = jnp.dot(parts, deal, preferred_element_type=jnp.float32)
         for i, c in enumerate(pair):
             piece = dealt[:, i * LANES : (i + 1) * LANES]
             for kind in range(2):
-                at = 2 * kind * rows_all
-                plain[kind, c, 0:rows_all, :] = piece[at : at + rows_all] + piece[at + rows_all : at + 2 * rows_all]
+                at = 2 * kind * height
+                own_ref[kind, c] = piece[at : at + height] + piece[at + height : at + 2 * height]
+
+
+def sweep(
+    steps, deal_ref, own_ref, far_ref, near_ref, force_ref,
+    grad_ref, sums_ref,
+    a, fx, fy, keeps, gains, plain,
+):
+    planes, height = own_ref.shape[1:3]
+    width = (planes - 1) * LANES
+    halo = 2 * steps
+    rows_all = height + 2 * halo
+    blocks = rows_all // 8
+    my_row, my_lon, row_tiles, lons = my_place()
+    has_top, has_bottom = my_row > 0, my_row < row_tiles - 1
+    has_right = my_lon < lons - 1
+    odd = (jnp.zeros((halo, planes * LANES), jnp.int32) + (my_row & 1)) == 1
+    lanes8 = lane_iota(8)
+
+    def up(value):
+        return pltpu.roll(value, 7, 0)
+
+    def down(value):
+        return pltpu.roll(value, 1, 0)
+
+    every = range(planes)
+    columns = planes * LANES
+
+    parts = []
+    for kind in range(2):
+        far, near = far_ref[kind], near_ref[kind]
+        parts += halves(jnp.concatenate([jnp.where(odd, near, far), jnp.where(odd, far, near)], axis=0))
+    parts = jnp.concatenate(parts, axis=0)
+    for first in range(0, planes, 2):
+        pair = range(first, min(first + 2, planes))
+        dealt = jnp.dot(
+            parts, deal_ref[:, first * LANES : (first + len(pair)) * LANES], preferred_element_type=jnp.float32
+        )
+        for i, c in enumerate(pair):
+            piece = dealt[:, i * LANES : (i + 1) * LANES]
+            for kind in range(2):
+                at = 4 * kind * halo
+                value = piece[at : at + 2 * halo] + piece[at + 2 * halo : at + 4 * halo]
+                plain[kind, c, 0:halo, :] = value[:halo]
+                plain[kind, c, halo : halo + height, :] = own_ref[kind, c]
+                plain[kind, c, halo + height : rows_all, :] = value[halo:]
     for kind, goal in enumerate((keeps, gains)):
         for q in range(blocks):
             for c in every:
@@ -468,18 +482,30 @@
     group = sorted(range(tiles), key=lambda tile: (tile % row_tiles in (0, row_tiles - 1), -(tile // row_tiles)))
     parcel = exchange(parcel, GRID_AXES, [group])
 
-    far, near = pl.pallas_call(
+    to_far, to_near = pl.pallas_call(
         functools.partial(give_rows, halo), out_shape=(f32(2, halo, planes * LANES),) * 2, in_specs=vmem(3),
         out_specs=tuple(vmem(2)), compiler_params=params, cost_estimate=hint(40), name="give_rows",
     )(keep, gain, right)
-    far = lax.ppermute(far, ROW_AXES, [pair for i in range(1, row_tiles - 1, 2) for pair in ((i, i + 1), (i + 1, i))])
-    near = lax.ppermute(near, ROW_AXES, [pair for i in range(0, row_tiles, 2) for pair in ((i, i + 1), (i + 1, i))])
+    far = lax.ppermute(to_far, ROW_AXES, [pair for i in range(1, row_tiles - 1, 2) for pair in ((i, i + 1), (i + 1, i))])
+    near = lax.ppermute(to_near, ROW_AXES, [pair for i in range(0, row_tiles, 2) for pair in ((i, i + 1), (i + 1, i))])
+
+    deal, own = pl.pallas_call(
+        functools.partial(deal_own, 2 * halo),
+        out_shape=(
+            jax.ShapeDtypeStruct((planes * LANES, planes * LANES), jnp.bfloat16), f32(2, planes, height, LANES),
+        ),
+        in_specs=vmem(3) + [pl.BlockSpec(memory_space=pl.ANY)],
+        out_specs=tuple(vmem(2)),
+        compiler_params=params,
+        cost_estimate=hint(4),
+        name="deal_own",
+    )(keep, gain, right, to_far)
 
     wide = max(2 * LANES, owned)
     pushes = pl.pallas_call(
         functools.partial(force, steps, halo, height, width),
         out_shape=f32(steps + 1, planes, spaced(rows_all), LANES),
-        in_specs=vmem(1),
+        in_specs=vmem(1) + [pl.BlockSpec(memory_space=pl.ANY)],
         out_specs=vmem(1)[0],
         scratch_shapes=[
             pltpu.VMEM((steps, wide), jnp.float32),
@@ -492,13 +518,13 @@
             transcendentals=0,
         ),
         name="force",
-    )(parcel)
+    )(parcel, deal)
 
     plane = pltpu.VMEM((planes, spaced(rows_all), LANES), jnp.float32)
     grad, sums = pl.pallas_call(
         functools.partial(sweep, steps),
         out_shape=(f32(height, planes * LANES), f32(lons, 8 + halo, height)),
-        in_specs=vmem(6),
+        in_specs=vmem(5),
         out_specs=tuple(vmem(2)),
         scratch_shapes=[plane] * 3 + [
             pltpu.VMEM((planes + 1, spaced(rows_all + 8), LANES), jnp.float32),
@@ -507,7 +533,7 @@
         ],
         compiler_params=params,
         name="sweep",
-    )(keep, gain, far, near, right, pushes)
+    )(deal, own, far, near, pushes)
 
     order = list(range(lons // 2, lons)) + list(range(lons // 2))[::-1]
     sums = exchange(sums, "lon", [order])

time: 37.5 us -> 36.9 us (0.984)
  starting transfers between devices: 18.6 us -> 15.8 us
  waiting for transfers between devices: 2.81 us -> 4.76 us
    ppermute x2, starting transfers between devices: 3.49 us -> 0.77 us  [the longest x1 0.66 us: local(): lax.ppermute(to_far, ROW_AXES, [pair for i in range(1, row_tiles - 1, 2)...]
    all_to_all x2, waiting for transfers between devices: 2.8 us -> 4.75 us  [exchange(): lax.all_to_all(array, axes, split_axis=0, concat_axis=0, axis_index_group...]
    pallas_call x0 -> x1, Pallas kernels: none -> 0.76 us  [local(): pl.pallas_call(functools.partial(deal_own, 2 * halo), out_shape=(jax.Shap...]
    pallas_call x1, Pallas kernels: 7.44 us -> 6.82 us  [local(): pl.pallas_call(functools.partial(sweep, steps), out_shape=(f32(height, pl...]
  transfers between devices with their start and end apart: 5 -> 5, of which waited for: 2 -> 2; matrix products, arithmetic and copies ran while one was open for 2% -> 2% of each run, Pallas kernels for 14% -> 16%
where the time goes in v24:
time: 36.9 us; the launch traced here: 36.6 us
  starting transfers between devices  15.8 us (43%)
  Pallas kernels  13.8 us (37%)
  waiting for transfers between devices  4.76 us (13%)
  other arithmetic  2.05 us (6%)
    all_to_all x2, starting transfers between devices, exchange(): lax.all_to_all(array, axes, split_axis=0, concat_axis=0, axis_index_group...  13.8 us
    pallas_call x1, Pallas kernels, local(): pl.pallas_call(functools.partial(sweep, steps), out_shape=(f32(height, pl...  6.82 us
    all_to_all x2, waiting for transfers between devices, exchange(): lax.all_to_all(array, axes, split_axis=0, concat_axis=0, axis_index_group...  4.75 us
    pallas_call x1, Pallas kernels, local(): pl.pallas_call(functools.partial(force, steps, halo, height, width), out_...  2.9 us
    pallas_call x1, Pallas kernels, local(): pl.pallas_call(functools.partial(smooth, halo, order), out_shape=(f32(hei...  1.42 us
    ppermute x1, starting transfers between devices, local(): right = lax.ppermute(west, 'lon', [(i + 1, i) for i in range(lons - 1)])  1.29 us
    mul x1, other arithmetic, local(): (courant * 0.5) ** 2 * jnp.maximum(depth + surface, depth_floor) * keep  1.29 us
    pallas_call x1, Pallas kernels, local(): pl.pallas_call(finish, out_shape=f32(height, width), in_specs=vmem(3), ou...  0.95 us
  transfers between devices with their start and end apart: 5, of which 2 were waited for; matrix products, arithmetic and copies ran while one was open for 2% of the time, Pallas kernels for 16%

profile of v24, /device:TPU:0, one launch (start us, length us, event | category | flops | bytes accessed | tf_op | source)
XLA Modules:
  0.0 36.6 jit_solution(10635862332253323455)
XLA Ops:
  0.0 1.3 %multiply_multiply_fusion = (f32[128,512]{1,0:T(8,128)S(1)}, f32[128,512]{1,0:T(8,128)S(1)}) fusion(f32[128,512]{1,0:T(8,128)} %param.9, f32[128,512]{1,0:T(8,128)} %param.10, s32[128,512]{1,0:T(8,128)} %param.12, f32[128,512]{1,0:T(8,128)} %param.11), kind=kLoop, calls=%fused_computation | loop fusion | flops 458752 | bytes 1572864 | tf_op jit(solution)/shard_map/mul | solution.py:446
  1.3 0.1 give_west.1.after_ref
  1.4 1.3 %collective-permute-start = (f32[256,128]{1,0:T(8,128)S(1)}, f32[256,128]{1,0:T(8,128)S(1)}, u32[]{:S(2)}, u32[]{:S(2)}) collective-permute-start(f32[256,128]{1,0:T(8,128)S(1)} %give_west.1.after_ref), channel_id=1, source_target_pairs={{4,0},{8,4},{12,8},{5,1},{9,5},{13,9},{6,2},{10,6},{14,10},{7,3},{... | collective-permute-start | bytes 393224 | tf_op jit(solution)/shard_map/ppermute | solution.py:466
  2.7 0.8 %pad_add_fusion.gauge_ref = f32[5,4,16]{2,1,0:T(4,128)S(1)} fusion(f32[2,4,16]{2,1,0:T(4,128)} %bitcast.7, s32[1,1,8]{2,1,0:T(1,128)} %bitcast.9, s32[1,1,16]{2,1,0:T(1,128)} %bitcast.10, s32[1,1,16]{2,1,0:T(1,128)} %bitcast.11, s32[2,4,16]{2,1,0:T(4,128)} %bitcast.8), kind=kLoop, calls=%fused_computation.2 | loop fusion | flops 1600 | bytes 2464 | tf_op jit(solution)/shard_map/add | solution.py:456
  3.4 0.8 %give_gauges.1 = f32[16,8,128]{2,1,0:T(8,128)} custom-call(f32[5,4,16]{2,1,0:T(4,128)S(1)} %pad_add_fusion.gauge_ref, f32[256,128]{1,0:T(8,128)S(1)} %give_west.1.after_ref), custom_call_target="tpu_custom_call" | custom-call | bytes 10000000 | tf_op jit(solution)/shard_map/give_gauges/pallas_call | solution.py:468
  4.2 8.7 %all-to-all-start = ((f32[16,8,128]{2,1,0:T(8,128)}), f32[16,8,128]{2,1,0:T(8,128)S(1)}, u32[]{:S(2)}, u32[]{:S(2)}) async-start(f32[16,8,128]{2,1,0:T(8,128)} %give_gauges.1), calls=%async_computation | async-start | bytes 131072 | tf_op jit(solution)/shard_map/all_to_all | solution.py:480
  12.9 0.0 collective-permute-done.right_ref
  12.9 0.1 give_rows.1
  13.0 0.1 collective-permute-start.2
  13.1 0.7 %collective-permute-start.1 = (f32[2,32,640]{2,1,0:T(8,128)S(1)}, f32[2,32,640]{2,1,0:T(8,128)S(1)}, u32[]{:S(2)}, u32[]{:S(2)}) collective-permute-start(f32[2,32,640]{2,1,0:T(8,128)S(1)} %get-tuple-element.13.after_ref), channel_id=1, source_target_pairs={{1,2},{2,1},{5,6},{6,5},{9,10},{10,9},{13,14},{14,13},{17,18},{18,... | collective-permute-start | bytes 491528 | tf_op jit(solution)/shard_map/ppermute | solution.py:489
  13.8 0.8 %deal_own.1 = (bf16[640,640]{1,0:T(8,128)(2,1)S(1)}, f32[2,5,128,128]{3,2,1,0:T(8,128)S(1)}) custom-call(f32[128,512]{1,0:T(8,128)S(1)} %get-tuple-element.22.keep_ref, f32[128,512]{1,0:T(8,128)S(1)} %get-tuple-element.21.gain_ref, f32[256,128]{1,0:T(8,128)S(1)} %collective-permute-done.right_ref, f32[2,32,640]{2,1,0:T(8,128)S(1)} %get-tuple-element.13.after_ref), custom_call_target="tpu_custom_call" | custom-call | bytes 4000000 | tf_op jit(solution)/shard_map/deal_own/pallas_call | solution.py:492
  14.6 2.3 %all-to-all-done.parcel_ref = f32[16,8,128]{2,1,0:T(8,128)S(1)} async-done(((f32[16,8,128]{2,1,0:T(8,128)}), f32[16,8,128]{2,1,0:T(8,128)S(1)}, u32[]{:S(2)}, u32[]{:S(2)}) %all-to-all-start) | async-done | bytes 65568 | tf_op jit(solution)/shard_map/all_to_all | solution.py:480
  16.9 2.9 %force.1.force_ref = f32[17,5,200,128]{3,2,1,0:T(8,128)S(1)} custom-call(f32[16,8,128]{2,1,0:T(8,128)S(1)} %all-to-all-done.parcel_ref, bf16[640,640]{1,0:T(8,128)(2,1)S(1)} %get-tuple-element.14.after_ref.deal_ref), custom_call_target="tpu_custom_call" | custom-call | flops 2013265920 | bytes 7864320 | tf_op jit(solution)/shard_map/force/pallas_call | solution.py:505
  19.8 0.0 collective-permute-done.2.near_ref
  19.8 0.0 collective-permute-done.1.far_ref
  19.8 6.8 %sweep.1 = (f32[128,640]{1,0:T(8,128)S(1)}, f32[4,40,128]{2,1,0:T(8,128)}) custom-call(bf16[640,640]{1,0:T(8,128)(2,1)S(1)} %get-tuple-element.14.after_ref.deal_ref, f32[2,5,128,128]{3,2,1,0:T(8,128)S(1)} %get-tuple-element.15.own_ref, f32[2,32,640]{2,1,0:T(8,128)S(1)} %collective-permute-done.1.far_ref, f32[2,32,640]{2,1,0:T(8,128)S(1)} %collective-permute-done.2.near_ref, ...), custom_call_target="tpu_custom_call" | custom-call | tf_op jit(solution)/shard_map/sweep/pallas_call | solution.py:524
  26.6 5.1 %all-to-all-start.1 = ((f32[4,40,128]{2,1,0:T(8,128)}), f32[4,40,128]{2,1,0:T(8,128)S(1)}, u32[]{:S(2)}, u32[]{:S(2)}) async-start(f32[4,40,128]{2,1,0:T(8,128)} %get-tuple-element.20), calls=%async_computation.1 | async-start | bytes 163840 | tf_op jit(solution)/shard_map/all_to_all | solution.py:480
  31.8 1.4 %smooth.1 = (f32[128,512]{1,0:T(8,128)S(1)}, bf16[480,512]{1,0:T(8,128)(2,1)S(1)}) custom-call(f32[128,640]{1,0:T(8,128)S(1)} %get-tuple-element.17.grad_ref), custom_call_target="tpu_custom_call" | custom-call | flops 402653184 | bytes 524288 | tf_op jit(solution)/shard_map/smooth/pallas_call | solution.py:540
  33.2 2.4 %all-to-all-done.1 = f32[4,40,128]{2,1,0:T(8,128)S(1)} async-done(((f32[4,40,128]{2,1,0:T(8,128)}), f32[4,40,128]{2,1,0:T(8,128)S(1)}, u32[]{:S(2)}, u32[]{:S(2)}) %all-to-all-start.1) | async-done | bytes 81952 | tf_op jit(solution)/shard_map/all_to_all | solution.py:480
  35.6 1.0 %finish.1 = f32[128,512]{1,0:T(8,128)} custom-call(f32[128,512]{1,0:T(8,128)S(1)} %get-tuple-element.18.own_ref, bf16[480,512]{1,0:T(8,128)(2,1)S(1)} %get-tuple-element.19.weights_ref, f32[160,128]{1,0:T(8,128)S(1)} %bitcast.6), custom_call_target="tpu_custom_call" | custom-call | tf_op jit(solution)/shard_map/finish/pallas_call | solution.py:552
Async XLA Ops:
  1.4 11.5 %collective-permute-start = (f32[256,128]{1,0:T(8,128)S(1)}, f32[256,128]{1,0:T(8,128)S(1)}, u32[]{:S(2)}, u32[]{:S(2)}) collective-permute-start(f32[256,128]{1,0:T(8,128)S(1)} %give_west.1.after_ref), channel_id=1, source_target_pairs={{4,0},{8,4},{12,8},{5,1},{9,5},{13,9},{6,2},{10,6},{14,10},{7,3},{... | collective-permute-start | bytes 393224 | tf_op jit(solution)/shard_map/ppermute | solution.py:466
  4.2 12.6 %all-to-all-start = ((f32[16,8,128]{2,1,0:T(8,128)}), f32[16,8,128]{2,1,0:T(8,128)S(1)}, u32[]{:S(2)}, u32[]{:S(2)}) async-start(f32[16,8,128]{2,1,0:T(8,128)} %give_gauges.1), calls=%async_computation | async-start | bytes 131072 | tf_op jit(solution)/shard_map/all_to_all | solution.py:480
  13.0 6.8 %collective-permute-start.2 = (f32[2,32,640]{2,1,0:T(8,128)S(1)}, f32[2,32,640]{2,1,0:T(8,128)S(1)}, u32[]{:S(2)}, u32[]{:S(2)}) collective-permute-start(f32[2,32,640]{2,1,0:T(8,128)S(1)} %get-tuple-element.16), channel_id=1, source_target_pairs={{0,1},{1,0},{2,3},{3,2},{4,5},{5,4},{6,7},{7,6},{8,9},{9,8},{10,11... | collective-permute-start | bytes 491528 | tf_op jit(solution)/shard_map/ppermute | solution.py:490
  13.1 6.7 %collective-permute-start.1 = (f32[2,32,640]{2,1,0:T(8,128)S(1)}, f32[2,32,640]{2,1,0:T(8,128)S(1)}, u32[]{:S(2)}, u32[]{:S(2)}) collective-permute-start(f32[2,32,640]{2,1,0:T(8,128)S(1)} %get-tuple-element.13.after_ref), channel_id=1, source_target_pairs={{1,2},{2,1},{5,6},{6,5},{9,10},{10,9},{13,14},{14,13},{17,18},{18,... | collective-permute-start | bytes 491528 | tf_op jit(solution)/shard_map/ppermute | solution.py:489
  26.6 9.0 %all-to-all-start.1 = ((f32[4,40,128]{2,1,0:T(8,128)}), f32[4,40,128]{2,1,0:T(8,128)S(1)}, u32[]{:S(2)}, u32[]{:S(2)}) async-start(f32[4,40,128]{2,1,0:T(8,128)} %get-tuple-element.20), calls=%async_computation.1 | async-start | bytes 163840 | tf_op jit(solution)/shard_map/all_to_all | solution.py:480

commit v25 on v24

--- a/solution.py
+++ b/solution.py
@@ -175,7 +175,10 @@
             levels_of(index * LEVELS, add)
             return carry
 
-        lax.fori_loop(0, steps // LEVELS, one, 0)
+        if steps == LEVELS:
+            levels_of(0, add)
+        else:
+            lax.fori_loop(0, steps // LEVELS, one, 0)
 
     force_ref[steps] = jnp.zeros_like(force_ref[steps])
     gather_gauges(0)
@@ -277,11 +280,7 @@
     for row, there in ((halo - 1, has_top), (halo + height, has_bottom)):
         row_mask[row % blocks] = jnp.where(sublane == row // blocks, jnp.where(there, 1.0, 0.0), 1.0)
 
-    fx[...] = jnp.zeros_like(fx)
-    fy[...] = jnp.zeros_like(fy)
-    a[:, 0:rows_all, :] = force_ref[steps - 1, :, 0:rows_all, :]
-
-    def step(index, carry):
+    def step(index, carry, opening=False):
         level = jnp.where(index < steps - 1, steps - 2 - index, steps)
         near, ahead, new_y, beside, total, behind = {}, {}, {}, {}, {}, {}
 
@@ -289,7 +288,8 @@
             return slice(8 * q, 8 * q + 8)
 
         def first(q):
-            near[q] = [a[c, rows(q % blocks), :] for c in every]
+            source = force_ref.at[steps - 1] if opening else a
+            near[q] = [source[c, rows(q % blocks), :] for c in every]
             if q < blocks:
                 ahead[q] = near[q][2:] + [roll_lanes(value, -1) for value in near[q][:2]]
             else:
@@ -300,15 +300,17 @@
 
         def second_y(q):
             beside[q + 1] = keep, gain = coefficients(q + 1)
-            new_y[q] = [keep[c] * fy[c, rows(q), :] + gain[c] * (near[q + 2][c] - near[q][c]) for c in every]
+            new_y[q] = [gain[c] * (near[q + 2][c] - near[q][c]) for c in every]
+            if not opening:
+                new_y[q] = [new_y[q][c] + keep[c] * fy[c, rows(q), :] for c in every]
             for c in every:
                 fy[c, rows(q), :] = new_y[q][c]
 
         def second_x(q):
             keep, gain = beside[q]
-            new_x = [
-                keep[c + 1] * fx[c, rows(q), :] + gain[c + 1] * (ahead[q][c] - near[q][c]) for c in every
-            ]
+            new_x = [gain[c + 1] * (ahead[q][c] - near[q][c]) for c in every]
+            if not opening:
+                new_x = [new_x[c] + keep[c + 1] * fx[c, rows(q), :] for c in every]
             behind[q] = [roll_lanes(value, 1) for value in new_x[-2:]] + new_x[:-2]
             before = new_y[q - 2] if q >= 2 else [down(fy[c, rows(q - 2 + blocks), :]) for c in every]
             push = [force_ref[level, c, rows(q), :] for c in every]
@@ -345,7 +347,8 @@
         third(1)
         return carry
 
-    lax.fori_loop(0, steps, step, 0)
+    step(0, 0, opening=True)
+    lax.fori_loop(1, steps, step, 0)
 
     start = jnp.where(my_lon > 0, halo, 0)
     for c in every:

time: 36.9 us -> 36.8 us (level)
  no operation moved by 1% of the time
where the time goes in v25:
time: 36.8 us; the launch traced here: 36.4 us
  starting transfers between devices  15.8 us (43%)
  Pallas kernels  13.7 us (37%)
  waiting for transfers between devices  4.76 us (13%)
  other arithmetic  2.05 us (6%)
    all_to_all x2, starting transfers between devices, exchange(): lax.all_to_all(array, axes, split_axis=0, concat_axis=0, axis_index_group...  13.8 us
    pallas_call x1, Pallas kernels, local(): pl.pallas_call(functools.partial(sweep, steps), out_shape=(f32(height, pl...  6.69 us
    all_to_all x2, waiting for transfers between devices, exchange(): lax.all_to_all(array, axes, split_axis=0, concat_axis=0, axis_index_group...  4.75 us
    pallas_call x1, Pallas kernels, local(): pl.pallas_call(functools.partial(force, steps, halo, height, width), out_...  2.9 us
    pallas_call x1, Pallas kernels, local(): pl.pallas_call(functools.partial(smooth, halo, order), out_shape=(f32(hei...  1.42 us
    ppermute x1, starting transfers between devices, local(): right = lax.ppermute(west, 'lon', [(i + 1, i) for i in range(lons - 1)])  1.29 us
    mul x1, other arithmetic, local(): (courant * 0.5) ** 2 * jnp.maximum(depth + surface, depth_floor) * keep  1.29 us
    pallas_call x1, Pallas kernels, local(): pl.pallas_call(finish, out_shape=f32(height, width), in_specs=vmem(3), ou...  0.95 us
  transfers between devices with their start and end apart: 5, of which 2 were waited for; matrix products, arithmetic and copies ran while one was open for 2% of the time, Pallas kernels for 16%

profile of v25, /device:TPU:0, one launch (start us, length us, event | category | flops | bytes accessed | tf_op | source)
XLA Modules:
  0.0 36.4 jit_solution(4535352027469318842)
XLA Ops:
  0.0 1.3 %multiply_multiply_fusion = (f32[128,512]{1,0:T(8,128)S(1)}, f32[128,512]{1,0:T(8,128)S(1)}) fusion(f32[128,512]{1,0:T(8,128)} %param.9, f32[128,512]{1,0:T(8,128)} %param.10, s32[128,512]{1,0:T(8,128)} %param.12, f32[128,512]{1,0:T(8,128)} %param.11), kind=kLoop, calls=%fused_computation | loop fusion | flops 458752 | bytes 1572864 | tf_op jit(solution)/shard_map/mul | solution.py:449
  1.3 0.1 give_west.1.after_ref
  1.4 1.3 %collective-permute-start = (f32[256,128]{1,0:T(8,128)S(1)}, f32[256,128]{1,0:T(8,128)S(1)}, u32[]{:S(2)}, u32[]{:S(2)}) collective-permute-start(f32[256,128]{1,0:T(8,128)S(1)} %give_west.1.after_ref), channel_id=1, source_target_pairs={{4,0},{8,4},{12,8},{5,1},{9,5},{13,9},{6,2},{10,6},{14,10},{7,3},{... | collective-permute-start | bytes 393224 | tf_op jit(solution)/shard_map/ppermute | solution.py:469
  2.7 0.8 %pad_add_fusion.gauge_ref = f32[5,4,16]{2,1,0:T(4,128)S(1)} fusion(f32[2,4,16]{2,1,0:T(4,128)} %bitcast.7, s32[1,1,8]{2,1,0:T(1,128)} %bitcast.9, s32[1,1,16]{2,1,0:T(1,128)} %bitcast.10, s32[1,1,16]{2,1,0:T(1,128)} %bitcast.11, s32[2,4,16]{2,1,0:T(4,128)} %bitcast.8), kind=kLoop, calls=%fused_computation.2 | loop fusion | flops 1600 | bytes 2464 | tf_op jit(solution)/shard_map/add | solution.py:459
  3.4 0.8 %give_gauges.1 = f32[16,8,128]{2,1,0:T(8,128)} custom-call(f32[5,4,16]{2,1,0:T(4,128)S(1)} %pad_add_fusion.gauge_ref, f32[256,128]{1,0:T(8,128)S(1)} %give_west.1.after_ref), custom_call_target="tpu_custom_call" | custom-call | bytes 10000000 | tf_op jit(solution)/shard_map/give_gauges/pallas_call | solution.py:471
  4.2 8.7 %all-to-all-start = ((f32[16,8,128]{2,1,0:T(8,128)}), f32[16,8,128]{2,1,0:T(8,128)S(1)}, u32[]{:S(2)}, u32[]{:S(2)}) async-start(f32[16,8,128]{2,1,0:T(8,128)} %give_gauges.1), calls=%async_computation | async-start | bytes 131072 | tf_op jit(solution)/shard_map/all_to_all | solution.py:483
  12.9 0.0 collective-permute-done.right_ref
  12.9 0.1 give_rows.1
  13.0 0.1 collective-permute-start.2
  13.1 0.7 %collective-permute-start.1 = (f32[2,32,640]{2,1,0:T(8,128)S(1)}, f32[2,32,640]{2,1,0:T(8,128)S(1)}, u32[]{:S(2)}, u32[]{:S(2)}) collective-permute-start(f32[2,32,640]{2,1,0:T(8,128)S(1)} %get-tuple-element.13.after_ref), channel_id=1, source_target_pairs={{1,2},{2,1},{5,6},{6,5},{9,10},{10,9},{13,14},{14,13},{17,18},{18,... | collective-permute-start | bytes 491528 | tf_op jit(solution)/shard_map/ppermute | solution.py:492
  13.8 0.8 %deal_own.1 = (bf16[640,640]{1,0:T(8,128)(2,1)S(1)}, f32[2,5,128,128]{3,2,1,0:T(8,128)S(1)}) custom-call(f32[128,512]{1,0:T(8,128)S(1)} %get-tuple-element.22.keep_ref, f32[128,512]{1,0:T(8,128)S(1)} %get-tuple-element.21.gain_ref, f32[256,128]{1,0:T(8,128)S(1)} %collective-permute-done.right_ref, f32[2,32,640]{2,1,0:T(8,128)S(1)} %get-tuple-element.13.after_ref), custom_call_target="tpu_custom_call" | custom-call | bytes 4000000 | tf_op jit(solution)/shard_map/deal_own/pallas_call | solution.py:495
  14.6 2.3 %all-to-all-done.parcel_ref = f32[16,8,128]{2,1,0:T(8,128)S(1)} async-done(((f32[16,8,128]{2,1,0:T(8,128)}), f32[16,8,128]{2,1,0:T(8,128)S(1)}, u32[]{:S(2)}, u32[]{:S(2)}) %all-to-all-start) | async-done | bytes 65568 | tf_op jit(solution)/shard_map/all_to_all | solution.py:483
  16.9 2.9 %force.1.force_ref = f32[17,5,200,128]{3,2,1,0:T(8,128)S(1)} custom-call(f32[16,8,128]{2,1,0:T(8,128)S(1)} %all-to-all-done.parcel_ref, bf16[640,640]{1,0:T(8,128)(2,1)S(1)} %get-tuple-element.14.after_ref.deal_ref), custom_call_target="tpu_custom_call" | custom-call | flops 2013265920 | bytes 7864320 | tf_op jit(solution)/shard_map/force/pallas_call | solution.py:508
  19.8 0.0 collective-permute-done.2.near_ref
  19.8 0.0 collective-permute-done.1.far_ref
  19.8 6.7 %sweep.1 = (f32[128,640]{1,0:T(8,128)S(1)}, f32[4,40,128]{2,1,0:T(8,128)}) custom-call(bf16[640,640]{1,0:T(8,128)(2,1)S(1)} %get-tuple-element.14.after_ref.deal_ref, f32[2,5,128,128]{3,2,1,0:T(8,128)S(1)} %get-tuple-element.15.own_ref, f32[2,32,640]{2,1,0:T(8,128)S(1)} %collective-permute-done.1.far_ref, f32[2,32,640]{2,1,0:T(8,128)S(1)} %collective-permute-done.2.near_ref, ...), custom_call_target="tpu_custom_call" | custom-call | tf_op jit(solution)/shard_map/sweep/pallas_call | solution.py:527
  26.5 5.1 %all-to-all-start.1 = ((f32[4,40,128]{2,1,0:T(8,128)}), f32[4,40,128]{2,1,0:T(8,128)S(1)}, u32[]{:S(2)}, u32[]{:S(2)}) async-start(f32[4,40,128]{2,1,0:T(8,128)} %get-tuple-element.20), calls=%async_computation.1 | async-start | bytes 163840 | tf_op jit(solution)/shard_map/all_to_all | solution.py:483
  31.6 1.4 %smooth.1 = (f32[128,512]{1,0:T(8,128)S(1)}, bf16[480,512]{1,0:T(8,128)(2,1)S(1)}) custom-call(f32[128,640]{1,0:T(8,128)S(1)} %get-tuple-element.17.grad_ref), custom_call_target="tpu_custom_call" | custom-call | flops 402653184 | bytes 524288 | tf_op jit(solution)/shard_map/smooth/pallas_call | solution.py:543
  33.0 2.4 %all-to-all-done.1 = f32[4,40,128]{2,1,0:T(8,128)S(1)} async-done(((f32[4,40,128]{2,1,0:T(8,128)}), f32[4,40,128]{2,1,0:T(8,128)S(1)}, u32[]{:S(2)}, u32[]{:S(2)}) %all-to-all-start.1) | async-done | bytes 81952 | tf_op jit(solution)/shard_map/all_to_all | solution.py:483
  35.5 1.0 %finish.1 = f32[128,512]{1,0:T(8,128)} custom-call(f32[128,512]{1,0:T(8,128)S(1)} %get-tuple-element.18.own_ref, bf16[480,512]{1,0:T(8,128)(2,1)S(1)} %get-tuple-element.19.weights_ref, f32[160,128]{1,0:T(8,128)S(1)} %bitcast.6), custom_call_target="tpu_custom_call" | custom-call | tf_op jit(solution)/shard_map/finish/pallas_call | solution.py:555
Async XLA Ops:
  1.4 11.5 %collective-permute-start = (f32[256,128]{1,0:T(8,128)S(1)}, f32[256,128]{1,0:T(8,128)S(1)}, u32[]{:S(2)}, u32[]{:S(2)}) collective-permute-start(f32[256,128]{1,0:T(8,128)S(1)} %give_west.1.after_ref), channel_id=1, source_target_pairs={{4,0},{8,4},{12,8},{5,1},{9,5},{13,9},{6,2},{10,6},{14,10},{7,3},{... | collective-permute-start | bytes 393224 | tf_op jit(solution)/shard_map/ppermute | solution.py:469
  4.2 12.6 %all-to-all-start = ((f32[16,8,128]{2,1,0:T(8,128)}), f32[16,8,128]{2,1,0:T(8,128)S(1)}, u32[]{:S(2)}, u32[]{:S(2)}) async-start(f32[16,8,128]{2,1,0:T(8,128)} %give_gauges.1), calls=%async_computation | async-start | bytes 131072 | tf_op jit(solution)/shard_map/all_to_all | solution.py:483
  13.0 6.8 %collective-permute-start.2 = (f32[2,32,640]{2,1,0:T(8,128)S(1)}, f32[2,32,640]{2,1,0:T(8,128)S(1)}, u32[]{:S(2)}, u32[]{:S(2)}) collective-permute-start(f32[2,32,640]{2,1,0:T(8,128)S(1)} %get-tuple-element.16), channel_id=1, source_target_pairs={{0,1},{1,0},{2,3},{3,2},{4,5},{5,4},{6,7},{7,6},{8,9},{9,8},{10,11... | collective-permute-start | bytes 491528 | tf_op jit(solution)/shard_map/ppermute | solution.py:493
  13.1 6.7 %collective-permute-start.1 = (f32[2,32,640]{2,1,0:T(8,128)S(1)}, f32[2,32,640]{2,1,0:T(8,128)S(1)}, u32[]{:S(2)}, u32[]{:S(2)}) collective-permute-start(f32[2,32,640]{2,1,0:T(8,128)S(1)} %get-tuple-element.13.after_ref), channel_id=1, source_target_pairs={{1,2},{2,1},{5,6},{6,5},{9,10},{10,9},{13,14},{14,13},{17,18},{18,... | collective-permute-start | bytes 491528 | tf_op jit(solution)/shard_map/ppermute | solution.py:492
  26.5 9.0 %all-to-all-start.1 = ((f32[4,40,128]{2,1,0:T(8,128)}), f32[4,40,128]{2,1,0:T(8,128)S(1)}, u32[]{:S(2)}, u32[]{:S(2)}) async-start(f32[4,40,128]{2,1,0:T(8,128)} %get-tuple-element.20), calls=%async_computation.1 | async-start | bytes 163840 | tf_op jit(solution)/shard_map/all_to_all | solution.py:483

commit v26 on v25

--- a/solution.py
+++ b/solution.py
@@ -407,12 +407,20 @@
         weights_ref[place * count : (place + 1) * count, :] = part
 
 
-def finish(own_ref, weights_ref, sums_ref, out_ref):
+def finish(own_ref, weights_ref, sums_ref, out_ref, here, left):
     high, low = halves(sums_ref[...])
-    out_ref[...] = own_ref[...] + lax.dot_general(
-        jnp.concatenate([high, low, high], axis=0), weights_ref[...], (((0,), (0,)), ((), ())),
-        preferred_element_type=jnp.float32,
-    )
+    sums = jnp.concatenate([high, low, high], axis=0)
+    half = own_ref.shape[1] // 2
+    copies = []
+    for i in range(2):
+        cols = slice(i * half, (i + 1) * half)
+        here[i] = own_ref[:, cols] + lax.dot_general(
+            sums, weights_ref[:, cols], (((0,), (0,)), ((), ())), preferred_element_type=jnp.float32
+        )
+        copies.append(pltpu.make_async_copy(here.at[i], out_ref.at[:, cols], left.at[i]))
+        copies[i].start()
+    for copy in copies:
+        copy.wait()
 
 
 def f32(*shape):
@@ -482,7 +490,9 @@
     def exchange(array, axes, groups=None):
         return lax.all_to_all(array, axes, split_axis=0, concat_axis=0, axis_index_groups=groups, tiled=True)
 
-    group = sorted(range(tiles), key=lambda tile: (tile % row_tiles in (0, row_tiles - 1), -(tile // row_tiles)))
+    ends = (row_tiles - 1, 0)
+    rank = [row for row in reversed(range(row_tiles)) if row not in ends] + list(ends)
+    group = sorted(range(tiles), key=lambda tile: (rank.index(tile % row_tiles), -(tile // row_tiles)))
     parcel = exchange(parcel, GRID_AXES, [group])
 
     to_far, to_near = pl.pallas_call(
@@ -538,7 +548,7 @@
         name="sweep",
     )(deal, own, far, near, pushes)
 
-    order = list(range(lons // 2, lons)) + list(range(lons // 2))[::-1]
+    order = list(range(lons))[::-1]
     sums = exchange(sums, "lon", [order])
     own, weights = pl.pallas_call(
         functools.partial(smooth, halo, order),
@@ -553,7 +563,13 @@
         name="smooth",
     )(grad)
     return pl.pallas_call(
-        finish, out_shape=f32(height, width), in_specs=vmem(3), out_specs=vmem(1)[0], compiler_params=params, name="finish",
+        finish,
+        out_shape=f32(height, width),
+        in_specs=vmem(3),
+        out_specs=pl.BlockSpec(memory_space=pl.ANY),
+        scratch_shapes=[pltpu.VMEM((2, height, width // 2), jnp.float32), pltpu.SemaphoreType.DMA((2,))],
+        compiler_params=params,
+        name="finish",
     )(own, weights, sums.reshape(lons * (8 + halo), height))
 
 

time: 36.8 us -> 37.9 us (1.030)
  starting transfers between devices: 15.8 us -> 18.7 us
  waiting for transfers between devices: 4.76 us -> 2.98 us
    all_to_all x2, starting transfers between devices: 13.8 us -> 16.6 us  [exchange(): lax.all_to_all(array, axes, split_axis=0, concat_axis=0, axis_index_group...]
    all_to_all x2, waiting for transfers between devices: 4.75 us -> 2.97 us  [exchange(): lax.all_to_all(array, axes, split_axis=0, concat_axis=0, axis_index_group...]
where the time goes in v26:
time: 37.9 us; the launch traced here: 37.5 us
  starting transfers between devices  18.7 us (49%)
  Pallas kernels  13.7 us (36%)
  waiting for transfers between devices  2.98 us (8%)
  other arithmetic  2.05 us (5%)
    all_to_all x2, starting transfers between devices, exchange(): lax.all_to_all(array, axes, split_axis=0, concat_axis=0, axis_index_group...  16.6 us
    pallas_call x1, Pallas kernels, local(): pl.pallas_call(functools.partial(sweep, steps), out_shape=(f32(height, pl...  6.69 us
    all_to_all x2, waiting for transfers between devices, exchange(): lax.all_to_all(array, axes, split_axis=0, concat_axis=0, axis_index_group...  2.97 us
    pallas_call x1, Pallas kernels, local(): pl.pallas_call(functools.partial(force, steps, halo, height, width), out_...  2.9 us
    pallas_call x1, Pallas kernels, local(): pl.pallas_call(functools.partial(smooth, halo, order), out_shape=(f32(hei...  1.42 us
    ppermute x1, starting transfers between devices, local(): right = lax.ppermute(west, 'lon', [(i + 1, i) for i in range(lons - 1)])  1.29 us
    mul x1, other arithmetic, local(): (courant * 0.5) ** 2 * jnp.maximum(depth + surface, depth_floor) * keep  1.29 us
    pallas_call x1, Pallas kernels, local(): pl.pallas_call(finish, out_shape=f32(height, width), in_specs=vmem(3), ou...  0.97 us
  transfers between devices with their start and end apart: 5, of which 2 were waited for; matrix products, arithmetic and copies ran while one was open for 2% of the time, Pallas kernels for 16%

profile of v26, /device:TPU:0, one launch (start us, length us, event | category | flops | bytes accessed | tf_op | source)
XLA Modules:
  0.0 37.5 jit_solution(16994562746820448641)
XLA Ops:
  0.0 1.3 %multiply_multiply_fusion = (f32[128,512]{1,0:T(8,128)S(1)}, f32[128,512]{1,0:T(8,128)S(1)}) fusion(f32[128,512]{1,0:T(8,128)} %param.9, f32[128,512]{1,0:T(8,128)} %param.10, s32[128,512]{1,0:T(8,128)} %param.12, f32[128,512]{1,0:T(8,128)} %param.11), kind=kLoop, calls=%fused_computation | loop fusion | flops 458752 | bytes 1572864 | tf_op jit(solution)/shard_map/mul | solution.py:457
  1.3 0.1 give_west.1.after_ref
  1.4 1.3 %collective-permute-start = (f32[256,128]{1,0:T(8,128)S(1)}, f32[256,128]{1,0:T(8,128)S(1)}, u32[]{:S(2)}, u32[]{:S(2)}) collective-permute-start(f32[256,128]{1,0:T(8,128)S(1)} %give_west.1.after_ref), channel_id=1, source_target_pairs={{4,0},{8,4},{12,8},{5,1},{9,5},{13,9},{6,2},{10,6},{14,10},{7,3},{... | collective-permute-start | bytes 393224 | tf_op jit(solution)/shard_map/ppermute | solution.py:477
  2.7 0.8 %pad_add_fusion.gauge_ref = f32[5,4,16]{2,1,0:T(4,128)S(1)} fusion(f32[2,4,16]{2,1,0:T(4,128)} %bitcast.7, s32[1,1,8]{2,1,0:T(1,128)} %bitcast.9, s32[1,1,16]{2,1,0:T(1,128)} %bitcast.10, s32[1,1,16]{2,1,0:T(1,128)} %bitcast.11, s32[2,4,16]{2,1,0:T(4,128)} %bitcast.8), kind=kLoop, calls=%fused_computation.2 | loop fusion | flops 1600 | bytes 2464 | tf_op jit(solution)/shard_map/add | solution.py:467
  3.4 0.8 %give_gauges.1 = f32[16,8,128]{2,1,0:T(8,128)} custom-call(f32[5,4,16]{2,1,0:T(4,128)S(1)} %pad_add_fusion.gauge_ref, f32[256,128]{1,0:T(8,128)S(1)} %give_west.1.after_ref), custom_call_target="tpu_custom_call" | custom-call | bytes 10000000 | tf_op jit(solution)/shard_map/give_gauges/pallas_call | solution.py:479
  4.2 10.4 %all-to-all-start = ((f32[16,8,128]{2,1,0:T(8,128)}), f32[16,8,128]{2,1,0:T(8,128)S(1)}, u32[]{:S(2)}, u32[]{:S(2)}) async-start(f32[16,8,128]{2,1,0:T(8,128)} %give_gauges.1), calls=%async_computation | async-start | bytes 131072 | tf_op jit(solution)/shard_map/all_to_all | solution.py:491
  14.7 0.0 collective-permute-done.right_ref
  14.7 0.1 give_rows.1
  14.8 0.1 collective-permute-start.2
  14.9 0.7 %collective-permute-start.1 = (f32[2,32,640]{2,1,0:T(8,128)S(1)}, f32[2,32,640]{2,1,0:T(8,128)S(1)}, u32[]{:S(2)}, u32[]{:S(2)}) collective-permute-start(f32[2,32,640]{2,1,0:T(8,128)S(1)} %get-tuple-element.13.after_ref), channel_id=1, source_target_pairs={{1,2},{2,1},{5,6},{6,5},{9,10},{10,9},{13,14},{14,13},{17,18},{18,... | collective-permute-start | bytes 491528 | tf_op jit(solution)/shard_map/ppermute | solution.py:502
  15.6 0.8 %deal_own.1 = (bf16[640,640]{1,0:T(8,128)(2,1)S(1)}, f32[2,5,128,128]{3,2,1,0:T(8,128)S(1)}) custom-call(f32[128,512]{1,0:T(8,128)S(1)} %get-tuple-element.22.keep_ref, f32[128,512]{1,0:T(8,128)S(1)} %get-tuple-element.21.gain_ref, f32[256,128]{1,0:T(8,128)S(1)} %collective-permute-done.right_ref, f32[2,32,640]{2,1,0:T(8,128)S(1)} %get-tuple-element.13.after_ref), custom_call_target="tpu_custom_call" | custom-call | bytes 4000000 | tf_op jit(solution)/shard_map/deal_own/pallas_call | solution.py:505
  16.3 1.4 %all-to-all-done.parcel_ref = f32[16,8,128]{2,1,0:T(8,128)S(1)} async-done(((f32[16,8,128]{2,1,0:T(8,128)}), f32[16,8,128]{2,1,0:T(8,128)S(1)}, u32[]{:S(2)}, u32[]{:S(2)}) %all-to-all-start) | async-done | bytes 65568 | tf_op jit(solution)/shard_map/all_to_all | solution.py:491
  17.7 2.9 %force.1.force_ref = f32[17,5,200,128]{3,2,1,0:T(8,128)S(1)} custom-call(f32[16,8,128]{2,1,0:T(8,128)S(1)} %all-to-all-done.parcel_ref, bf16[640,640]{1,0:T(8,128)(2,1)S(1)} %get-tuple-element.14.after_ref.deal_ref), custom_call_target="tpu_custom_call" | custom-call | flops 2013265920 | bytes 7864320 | tf_op jit(solution)/shard_map/force/pallas_call | solution.py:518
  20.6 0.0 collective-permute-done.2.near_ref
  20.6 0.0 collective-permute-done.1.far_ref
  20.7 6.7 %sweep.1 = (f32[128,640]{1,0:T(8,128)S(1)}, f32[4,40,128]{2,1,0:T(8,128)}) custom-call(bf16[640,640]{1,0:T(8,128)(2,1)S(1)} %get-tuple-element.14.after_ref.deal_ref, f32[2,5,128,128]{3,2,1,0:T(8,128)S(1)} %get-tuple-element.15.own_ref, f32[2,32,640]{2,1,0:T(8,128)S(1)} %collective-permute-done.1.far_ref, f32[2,32,640]{2,1,0:T(8,128)S(1)} %collective-permute-done.2.near_ref, ...), custom_call_target="tpu_custom_call" | custom-call | tf_op jit(solution)/shard_map/sweep/pallas_call | solution.py:537
  27.3 6.2 %all-to-all-start.1 = ((f32[4,40,128]{2,1,0:T(8,128)}), f32[4,40,128]{2,1,0:T(8,128)S(1)}, u32[]{:S(2)}, u32[]{:S(2)}) async-start(f32[4,40,128]{2,1,0:T(8,128)} %get-tuple-element.20), calls=%async_computation.1 | async-start | bytes 163840 | tf_op jit(solution)/shard_map/all_to_all | solution.py:491
  33.6 1.4 %smooth.1 = (f32[128,512]{1,0:T(8,128)S(1)}, bf16[480,512]{1,0:T(8,128)(2,1)S(1)}) custom-call(f32[128,640]{1,0:T(8,128)S(1)} %get-tuple-element.17.grad_ref), custom_call_target="tpu_custom_call" | custom-call | flops 402653184 | bytes 524288 | tf_op jit(solution)/shard_map/smooth/pallas_call | solution.py:553
  35.0 1.6 %all-to-all-done.1 = f32[4,40,128]{2,1,0:T(8,128)S(1)} async-done(((f32[4,40,128]{2,1,0:T(8,128)}), f32[4,40,128]{2,1,0:T(8,128)S(1)}, u32[]{:S(2)}, u32[]{:S(2)}) %all-to-all-start.1) | async-done | bytes 81952 | tf_op jit(solution)/shard_map/all_to_all | solution.py:491
  36.5 1.0 %finish.1 = f32[128,512]{1,0:T(8,128)} custom-call(f32[128,512]{1,0:T(8,128)S(1)} %get-tuple-element.18.own_ref, bf16[480,512]{1,0:T(8,128)(2,1)S(1)} %get-tuple-element.19.weights_ref, f32[160,128]{1,0:T(8,128)S(1)} %bitcast.6), custom_call_target="tpu_custom_call" | custom-call | tf_op jit(solution)/shard_map/finish/pallas_call | solution.py:565
Async XLA Ops:
  1.4 13.3 %collective-permute-start = (f32[256,128]{1,0:T(8,128)S(1)}, f32[256,128]{1,0:T(8,128)S(1)}, u32[]{:S(2)}, u32[]{:S(2)}) collective-permute-start(f32[256,128]{1,0:T(8,128)S(1)} %give_west.1.after_ref), channel_id=1, source_target_pairs={{4,0},{8,4},{12,8},{5,1},{9,5},{13,9},{6,2},{10,6},{14,10},{7,3},{... | collective-permute-start | bytes 393224 | tf_op jit(solution)/shard_map/ppermute | solution.py:477
  4.2 13.5 %all-to-all-start = ((f32[16,8,128]{2,1,0:T(8,128)}), f32[16,8,128]{2,1,0:T(8,128)S(1)}, u32[]{:S(2)}, u32[]{:S(2)}) async-start(f32[16,8,128]{2,1,0:T(8,128)} %give_gauges.1), calls=%async_computation | async-start | bytes 131072 | tf_op jit(solution)/shard_map/all_to_all | solution.py:491
  14.8 5.9 %collective-permute-start.2 = (f32[2,32,640]{2,1,0:T(8,128)S(1)}, f32[2,32,640]{2,1,0:T(8,128)S(1)}, u32[]{:S(2)}, u32[]{:S(2)}) collective-permute-start(f32[2,32,640]{2,1,0:T(8,128)S(1)} %get-tuple-element.16), channel_id=1, source_target_pairs={{0,1},{1,0},{2,3},{3,2},{4,5},{5,4},{6,7},{7,6},{8,9},{9,8},{10,11... | collective-permute-start | bytes 491528 | tf_op jit(solution)/shard_map/ppermute | solution.py:503
  14.9 5.8 %collective-permute-start.1 = (f32[2,32,640]{2,1,0:T(8,128)S(1)}, f32[2,32,640]{2,1,0:T(8,128)S(1)}, u32[]{:S(2)}, u32[]{:S(2)}) collective-permute-start(f32[2,32,640]{2,1,0:T(8,128)S(1)} %get-tuple-element.13.after_ref), channel_id=1, source_target_pairs={{1,2},{2,1},{5,6},{6,5},{9,10},{10,9},{13,14},{14,13},{17,18},{18,... | collective-permute-start | bytes 491528 | tf_op jit(solution)/shard_map/ppermute | solution.py:502
  27.3 9.2 %all-to-all-start.1 = ((f32[4,40,128]{2,1,0:T(8,128)}), f32[4,40,128]{2,1,0:T(8,128)S(1)}, u32[]{:S(2)}, u32[]{:S(2)}) async-start(f32[4,40,128]{2,1,0:T(8,128)} %get-tuple-element.20), calls=%async_computation.1 | async-start | bytes 163840 | tf_op jit(solution)/shard_map/all_to_all | solution.py:491

commit v27 on v25

--- a/solution.py
+++ b/solution.py
@@ -360,7 +360,7 @@
             value = jnp.where(known & (keeps[c, strided, :] > 0.0), a[c, strided, :], 0.0)
             grad_ref[r : r + 8, c * LANES : (c + 1) * LANES] = value
     length = 2.0 * width
-    shape = (8 + halo, planes * LANES)
+    shape = (16 + halo, planes * LANES)
     kind = lax.broadcasted_iota(jnp.int32, shape, 0)
     column = dealt_column(lax.broadcasted_iota(jnp.int32, shape, 1), planes)
     beyond = column - width
@@ -368,10 +368,11 @@
     mine = ((kind < 2) & (beyond < 0)) | ((kind >= 2) & (kind < 4) & (beyond >= 0))
     weights = jnp.where(mine, jnp.exp(-jnp.maximum(off, 0).astype(jnp.float32) / length), 0.0)
     weights = jnp.where((kind >= 8) & (beyond == kind - 8), 1.0, weights)
+    (w_high, w_low), (g_high, g_low) = halves(weights), halves(grad_ref[...])
     sums = lax.dot_general(
-        weights, grad_ref[...], (((1,), (1,)), ((), ())), precision=lax.Precision.HIGHEST,
-        preferred_element_type=jnp.float32,
-    )
+        jnp.concatenate([w_high, w_high, w_low], axis=1), jnp.concatenate([g_high, g_low, g_high], axis=1),
+        (((1,), (1,)), ((), ())), preferred_element_type=jnp.float32,
+    )[: 8 + halo]
     for i in range(sums_ref.shape[0]):
         sums_ref[i] = sums
 
@@ -482,7 +483,8 @@
     def exchange(array, axes, groups=None):
         return lax.all_to_all(array, axes, split_axis=0, concat_axis=0, axis_index_groups=groups, tiled=True)
 
-    group = sorted(range(tiles), key=lambda tile: (tile % row_tiles in (0, row_tiles - 1), -(tile // row_tiles)))
+    rank = {row_tiles - 1: 1, 0: 2}
+    group = sorted(range(tiles), key=lambda tile: (rank.get(tile % row_tiles, 0), -(tile // row_tiles)))
     parcel = exchange(parcel, GRID_AXES, [group])
 
     to_far, to_near = pl.pallas_call(

time: 36.8 us -> 36.1 us (0.981)
  Pallas kernels: 13.7 us -> 13.3 us
    pallas_call x1, Pallas kernels: 6.69 us -> 6.23 us  [local(): pl.pallas_call(functools.partial(sweep, steps), out_shape=(f32(height, pl...]
  transfers between devices with their start and end apart: 5 -> 5, of which waited for: 2 -> 2; matrix products, arithmetic and copies ran while one was open for 2% -> 2% of each run, Pallas kernels for 16% -> 17%
where the time goes in v27:
time: 36.1 us; the launch traced here: 35.7 us
  starting transfers between devices  15.9 us (44%)
  Pallas kernels  13.3 us (37%)
  waiting for transfers between devices  4.47 us (12%)
  other arithmetic  2.05 us (6%)
    all_to_all x2, starting transfers between devices, exchange(): lax.all_to_all(array, axes, split_axis=0, concat_axis=0, axis_index_group...  13.8 us
    pallas_call x1, Pallas kernels, local(): pl.pallas_call(functools.partial(sweep, steps), out_shape=(f32(height, pl...  6.23 us
    all_to_all x2, waiting for transfers between devices, exchange(): lax.all_to_all(array, axes, split_axis=0, concat_axis=0, axis_index_group...  4.47 us
    pallas_call x1, Pallas kernels, local(): pl.pallas_call(functools.partial(force, steps, halo, height, width), out_...  2.9 us
    pallas_call x1, Pallas kernels, local(): pl.pallas_call(functools.partial(smooth, halo, order), out_shape=(f32(hei...  1.42 us
    ppermute x1, starting transfers between devices, local(): right = lax.ppermute(west, 'lon', [(i + 1, i) for i in range(lons - 1)])  1.29 us
    mul x1, other arithmetic, local(): (courant * 0.5) ** 2 * jnp.maximum(depth + surface, depth_floor) * keep  1.29 us
    pallas_call x1, Pallas kernels, local(): pl.pallas_call(finish, out_shape=f32(height, width), in_specs=vmem(3), ou...  0.96 us
  transfers between devices with their start and end apart: 5, of which 2 were waited for; matrix products, arithmetic and copies ran while one was open for 2% of the time, Pallas kernels for 17%

profile of v27, /device:TPU:0, one launch (start us, length us, event | category | flops | bytes accessed | tf_op | source)
XLA Modules:
  0.0 35.7 jit_solution(14384535885014218760)
XLA Ops:
  0.0 1.3 %multiply_multiply_fusion = (f32[128,512]{1,0:T(8,128)S(1)}, f32[128,512]{1,0:T(8,128)S(1)}) fusion(f32[128,512]{1,0:T(8,128)} %param.9, f32[128,512]{1,0:T(8,128)} %param.10, s32[128,512]{1,0:T(8,128)} %param.12, f32[128,512]{1,0:T(8,128)} %param.11), kind=kLoop, calls=%fused_computation | loop fusion | flops 458752 | bytes 1572864 | tf_op jit(solution)/shard_map/mul | solution.py:450
  1.3 0.1 give_west.1.after_ref
  1.4 1.3 %collective-permute-start = (f32[256,128]{1,0:T(8,128)S(1)}, f32[256,128]{1,0:T(8,128)S(1)}, u32[]{:S(2)}, u32[]{:S(2)}) collective-permute-start(f32[256,128]{1,0:T(8,128)S(1)} %give_west.1.after_ref), channel_id=1, source_target_pairs={{4,0},{8,4},{12,8},{5,1},{9,5},{13,9},{6,2},{10,6},{14,10},{7,3},{... | collective-permute-start | bytes 393224 | tf_op jit(solution)/shard_map/ppermute | solution.py:470
  2.7 0.8 %pad_add_fusion.gauge_ref = f32[5,4,16]{2,1,0:T(4,128)S(1)} fusion(f32[2,4,16]{2,1,0:T(4,128)} %bitcast.7, s32[1,1,8]{2,1,0:T(1,128)} %bitcast.9, s32[1,1,16]{2,1,0:T(1,128)} %bitcast.10, s32[1,1,16]{2,1,0:T(1,128)} %bitcast.11, s32[2,4,16]{2,1,0:T(4,128)} %bitcast.8), kind=kLoop, calls=%fused_computation.2 | loop fusion | flops 1600 | bytes 2464 | tf_op jit(solution)/shard_map/add | solution.py:460
  3.4 0.8 %give_gauges.1 = f32[16,8,128]{2,1,0:T(8,128)} custom-call(f32[5,4,16]{2,1,0:T(4,128)S(1)} %pad_add_fusion.gauge_ref, f32[256,128]{1,0:T(8,128)S(1)} %give_west.1.after_ref), custom_call_target="tpu_custom_call" | custom-call | bytes 10000000 | tf_op jit(solution)/shard_map/give_gauges/pallas_call | solution.py:472
  4.2 8.7 %all-to-all-start = ((f32[16,8,128]{2,1,0:T(8,128)}), f32[16,8,128]{2,1,0:T(8,128)S(1)}, u32[]{:S(2)}, u32[]{:S(2)}) async-start(f32[16,8,128]{2,1,0:T(8,128)} %give_gauges.1), calls=%async_computation | async-start | bytes 131072 | tf_op jit(solution)/shard_map/all_to_all | solution.py:484
  12.9 0.0 collective-permute-done.right_ref
  12.9 0.1 give_rows.1
  13.0 0.1 collective-permute-start.2
  13.1 0.7 %collective-permute-start.1 = (f32[2,32,640]{2,1,0:T(8,128)S(1)}, f32[2,32,640]{2,1,0:T(8,128)S(1)}, u32[]{:S(2)}, u32[]{:S(2)}) collective-permute-start(f32[2,32,640]{2,1,0:T(8,128)S(1)} %get-tuple-element.13.after_ref), channel_id=1, source_target_pairs={{1,2},{2,1},{5,6},{6,5},{9,10},{10,9},{13,14},{14,13},{17,18},{18,... | collective-permute-start | bytes 491528 | tf_op jit(solution)/shard_map/ppermute | solution.py:494
  13.8 0.8 %deal_own.1 = (bf16[640,640]{1,0:T(8,128)(2,1)S(1)}, f32[2,5,128,128]{3,2,1,0:T(8,128)S(1)}) custom-call(f32[128,512]{1,0:T(8,128)S(1)} %get-tuple-element.22.keep_ref, f32[128,512]{1,0:T(8,128)S(1)} %get-tuple-element.21.gain_ref, f32[256,128]{1,0:T(8,128)S(1)} %collective-permute-done.right_ref, f32[2,32,640]{2,1,0:T(8,128)S(1)} %get-tuple-element.13.after_ref), custom_call_target="tpu_custom_call" | custom-call | bytes 4000000 | tf_op jit(solution)/shard_map/deal_own/pallas_call | solution.py:497
  14.6 2.0 %all-to-all-done.parcel_ref = f32[16,8,128]{2,1,0:T(8,128)S(1)} async-done(((f32[16,8,128]{2,1,0:T(8,128)}), f32[16,8,128]{2,1,0:T(8,128)S(1)}, u32[]{:S(2)}, u32[]{:S(2)}) %all-to-all-start) | async-done | bytes 65568 | tf_op jit(solution)/shard_map/all_to_all | solution.py:484
  16.6 2.9 %force.1.force_ref = f32[17,5,200,128]{3,2,1,0:T(8,128)S(1)} custom-call(f32[16,8,128]{2,1,0:T(8,128)S(1)} %all-to-all-done.parcel_ref, bf16[640,640]{1,0:T(8,128)(2,1)S(1)} %get-tuple-element.14.after_ref.deal_ref), custom_call_target="tpu_custom_call" | custom-call | flops 2013265920 | bytes 7864320 | tf_op jit(solution)/shard_map/force/pallas_call | solution.py:510
  19.5 0.0 collective-permute-done.2.near_ref
  19.5 0.0 collective-permute-done.1.far_ref
  19.5 6.2 %sweep.1 = (f32[128,640]{1,0:T(8,128)S(1)}, f32[4,40,128]{2,1,0:T(8,128)}) custom-call(bf16[640,640]{1,0:T(8,128)(2,1)S(1)} %get-tuple-element.14.after_ref.deal_ref, f32[2,5,128,128]{3,2,1,0:T(8,128)S(1)} %get-tuple-element.15.own_ref, f32[2,32,640]{2,1,0:T(8,128)S(1)} %collective-permute-done.1.far_ref, f32[2,32,640]{2,1,0:T(8,128)S(1)} %collective-permute-done.2.near_ref, ...), custom_call_target="tpu_custom_call" | custom-call | tf_op jit(solution)/shard_map/sweep/pallas_call | solution.py:529
  25.8 5.1 %all-to-all-start.1 = ((f32[4,40,128]{2,1,0:T(8,128)}), f32[4,40,128]{2,1,0:T(8,128)S(1)}, u32[]{:S(2)}, u32[]{:S(2)}) async-start(f32[4,40,128]{2,1,0:T(8,128)} %get-tuple-element.20), calls=%async_computation.1 | async-start | bytes 163840 | tf_op jit(solution)/shard_map/all_to_all | solution.py:484
  30.9 1.4 %smooth.1 = (f32[128,512]{1,0:T(8,128)S(1)}, bf16[480,512]{1,0:T(8,128)(2,1)S(1)}) custom-call(f32[128,640]{1,0:T(8,128)S(1)} %get-tuple-element.17.grad_ref), custom_call_target="tpu_custom_call" | custom-call | flops 402653184 | bytes 524288 | tf_op jit(solution)/shard_map/smooth/pallas_call | solution.py:545
  32.3 2.4 %all-to-all-done.1 = f32[4,40,128]{2,1,0:T(8,128)S(1)} async-done(((f32[4,40,128]{2,1,0:T(8,128)}), f32[4,40,128]{2,1,0:T(8,128)S(1)}, u32[]{:S(2)}, u32[]{:S(2)}) %all-to-all-start.1) | async-done | bytes 81952 | tf_op jit(solution)/shard_map/all_to_all | solution.py:484
  34.8 1.0 %finish.1 = f32[128,512]{1,0:T(8,128)} custom-call(f32[128,512]{1,0:T(8,128)S(1)} %get-tuple-element.18.own_ref, bf16[480,512]{1,0:T(8,128)(2,1)S(1)} %get-tuple-element.19.weights_ref, f32[160,128]{1,0:T(8,128)S(1)} %bitcast.6), custom_call_target="tpu_custom_call" | custom-call | tf_op jit(solution)/shard_map/finish/pallas_call | solution.py:557
Async XLA Ops:
  1.4 11.5 %collective-permute-start = (f32[256,128]{1,0:T(8,128)S(1)}, f32[256,128]{1,0:T(8,128)S(1)}, u32[]{:S(2)}, u32[]{:S(2)}) collective-permute-start(f32[256,128]{1,0:T(8,128)S(1)} %give_west.1.after_ref), channel_id=1, source_target_pairs={{4,0},{8,4},{12,8},{5,1},{9,5},{13,9},{6,2},{10,6},{14,10},{7,3},{... | collective-permute-start | bytes 393224 | tf_op jit(solution)/shard_map/ppermute | solution.py:470
  4.2 12.4 %all-to-all-start = ((f32[16,8,128]{2,1,0:T(8,128)}), f32[16,8,128]{2,1,0:T(8,128)S(1)}, u32[]{:S(2)}, u32[]{:S(2)}) async-start(f32[16,8,128]{2,1,0:T(8,128)} %give_gauges.1), calls=%async_computation | async-start | bytes 131072 | tf_op jit(solution)/shard_map/all_to_all | solution.py:484
  13.0 6.5 %collective-permute-start.2 = (f32[2,32,640]{2,1,0:T(8,128)S(1)}, f32[2,32,640]{2,1,0:T(8,128)S(1)}, u32[]{:S(2)}, u32[]{:S(2)}) collective-permute-start(f32[2,32,640]{2,1,0:T(8,128)S(1)} %get-tuple-element.16), channel_id=1, source_target_pairs={{0,1},{1,0},{2,3},{3,2},{4,5},{5,4},{6,7},{7,6},{8,9},{9,8},{10,11... | collective-permute-start | bytes 491528 | tf_op jit(solution)/shard_map/ppermute | solution.py:495
  13.1 6.4 %collective-permute-start.1 = (f32[2,32,640]{2,1,0:T(8,128)S(1)}, f32[2,32,640]{2,1,0:T(8,128)S(1)}, u32[]{:S(2)}, u32[]{:S(2)}) collective-permute-start(f32[2,32,640]{2,1,0:T(8,128)S(1)} %get-tuple-element.13.after_ref), channel_id=1, source_target_pairs={{1,2},{2,1},{5,6},{6,5},{9,10},{10,9},{13,14},{14,13},{17,18},{18,... | collective-permute-start | bytes 491528 | tf_op jit(solution)/shard_map/ppermute | solution.py:494
  25.8 9.0 %all-to-all-start.1 = ((f32[4,40,128]{2,1,0:T(8,128)}), f32[4,40,128]{2,1,0:T(8,128)S(1)}, u32[]{:S(2)}, u32[]{:S(2)}) async-start(f32[4,40,128]{2,1,0:T(8,128)} %get-tuple-element.20), calls=%async_computation.1 | async-start | bytes 163840 | tf_op jit(solution)/shard_map/all_to_all | solution.py:484

commit v28 on v27

--- a/solution.py
+++ b/solution.py
@@ -193,7 +193,7 @@
         lax.fori_loop(1, groups, more, 0)
 
 
-def deal_own(reach, keep_ref, gain_ref, right_ref, after_ref, deal_ref, own_ref):
+def deal_own(reach, keep_ref, gain_ref, right_ref, after_ref, deal_ref, own_ref, weights_ref):
     height, width = keep_ref.shape
     planes = own_ref.shape[1]
     columns = planes * LANES
@@ -215,9 +215,22 @@
                 at = 2 * kind * height
                 own_ref[kind, c] = piece[at : at + height] + piece[at + height : at + 2 * height]
 
+    halo = reach // 2
+    length = 2.0 * width
+    shape = (16 + halo, planes * LANES)
+    kind = lax.broadcasted_iota(jnp.int32, shape, 0)
+    column = dealt_column(lax.broadcasted_iota(jnp.int32, shape, 1), planes)
+    beyond = column - width
+    off = jnp.where(kind == 0, column, jnp.where(kind == 1, -1 - beyond, jnp.where(kind == 2, beyond, width - 1 - beyond)))
+    mine = ((kind < 2) & (beyond < 0)) | ((kind >= 2) & (kind < 4) & (beyond >= 0))
+    weights = jnp.where(mine, jnp.exp(-jnp.maximum(off, 0).astype(jnp.float32) / length), 0.0)
+    weights = jnp.where((kind >= 8) & (beyond == kind - 8), 1.0, weights)
+    high, low = halves(weights)
+    weights_ref[...] = jnp.concatenate([high, high, low], axis=1)
+
 
 def sweep(
-    steps, deal_ref, own_ref, far_ref, near_ref, force_ref,
+    steps, deal_ref, own_ref, weights_ref, far_ref, near_ref, force_ref,
     grad_ref, sums_ref,
     a, fx, fy, keeps, gains, plain,
 ):
@@ -359,19 +372,10 @@
             strided = pl.ds(8 * q + s, 8, stride=8)
             value = jnp.where(known & (keeps[c, strided, :] > 0.0), a[c, strided, :], 0.0)
             grad_ref[r : r + 8, c * LANES : (c + 1) * LANES] = value
-    length = 2.0 * width
-    shape = (16 + halo, planes * LANES)
-    kind = lax.broadcasted_iota(jnp.int32, shape, 0)
-    column = dealt_column(lax.broadcasted_iota(jnp.int32, shape, 1), planes)
-    beyond = column - width
-    off = jnp.where(kind == 0, column, jnp.where(kind == 1, -1 - beyond, jnp.where(kind == 2, beyond, width - 1 - beyond)))
-    mine = ((kind < 2) & (beyond < 0)) | ((kind >= 2) & (kind < 4) & (beyond >= 0))
-    weights = jnp.where(mine, jnp.exp(-jnp.maximum(off, 0).astype(jnp.float32) / length), 0.0)
-    weights = jnp.where((kind >= 8) & (beyond == kind - 8), 1.0, weights)
-    (w_high, w_low), (g_high, g_low) = halves(weights), halves(grad_ref[...])
+    high, low = halves(grad_ref[...])
     sums = lax.dot_general(
-        jnp.concatenate([w_high, w_high, w_low], axis=1), jnp.concatenate([g_high, g_low, g_high], axis=1),
-        (((1,), (1,)), ((), ())), preferred_element_type=jnp.float32,
+        weights_ref[...], jnp.concatenate([high, low, high], axis=1), (((1,), (1,)), ((), ())),
+        preferred_element_type=jnp.float32,
     )[: 8 + halo]
     for i in range(sums_ref.shape[0]):
         sums_ref[i] = sums
@@ -494,13 +498,14 @@
     far = lax.ppermute(to_far, ROW_AXES, [pair for i in range(1, row_tiles - 1, 2) for pair in ((i, i + 1), (i + 1, i))])
     near = lax.ppermute(to_near, ROW_AXES, [pair for i in range(0, row_tiles, 2) for pair in ((i, i + 1), (i + 1, i))])
 
-    deal, own = pl.pallas_call(
+    deal, own, weights = pl.pallas_call(
         functools.partial(deal_own, 2 * halo),
         out_shape=(
             jax.ShapeDtypeStruct((planes * LANES, planes * LANES), jnp.bfloat16), f32(2, planes, height, LANES),
+            jax.ShapeDtypeStruct((16 + halo, 3 * planes * LANES), jnp.bfloat16),
         ),
         in_specs=vmem(3) + [pl.BlockSpec(memory_space=pl.ANY)],
-        out_specs=tuple(vmem(2)),
+        out_specs=tuple(vmem(3)),
         compiler_params=params,
         cost_estimate=hint(4),
         name="deal_own",
@@ -529,7 +534,7 @@
     grad, sums = pl.pallas_call(
         functools.partial(sweep, steps),
         out_shape=(f32(height, planes * LANES), f32(lons, 8 + halo, height)),
-        in_specs=vmem(5),
+        in_specs=vmem(6),
         out_specs=tuple(vmem(2)),
         scratch_shapes=[plane] * 3 + [
             pltpu.VMEM((planes + 1, spaced(rows_all + 8), LANES), jnp.float32),
@@ -538,7 +543,7 @@
         ],
         compiler_params=params,
         name="sweep",
-    )(deal, own, far, near, pushes)
+    )(deal, own, weights, far, near, pushes)
 
     order = list(range(lons // 2, lons)) + list(range(lons // 2))[::-1]
     sums = exchange(sums, "lon", [order])

time: 36.1 us -> 36.2 us (level)
  no operation moved by 1% of the time
where the time goes in v28:
time: 36.2 us; the launch traced here: 35.8 us
  starting transfers between devices  15.9 us (44%)
  Pallas kernels  13.4 us (37%)
  waiting for transfers between devices  4.43 us (12%)
  other arithmetic  2.05 us (6%)
    all_to_all x2, starting transfers between devices, exchange(): lax.all_to_all(array, axes, split_axis=0, concat_axis=0, axis_index_group...  13.8 us
    pallas_call x1, Pallas kernels, local(): pl.pallas_call(functools.partial(sweep, steps), out_shape=(f32(height, pl...  6.35 us
    all_to_all x2, waiting for transfers between devices, exchange(): lax.all_to_all(array, axes, split_axis=0, concat_axis=0, axis_index_group...  4.43 us
    pallas_call x1, Pallas kernels, local(): pl.pallas_call(functools.partial(force, steps, halo, height, width), out_...  2.9 us
    pallas_call x1, Pallas kernels, local(): pl.pallas_call(functools.partial(smooth, halo, order), out_shape=(f32(hei...  1.42 us
    ppermute x1, starting transfers between devices, local(): right = lax.ppermute(west, 'lon', [(i + 1, i) for i in range(lons - 1)])  1.29 us
    mul x1, other arithmetic, local(): (courant * 0.5) ** 2 * jnp.maximum(depth + surface, depth_floor) * keep  1.29 us
    pallas_call x1, Pallas kernels, local(): pl.pallas_call(finish, out_shape=f32(height, width), in_specs=vmem(3), ou...  0.95 us
  transfers between devices with their start and end apart: 5, of which 2 were waited for; matrix products, arithmetic and copies ran while one was open for 2% of the time, Pallas kernels for 17%

profile of v28, /device:TPU:0, one launch (start us, length us, event | category | flops | bytes accessed | tf_op | source)
XLA Modules:
  0.0 35.8 jit_solution(9748089607400877637)
XLA Ops:
  0.0 1.3 %multiply_multiply_fusion = (f32[128,512]{1,0:T(8,128)S(1)}, f32[128,512]{1,0:T(8,128)S(1)}) fusion(f32[128,512]{1,0:T(8,128)} %param.9, f32[128,512]{1,0:T(8,128)} %param.10, s32[128,512]{1,0:T(8,128)} %param.12, f32[128,512]{1,0:T(8,128)} %param.11), kind=kLoop, calls=%fused_computation | loop fusion | flops 458752 | bytes 1572864 | tf_op jit(solution)/shard_map/mul | solution.py:454
  1.3 0.1 give_west.1.after_ref
  1.4 1.3 %collective-permute-start = (f32[256,128]{1,0:T(8,128)S(1)}, f32[256,128]{1,0:T(8,128)S(1)}, u32[]{:S(2)}, u32[]{:S(2)}) collective-permute-start(f32[256,128]{1,0:T(8,128)S(1)} %give_west.1.after_ref), channel_id=1, source_target_pairs={{4,0},{8,4},{12,8},{5,1},{9,5},{13,9},{6,2},{10,6},{14,10},{7,3},{... | collective-permute-start | bytes 393224 | tf_op jit(solution)/shard_map/ppermute | solution.py:474
  2.7 0.8 %pad_add_fusion.gauge_ref = f32[5,4,16]{2,1,0:T(4,128)S(1)} fusion(f32[2,4,16]{2,1,0:T(4,128)} %bitcast.7, s32[1,1,8]{2,1,0:T(1,128)} %bitcast.9, s32[1,1,16]{2,1,0:T(1,128)} %bitcast.10, s32[1,1,16]{2,1,0:T(1,128)} %bitcast.11, s32[2,4,16]{2,1,0:T(4,128)} %bitcast.8), kind=kLoop, calls=%fused_computation.2 | loop fusion | flops 1600 | bytes 2464 | tf_op jit(solution)/shard_map/add | solution.py:464
  3.4 0.8 %give_gauges.1 = f32[16,8,128]{2,1,0:T(8,128)} custom-call(f32[5,4,16]{2,1,0:T(4,128)S(1)} %pad_add_fusion.gauge_ref, f32[256,128]{1,0:T(8,128)S(1)} %give_west.1.after_ref), custom_call_target="tpu_custom_call" | custom-call | bytes 10000000 | tf_op jit(solution)/shard_map/give_gauges/pallas_call | solution.py:476
  4.2 8.7 %all-to-all-start = ((f32[16,8,128]{2,1,0:T(8,128)}), f32[16,8,128]{2,1,0:T(8,128)S(1)}, u32[]{:S(2)}, u32[]{:S(2)}) async-start(f32[16,8,128]{2,1,0:T(8,128)} %give_gauges.1), calls=%async_computation | async-start | bytes 131072 | tf_op jit(solution)/shard_map/all_to_all | solution.py:488
  12.9 0.0 collective-permute-done.right_ref
  12.9 0.1 give_rows.1
  13.0 0.1 collective-permute-start.2
  13.1 0.7 %collective-permute-start.1 = (f32[2,32,640]{2,1,0:T(8,128)S(1)}, f32[2,32,640]{2,1,0:T(8,128)S(1)}, u32[]{:S(2)}, u32[]{:S(2)}) collective-permute-start(f32[2,32,640]{2,1,0:T(8,128)S(1)} %get-tuple-element.14.after_ref), channel_id=1, source_target_pairs={{1,2},{2,1},{5,6},{6,5},{9,10},{10,9},{13,14},{14,13},{17,18},{18,... | collective-permute-start | bytes 491528 | tf_op jit(solution)/shard_map/ppermute | solution.py:498
  13.8 0.8 %deal_own.1 = (bf16[640,640]{1,0:T(8,128)(2,1)S(1)}, f32[2,5,128,128]{3,2,1,0:T(8,128)S(1)}, bf16[48,1920]{1,0:T(8,128)(2,1)S(1)}) custom-call(f32[128,512]{1,0:T(8,128)S(1)} %get-tuple-element.24.keep_ref, f32[128,512]{1,0:T(8,128)S(1)} %get-tuple-element.23.gain_ref, f32[256,128]{1,0:T(8,128)S(1)} %collective-permute-done.right_ref, ...), custom_call_target="tpu_custom_call" | custom-call | bytes 4000000 | tf_op jit(solution)/shard_map/deal_own/pallas_call | solution.py:501
  14.6 2.0 %all-to-all-done.parcel_ref = f32[16,8,128]{2,1,0:T(8,128)S(1)} async-done(((f32[16,8,128]{2,1,0:T(8,128)}), f32[16,8,128]{2,1,0:T(8,128)S(1)}, u32[]{:S(2)}, u32[]{:S(2)}) %all-to-all-start) | async-done | bytes 65568 | tf_op jit(solution)/shard_map/all_to_all | solution.py:488
  16.6 2.9 %force.1.force_ref = f32[17,5,200,128]{3,2,1,0:T(8,128)S(1)} custom-call(f32[16,8,128]{2,1,0:T(8,128)S(1)} %all-to-all-done.parcel_ref, bf16[640,640]{1,0:T(8,128)(2,1)S(1)} %get-tuple-element.15.after_ref.deal_ref), custom_call_target="tpu_custom_call" | custom-call | flops 2013265920 | bytes 7864320 | tf_op jit(solution)/shard_map/force/pallas_call | solution.py:515
  19.5 0.0 collective-permute-done.2.near_ref
  19.5 0.0 collective-permute-done.1.far_ref
  19.5 6.4 %sweep.1 = (f32[128,640]{1,0:T(8,128)S(1)}, f32[4,40,128]{2,1,0:T(8,128)}) custom-call(bf16[640,640]{1,0:T(8,128)(2,1)S(1)} %get-tuple-element.15.after_ref.deal_ref, f32[2,5,128,128]{3,2,1,0:T(8,128)S(1)} %get-tuple-element.16.own_ref, bf16[48,1920]{1,0:T(8,128)(2,1)S(1)} %get-tuple-element.17.weights_ref, ...), custom_call_target="tpu_custom_call" | custom-call | tf_op jit(solution)/shard_map/sweep/pallas_call | solution.py:534
  25.9 5.1 %all-to-all-start.1 = ((f32[4,40,128]{2,1,0:T(8,128)}), f32[4,40,128]{2,1,0:T(8,128)S(1)}, u32[]{:S(2)}, u32[]{:S(2)}) async-start(f32[4,40,128]{2,1,0:T(8,128)} %get-tuple-element.22), calls=%async_computation.1 | async-start | bytes 163840 | tf_op jit(solution)/shard_map/all_to_all | solution.py:488
  31.0 1.4 %smooth.1 = (f32[128,512]{1,0:T(8,128)S(1)}, bf16[480,512]{1,0:T(8,128)(2,1)S(1)}) custom-call(f32[128,640]{1,0:T(8,128)S(1)} %get-tuple-element.19.grad_ref), custom_call_target="tpu_custom_call" | custom-call | flops 402653184 | bytes 524288 | tf_op jit(solution)/shard_map/smooth/pallas_call | solution.py:550
  32.4 2.4 %all-to-all-done.1 = f32[4,40,128]{2,1,0:T(8,128)S(1)} async-done(((f32[4,40,128]{2,1,0:T(8,128)}), f32[4,40,128]{2,1,0:T(8,128)S(1)}, u32[]{:S(2)}, u32[]{:S(2)}) %all-to-all-start.1) | async-done | bytes 81952 | tf_op jit(solution)/shard_map/all_to_all | solution.py:488
  34.9 1.0 %finish.1 = f32[128,512]{1,0:T(8,128)} custom-call(f32[128,512]{1,0:T(8,128)S(1)} %get-tuple-element.20.own_ref, bf16[480,512]{1,0:T(8,128)(2,1)S(1)} %get-tuple-element.21.weights_ref, f32[160,128]{1,0:T(8,128)S(1)} %bitcast.6), custom_call_target="tpu_custom_call" | custom-call | tf_op jit(solution)/shard_map/finish/pallas_call | solution.py:562
Async XLA Ops:
  1.4 11.5 %collective-permute-start = (f32[256,128]{1,0:T(8,128)S(1)}, f32[256,128]{1,0:T(8,128)S(1)}, u32[]{:S(2)}, u32[]{:S(2)}) collective-permute-start(f32[256,128]{1,0:T(8,128)S(1)} %give_west.1.after_ref), channel_id=1, source_target_pairs={{4,0},{8,4},{12,8},{5,1},{9,5},{13,9},{6,2},{10,6},{14,10},{7,3},{... | collective-permute-start | bytes 393224 | tf_op jit(solution)/shard_map/ppermute | solution.py:474
  4.2 12.4 %all-to-all-start = ((f32[16,8,128]{2,1,0:T(8,128)}), f32[16,8,128]{2,1,0:T(8,128)S(1)}, u32[]{:S(2)}, u32[]{:S(2)}) async-start(f32[16,8,128]{2,1,0:T(8,128)} %give_gauges.1), calls=%async_computation | async-start | bytes 131072 | tf_op jit(solution)/shard_map/all_to_all | solution.py:488
  13.0 6.5 %collective-permute-start.2 = (f32[2,32,640]{2,1,0:T(8,128)S(1)}, f32[2,32,640]{2,1,0:T(8,128)S(1)}, u32[]{:S(2)}, u32[]{:S(2)}) collective-permute-start(f32[2,32,640]{2,1,0:T(8,128)S(1)} %get-tuple-element.18), channel_id=1, source_target_pairs={{0,1},{1,0},{2,3},{3,2},{4,5},{5,4},{6,7},{7,6},{8,9},{9,8},{10,11... | collective-permute-start | bytes 491528 | tf_op jit(solution)/shard_map/ppermute | solution.py:499
  13.1 6.4 %collective-permute-start.1 = (f32[2,32,640]{2,1,0:T(8,128)S(1)}, f32[2,32,640]{2,1,0:T(8,128)S(1)}, u32[]{:S(2)}, u32[]{:S(2)}) collective-permute-start(f32[2,32,640]{2,1,0:T(8,128)S(1)} %get-tuple-element.14.after_ref), channel_id=1, source_target_pairs={{1,2},{2,1},{5,6},{6,5},{9,10},{10,9},{13,14},{14,13},{17,18},{18,... | collective-permute-start | bytes 491528 | tf_op jit(solution)/shard_map/ppermute | solution.py:498
  25.9 9.0 %all-to-all-start.1 = ((f32[4,40,128]{2,1,0:T(8,128)}), f32[4,40,128]{2,1,0:T(8,128)S(1)}, u32[]{:S(2)}, u32[]{:S(2)}) async-start(f32[4,40,128]{2,1,0:T(8,128)} %get-tuple-element.22), calls=%async_computation.1 | async-start | bytes 163840 | tf_op jit(solution)/shard_map/all_to_all | solution.py:488

commit v29 on v28

--- a/solution.py
+++ b/solution.py
@@ -217,16 +217,16 @@
 
     halo = reach // 2
     length = 2.0 * width
-    shape = (16 + halo, planes * LANES)
-    kind = lax.broadcasted_iota(jnp.int32, shape, 0)
-    column = dealt_column(lax.broadcasted_iota(jnp.int32, shape, 1), planes)
+    shape = (planes * LANES, LANES)
+    kind = lax.broadcasted_iota(jnp.int32, shape, 1)
+    column = dealt_column(lax.broadcasted_iota(jnp.int32, shape, 0), planes)
     beyond = column - width
     off = jnp.where(kind == 0, column, jnp.where(kind == 1, -1 - beyond, jnp.where(kind == 2, beyond, width - 1 - beyond)))
     mine = ((kind < 2) & (beyond < 0)) | ((kind >= 2) & (kind < 4) & (beyond >= 0))
     weights = jnp.where(mine, jnp.exp(-jnp.maximum(off, 0).astype(jnp.float32) / length), 0.0)
     weights = jnp.where((kind >= 8) & (beyond == kind - 8), 1.0, weights)
     high, low = halves(weights)
-    weights_ref[...] = jnp.concatenate([high, high, low], axis=1)
+    weights_ref[...] = jnp.concatenate([high, high, low], axis=0)
 
 
 def sweep(
@@ -373,10 +373,10 @@
             value = jnp.where(known & (keeps[c, strided, :] > 0.0), a[c, strided, :], 0.0)
             grad_ref[r : r + 8, c * LANES : (c + 1) * LANES] = value
     high, low = halves(grad_ref[...])
-    sums = lax.dot_general(
-        weights_ref[...], jnp.concatenate([high, low, high], axis=1), (((1,), (1,)), ((), ())),
-        preferred_element_type=jnp.float32,
-    )[: 8 + halo]
+    sums = jnp.dot(
+        jnp.concatenate([high, low, high], axis=1), weights_ref[...], preferred_element_type=jnp.float32
+    )
+    sums = jnp.transpose(sums)[: 8 + halo]
     for i in range(sums_ref.shape[0]):
         sums_ref[i] = sums
 
@@ -502,7 +502,7 @@
         functools.partial(deal_own, 2 * halo),
         out_shape=(
             jax.ShapeDtypeStruct((planes * LANES, planes * LANES), jnp.bfloat16), f32(2, planes, height, LANES),
-            jax.ShapeDtypeStruct((16 + halo, 3 * planes * LANES), jnp.bfloat16),
+            jax.ShapeDtypeStruct((3 * planes * LANES, LANES), jnp.bfloat16),
         ),
         in_specs=vmem(3) + [pl.BlockSpec(memory_space=pl.ANY)],
         out_specs=tuple(vmem(3)),

time: 36.2 us -> 36 us (level)
  transfers between devices with their start and end apart: 5 -> 5, of which waited for: 2 -> 2; matrix products, arithmetic and copies ran while one was open for 2% -> 2% of each run, Pallas kernels for 17% -> 18%
where the time goes in v29:
time: 36 us; the launch traced here: 35.7 us
  starting transfers between devices  15.9 us (44%)
  Pallas kernels  13.5 us (38%)
  waiting for transfers between devices  4.19 us (12%)
  other arithmetic  2.05 us (6%)
    all_to_all x2, starting transfers between devices, exchange(): lax.all_to_all(array, axes, split_axis=0, concat_axis=0, axis_index_group...  13.8 us
    pallas_call x1, Pallas kernels, local(): pl.pallas_call(functools.partial(sweep, steps), out_shape=(f32(height, pl...  6.18 us
    all_to_all x2, waiting for transfers between devices, exchange(): lax.all_to_all(array, axes, split_axis=0, concat_axis=0, axis_index_group...  4.18 us
    pallas_call x1, Pallas kernels, local(): pl.pallas_call(functools.partial(force, steps, halo, height, width), out_...  2.9 us
    pallas_call x1, Pallas kernels, local(): pl.pallas_call(functools.partial(smooth, halo, order), out_shape=(f32(hei...  1.42 us
    ppermute x1, starting transfers between devices, local(): right = lax.ppermute(west, 'lon', [(i + 1, i) for i in range(lons - 1)])  1.29 us
    mul x1, other arithmetic, local(): (courant * 0.5) ** 2 * jnp.maximum(depth + surface, depth_floor) * keep  1.29 us
    pallas_call x1, Pallas kernels, local(): pl.pallas_call(functools.partial(deal_own, 2 * halo), out_shape=(jax.Shap...  1.05 us
  transfers between devices with their start and end apart: 5, of which 2 were waited for; matrix products, arithmetic and copies ran while one was open for 2% of the time, Pallas kernels for 18%

profile of v29, /device:TPU:0, one launch (start us, length us, event | category | flops | bytes accessed | tf_op | source)
XLA Modules:
  0.0 35.7 jit_solution(3187589112894526006)
XLA Ops:
  0.0 1.3 %multiply_multiply_fusion = (f32[128,512]{1,0:T(8,128)S(1)}, f32[128,512]{1,0:T(8,128)S(1)}) fusion(f32[128,512]{1,0:T(8,128)} %param.9, f32[128,512]{1,0:T(8,128)} %param.10, s32[128,512]{1,0:T(8,128)} %param.12, f32[128,512]{1,0:T(8,128)} %param.11), kind=kLoop, calls=%fused_computation | loop fusion | flops 458752 | bytes 1572864 | tf_op jit(solution)/shard_map/mul | solution.py:454
  1.3 0.1 give_west.1.after_ref
  1.4 1.3 %collective-permute-start = (f32[256,128]{1,0:T(8,128)S(1)}, f32[256,128]{1,0:T(8,128)S(1)}, u32[]{:S(2)}, u32[]{:S(2)}) collective-permute-start(f32[256,128]{1,0:T(8,128)S(1)} %give_west.1.after_ref), channel_id=1, source_target_pairs={{4,0},{8,4},{12,8},{5,1},{9,5},{13,9},{6,2},{10,6},{14,10},{7,3},{... | collective-permute-start | bytes 393224 | tf_op jit(solution)/shard_map/ppermute | solution.py:474
  2.7 0.8 %pad_add_fusion.gauge_ref = f32[5,4,16]{2,1,0:T(4,128)S(1)} fusion(f32[2,4,16]{2,1,0:T(4,128)} %bitcast.7, s32[1,1,8]{2,1,0:T(1,128)} %bitcast.9, s32[1,1,16]{2,1,0:T(1,128)} %bitcast.10, s32[1,1,16]{2,1,0:T(1,128)} %bitcast.11, s32[2,4,16]{2,1,0:T(4,128)} %bitcast.8), kind=kLoop, calls=%fused_computation.2 | loop fusion | flops 1600 | bytes 2464 | tf_op jit(solution)/shard_map/add | solution.py:464
  3.4 0.8 %give_gauges.1 = f32[16,8,128]{2,1,0:T(8,128)} custom-call(f32[5,4,16]{2,1,0:T(4,128)S(1)} %pad_add_fusion.gauge_ref, f32[256,128]{1,0:T(8,128)S(1)} %give_west.1.after_ref), custom_call_target="tpu_custom_call" | custom-call | bytes 10000000 | tf_op jit(solution)/shard_map/give_gauges/pallas_call | solution.py:476
  4.2 8.7 %all-to-all-start = ((f32[16,8,128]{2,1,0:T(8,128)}), f32[16,8,128]{2,1,0:T(8,128)S(1)}, u32[]{:S(2)}, u32[]{:S(2)}) async-start(f32[16,8,128]{2,1,0:T(8,128)} %give_gauges.1), calls=%async_computation | async-start | bytes 131072 | tf_op jit(solution)/shard_map/all_to_all | solution.py:488
  12.9 0.0 collective-permute-done.right_ref
  12.9 0.1 give_rows.1
  13.0 0.1 collective-permute-start.2
  13.1 0.7 %collective-permute-start.1 = (f32[2,32,640]{2,1,0:T(8,128)S(1)}, f32[2,32,640]{2,1,0:T(8,128)S(1)}, u32[]{:S(2)}, u32[]{:S(2)}) collective-permute-start(f32[2,32,640]{2,1,0:T(8,128)S(1)} %get-tuple-element.14.after_ref), channel_id=1, source_target_pairs={{1,2},{2,1},{5,6},{6,5},{9,10},{10,9},{13,14},{14,13},{17,18},{18,... | collective-permute-start | bytes 491528 | tf_op jit(solution)/shard_map/ppermute | solution.py:498
  13.8 1.0 %deal_own.1 = (bf16[640,640]{1,0:T(8,128)(2,1)S(1)}, f32[2,5,128,128]{3,2,1,0:T(8,128)S(1)}, bf16[1920,128]{1,0:T(8,128)(2,1)S(1)}) custom-call(f32[128,512]{1,0:T(8,128)S(1)} %get-tuple-element.24.keep_ref, f32[128,512]{1,0:T(8,128)S(1)} %get-tuple-element.23.gain_ref, f32[256,128]{1,0:T(8,128)S(1)} %collective-permute-done.right_ref, ...), custom_call_target="tpu_custom_call" | custom-call | bytes 4000000 | tf_op jit(solution)/shard_map/deal_own/pallas_call | solution.py:501
  14.8 1.7 %all-to-all-done.parcel_ref = f32[16,8,128]{2,1,0:T(8,128)S(1)} async-done(((f32[16,8,128]{2,1,0:T(8,128)}), f32[16,8,128]{2,1,0:T(8,128)S(1)}, u32[]{:S(2)}, u32[]{:S(2)}) %all-to-all-start) | async-done | bytes 65568 | tf_op jit(solution)/shard_map/all_to_all | solution.py:488
  16.6 2.9 %force.1.force_ref = f32[17,5,200,128]{3,2,1,0:T(8,128)S(1)} custom-call(f32[16,8,128]{2,1,0:T(8,128)S(1)} %all-to-all-done.parcel_ref, bf16[640,640]{1,0:T(8,128)(2,1)S(1)} %get-tuple-element.15.after_ref.deal_ref), custom_call_target="tpu_custom_call" | custom-call | flops 2013265920 | bytes 7864320 | tf_op jit(solution)/shard_map/force/pallas_call | solution.py:515
  19.5 0.0 collective-permute-done.2.near_ref
  19.5 0.0 collective-permute-done.1.far_ref
  19.5 6.2 %sweep.1 = (f32[128,640]{1,0:T(8,128)S(1)}, f32[4,40,128]{2,1,0:T(8,128)}) custom-call(bf16[640,640]{1,0:T(8,128)(2,1)S(1)} %get-tuple-element.15.after_ref.deal_ref, f32[2,5,128,128]{3,2,1,0:T(8,128)S(1)} %get-tuple-element.16.own_ref, bf16[1920,128]{1,0:T(8,128)(2,1)S(1)} %get-tuple-element.17.weights_ref, ...), custom_call_target="tpu_custom_call" | custom-call | tf_op jit(solution)/shard_map/sweep/pallas_call | solution.py:534
  25.7 5.1 %all-to-all-start.1 = ((f32[4,40,128]{2,1,0:T(8,128)}), f32[4,40,128]{2,1,0:T(8,128)S(1)}, u32[]{:S(2)}, u32[]{:S(2)}) async-start(f32[4,40,128]{2,1,0:T(8,128)} %get-tuple-element.22), calls=%async_computation.1 | async-start | bytes 163840 | tf_op jit(solution)/shard_map/all_to_all | solution.py:488
  30.8 1.4 %smooth.1 = (f32[128,512]{1,0:T(8,128)S(1)}, bf16[480,512]{1,0:T(8,128)(2,1)S(1)}) custom-call(f32[128,640]{1,0:T(8,128)S(1)} %get-tuple-element.19.grad_ref), custom_call_target="tpu_custom_call" | custom-call | flops 402653184 | bytes 524288 | tf_op jit(solution)/shard_map/smooth/pallas_call | solution.py:550
  32.3 2.4 %all-to-all-done.1 = f32[4,40,128]{2,1,0:T(8,128)S(1)} async-done(((f32[4,40,128]{2,1,0:T(8,128)}), f32[4,40,128]{2,1,0:T(8,128)S(1)}, u32[]{:S(2)}, u32[]{:S(2)}) %all-to-all-start.1) | async-done | bytes 81952 | tf_op jit(solution)/shard_map/all_to_all | solution.py:488
  34.7 1.0 %finish.1 = f32[128,512]{1,0:T(8,128)} custom-call(f32[128,512]{1,0:T(8,128)S(1)} %get-tuple-element.20.own_ref, bf16[480,512]{1,0:T(8,128)(2,1)S(1)} %get-tuple-element.21.weights_ref, f32[160,128]{1,0:T(8,128)S(1)} %bitcast.6), custom_call_target="tpu_custom_call" | custom-call | tf_op jit(solution)/shard_map/finish/pallas_call | solution.py:562
Async XLA Ops:
  1.4 11.5 %collective-permute-start = (f32[256,128]{1,0:T(8,128)S(1)}, f32[256,128]{1,0:T(8,128)S(1)}, u32[]{:S(2)}, u32[]{:S(2)}) collective-permute-start(f32[256,128]{1,0:T(8,128)S(1)} %give_west.1.after_ref), channel_id=1, source_target_pairs={{4,0},{8,4},{12,8},{5,1},{9,5},{13,9},{6,2},{10,6},{14,10},{7,3},{... | collective-permute-start | bytes 393224 | tf_op jit(solution)/shard_map/ppermute | solution.py:474
  4.2 12.4 %all-to-all-start = ((f32[16,8,128]{2,1,0:T(8,128)}), f32[16,8,128]{2,1,0:T(8,128)S(1)}, u32[]{:S(2)}, u32[]{:S(2)}) async-start(f32[16,8,128]{2,1,0:T(8,128)} %give_gauges.1), calls=%async_computation | async-start | bytes 131072 | tf_op jit(solution)/shard_map/all_to_all | solution.py:488
  13.0 6.5 %collective-permute-start.2 = (f32[2,32,640]{2,1,0:T(8,128)S(1)}, f32[2,32,640]{2,1,0:T(8,128)S(1)}, u32[]{:S(2)}, u32[]{:S(2)}) collective-permute-start(f32[2,32,640]{2,1,0:T(8,128)S(1)} %get-tuple-element.18), channel_id=1, source_target_pairs={{0,1},{1,0},{2,3},{3,2},{4,5},{5,4},{6,7},{7,6},{8,9},{9,8},{10,11... | collective-permute-start | bytes 491528 | tf_op jit(solution)/shard_map/ppermute | solution.py:499
  13.1 6.4 %collective-permute-start.1 = (f32[2,32,640]{2,1,0:T(8,128)S(1)}, f32[2,32,640]{2,1,0:T(8,128)S(1)}, u32[]{:S(2)}, u32[]{:S(2)}) collective-permute-start(f32[2,32,640]{2,1,0:T(8,128)S(1)} %get-tuple-element.14.after_ref), channel_id=1, source_target_pairs={{1,2},{2,1},{5,6},{6,5},{9,10},{10,9},{13,14},{14,13},{17,18},{18,... | collective-permute-start | bytes 491528 | tf_op jit(solution)/shard_map/ppermute | solution.py:498
  25.7 9.0 %all-to-all-start.1 = ((f32[4,40,128]{2,1,0:T(8,128)}), f32[4,40,128]{2,1,0:T(8,128)S(1)}, u32[]{:S(2)}, u32[]{:S(2)}) async-start(f32[4,40,128]{2,1,0:T(8,128)} %get-tuple-element.22), calls=%async_computation.1 | async-start | bytes 163840 | tf_op jit(solution)/shard_map/all_to_all | solution.py:488

commit v30 on v29

--- a/solution.py
+++ b/solution.py
@@ -488,7 +488,14 @@
         return lax.all_to_all(array, axes, split_axis=0, concat_axis=0, axis_index_groups=groups, tiled=True)
 
     rank = {row_tiles - 1: 1, 0: 2}
-    group = sorted(range(tiles), key=lambda tile: (rank.get(tile % row_tiles, 0), -(tile // row_tiles)))
+    inside = list(range(lons))[::-1]
+    ends = list(range(1, lons - 1))[::-1] + [lons - 1, 0]
+
+    def place(tile):
+        row, lon = tile % row_tiles, tile // row_tiles
+        return rank.get(row, 0), (ends if row in rank else inside).index(lon)
+
+    group = sorted(range(tiles), key=place)
     parcel = exchange(parcel, GRID_AXES, [group])
 
     to_far, to_near = pl.pallas_call(

time: 36 us -> 36.3 us (level)
  transfers between devices with their start and end apart: 5 -> 5, of which waited for: 2 -> 2; matrix products, arithmetic and copies ran while one was open for 2% -> 2% of each run, Pallas kernels for 18% -> 17%
where the time goes in v30:
time: 36.3 us; the launch traced here: 35.9 us
  starting transfers between devices  15.9 us (44%)
  Pallas kernels  13.5 us (37%)
  waiting for transfers between devices  4.39 us (12%)
  other arithmetic  2.05 us (6%)
    all_to_all x2, starting transfers between devices, exchange(): lax.all_to_all(array, axes, split_axis=0, concat_axis=0, axis_index_group...  13.9 us
    pallas_call x1, Pallas kernels, local(): pl.pallas_call(functools.partial(sweep, steps), out_shape=(f32(height, pl...  6.18 us
    all_to_all x2, waiting for transfers between devices, exchange(): lax.all_to_all(array, axes, split_axis=0, concat_axis=0, axis_index_group...  4.38 us
    pallas_call x1, Pallas kernels, local(): pl.pallas_call(functools.partial(force, steps, halo, height, width), out_...  2.9 us
    pallas_call x1, Pallas kernels, local(): pl.pallas_call(functools.partial(smooth, halo, order), out_shape=(f32(hei...  1.42 us
    ppermute x1, starting transfers between devices, local(): right = lax.ppermute(west, 'lon', [(i + 1, i) for i in range(lons - 1)])  1.29 us
    mul x1, other arithmetic, local(): (courant * 0.5) ** 2 * jnp.maximum(depth + surface, depth_floor) * keep  1.29 us
    pallas_call x1, Pallas kernels, local(): pl.pallas_call(functools.partial(deal_own, 2 * halo), out_shape=(jax.Shap...  1.05 us
  transfers between devices with their start and end apart: 5, of which 2 were waited for; matrix products, arithmetic and copies ran while one was open for 2% of the time, Pallas kernels for 17%

profile of v30, /device:TPU:0, one launch (start us, length us, event | category | flops | bytes accessed | tf_op | source)
XLA Modules:
  0.0 35.9 jit_solution(895990227144243705)
XLA Ops:
  0.0 1.3 %multiply_multiply_fusion = (f32[128,512]{1,0:T(8,128)S(1)}, f32[128,512]{1,0:T(8,128)S(1)}) fusion(f32[128,512]{1,0:T(8,128)} %param.9, f32[128,512]{1,0:T(8,128)} %param.10, s32[128,512]{1,0:T(8,128)} %param.12, f32[128,512]{1,0:T(8,128)} %param.11), kind=kLoop, calls=%fused_computation | loop fusion | flops 458752 | bytes 1572864 | tf_op jit(solution)/shard_map/mul | solution.py:454
  1.3 0.1 give_west.1.after_ref
  1.4 1.3 %collective-permute-start = (f32[256,128]{1,0:T(8,128)S(1)}, f32[256,128]{1,0:T(8,128)S(1)}, u32[]{:S(2)}, u32[]{:S(2)}) collective-permute-start(f32[256,128]{1,0:T(8,128)S(1)} %give_west.1.after_ref), channel_id=1, source_target_pairs={{4,0},{8,4},{12,8},{5,1},{9,5},{13,9},{6,2},{10,6},{14,10},{7,3},{... | collective-permute-start | bytes 393224 | tf_op jit(solution)/shard_map/ppermute | solution.py:474
  2.7 0.8 %pad_add_fusion.gauge_ref = f32[5,4,16]{2,1,0:T(4,128)S(1)} fusion(f32[2,4,16]{2,1,0:T(4,128)} %bitcast.7, s32[1,1,8]{2,1,0:T(1,128)} %bitcast.9, s32[1,1,16]{2,1,0:T(1,128)} %bitcast.10, s32[1,1,16]{2,1,0:T(1,128)} %bitcast.11, s32[2,4,16]{2,1,0:T(4,128)} %bitcast.8), kind=kLoop, calls=%fused_computation.2 | loop fusion | flops 1600 | bytes 2464 | tf_op jit(solution)/shard_map/add | solution.py:464
  3.4 0.8 %give_gauges.1 = f32[16,8,128]{2,1,0:T(8,128)} custom-call(f32[5,4,16]{2,1,0:T(4,128)S(1)} %pad_add_fusion.gauge_ref, f32[256,128]{1,0:T(8,128)S(1)} %give_west.1.after_ref), custom_call_target="tpu_custom_call" | custom-call | bytes 10000000 | tf_op jit(solution)/shard_map/give_gauges/pallas_call | solution.py:476
  4.2 8.7 %all-to-all-start = ((f32[16,8,128]{2,1,0:T(8,128)}), f32[16,8,128]{2,1,0:T(8,128)S(1)}, u32[]{:S(2)}, u32[]{:S(2)}) async-start(f32[16,8,128]{2,1,0:T(8,128)} %give_gauges.1), calls=%async_computation | async-start | bytes 131072 | tf_op jit(solution)/shard_map/all_to_all | solution.py:488
  12.9 0.0 collective-permute-done.right_ref
  12.9 0.1 give_rows.1
  13.0 0.1 collective-permute-start.2
  13.1 0.7 %collective-permute-start.1 = (f32[2,32,640]{2,1,0:T(8,128)S(1)}, f32[2,32,640]{2,1,0:T(8,128)S(1)}, u32[]{:S(2)}, u32[]{:S(2)}) collective-permute-start(f32[2,32,640]{2,1,0:T(8,128)S(1)} %get-tuple-element.14.after_ref), channel_id=1, source_target_pairs={{1,2},{2,1},{5,6},{6,5},{9,10},{10,9},{13,14},{14,13},{17,18},{18,... | collective-permute-start | bytes 491528 | tf_op jit(solution)/shard_map/ppermute | solution.py:505
  13.8 1.0 %deal_own.1 = (bf16[640,640]{1,0:T(8,128)(2,1)S(1)}, f32[2,5,128,128]{3,2,1,0:T(8,128)S(1)}, bf16[1920,128]{1,0:T(8,128)(2,1)S(1)}) custom-call(f32[128,512]{1,0:T(8,128)S(1)} %get-tuple-element.24.keep_ref, f32[128,512]{1,0:T(8,128)S(1)} %get-tuple-element.23.gain_ref, f32[256,128]{1,0:T(8,128)S(1)} %collective-permute-done.right_ref, ...), custom_call_target="tpu_custom_call" | custom-call | bytes 4000000 | tf_op jit(solution)/shard_map/deal_own/pallas_call | solution.py:508
  14.8 2.0 %all-to-all-done.parcel_ref = f32[16,8,128]{2,1,0:T(8,128)S(1)} async-done(((f32[16,8,128]{2,1,0:T(8,128)}), f32[16,8,128]{2,1,0:T(8,128)S(1)}, u32[]{:S(2)}, u32[]{:S(2)}) %all-to-all-start) | async-done | bytes 65568 | tf_op jit(solution)/shard_map/all_to_all | solution.py:488
  16.8 2.9 %force.1.force_ref = f32[17,5,200,128]{3,2,1,0:T(8,128)S(1)} custom-call(f32[16,8,128]{2,1,0:T(8,128)S(1)} %all-to-all-done.parcel_ref, bf16[640,640]{1,0:T(8,128)(2,1)S(1)} %get-tuple-element.15.after_ref.deal_ref), custom_call_target="tpu_custom_call" | custom-call | flops 2013265920 | bytes 7864320 | tf_op jit(solution)/shard_map/force/pallas_call | solution.py:522
  19.7 0.0 collective-permute-done.2.near_ref
  19.7 0.0 collective-permute-done.1.far_ref
  19.7 6.2 %sweep.1 = (f32[128,640]{1,0:T(8,128)S(1)}, f32[4,40,128]{2,1,0:T(8,128)}) custom-call(bf16[640,640]{1,0:T(8,128)(2,1)S(1)} %get-tuple-element.15.after_ref.deal_ref, f32[2,5,128,128]{3,2,1,0:T(8,128)S(1)} %get-tuple-element.16.own_ref, bf16[1920,128]{1,0:T(8,128)(2,1)S(1)} %get-tuple-element.17.weights_ref, ...), custom_call_target="tpu_custom_call" | custom-call | tf_op jit(solution)/shard_map/sweep/pallas_call | solution.py:541
  25.9 5.2 %all-to-all-start.1 = ((f32[4,40,128]{2,1,0:T(8,128)}), f32[4,40,128]{2,1,0:T(8,128)S(1)}, u32[]{:S(2)}, u32[]{:S(2)}) async-start(f32[4,40,128]{2,1,0:T(8,128)} %get-tuple-element.22), calls=%async_computation.1 | async-start | bytes 163840 | tf_op jit(solution)/shard_map/all_to_all | solution.py:488
  31.1 1.4 %smooth.1 = (f32[128,512]{1,0:T(8,128)S(1)}, bf16[480,512]{1,0:T(8,128)(2,1)S(1)}) custom-call(f32[128,640]{1,0:T(8,128)S(1)} %get-tuple-element.19.grad_ref), custom_call_target="tpu_custom_call" | custom-call | flops 402653184 | bytes 524288 | tf_op jit(solution)/shard_map/smooth/pallas_call | solution.py:557
  32.5 2.4 %all-to-all-done.1 = f32[4,40,128]{2,1,0:T(8,128)S(1)} async-done(((f32[4,40,128]{2,1,0:T(8,128)}), f32[4,40,128]{2,1,0:T(8,128)S(1)}, u32[]{:S(2)}, u32[]{:S(2)}) %all-to-all-start.1) | async-done | bytes 81952 | tf_op jit(solution)/shard_map/all_to_all | solution.py:488
  35.0 1.0 %finish.1 = f32[128,512]{1,0:T(8,128)} custom-call(f32[128,512]{1,0:T(8,128)S(1)} %get-tuple-element.20.own_ref, bf16[480,512]{1,0:T(8,128)(2,1)S(1)} %get-tuple-element.21.weights_ref, f32[160,128]{1,0:T(8,128)S(1)} %bitcast.6), custom_call_target="tpu_custom_call" | custom-call | tf_op jit(solution)/shard_map/finish/pallas_call | solution.py:569
Async XLA Ops:
  1.4 11.5 %collective-permute-start = (f32[256,128]{1,0:T(8,128)S(1)}, f32[256,128]{1,0:T(8,128)S(1)}, u32[]{:S(2)}, u32[]{:S(2)}) collective-permute-start(f32[256,128]{1,0:T(8,128)S(1)} %give_west.1.after_ref), channel_id=1, source_target_pairs={{4,0},{8,4},{12,8},{5,1},{9,5},{13,9},{6,2},{10,6},{14,10},{7,3},{... | collective-permute-start | bytes 393224 | tf_op jit(solution)/shard_map/ppermute | solution.py:474
  4.2 12.6 %all-to-all-start = ((f32[16,8,128]{2,1,0:T(8,128)}), f32[16,8,128]{2,1,0:T(8,128)S(1)}, u32[]{:S(2)}, u32[]{:S(2)}) async-start(f32[16,8,128]{2,1,0:T(8,128)} %give_gauges.1), calls=%async_computation | async-start | bytes 131072 | tf_op jit(solution)/shard_map/all_to_all | solution.py:488
  13.0 6.7 %collective-permute-start.2 = (f32[2,32,640]{2,1,0:T(8,128)S(1)}, f32[2,32,640]{2,1,0:T(8,128)S(1)}, u32[]{:S(2)}, u32[]{:S(2)}) collective-permute-start(f32[2,32,640]{2,1,0:T(8,128)S(1)} %get-tuple-element.18), channel_id=1, source_target_pairs={{0,1},{1,0},{2,3},{3,2},{4,5},{5,4},{6,7},{7,6},{8,9},{9,8},{10,11... | collective-permute-start | bytes 491528 | tf_op jit(solution)/shard_map/ppermute | solution.py:506
  13.1 6.6 %collective-permute-start.1 = (f32[2,32,640]{2,1,0:T(8,128)S(1)}, f32[2,32,640]{2,1,0:T(8,128)S(1)}, u32[]{:S(2)}, u32[]{:S(2)}) collective-permute-start(f32[2,32,640]{2,1,0:T(8,128)S(1)} %get-tuple-element.14.after_ref), channel_id=1, source_target_pairs={{1,2},{2,1},{5,6},{6,5},{9,10},{10,9},{13,14},{14,13},{17,18},{18,... | collective-permute-start | bytes 491528 | tf_op jit(solution)/shard_map/ppermute | solution.py:505
  25.9 9.1 %all-to-all-start.1 = ((f32[4,40,128]{2,1,0:T(8,128)}), f32[4,40,128]{2,1,0:T(8,128)S(1)}, u32[]{:S(2)}, u32[]{:S(2)}) async-start(f32[4,40,128]{2,1,0:T(8,128)} %get-tuple-element.22), calls=%async_computation.1 | async-start | bytes 163840 | tf_op jit(solution)/shard_map/all_to_all | solution.py:488

commit v31 on v29

--- a/solution.py
+++ b/solution.py
@@ -468,7 +468,7 @@
         + put(coastal_tiles.reshape(1, 1, coast_count), 2 * blocks, 2)
     ).astype(jnp.float32) + put(jnp.transpose(gauge_resid, (1, 2, 0)), blocks, 0)
     west = pl.pallas_call(
-        functools.partial(give_west, 2 * halo), out_shape=f32(2 * height, LANES), in_specs=vmem(2), out_specs=vmem(1)[0],
+        functools.partial(give_west, 2 * halo), out_shape=f32(height + 64, LANES), in_specs=vmem(2), out_specs=vmem(1)[0],
         compiler_params=params, name="give_west",
     )(keep, gain)
     right = lax.ppermute(west, "lon", [(i + 1, i) for i in range(lons - 1)])

time: 36 us -> 38.8 us (1.078)
  the two profiles are of different devices: /device:TPU:0 before, /device:TPU:1 now
where the time goes in v31:
time: 38.8 us; the launch traced here: 38.4 us
  starting transfers between devices  16.8 us (43%)
  Pallas kernels  13.5 us (35%)
  waiting for transfers between devices  6.08 us (16%)
  other arithmetic  2.05 us (5%)
    all_to_all x2, starting transfers between devices, exchange(): lax.all_to_all(array, axes, split_axis=0, concat_axis=0, axis_index_group...  11.1 us
    pallas_call x1, Pallas kernels, local(): pl.pallas_call(functools.partial(sweep, steps), out_shape=(f32(height, pl...  6.18 us
    ppermute x1, waiting for transfers between devices, local(): right = lax.ppermute(west, 'lon', [(i + 1, i) for i in range(lons - 1)])  4.5 us
    ppermute x1, starting transfers between devices, local(): lax.ppermute(to_far, ROW_AXES, [pair for i in range(1, row_tiles - 1, 2)...  3.04 us
    pallas_call x1, Pallas kernels, local(): pl.pallas_call(functools.partial(force, steps, halo, height, width), out_...  2.9 us
    all_to_all x2, waiting for transfers between devices, exchange(): lax.all_to_all(array, axes, split_axis=0, concat_axis=0, axis_index_group...  1.57 us
    pallas_call x1, Pallas kernels, local(): pl.pallas_call(functools.partial(smooth, halo, order), out_shape=(f32(hei...  1.42 us
    ppermute x1, starting transfers between devices, local(): lax.ppermute(to_near, ROW_AXES, [pair for i in range(0, row_tiles, 2) for...  1.34 us
  transfers between devices with their start and end apart: 5, of which 2 were waited for; matrix products, arithmetic and copies ran while one was open for 0% of the time, Pallas kernels for 14%

profile of v31, /device:TPU:1, one launch (start us, length us, event | category | flops | bytes accessed | tf_op | source)
XLA Modules:
  0.0 38.4 jit_solution(15432187461921447751)
XLA Ops:
  0.0 1.3 %multiply_multiply_fusion = (f32[128,512]{1,0:T(8,128)S(1)}, f32[128,512]{1,0:T(8,128)S(1)}) fusion(f32[128,512]{1,0:T(8,128)} %param.9, f32[128,512]{1,0:T(8,128)} %param.10, s32[128,512]{1,0:T(8,128)} %param.12, f32[128,512]{1,0:T(8,128)} %param.11), kind=kLoop, calls=%fused_computation | loop fusion | flops 458752 | bytes 1572864 | tf_op jit(solution)/shard_map/mul | solution.py:454
  1.3 0.1 give_west.1.after_ref
  1.4 0.8 %pad_add_fusion.gauge_ref = f32[5,4,16]{2,1,0:T(4,128)S(1)} fusion(f32[2,4,16]{2,1,0:T(4,128)} %bitcast.7, s32[1,1,8]{2,1,0:T(1,128)} %bitcast.9, s32[1,1,16]{2,1,0:T(1,128)} %bitcast.10, s32[1,1,16]{2,1,0:T(1,128)} %bitcast.11, s32[2,4,16]{2,1,0:T(4,128)} %bitcast.8), kind=kLoop, calls=%fused_computation.2 | loop fusion | flops 1600 | bytes 2464 | tf_op jit(solution)/shard_map/add | solution.py:464
  2.1 0.8 %give_gauges.1 = f32[16,8,128]{2,1,0:T(8,128)} custom-call(f32[5,4,16]{2,1,0:T(4,128)S(1)} %pad_add_fusion.gauge_ref, f32[192,128]{1,0:T(8,128)S(1)} %give_west.1.after_ref), custom_call_target="tpu_custom_call" | custom-call | bytes 10000000 | tf_op jit(solution)/shard_map/give_gauges/pallas_call | solution.py:476
  2.9 7.5 %all-to-all-start = ((f32[16,8,128]{2,1,0:T(8,128)}), f32[16,8,128]{2,1,0:T(8,128)S(1)}, u32[]{:S(2)}, u32[]{:S(2)}) async-start(f32[16,8,128]{2,1,0:T(8,128)} %give_gauges.1), calls=%async_computation | async-start | bytes 131072 | tf_op jit(solution)/shard_map/all_to_all | solution.py:488
  10.4 1.3 %collective-permute-start = (f32[192,128]{1,0:T(8,128)S(1)}, f32[192,128]{1,0:T(8,128)S(1)}, u32[]{:S(2)}, u32[]{:S(2)}) collective-permute-start(f32[192,128]{1,0:T(8,128)S(1)} %give_west.1.after_ref), channel_id=1, source_target_pairs={{4,0},{8,4},{12,8},{5,1},{9,5},{13,9},{6,2},{10,6},{14,10},{7,3},{... | collective-permute-start | bytes 294920 | tf_op jit(solution)/shard_map/ppermute | solution.py:474
  11.7 4.5 %collective-permute-done.right_ref = f32[192,128]{1,0:T(8,128)S(1)} collective-permute-done((f32[192,128]{1,0:T(8,128)S(1)}, f32[192,128]{1,0:T(8,128)S(1)}, u32[]{:S(2)}, u32[]{:S(2)}) %collective-permute-start) | collective-permute-done | bytes 98336 | tf_op jit(solution)/shard_map/ppermute | solution.py:474
  16.2 0.1 give_rows.1
  16.3 1.3 %collective-permute-start.2 = (f32[2,32,640]{2,1,0:T(8,128)S(1)}, f32[2,32,640]{2,1,0:T(8,128)S(1)}, u32[]{:S(2)}, u32[]{:S(2)}) collective-permute-start(f32[2,32,640]{2,1,0:T(8,128)S(1)} %get-tuple-element.18), channel_id=1, source_target_pairs={{0,1},{1,0},{2,3},{3,2},{4,5},{5,4},{6,7},{7,6},{8,9},{9,8},{10,11... | collective-permute-start | bytes 491528 | tf_op jit(solution)/shard_map/ppermute | solution.py:499
  17.6 3.0 %collective-permute-start.1 = (f32[2,32,640]{2,1,0:T(8,128)S(1)}, f32[2,32,640]{2,1,0:T(8,128)S(1)}, u32[]{:S(2)}, u32[]{:S(2)}) collective-permute-start(f32[2,32,640]{2,1,0:T(8,128)S(1)} %get-tuple-element.14.after_ref), channel_id=1, source_target_pairs={{1,2},{2,1},{5,6},{6,5},{9,10},{10,9},{13,14},{14,13},{17,18},{18,... | collective-permute-start | bytes 491528 | tf_op jit(solution)/shard_map/ppermute | solution.py:498
  20.7 1.0 %deal_own.1 = (bf16[640,640]{1,0:T(8,128)(2,1)S(1)}, f32[2,5,128,128]{3,2,1,0:T(8,128)S(1)}, bf16[1920,128]{1,0:T(8,128)(2,1)S(1)}) custom-call(f32[128,512]{1,0:T(8,128)S(1)} %get-tuple-element.24.keep_ref, f32[128,512]{1,0:T(8,128)S(1)} %get-tuple-element.23.gain_ref, f32[192,128]{1,0:T(8,128)S(1)} %collective-permute-done.right_ref, ...), custom_call_target="tpu_custom_call" | custom-call | bytes 4000000 | tf_op jit(solution)/shard_map/deal_own/pallas_call | solution.py:501
  21.7 0.0 all-to-all-done.parcel_ref
  21.8 2.9 %force.1.force_ref = f32[17,5,200,128]{3,2,1,0:T(8,128)S(1)} custom-call(f32[16,8,128]{2,1,0:T(8,128)S(1)} %all-to-all-done.parcel_ref, bf16[640,640]{1,0:T(8,128)(2,1)S(1)} %get-tuple-element.15.after_ref.deal_ref), custom_call_target="tpu_custom_call" | custom-call | flops 2013265920 | bytes 7864320 | tf_op jit(solution)/shard_map/force/pallas_call | solution.py:515
  24.7 0.0 collective-permute-done.2.near_ref
  24.7 0.0 collective-permute-done.1.far_ref
  24.7 6.2 %sweep.1 = (f32[128,640]{1,0:T(8,128)S(1)}, f32[4,40,128]{2,1,0:T(8,128)}) custom-call(bf16[640,640]{1,0:T(8,128)(2,1)S(1)} %get-tuple-element.15.after_ref.deal_ref, f32[2,5,128,128]{3,2,1,0:T(8,128)S(1)} %get-tuple-element.16.own_ref, bf16[1920,128]{1,0:T(8,128)(2,1)S(1)} %get-tuple-element.17.weights_ref, ...), custom_call_target="tpu_custom_call" | custom-call | tf_op jit(solution)/shard_map/sweep/pallas_call | solution.py:534
  30.9 3.6 %all-to-all-start.1 = ((f32[4,40,128]{2,1,0:T(8,128)}), f32[4,40,128]{2,1,0:T(8,128)S(1)}, u32[]{:S(2)}, u32[]{:S(2)}) async-start(f32[4,40,128]{2,1,0:T(8,128)} %get-tuple-element.22), calls=%async_computation.1 | async-start | bytes 163840 | tf_op jit(solution)/shard_map/all_to_all | solution.py:488
  34.5 1.4 %smooth.1 = (f32[128,512]{1,0:T(8,128)S(1)}, bf16[480,512]{1,0:T(8,128)(2,1)S(1)}) custom-call(f32[128,640]{1,0:T(8,128)S(1)} %get-tuple-element.19.grad_ref), custom_call_target="tpu_custom_call" | custom-call | flops 402653184 | bytes 524288 | tf_op jit(solution)/shard_map/smooth/pallas_call | solution.py:550
  35.9 1.6 %all-to-all-done.1 = f32[4,40,128]{2,1,0:T(8,128)S(1)} async-done(((f32[4,40,128]{2,1,0:T(8,128)}), f32[4,40,128]{2,1,0:T(8,128)S(1)}, u32[]{:S(2)}, u32[]{:S(2)}) %all-to-all-start.1) | async-done | bytes 81952 | tf_op jit(solution)/shard_map/all_to_all | solution.py:488
  37.5 1.0 %finish.1 = f32[128,512]{1,0:T(8,128)} custom-call(f32[128,512]{1,0:T(8,128)S(1)} %get-tuple-element.20.own_ref, bf16[480,512]{1,0:T(8,128)(2,1)S(1)} %get-tuple-element.21.weights_ref, f32[160,128]{1,0:T(8,128)S(1)} %bitcast.6), custom_call_target="tpu_custom_call" | custom-call | tf_op jit(solution)/shard_map/finish/pallas_call | solution.py:562
Async XLA Ops:
  2.9 18.8 %all-to-all-start = ((f32[16,8,128]{2,1,0:T(8,128)}), f32[16,8,128]{2,1,0:T(8,128)S(1)}, u32[]{:S(2)}, u32[]{:S(2)}) async-start(f32[16,8,128]{2,1,0:T(8,128)} %give_gauges.1), calls=%async_computation | async-start | bytes 131072 | tf_op jit(solution)/shard_map/all_to_all | solution.py:488
  10.4 5.8 %collective-permute-start = (f32[192,128]{1,0:T(8,128)S(1)}, f32[192,128]{1,0:T(8,128)S(1)}, u32[]{:S(2)}, u32[]{:S(2)}) collective-permute-start(f32[192,128]{1,0:T(8,128)S(1)} %give_west.1.after_ref), channel_id=1, source_target_pairs={{4,0},{8,4},{12,8},{5,1},{9,5},{13,9},{6,2},{10,6},{14,10},{7,3},{... | collective-permute-start | bytes 294920 | tf_op jit(solution)/shard_map/ppermute | solution.py:474
  16.3 8.4 %collective-permute-start.2 = (f32[2,32,640]{2,1,0:T(8,128)S(1)}, f32[2,32,640]{2,1,0:T(8,128)S(1)}, u32[]{:S(2)}, u32[]{:S(2)}) collective-permute-start(f32[2,32,640]{2,1,0:T(8,128)S(1)} %get-tuple-element.18), channel_id=1, source_target_pairs={{0,1},{1,0},{2,3},{3,2},{4,5},{5,4},{6,7},{7,6},{8,9},{9,8},{10,11... | collective-permute-start | bytes 491528 | tf_op jit(solution)/shard_map/ppermute | solution.py:499
  17.6 7.0 %collective-permute-start.1 = (f32[2,32,640]{2,1,0:T(8,128)S(1)}, f32[2,32,640]{2,1,0:T(8,128)S(1)}, u32[]{:S(2)}, u32[]{:S(2)}) collective-permute-start(f32[2,32,640]{2,1,0:T(8,128)S(1)} %get-tuple-element.14.after_ref), channel_id=1, source_target_pairs={{1,2},{2,1},{5,6},{6,5},{9,10},{10,9},{13,14},{14,13},{17,18},{18,... | collective-permute-start | bytes 491528 | tf_op jit(solution)/shard_map/ppermute | solution.py:498
  30.9 6.6 %all-to-all-start.1 = ((f32[4,40,128]{2,1,0:T(8,128)}), f32[4,40,128]{2,1,0:T(8,128)S(1)}, u32[]{:S(2)}, u32[]{:S(2)}) async-start(f32[4,40,128]{2,1,0:T(8,128)} %get-tuple-element.22), calls=%async_computation.1 | async-start | bytes 163840 | tf_op jit(solution)/shard_map/all_to_all | solution.py:488

commit v32 on v29

--- a/solution.py
+++ b/solution.py
@@ -180,7 +180,6 @@
         else:
             lax.fori_loop(0, steps // LEVELS, one, 0)
 
-    force_ref[steps] = jnp.zeros_like(force_ref[steps])
     gather_gauges(0)
     levels(False)
     if groups > 1:
@@ -293,8 +292,8 @@
     for row, there in ((halo - 1, has_top), (halo + height, has_bottom)):
         row_mask[row % blocks] = jnp.where(sublane == row // blocks, jnp.where(there, 1.0, 0.0), 1.0)
 
-    def step(index, carry, opening=False):
-        level = jnp.where(index < steps - 1, steps - 2 - index, steps)
+    def step(index, carry, opening=False, closing=False):
+        level = steps - 2 - index
         near, ahead, new_y, beside, total, behind = {}, {}, {}, {}, {}, {}
 
         def rows(q):
@@ -326,8 +325,8 @@
                 new_x = [new_x[c] + keep[c + 1] * fx[c, rows(q), :] for c in every]
             behind[q] = [roll_lanes(value, 1) for value in new_x[-2:]] + new_x[:-2]
             before = new_y[q - 2] if q >= 2 else [down(fy[c, rows(q - 2 + blocks), :]) for c in every]
-            push = [force_ref[level, c, rows(q), :] for c in every]
-            total[q] = [(near[q][c] + push[c]) + (new_y[q][c] - before[c]) + new_x[c] for c in every]
+            total[q] = near[q] if closing else [near[q][c] + force_ref[level, c, rows(q), :] for c in every]
+            total[q] = [total[q][c] + (new_y[q][c] - before[c]) + new_x[c] for c in every]
             for c in every:
                 fx[c, rows(q), :] = new_x[c]
 
@@ -361,7 +360,8 @@
         return carry
 
     step(0, 0, opening=True)
-    lax.fori_loop(1, steps, step, 0)
+    lax.fori_loop(1, steps - 1, step, 0)
+    step(steps - 1, 0, closing=True)
 
     start = jnp.where(my_lon > 0, halo, 0)
     for c in every:
@@ -514,7 +514,7 @@
     wide = max(2 * LANES, owned)
     pushes = pl.pallas_call(
         functools.partial(force, steps, halo, height, width),
-        out_shape=f32(steps + 1, planes, spaced(rows_all), LANES),
+        out_shape=f32(steps, planes, spaced(rows_all), LANES),
         in_specs=vmem(1) + [pl.BlockSpec(memory_space=pl.ANY)],
         out_specs=vmem(1)[0],
         scratch_shapes=[

time: 36 us -> 35.9 us (level)
  transfers between devices with their start and end apart: 5 -> 5, of which waited for: 2 -> 2; matrix products, arithmetic and copies ran while one was open for 2% -> 2% of each run, Pallas kernels for 18% -> 17%
where the time goes in v32:
time: 35.9 us; the launch traced here: 35.6 us
  starting transfers between devices  15.9 us (44%)
  Pallas kernels  13.4 us (37%)
  waiting for transfers between devices  4.19 us (12%)
  other arithmetic  2.05 us (6%)
    all_to_all x2, starting transfers between devices, exchange(): lax.all_to_all(array, axes, split_axis=0, concat_axis=0, axis_index_group...  13.8 us
    pallas_call x1, Pallas kernels, local(): pl.pallas_call(functools.partial(sweep, steps), out_shape=(f32(height, pl...  6.15 us
    all_to_all x2, waiting for transfers between devices, exchange(): lax.all_to_all(array, axes, split_axis=0, concat_axis=0, axis_index_group...  4.18 us
    pallas_call x1, Pallas kernels, local(): pl.pallas_call(functools.partial(force, steps, halo, height, width), out_...  2.86 us
    pallas_call x1, Pallas kernels, local(): pl.pallas_call(functools.partial(smooth, halo, order), out_shape=(f32(hei...  1.42 us
    ppermute x1, starting transfers between devices, local(): right = lax.ppermute(west, 'lon', [(i + 1, i) for i in range(lons - 1)])  1.29 us
    mul x1, other arithmetic, local(): (courant * 0.5) ** 2 * jnp.maximum(depth + surface, depth_floor) * keep  1.29 us
    pallas_call x1, Pallas kernels, local(): pl.pallas_call(functools.partial(deal_own, 2 * halo), out_shape=(jax.Shap...  1.05 us
  transfers between devices with their start and end apart: 5, of which 2 were waited for; matrix products, arithmetic and copies ran while one was open for 2% of the time, Pallas kernels for 17%

profile of v32, /device:TPU:0, one launch (start us, length us, event | category | flops | bytes accessed | tf_op | source)
XLA Modules:
  0.0 35.6 jit_solution(2125118884860375691)
XLA Ops:
  0.0 1.3 %multiply_multiply_fusion = (f32[128,512]{1,0:T(8,128)S(1)}, f32[128,512]{1,0:T(8,128)S(1)}) fusion(f32[128,512]{1,0:T(8,128)} %param.9, f32[128,512]{1,0:T(8,128)} %param.10, s32[128,512]{1,0:T(8,128)} %param.12, f32[128,512]{1,0:T(8,128)} %param.11), kind=kLoop, calls=%fused_computation | loop fusion | flops 458752 | bytes 1572864 | tf_op jit(solution)/shard_map/mul | solution.py:454
  1.3 0.1 give_west.1.after_ref
  1.4 1.3 %collective-permute-start = (f32[256,128]{1,0:T(8,128)S(1)}, f32[256,128]{1,0:T(8,128)S(1)}, u32[]{:S(2)}, u32[]{:S(2)}) collective-permute-start(f32[256,128]{1,0:T(8,128)S(1)} %give_west.1.after_ref), channel_id=1, source_target_pairs={{4,0},{8,4},{12,8},{5,1},{9,5},{13,9},{6,2},{10,6},{14,10},{7,3},{... | collective-permute-start | bytes 393224 | tf_op jit(solution)/shard_map/ppermute | solution.py:474
  2.7 0.8 %pad_add_fusion.gauge_ref = f32[5,4,16]{2,1,0:T(4,128)S(1)} fusion(f32[2,4,16]{2,1,0:T(4,128)} %bitcast.7, s32[1,1,8]{2,1,0:T(1,128)} %bitcast.9, s32[1,1,16]{2,1,0:T(1,128)} %bitcast.10, s32[1,1,16]{2,1,0:T(1,128)} %bitcast.11, s32[2,4,16]{2,1,0:T(4,128)} %bitcast.8), kind=kLoop, calls=%fused_computation.2 | loop fusion | flops 1600 | bytes 2464 | tf_op jit(solution)/shard_map/add | solution.py:464
  3.4 0.8 %give_gauges.1 = f32[16,8,128]{2,1,0:T(8,128)} custom-call(f32[5,4,16]{2,1,0:T(4,128)S(1)} %pad_add_fusion.gauge_ref, f32[256,128]{1,0:T(8,128)S(1)} %give_west.1.after_ref), custom_call_target="tpu_custom_call" | custom-call | bytes 10000000 | tf_op jit(solution)/shard_map/give_gauges/pallas_call | solution.py:476
  4.2 8.7 %all-to-all-start = ((f32[16,8,128]{2,1,0:T(8,128)}), f32[16,8,128]{2,1,0:T(8,128)S(1)}, u32[]{:S(2)}, u32[]{:S(2)}) async-start(f32[16,8,128]{2,1,0:T(8,128)} %give_gauges.1), calls=%async_computation | async-start | bytes 131072 | tf_op jit(solution)/shard_map/all_to_all | solution.py:488
  12.9 0.0 collective-permute-done.right_ref
  12.9 0.1 give_rows.1
  13.0 0.1 collective-permute-start.2
  13.1 0.7 %collective-permute-start.1 = (f32[2,32,640]{2,1,0:T(8,128)S(1)}, f32[2,32,640]{2,1,0:T(8,128)S(1)}, u32[]{:S(2)}, u32[]{:S(2)}) collective-permute-start(f32[2,32,640]{2,1,0:T(8,128)S(1)} %get-tuple-element.14.after_ref), channel_id=1, source_target_pairs={{1,2},{2,1},{5,6},{6,5},{9,10},{10,9},{13,14},{14,13},{17,18},{18,... | collective-permute-start | bytes 491528 | tf_op jit(solution)/shard_map/ppermute | solution.py:498
  13.8 1.0 %deal_own.1 = (bf16[640,640]{1,0:T(8,128)(2,1)S(1)}, f32[2,5,128,128]{3,2,1,0:T(8,128)S(1)}, bf16[1920,128]{1,0:T(8,128)(2,1)S(1)}) custom-call(f32[128,512]{1,0:T(8,128)S(1)} %get-tuple-element.24.keep_ref, f32[128,512]{1,0:T(8,128)S(1)} %get-tuple-element.23.gain_ref, f32[256,128]{1,0:T(8,128)S(1)} %collective-permute-done.right_ref, ...), custom_call_target="tpu_custom_call" | custom-call | bytes 4000000 | tf_op jit(solution)/shard_map/deal_own/pallas_call | solution.py:501
  14.8 1.7 %all-to-all-done.parcel_ref = f32[16,8,128]{2,1,0:T(8,128)S(1)} async-done(((f32[16,8,128]{2,1,0:T(8,128)}), f32[16,8,128]{2,1,0:T(8,128)S(1)}, u32[]{:S(2)}, u32[]{:S(2)}) %all-to-all-start) | async-done | bytes 65568 | tf_op jit(solution)/shard_map/all_to_all | solution.py:488
  16.6 2.9 %force.1.force_ref = f32[16,5,200,128]{3,2,1,0:T(8,128)S(1)} custom-call(f32[16,8,128]{2,1,0:T(8,128)S(1)} %all-to-all-done.parcel_ref, bf16[640,640]{1,0:T(8,128)(2,1)S(1)} %get-tuple-element.15.after_ref.deal_ref), custom_call_target="tpu_custom_call" | custom-call | flops 2013265920 | bytes 7864320 | tf_op jit(solution)/shard_map/force/pallas_call | solution.py:515
  19.5 0.0 collective-permute-done.2.near_ref
  19.5 0.0 collective-permute-done.1.far_ref
  19.5 6.2 %sweep.1 = (f32[128,640]{1,0:T(8,128)S(1)}, f32[4,40,128]{2,1,0:T(8,128)}) custom-call(bf16[640,640]{1,0:T(8,128)(2,1)S(1)} %get-tuple-element.15.after_ref.deal_ref, f32[2,5,128,128]{3,2,1,0:T(8,128)S(1)} %get-tuple-element.16.own_ref, bf16[1920,128]{1,0:T(8,128)(2,1)S(1)} %get-tuple-element.17.weights_ref, ...), custom_call_target="tpu_custom_call" | custom-call | tf_op jit(solution)/shard_map/sweep/pallas_call | solution.py:534
  25.6 5.1 %all-to-all-start.1 = ((f32[4,40,128]{2,1,0:T(8,128)}), f32[4,40,128]{2,1,0:T(8,128)S(1)}, u32[]{:S(2)}, u32[]{:S(2)}) async-start(f32[4,40,128]{2,1,0:T(8,128)} %get-tuple-element.22), calls=%async_computation.1 | async-start | bytes 163840 | tf_op jit(solution)/shard_map/all_to_all | solution.py:488
  30.8 1.4 %smooth.1 = (f32[128,512]{1,0:T(8,128)S(1)}, bf16[480,512]{1,0:T(8,128)(2,1)S(1)}) custom-call(f32[128,640]{1,0:T(8,128)S(1)} %get-tuple-element.19.grad_ref), custom_call_target="tpu_custom_call" | custom-call | flops 402653184 | bytes 524288 | tf_op jit(solution)/shard_map/smooth/pallas_call | solution.py:550
  32.2 2.4 %all-to-all-done.1 = f32[4,40,128]{2,1,0:T(8,128)S(1)} async-done(((f32[4,40,128]{2,1,0:T(8,128)}), f32[4,40,128]{2,1,0:T(8,128)S(1)}, u32[]{:S(2)}, u32[]{:S(2)}) %all-to-all-start.1) | async-done | bytes 81952 | tf_op jit(solution)/shard_map/all_to_all | solution.py:488
  34.6 1.0 %finish.1 = f32[128,512]{1,0:T(8,128)} custom-call(f32[128,512]{1,0:T(8,128)S(1)} %get-tuple-element.20.own_ref, bf16[480,512]{1,0:T(8,128)(2,1)S(1)} %get-tuple-element.21.weights_ref, f32[160,128]{1,0:T(8,128)S(1)} %bitcast.6), custom_call_target="tpu_custom_call" | custom-call | tf_op jit(solution)/shard_map/finish/pallas_call | solution.py:562
Async XLA Ops:
  1.4 11.5 %collective-permute-start = (f32[256,128]{1,0:T(8,128)S(1)}, f32[256,128]{1,0:T(8,128)S(1)}, u32[]{:S(2)}, u32[]{:S(2)}) collective-permute-start(f32[256,128]{1,0:T(8,128)S(1)} %give_west.1.after_ref), channel_id=1, source_target_pairs={{4,0},{8,4},{12,8},{5,1},{9,5},{13,9},{6,2},{10,6},{14,10},{7,3},{... | collective-permute-start | bytes 393224 | tf_op jit(solution)/shard_map/ppermute | solution.py:474
  4.2 12.4 %all-to-all-start = ((f32[16,8,128]{2,1,0:T(8,128)}), f32[16,8,128]{2,1,0:T(8,128)S(1)}, u32[]{:S(2)}, u32[]{:S(2)}) async-start(f32[16,8,128]{2,1,0:T(8,128)} %give_gauges.1), calls=%async_computation | async-start | bytes 131072 | tf_op jit(solution)/shard_map/all_to_all | solution.py:488
  13.0 6.4 %collective-permute-start.2 = (f32[2,32,640]{2,1,0:T(8,128)S(1)}, f32[2,32,640]{2,1,0:T(8,128)S(1)}, u32[]{:S(2)}, u32[]{:S(2)}) collective-permute-start(f32[2,32,640]{2,1,0:T(8,128)S(1)} %get-tuple-element.18), channel_id=1, source_target_pairs={{0,1},{1,0},{2,3},{3,2},{4,5},{5,4},{6,7},{7,6},{8,9},{9,8},{10,11... | collective-permute-start | bytes 491528 | tf_op jit(solution)/shard_map/ppermute | solution.py:499
  13.1 6.3 %collective-permute-start.1 = (f32[2,32,640]{2,1,0:T(8,128)S(1)}, f32[2,32,640]{2,1,0:T(8,128)S(1)}, u32[]{:S(2)}, u32[]{:S(2)}) collective-permute-start(f32[2,32,640]{2,1,0:T(8,128)S(1)} %get-tuple-element.14.after_ref), channel_id=1, source_target_pairs={{1,2},{2,1},{5,6},{6,5},{9,10},{10,9},{13,14},{14,13},{17,18},{18,... | collective-permute-start | bytes 491528 | tf_op jit(solution)/shard_map/ppermute | solution.py:498
  25.6 9.0 %all-to-all-start.1 = ((f32[4,40,128]{2,1,0:T(8,128)}), f32[4,40,128]{2,1,0:T(8,128)S(1)}, u32[]{:S(2)}, u32[]{:S(2)}) async-start(f32[4,40,128]{2,1,0:T(8,128)} %get-tuple-element.22), calls=%async_computation.1 | async-start | bytes 163840 | tf_op jit(solution)/shard_map/all_to_all | solution.py:488
